TPU v7x, 32 devices: a whole 2x2x4 slice. The times are simulated.
32 devices in a mesh: atom: 16 (over z, y, x), chan: 2 (over core).
Axes of the slice: x: 2, y: 2, z: 4, core: 2. Of those that a mesh axis runs over, the one named last changes fastest.
Arguments:
- features: bfloat16 [128, 49, 4096], P('chan', None, 'atom'), may hold values from -6 to 6
- weights: bfloat16 [3, 7, 128, 128], P(None, None, None, 'chan'), may hold values from -2 to 2
- cotangent: bfloat16 [128, 49, 4096], P('chan', None, 'atom'), may hold values from -6 to 6
- edge_bias: float32 [8, 16, 4096], P('chan', None, 'atom'), may hold values from -5 to 5
- neighbours: int32 [16, 4096], P(None, 'atom'), may hold values from 0 to 4095, as said below
- valid_mask: int32 [16, 4096], P(None, 'atom'), may hold values from 0 to 1, as said below
Outputs:
- grad_features: bfloat16 [128, 49, 4096], P('chan', None, 'atom')
- grad_weights: float32 [3, 7, 128, 128], P(None, None, None, 'chan')
- grad_bias: float32 [8, 16, 4096], P('chan', None, 'atom')
Inputs may be any that keep to these rules, and one draw needn't show every extreme that they name: neighbours[s, a] = (a + o) mod 4096 with -128 <= o <= 128; offsets of -128 and 128 both occur, and slot 0 always holds (a - 1) mod 4096. `valid_mask`: slot 0 of every atom is valid; the share of valid slots rises along the atom order from about a quarter to nearly all.
All inputs are finite; a program needn't handle non-finite values.
Results may differ from a plain program's by a relative error of at most 0.005.
The roundings to bfloat16 on the way count: a program that leaves them out, or rounds other values in their place, can miss the bound.
Values may be sent and summed in bfloat16 or wider, within the bound.
No kernel may reach another device: no remote copies, remote signals or barrier semaphores. Data moves between devices by JAX's collectives and lax.ppermute only.
A program may use at most 128 MiB of HBM per device.

v0:
```python
import math

import jax
import jax.numpy as jnp
from jax import lax
from jax.sharding import PartitionSpec as P

LMAX = 6
HALO = 128


soft_cap = 10.0
highest = lax.Precision.HIGHEST


def extended_2(cells, sides, width):
    for axis, dim in sides:
        count = lax.axis_size(axis)
        head = lax.slice_in_dim(cells, 0, width, axis=dim)
        tail = lax.slice_in_dim(cells, cells.shape[dim] - width, cells.shape[dim], axis=dim)
        cells = jnp.concatenate(
            [
                lax.ppermute(tail, axis, [(i, (i + 1) % count) for i in range(count)]),
                cells,
                lax.ppermute(head, axis, [((i + 1) % count, i) for i in range(count)]),
            ],
            axis=dim,
        )
    return cells


def shifted(value, axis, steps):
    count = lax.axis_size(axis)
    pairs = [(source, (source + steps) % count) for source in range(count)]
    return lax.ppermute(value, axis, pairs)


def degree_bounds():
    return [(degree * degree, (degree + 1) * (degree + 1)) for degree in range(LMAX + 1)]


def on_device(features, weights, cotangent, edge_bias, neighbours, valid_mask):
    chan_local = features.shape[0]
    comps = features.shape[1]
    atoms_dev = features.shape[2]
    heads_local = edge_bias.shape[0]
    head_rows = chan_local // heads_local * comps
    score_scale = 1.0 / math.sqrt(head_rows)
    total_atoms = atoms_dev * lax.axis_size("atom")
    extended = atoms_dev + 2 * HALO
    gathered = lax.all_gather(features, "chan", axis=0, tiled=True)
    projected = jnp.concatenate(
        [
            jnp.einsum(
                "cma,gcd->gdma",
                gathered[:, low_comp:high_comp],
                weights[:, degree],
                preferred_element_type=jnp.float32,
            )
            for degree, (low_comp, high_comp) in enumerate(degree_bounds())
        ],
        axis=2,
    ).astype(jnp.bfloat16)
    keyval = extended_2(projected[1:3], (("atom", 3),), HALO)
    keyval = keyval.reshape(2, heads_local, head_rows, extended)
    query_all = projected[0].reshape(heads_local, head_rows, atoms_dev)
    grad_out = cotangent.reshape(heads_local, head_rows, atoms_dev)
    first_atom = lax.axis_index("atom") * atoms_dev
    local_index = (neighbours - first_atom + HALO) % total_atoms
    slot_table = jnp.where(
        local_index[:, None, :] == jnp.arange(extended, dtype=jnp.int32)[None, :, None],
        jnp.float32(1.0),
        jnp.float32(0.0),
    )
    live_slots = valid_mask > 0
    query_grads = []
    scatter_list = []
    logit_grads = []
    for head in range(heads_local):
        query_h = query_all[head]
        grad_h = grad_out[head]
        keys_h = keyval[0, head]
        values_h = keyval[1, head]
        query_keys = jnp.einsum("fa,fj->aj", query_h, keys_h, preferred_element_type=jnp.float32)
        grad_values = jnp.einsum("fa,fj->aj", grad_h, values_h, preferred_element_type=jnp.float32)
        raw_score = score_scale * jnp.einsum(
            "aj,sja->sa", query_keys, slot_table, precision=highest
        )
        squashed = jnp.tanh(raw_score / soft_cap)
        logits = soft_cap * squashed + edge_bias[head]
        exp_logit = jnp.where(live_slots, jnp.exp(logits), jnp.float32(0.0))
        attention = exp_logit / jnp.sum(exp_logit, axis=0, keepdims=True)
        grad_attn = jnp.einsum("aj,sja->sa", grad_values, slot_table, precision=highest)
        grad_logit = attention * (grad_attn - jnp.sum(attention * grad_attn, axis=0, keepdims=True))
        grad_raw = score_scale * grad_logit * (1.0 - squashed * squashed)
        raw_spread = jnp.einsum("sa,sja->ja", grad_raw, slot_table, precision=highest)
        attn_spread = jnp.einsum("sa,sja->ja", attention, slot_table, precision=highest)
        grad_query = jnp.einsum(
            "fj,ja->fa", keys_h.astype(jnp.float32), raw_spread, precision=highest
        )
        key_sums = jnp.einsum(
            "fa,ja->fj", query_h.astype(jnp.float32), raw_spread, precision=highest
        )
        value_sums = jnp.einsum(
            "fa,ja->fj", grad_h.astype(jnp.float32), attn_spread, precision=highest
        )
        query_grads.append(grad_query)
        scatter_list.append(jnp.stack([key_sums, value_sums]))
        logit_grads.append(grad_logit)
    sums_all = jnp.stack(scatter_list, axis=1)
    own_rows = sums_all[..., HALO : HALO + atoms_dev]
    left_rim = sums_all[..., :HALO]
    right_rim = sums_all[..., HALO + atoms_dev :]
    from_next = shifted(left_rim, "atom", -1)
    from_prev = shifted(right_rim.astype(jnp.bfloat16), "atom", 1).astype(right_rim.dtype)
    own_rows = own_rows.at[..., :HALO].add(from_prev)
    own_rows = own_rows.at[..., atoms_dev - HALO :].add(from_next)
    grads = jnp.stack([jnp.stack(query_grads), own_rows[0], own_rows[1]]).astype(jnp.bfloat16)
    grads = grads.reshape(3, chan_local, comps, atoms_dev)
    weight_terms = jnp.stack(
        [
            jnp.einsum(
                "cma,gdma->gcd",
                gathered[:, low_comp:high_comp],
                grads[:, :, low_comp:high_comp],
                preferred_element_type=jnp.float32,
            )
            for low_comp, high_comp in degree_bounds()
        ],
        axis=1,
    )
    grad_weights = lax.psum(weight_terms, "atom")
    grad_features = lax.psum_scatter(
        jnp.concatenate(
            [
                jnp.einsum(
                    "gcd,gdma->cma",
                    weights[:, degree],
                    grads[:, :, low_comp:high_comp],
                    preferred_element_type=jnp.float32,
                )
                for degree, (low_comp, high_comp) in enumerate(degree_bounds())
            ],
            axis=1,
        ),
        "chan",
        scatter_dimension=0,
        tiled=True,
    )
    return (grad_features.astype(jnp.bfloat16), grad_weights, jnp.stack(logit_grads))


def solution(mesh):
    in_specs = (
        P("chan", None, "atom"),
        P(None, None, None, "chan"),
        P("chan", None, "atom"),
        P("chan", None, "atom"),
        P(None, "atom"),
        P(None, "atom"),
    )
    out_specs = (P("chan", None, "atom"), P(None, None, None, "chan"), P("chan", None, "atom"))
    return jax.shard_map(
        on_device, mesh=mesh, in_specs=in_specs, out_specs=out_specs, check_vma=False
    )
```

profile of v0, /device:TPU:0, one launch (start us, length us, event | category | flops | bytes accessed | tf_op | source)
XLA Modules:
  0.0 450.1 jit_solution(4430102171855474438)
XLA Ops:
  8.0 16.6 %all-gather.2.cloned.1.call-done = bf16[128,49,256]{2,0,1:T(8,128)(2,1)} async-done(((bf16[64,49,256]{2,0,1:T(8,128)(2,1)}), bf16[128,49,256]{2,0,1:T(8,128)(2,1)}) %all-gather.2.cloned.1.call-update) | async-done | bytes 3211280 | tf_op jit(solution)/shard_map/all_gather | solution.py:51
  25.5 1.2 fusion.43
  26.7 1.3 fusion.41
  28.0 1.3 fusion.39
  29.4 1.4 fusion.37
  30.8 1.5 fusion.35
  32.4 1.6 fusion.34
  34.0 2.6 fusion.171
  37.2 1.7 collective-permute-start
  38.9 3.9 collective-permute-start.1
  47.0 2.1 slice.297
  49.1 2.5 fusion.170
  52.5 1.9 squeeze.96
  54.4 1.9 copy.91
  56.3 1.9 squeeze.111
  58.2 1.9 copy.89
  60.1 1.9 squeeze.106
  62.0 1.9 copy.87
  63.9 1.9 squeeze.101
  65.8 42.6 %collective-permute-done = bf16[2,64,49,128]{3,1,2,0:T(8,128)(2,1)} collective-permute-done((bf16[2,64,49,128]{3,1,2,0:T(8,128)(2,1)}, bf16[2,64,49,128]{3,1,2,0:T(8,128)(2,1)}, u32[]{:S(2)}, u32[]{:S(2)}) %collective-permute-start) | collective-permute-done | bytes 1605664 | tf_op jit(solution)/shard_map/ppermute | solution.py:23
  108.4 1.9 collective-permute-done.1
  110.4 3.7 pad_maximum_fusion.1
  114.0 26.7 %copy.84 = bf16[2,64,49,512]{3,0,2,1:T(2,128)(2,1)S(1)} copy(bf16[2,64,49,512]{3,1,2,0:T(8,128)(2,1)S(1)} %pad_maximum_fusion.1) | data formatting | bytes 12845056 | tf_op jit(solution)/shard_map/concatenate | solution.py:21
  140.7 9.3 %fusion.169 = (bf16[1,1,784,512]{3,0,2,1:T(2,128)(2,1)S(1)}, bf16[1,1,784,512]{3,0,2,1:T(2,128)(2,1)S(1)}, bf16[1,1,784,512]{3,0,2,1:T(2,128)(2,1)S(1)}, bf16[1,...) fusion(bf16[2,4,784,512]{3,0,2,1:T(2,128)(2,1)S(1)} %bitcast.588), kind=kLoop, calls=%fused_computation.252 | loop fusion | bytes 12845056 | tf_op jit(solution)/shard_map/slice | solution.py:82
  154.5 8.8 %fusion.25 = (f32[256,16]{0,1:T(8,128)S(1)}, f32[256,16]{0,1:T(8,128)S(1)}, f32[256,16]{0,1:T(8,128)S(1)}, f32[256,16]{0,1:T(8,128)S(1)}, f32[256,16]{0,1:T(8,12...) fusion(f32[256,512]{0,1:T(8,128)S(1)} %convolution_bitcast_fusion.15, ...), kind=kLoop, calls=%fused_computation.28 | loop fusion | flops 37715968 | bytes 4341760 | tf_op jit(solution)/shard_map/aj,sja->sa/dot_general | solution.py:93
  163.4 6.7 %fusion.20 = (f32[256,512]{0,1:T(8,128)S(1)}, f32[256,512]{0,1:T(8,128)S(1)}, f32[256,512]{0,1:T(8,128)S(1)}, f32[256,512]{0,1:T(8,128)S(1)}, f32[256,512]{0,1:T...) fusion(f32[256,16]{0,1:T(8,128)S(1)} %bitcast.593, ...), kind=kLoop, calls=%fused_computation.23 | loop fusion | flops 36700160 | bytes 4341760 | tf_op jit(solution)/shard_map/sa,sja->ja/dot_general | solution.py:97
  178.4 1.6 pad_maximum_fusion
  180.4 1.5 collective-permute-start.2
  182.8 37.9 %collective-permute-done.2 = bf16[2,4,784,128]{3,2,0,1:T(8,128)(2,1)} collective-permute-done((bf16[2,4,784,128]{3,2,0,1:T(8,128)(2,1)S(1)}, bf16[2,4,784,128]{3,2,0,1:T(8,128)(2,1)}, u32[]{:S(2)}, u32[]{:S(2)}) %collective-permute-start.2) | collective-permute-done | bytes 1605664 | tf_op jit(solution)/shard_map/ppermute | solution.py:35
  220.7 3.7 fusion.168
  224.4 1.1 collective-permute-start.3
  225.5 3.5 fusion.44
  232.7 62.2 %collective-permute-done.3 = f32[2,4,784,128]{3,2,0,1:T(8,128)} collective-permute-done((f32[2,4,784,128]{3,2,0,1:T(8,128)}, f32[2,4,784,128]{3,2,0,1:T(8,128)}, u32[]{:S(2)}, u32[]{:S(2)}) %collective-permute-start.3) | collective-permute-done | bytes 3211296 | tf_op jit(solution)/shard_map/ppermute | solution.py:35
  294.9 4.9 %fusion.32 = f32[2,4,784,256]{3,2,0,1:T(8,128)} fusion(f32[2,4,784,256]{3,2,0,1:T(8,128)} %copy-done, f32[2,4,784,128]{3,2,0,1:T(8,128)} %collective-permute-done.3), kind=kLoop, calls=%fused_computation.38 | loop fusion | flops 802816 | bytes 9633792 | tf_op jit(solution)/shard_map/scatter-add | solution.py:117
  299.8 3.1 convert.59
  303.0 2.5 copy.93
  311.3 2.2 fusion.48
  313.5 2.3 fusion.42
  315.8 2.6 fusion.40
  318.3 2.7 fusion.38
  321.0 1.7 fusion.36
  322.7 1.9 bitcast_dynamic-update-slice_fusion
  324.7 8.3 %copy.96 = f32[128,49,256]{2,1,0:T(8,128)} copy(f32[128,49,256]{0,2,1:T(8,128)} %bitcast_dynamic-update-slice_fusion) | data formatting | bytes 12845056 | tf_op jit(solution)/shard_map/concatenate | solution.py:134
  333.6 88.6 %all-reduce.2.cloned.1.call-done = f32[3,7,128,64]{2,3,0,1:T(8,128)} async-done(((f32[3,7,128,64]{2,3,0,1:T(8,128)}), f32[3,7,128,64]{2,3,0,1:T(8,128)}) %all-reduce.2.cloned.1.call-update) | async-done | bytes 688144 | tf_op jit(solution)/shard_map/psum | solution.py:132
  422.2 2.0 copy.98
  424.2 15.3 %reduce-scatter.2.cloned.1.call-done = f32[64,49,256]{2,1,0:T(8,128)} async-done(((f32[128,49,256]{2,1,0:T(8,128)}), f32[64,49,256]{2,1,0:T(8,128)}) %reduce-scatter.2.cloned.1.call-update) | async-done | bytes 3211280 | tf_op jit(solution)/shard_map/reduce_scatter | solution.py:133
  439.6 2.2 convert_element_type.6
  441.8 1.5 copy.97
  (102 shorter events, 31.3 us)
Async XLA Ops:
  7.2 20.9 %copy-start.15 = (bf16[3,7,128,64]{2,3,1,0:T(8,128)(2,1)S(1)}, bf16[3,7,128,64]{2,3,1,0:T(8,128)(2,1)}, u32[]{:S(2)}) copy-start(bf16[3,7,128,64]{2,3,1,0:T(8,128)(2,1)} %param.11) | copy-start | bytes 1032196
  7.2 17.3 %all-gather.2.cloned.1.call-start = ((), (), s32[]{:S(2)}) async-start(), calls=%async_computation.1 | async-start | bytes 4816896 | tf_op jit(solution)/shard_map/all_gather | solution.py:51
  7.9 414.3 %all-reduce.2.cloned.1.call-start = ((), (), s32[]{:S(2)}) async-start(), calls=%async_computation.3 | async-start | bytes 1376256 | tf_op jit(solution)/shard_map/psum | solution.py:132
  34.0 3.2 copy-start.3
  34.0 8.8 %copy-start.6 = (bf16[64,49,256]{2,0,1:T(8,128)(2,1)S(1)}, bf16[64,49,256]{2,0,1:T(8,128)(2,1)}, u32[]{:S(2)}) copy-start(bf16[64,49,256]{2,0,1:T(8,128)(2,1)} %param.12) | copy-start | bytes 4816900
  37.2 71.3 %collective-permute-start = (bf16[2,64,49,128]{3,1,2,0:T(8,128)(2,1)}, bf16[2,64,49,128]{3,1,2,0:T(8,128)(2,1)}, u32[]{:S(2)}, u32[]{:S(2)}) collective-permute-start(bf16[2,64,49,128]{3,1,2,0:T(8,128)(2,1)} %get-tuple-element.82), channel_id=1, source_target_pairs={{0,2},{2,4},{4,6},{6,8},{8,10},{10,12},{12,14},{14,16},{16,18},{18... | collective-permute-start | bytes 4816904 | tf_op jit(solution)/shard_map/ppermute | solution.py:23
  38.9 71.5 %collective-permute-start.1 = (bf16[2,64,49,128]{3,1,2,0:T(8,128)(2,1)}, bf16[2,64,49,128]{3,1,2,0:T(8,128)(2,1)}, u32[]{:S(2)}, u32[]{:S(2)}) collective-permute-start(bf16[2,64,49,128]{3,1,2,0:T(8,128)(2,1)} %get-tuple-element.83), channel_id=1, source_target_pairs={{2,0},{4,2},{6,4},{8,6},{10,8},{12,10},{14,12},{16,14},{18,16},{20... | collective-permute-start | bytes 4816904 | tf_op jit(solution)/shard_map/ppermute | solution.py:25
  43.0 4.0 copy-start.20
  140.7 9.3 %copy-start.7 = (bf16[784,256]{1,0:T(8,128)(2,1)S(1)}, bf16[784,256]{1,0:T(8,128)(2,1)}, u32[]{:S(2)}) copy-start(bf16[784,256]{1,0:T(8,128)(2,1)} %squeeze.114) | copy-start | bytes 1204228
  140.7 9.8 %copy-start.9 = (bf16[784,256]{1,0:T(8,128)(2,1)S(1)}, bf16[784,256]{1,0:T(8,128)(2,1)}, u32[]{:S(2)}) copy-start(bf16[784,256]{1,0:T(8,128)(2,1)} %squeeze.109) | copy-start | bytes 1204228
  150.0 2.3 copy-start.5
  150.0 1.3 copy-start.8
  150.0 1.8 copy-start.10
  150.5 1.8 copy-start.11
  151.3 1.5 copy-start.12
  151.8 1.6 copy-start.13
  152.3 1.7 copy-start.14
  153.9 9.3 %copy-start.18 = (f32[4,16,256]{2,1,0:T(8,128)S(1)}, f32[4,16,256]{2,1,0:T(8,128)}, u32[]{:S(2)}) copy-start(f32[4,16,256]{2,1,0:T(8,128)} %param.13) | copy-start | bytes 196612
  153.9 9.3 %copy-start.19 = (s32[16,256]{1,0:T(8,128)S(1)}, s32[16,256]{1,0:T(8,128)}, u32[]{:S(2)}) copy-start(s32[16,256]{1,0:T(8,128)} %param.15) | copy-start | bytes 49156
  180.4 40.2 %collective-permute-start.2 = (bf16[2,4,784,128]{3,2,0,1:T(8,128)(2,1)S(1)}, bf16[2,4,784,128]{3,2,0,1:T(8,128)(2,1)}, u32[]{:S(2)}, u32[]{:S(2)}) collective-permute-start(bf16[2,4,784,128]{3,2,0,1:T(8,128)(2,1)S(1)} %slice.454), channel_id=1, source_target_pairs={{0,2},{2,4},{4,6},{6,8},{8,10},{10,12},{12,14},{14,16},{16,18},{18... | collective-permute-start | bytes 4816904 | tf_op jit(solution)/shard_map/ppermute | solution.py:35
  224.4 7.1 %copy-start = (f32[2,4,784,256]{3,2,0,1:T(8,128)}, f32[2,4,784,256]{3,2,0,1:T(8,128)S(1)}, u32[]{:S(2)}) copy-start(f32[2,4,784,256]{3,2,0,1:T(8,128)S(1)} %get-tuple-element.69) | copy-start | bytes 19267588
  224.4 70.5 %collective-permute-start.3 = (f32[2,4,784,128]{3,2,0,1:T(8,128)}, f32[2,4,784,128]{3,2,0,1:T(8,128)}, u32[]{:S(2)}, u32[]{:S(2)}) collective-permute-start(f32[2,4,784,128]{3,2,0,1:T(8,128)} %get-tuple-element.68), channel_id=1, source_target_pairs={{0,30},{2,0},{4,2},{6,4},{8,6},{10,8},{12,10},{14,12},{16,14},{18,... | collective-permute-start | bytes 9633800 | tf_op jit(solution)/shard_map/ppermute | solution.py:35
  305.5 1.0 copy-start.16
  305.5 2.2 copy-start.4
  306.4 3.2 copy-start.1
  310.1 0.8 copy-start.17
  311.0 128.6 %reduce-scatter.2.cloned.1.call-start = ((), (), s32[]{:S(2)}) async-start(), calls=%async_computation.2 | async-start | bytes 11010048 | tf_op jit(solution)/shard_map/reduce_scatter | solution.py:133
  311.3 9.7 %copy-start.2 = (bf16[3,64,49,256]{3,1,0,2:T(8,128)(2,1)S(1)}, bf16[3,64,49,256]{3,1,0,2:T(8,128)(2,1)}, u32[]{:S(2)}) copy-start(bf16[3,64,49,256]{3,1,0,2:T(8,128)(2,1)} %copy-done.1) | copy-start | bytes 14450692
Sparse Core Ops, SparseCore 0:
  9.6 14.9 all-gather.1
  311.1 111.0 all-reduce.1
  424.5 15.0 reduce-scatter.1
where the time goes:
time: 456 us; the launch traced here: 450 us
  waiting for transfers between devices  266 us (58%)
  local copies, waits for them, and re-layouts  80.9 us (18%)
  matrix products  43 us (9%)
  other arithmetic  37 us (8%)
  between operations  14.7 us (3%)
  starting transfers between devices  8.6 us (2%)
    ppermute x2, waiting for transfers between devices, shifted(): return lax.ppermute(value, axis, pairs)  100 us
    psum x1, waiting for transfers between devices, on_device(): grad_weights = lax.psum(weight_terms, 'atom')  88.6 us
    ppermute x1, waiting for transfers between devices, extended_2(): lax.ppermute(tail, axis, [(i, (i + 1) % count) for i in range(count)])  42.6 us
    concatenate x1, local copies, waits for them, and re-layouts, extended_2(): jnp.concatenate([lax.ppermute(tail, axis, [(i, (i + 1) % count) for i in...  26.7 us
    all_gather x1, waiting for transfers between devices, on_device(): gathered = lax.all_gather(features, 'chan', axis=0, tiled=True)  16.6 us
    reduce_scatter x1, waiting for transfers between devices, on_device(): lax.psum_scatter(jnp.concatenate([jnp.einsum('gcd,gdma->cma', weights[:,...  15.3 us
    dot_general x7, matrix products, on_device(): jnp.einsum('gcd,gdma->cma', weights[:, degree], grads[:, :, low_comp:high...  14.2 us
    dot_general x7, matrix products, on_device(): jnp.einsum('cma,gcd->gdma', gathered[:, low_comp:high_comp], weights[:, d...  9.45 us
  transfers between devices with their start and end apart: 7, of which 7 were waited for; matrix products, arithmetic and copies ran while one was open for 12% of the time, Pallas kernels for 0%

commit v1 on v0

v1 whole, which is shorter than its diff:
```python
import functools
import math

import jax
import jax.numpy as jnp
from jax import lax
from jax.experimental import pallas as pl
from jax.experimental.pallas import tpu as pltpu
from jax.sharding import PartitionSpec as P

LMAX = 6
HALO = 128
SOFT_CAP = 10.0
F32 = jnp.float32
BF16 = jnp.bfloat16


def degree_of(comp):
    return math.isqrt(comp)


def nn(lhs, rhs):
    return lax.dot_general(lhs, rhs, (((1,), (0,)), ((), ())), preferred_element_type=F32)


def nt(lhs, rhs):
    return lax.dot_general(lhs, rhs, (((1,), (1,)), ((), ())), preferred_element_type=F32)


def tn(lhs, rhs):
    return lax.dot_general(lhs, rhs, (((0,), (0,)), ((), ())), preferred_element_type=F32)


def pick(table, index):
    return jnp.take_along_axis(table, index, axis=1, mode="promise_in_bounds")


def head_rows_of(ref, first_row, rows):
    block = ref[:, first_row : first_row + rows, :]
    return block.reshape(block.shape[0] * rows, block.shape[2])


def slot_tile(window_index, tile):
    atoms, slots = window_index.shape
    lane = lax.broadcasted_iota(jnp.int32, (atoms, HALO), 1) + tile * HALO
    found = jnp.full((atoms, HALO), -1, jnp.int32)
    for slot in range(slots):
        found = jnp.where(window_index[:, slot : slot + 1] == lane, slot, found)
    return found


def spread(slot, coef, quantity, slots):
    values = pick(coef, jnp.maximum(slot, 0) + quantity * slots)
    return jnp.where(slot >= 0, values, 0.0).astype(BF16)


def own_kernel(heads, fa, fb, oa, ob, ca, cb, wp, own_index, left_index, right_index,
               qkv, scores, slot_own, slot_left, slot_right):
    comps, chan_local = fa.shape[0], fa.shape[1]
    rows = chan_local // heads
    for comp in range(comps):
        feats = jnp.concatenate(
            [
                jnp.concatenate([fa[comp], fb[comp]], axis=1),
                jnp.concatenate([oa[comp], ob[comp]], axis=1),
            ],
            axis=0,
        )
        qkv[comp] = nn(wp[degree_of(comp)], feats).astype(BF16)
    for head in range(heads):
        query = head_rows_of(qkv, head * rows, rows)
        key = head_rows_of(qkv, chan_local + head * rows, rows)
        value = head_rows_of(qkv, 2 * chan_local + head * rows, rows)
        cot = jnp.concatenate(
            [head_rows_of(ca, head * rows, rows), head_rows_of(cb, head * rows, rows)], axis=1
        )
        scores[head] = tn(query, key)
        scores[heads + head] = tn(cot, value)
    for half in range(2):
        index = own_index[half * HALO : (half + 1) * HALO, :]
        for tile in range(3):
            slot_own[half, tile] = slot_tile(index, tile)
    slot_left[...] = slot_tile(left_index[...], 2)
    slot_right[...] = slot_tile(right_index[...], 0)


def edge_kernel(heads, slots, score_scale, flm, flo, frm, fro, wp, qkv, ca, cb, scores, bias, valid,
                index_rows, index_wide, halo_qkv, grad_bias, coef):
    comps, chan_local = flm.shape[0], flm.shape[1]
    rows = chan_local // heads
    for comp in range(comps):
        feats = jnp.concatenate(
            [
                jnp.concatenate([flm[comp], frm[comp]], axis=1),
                jnp.concatenate([flo[comp], fro[comp]], axis=1),
            ],
            axis=0,
        )
        halo_qkv[comp] = nn(wp[degree_of(comp)], feats).astype(BF16)
    lane = lax.broadcasted_iota(jnp.int32, (HALO, 2 * heads * slots), 1)
    gathered = [jnp.zeros((HALO, 2 * heads * slots), F32) for _ in range(2)]
    for quantity in range(2 * heads):
        head = quantity % heads
        if quantity < heads:
            mine = head_rows_of(qkv, head * rows, rows)
            theirs = head_rows_of(halo_qkv, chan_local + head * rows, rows)
        else:
            mine = jnp.concatenate(
                [head_rows_of(ca, head * rows, rows), head_rows_of(cb, head * rows, rows)], axis=1
            )
            theirs = head_rows_of(halo_qkv, 2 * chan_local + head * rows, rows)
        left = tn(mine[:, :HALO], theirs[:, :HALO])
        right = tn(mine[:, HALO:], theirs[:, HALO:])
        for half in range(2):
            own = scores[quantity, half * HALO : (half + 1) * HALO, :]
            own = [own[:, :HALO], own[:, HALO:]]
            tiles = [left] + own if half == 0 else own + [right]
            index = index_wide[half * HALO : (half + 1) * HALO, :]
            inner, tile_of = index & (HALO - 1), index >> 7
            values = jnp.where(
                tile_of == 0,
                pick(tiles[0], inner),
                jnp.where(tile_of == 1, pick(tiles[1], inner), pick(tiles[2], inner)),
            )
            gathered[half] = jnp.where(lane // slots == quantity, values, gathered[half])
    for half in range(2):
        span = slice(half * HALO, (half + 1) * HALO)
        edges = gathered[half].T.reshape(2, heads, slots, HALO)
        squashed = jnp.tanh(edges[0] * (score_scale / SOFT_CAP))
        logits = SOFT_CAP * squashed + bias[:, :, span]
        live = valid[:, span][None] > 0
        weight = jnp.where(live, jnp.exp(logits), 0.0)
        attention = weight / jnp.sum(weight, axis=1, keepdims=True)
        grad_attn = edges[1]
        grad_logit = attention * (
            grad_attn - jnp.sum(attention * grad_attn, axis=1, keepdims=True)
        )
        grad_bias[:, :, span] = grad_logit
        grad_raw = score_scale * grad_logit * (1.0 - squashed * squashed)
        index = index_rows[:, span]
        both = jnp.stack([grad_raw, attention]).reshape(2 * heads, slots, HALO)
        merged = jnp.zeros_like(both)
        for slot in range(slots):
            same = (index == index[slot : slot + 1, :])[None]
            merged = merged + jnp.where(same, both[:, slot : slot + 1, :], 0.0)
        coef[span, :] = merged.reshape(2 * heads * slots, HALO).T.astype(BF16)


def grads_kernel(heads, slots, fa, fb, oa, ob, flm, flo, frm, fro, qkv, halo_qkv, ca, cb, slot_own,
                 coef, grad_query, own_key, own_value, weight_terms, ext):
    comps, chan_local = fa.shape[0], fa.shape[1]
    rows = chan_local // heads
    atoms = 2 * HALO
    empty = jnp.zeros((HALO, HALO), BF16)
    for head in range(heads):
        tables = []
        for quantity in (head, heads + head):
            halves = []
            for half in range(2):
                table = coef[half * HALO : (half + 1) * HALO, :].astype(F32)
                tiles = [spread(slot_own[half, tile], table, quantity, slots) for tile in range(3)]
                tiles = tiles + [empty] if half == 0 else [empty] + tiles
                halves.append(jnp.concatenate(tiles, axis=1))
            tables.append(jnp.concatenate(halves, axis=0))
        raw_table, attn_table = tables
        query = head_rows_of(qkv, head * rows, rows)
        key = head_rows_of(qkv, chan_local + head * rows, rows)
        halo_key = head_rows_of(halo_qkv, chan_local + head * rows, rows)
        cot = jnp.concatenate(
            [head_rows_of(ca, head * rows, rows), head_rows_of(cb, head * rows, rows)], axis=1
        )
        key_ext = jnp.concatenate([halo_key[:, :HALO], key, halo_key[:, HALO:]], axis=1)
        span = slice(head * rows, (head + 1) * rows)
        value_span = slice(chan_local + head * rows, chan_local + (head + 1) * rows)
        grad_query[:, span, :] = nt(key_ext, raw_table).astype(BF16).reshape(comps, rows, atoms)
        key_sums = nn(query, raw_table)
        own_key[:, span, :] = key_sums[:, HALO : HALO + atoms].reshape(comps, rows, atoms)
        ext[:, span, :] = key_sums.astype(BF16).reshape(comps, rows, atoms + 2 * HALO)
        value_sums = nn(cot, attn_table)
        own_value[:, span, :] = value_sums[:, HALO : HALO + atoms].reshape(comps, rows, atoms)
        ext[:, value_span, :] = value_sums.astype(BF16).reshape(comps, rows, atoms + 2 * HALO)
    for degree in range(LMAX + 1):
        query_total = jnp.zeros((chan_local, 2 * chan_local), F32)
        keyval_total = jnp.zeros((2 * chan_local, 2 * chan_local), F32)
        for comp in range(degree * degree, (degree + 1) * (degree + 1)):
            own = jnp.concatenate(
                [
                    jnp.concatenate([fa[comp], fb[comp]], axis=1),
                    jnp.concatenate([oa[comp], ob[comp]], axis=1),
                ],
                axis=0,
            )
            wide = jnp.concatenate(
                [
                    jnp.concatenate([flm[comp], fa[comp], fb[comp], frm[comp]], axis=1),
                    jnp.concatenate([flo[comp], oa[comp], ob[comp], fro[comp]], axis=1),
                ],
                axis=0,
            )
            query_total = query_total + nt(grad_query[comp], own)
            keyval_total = keyval_total + nt(ext[comp], wide)
        weight_terms[degree, :chan_local, :] = query_total
        weight_terms[degree, chan_local:, :] = keyval_total


def key_kernel(heads, slots, grad_query, own_key, halo_qkv, coef_left, coef_right, slot_left,
               slot_right, wc, terms, grad):
    comps, chan_local = grad_query.shape[0], grad_query.shape[1]
    rows = chan_local // heads
    grad[:, :chan_local, :] = grad_query[...]
    left, right = coef_left[...].astype(F32), coef_right[...].astype(F32)
    for head in range(heads):
        query = head_rows_of(halo_qkv, head * rows, rows)
        rim = jnp.concatenate(
            [
                nn(query[:, :HALO], spread(slot_left[...], left, head, slots)),
                nn(query[:, HALO:], spread(slot_right[...], right, head, slots)),
            ],
            axis=1,
        )
        total = head_rows_of(own_key, head * rows, rows) + rim
        span = slice(chan_local + head * rows, chan_local + (head + 1) * rows)
        grad[:, span, :] = total.astype(BF16).reshape(comps, rows, 2 * HALO)
    for comp in range(comps):
        terms[comp] = nn(wc[degree_of(comp)][:, : 2 * chan_local], grad[comp])


def value_kernel(heads, slots, own_value, cl, cr, coef_left, coef_right, slot_left, slot_right, wc,
                 terms, mine, theirs, grad):
    comps, chan_local = own_value.shape[0], own_value.shape[1]
    rows = chan_local // heads
    left, right = coef_left[...].astype(F32), coef_right[...].astype(F32)
    for head in range(heads):
        rim = jnp.concatenate(
            [
                nn(head_rows_of(cl, head * rows, rows),
                   spread(slot_left[...], left, heads + head, slots)),
                nn(head_rows_of(cr, head * rows, rows),
                   spread(slot_right[...], right, heads + head, slots)),
            ],
            axis=1,
        )
        total = head_rows_of(own_value, head * rows, rows) + rim
        span = slice(head * rows, (head + 1) * rows)
        grad[:, span, :] = total.astype(BF16).reshape(comps, rows, 2 * HALO)
    for comp in range(comps):
        total = terms[comp] + nn(wc[degree_of(comp)][:, 2 * chan_local :], grad[comp])
        mine[comp] = total[:chan_local]
        theirs[comp] = total[chan_local:].astype(BF16)


def call(kernel, args, outs, scratch=(), flops=0):
    whole = pl.BlockSpec(memory_space=pltpu.VMEM)
    moved = sum(math.prod(a.shape) * a.dtype.itemsize for a in list(args) + list(outs))
    return pl.pallas_call(
        kernel,
        out_shape=tuple(outs),
        in_specs=[whole] * len(args),
        out_specs=tuple([whole] * len(outs)),
        scratch_shapes=list(scratch),
        compiler_params=pltpu.CompilerParams(vmem_limit_bytes=56 * 1024 * 1024),
        cost_estimate=pl.CostEstimate(flops=flops, bytes_accessed=moved, transcendentals=0),
    )(*args)


def shifted(value, axis, steps):
    count = lax.axis_size(axis)
    pairs = [(source, (source + steps) % count) for source in range(count)]
    return lax.ppermute(value, axis, pairs)


def summed_over(value, axis):
    count = lax.axis_size(axis)
    if count & (count - 1):
        return lax.psum(value, axis)
    place = lax.axis_index(axis)
    bits = list(reversed(range(count.bit_length() - 1)))
    halved = []
    for at, bit in enumerate(bits):
        pairs = [(source, source ^ (1 << bit)) for source in range(count)]
        upper = (place >> bit) & 1
        half = value.shape[1] // 2
        if at < len(bits) - 1 and value.shape[1] % 16 == 0 and half >= 24:
            low, high = value[:, :half], value[:, half:]
            keep = jnp.where(upper == 1, high, low)
            send = jnp.where(upper == 1, low, high)
            if at == 0:
                send = send.astype(BF16)
            value = keep + lax.ppermute(send, axis, pairs).astype(F32)
            halved.append((bit, pairs))
        else:
            value = value + lax.ppermute(value, axis, pairs)
    value = value.astype(BF16)
    for bit, pairs in reversed(halved):
        upper = (place >> bit) & 1
        other = lax.ppermute(value, axis, pairs)
        value = jnp.concatenate(
            [jnp.where(upper == 1, other, value), jnp.where(upper == 1, value, other)], axis=1
        )
    return value.astype(F32)


def on_device(features, weights, cotangent, edge_bias, neighbours, valid_mask):
    chan_local, comps, atoms_dev = features.shape
    heads, slots = edge_bias.shape[0], edge_bias.shape[1]
    channels = weights.shape[2]
    assert atoms_dev == 2 * HALO and channels == 2 * chan_local
    score_scale = 1.0 / math.sqrt(chan_local // heads * comps)
    total_atoms = atoms_dev * lax.axis_size("atom")
    first_atom = lax.axis_index("atom") * atoms_dev
    core = lax.axis_index("chan")

    def shape(*dims, dtype=F32):
        return jax.ShapeDtypeStruct(dims, dtype)

    def halves(array):
        return (
            jnp.transpose(array[:, :, :HALO], (1, 0, 2)),
            jnp.transpose(array[:, :, HALO:], (1, 0, 2)),
        )

    fa, fb = halves(features)
    ca, cb = halves(cotangent)
    flm = shifted(fb, "atom", 1)
    frm = shifted(fa, "atom", -1)
    oa = shifted(fa, "chan", 1)
    ob = shifted(fb, "chan", 1)
    flo = shifted(flm, "chan", 1)
    fro = shifted(frm, "chan", 1)
    ca_out, cb_out, flm, frm = lax.optimization_barrier((ca, cb, flm, frm))
    cl = shifted(cb_out, "atom", 1)
    cr = shifted(ca_out, "atom", -1)

    atom_ids = first_atom + jnp.arange(atoms_dev, dtype=jnp.int32)
    half_start = atom_ids - jnp.arange(atoms_dev, dtype=jnp.int32) % HALO
    window = (neighbours - half_start[None] + HALO + total_atoms) % total_atoms
    left_index = shifted(window[:, HALO:], "atom", 1)
    right_index = shifted(window[:, :HALO], "atom", -1)
    window_t = window.T
    window_wide = jnp.tile(window_t, (1, 2 * heads))

    swapped = jnp.where(core == 0, weights, jnp.roll(weights, chan_local, axis=2))
    wp = jnp.transpose(swapped, (1, 0, 3, 2)).reshape(LMAX + 1, 3 * chan_local, channels)
    wc = jnp.transpose(swapped, (1, 2, 0, 3)).reshape(LMAX + 1, channels, 3 * chan_local)

    rows = chan_local // heads * comps
    pair_flops = 2 * heads * rows * HALO * HALO
    mix_flops = 2 * comps * channels * 3 * chan_local * atoms_dev
    qkv, scores, slot_own, slot_left, slot_right = call(
        functools.partial(own_kernel, heads),
        (fa, fb, oa, ob, ca, cb, wp, window_t, left_index.T, right_index.T),
        (
            shape(comps, 3 * chan_local, atoms_dev, dtype=BF16),
            shape(2 * heads, atoms_dev, atoms_dev),
            shape(2, 3, HALO, HALO, dtype=jnp.int32),
            shape(HALO, HALO, dtype=jnp.int32),
            shape(HALO, HALO, dtype=jnp.int32),
        ),
        flops=mix_flops + 8 * pair_flops,
    )
    halo_qkv, grad_bias, coef = call(
        functools.partial(edge_kernel, heads, slots, score_scale),
        (flm, flo, frm, fro, wp, qkv, ca, cb, scores, edge_bias, valid_mask, window, window_wide),
        (
            shape(comps, 3 * chan_local, atoms_dev, dtype=BF16),
            shape(heads, slots, atoms_dev),
            shape(atoms_dev, 2 * heads * slots, dtype=BF16),
        ),
        flops=mix_flops + 4 * pair_flops,
    )
    coef_left = shifted(coef[HALO:], "atom", 1)
    coef_right = shifted(coef[:HALO], "atom", -1)
    grad_query, own_key, own_value, weight_terms = call(
        functools.partial(grads_kernel, heads, slots),
        (fa, fb, oa, ob, flm, flo, frm, fro, qkv, halo_qkv, ca, cb, slot_own, coef),
        (
            shape(comps, chan_local, atoms_dev, dtype=BF16),
            shape(comps, chan_local, atoms_dev),
            shape(comps, chan_local, atoms_dev),
            shape(LMAX + 1, 3 * chan_local, channels),
        ),
        scratch=[pltpu.VMEM((comps, 2 * chan_local, 2 * atoms_dev), BF16)],
        flops=24 * pair_flops + 2 * mix_flops,
    )
    grad_weights = summed_over(weight_terms, "atom")
    (terms,) = call(
        functools.partial(key_kernel, heads, slots),
        (grad_query, own_key, halo_qkv, coef_left, coef_right, slot_left, slot_right, wc),
        (shape(comps, channels, atoms_dev),),
        scratch=[pltpu.VMEM((comps, 2 * chan_local, atoms_dev), BF16)],
        flops=2 * pair_flops + mix_flops,
    )
    mine, theirs = call(
        functools.partial(value_kernel, heads, slots),
        (own_value, cl, cr, coef_left, coef_right, slot_left, slot_right, wc, terms),
        (
            shape(comps, chan_local, atoms_dev),
            shape(comps, chan_local, atoms_dev, dtype=BF16),
        ),
        scratch=[pltpu.VMEM((comps, chan_local, atoms_dev), BF16)],
        flops=2 * pair_flops + mix_flops // 2,
    )
    total = mine + shifted(theirs, "chan", 1).astype(F32)
    grad_features = jnp.transpose(total.astype(BF16), (1, 0, 2))
    grad_weights = grad_weights.reshape(LMAX + 1, 3, chan_local, channels)
    grad_weights = jnp.transpose(grad_weights, (1, 0, 3, 2))
    grad_weights = jnp.where(core == 0, grad_weights, jnp.roll(grad_weights, chan_local, axis=2))
    return grad_features, grad_weights, grad_bias


def solution(mesh):
    in_specs = (
        P("chan", None, "atom"),
        P(None, None, None, "chan"),
        P("chan", None, "atom"),
        P("chan", None, "atom"),
        P(None, "atom"),
        P(None, "atom"),
    )
    out_specs = (P("chan", None, "atom"), P(None, None, None, "chan"), P("chan", None, "atom"))
    return jax.shard_map(
        on_device, mesh=mesh, in_specs=in_specs, out_specs=out_specs, check_vma=False
    )
```

time: 456 us -> 179 us (0.39); the launches traced: 450 us -> 179 us
  waiting for transfers between devices: 266 us -> 67.3 us
  local copies, waits for them, and re-layouts: 80.9 us -> 14.2 us
  Pallas kernels: 0 us -> 48.1 us
  matrix products: 43 us -> 0 us
  starting transfers between devices: 8.6 us -> 41.6 us
  other arithmetic: 37 us -> 6.44 us
  between operations: 14.7 us -> 0.94 us
    psum x1 -> x0, waiting for transfers between devices: 88.6 us -> none  [on_device(): grad_weights = lax.psum(weight_terms, 'atom')]
    ppermute x2 -> x13, waiting for transfers between devices: 100 us -> 38.3 us  [shifted(): return lax.ppermute(value, axis, pairs)]
    pallas_call x0 -> x5, Pallas kernels: none -> 48.1 us  [call(): pl.pallas_call(kernel, out_shape=tuple(outs), in_specs=[whole] * len(args...]
    dot_general x37 -> x0, matrix products: 40.9 us -> none  [the longest x7 14.2 us: on_device(): jnp.einsum('gcd,gdma->cma', weights[:, degree], grads[:, :, low_comp:high...]
    concatenate x2 -> x0, local copies, waits for them, and re-layouts: 35 us -> none  [the longest x1 26.7 us: extended_2(): jnp.concatenate([lax.ppermute(tail, axis, [(i, (i + 1) % count) for i in...]
    ppermute x2 -> x13, starting transfers between devices: 2.61 us -> 35.6 us  [shifted(): return lax.ppermute(value, axis, pairs)]
    slice x15 -> x4, local copies, waits for them, and re-layouts: 24.8 us -> 1.06 us  [the longest x1 0.6 us: on_device(): right_index = shifted(window[:, :HALO], 'atom', -1)]
    all_gather x1 -> x0, waiting for transfers between devices: 16.6 us -> none  [on_device(): gathered = lax.all_gather(features, 'chan', axis=0, tiled=True)]
  transfers between devices with their start and end apart: 7 -> 20, of which waited for: 7 -> 8; matrix products, arithmetic and copies ran while one was open for 12% -> 6% of each run, Pallas kernels for 0% -> 15%
where the time goes in v1:
time: 179 us
  waiting for transfers between devices  67.3 us (38%)
  Pallas kernels  48.1 us (27%)
  starting transfers between devices  41.6 us (23%)
  local copies, waits for them, and re-layouts  14.2 us (8%)
  other arithmetic  6.44 us (4%)
    pallas_call x5, Pallas kernels, call(): pl.pallas_call(kernel, out_shape=tuple(outs), in_specs=[whole] * len(args...  48.1 us
    ppermute x13, waiting for transfers between devices, shifted(): return lax.ppermute(value, axis, pairs)  38.3 us
    ppermute x13, starting transfers between devices, shifted(): return lax.ppermute(value, axis, pairs)  35.6 us
    ppermute x3, waiting for transfers between devices, summed_over(): value = keep + lax.ppermute(send, axis, pairs).astype(F32)  20.3 us
    ppermute x3, waiting for transfers between devices, summed_over(): other = lax.ppermute(value, axis, pairs)  8.73 us
    ppermute x3, starting transfers between devices, summed_over(): other = lax.ppermute(value, axis, pairs)  5.65 us
    unnamed x37, local copies, waits for them, and re-layouts  4.3 us
    transpose x2, local copies, waits for them, and re-layouts, halves(): jnp.transpose(array[:, :, HALO:], (1, 0, 2))  4.18 us
  transfers between devices with their start and end apart: 20, of which 8 were waited for; matrix products, arithmetic and copies ran while one was open for 6% of the time, Pallas kernels for 15%

profile of v1, /device:TPU:0, one launch (start us, length us, event | category | flops | bytes accessed | tf_op | source)
XLA Modules:
  0.0 178.5 jit_solution(3357648837065110958)
XLA Ops:
  0.6 1.5 slice_bitcast_fusion.2
  2.2 0.5 collective-permute-start.1
  2.7 2.6 %collective-permute-start.2 = (bf16[49,64,128]{2,1,0:T(8,128)(2,1)S(1)}, bf16[49,64,128]{2,1,0:T(8,128)(2,1)S(1)}, u32[]{:S(2)}, u32[]{:S(2)}) collective-permute-start(bf16[49,64,128]{2,1,0:T(8,128)(2,1)S(1)} %get-tuple-element.44.fb), channel_id=1, source_target_pairs={{0,2},{2,4},{4,6},{6,8},{8,10},{10,12},{12,14},{14,16},{16,18},{18... | collective-permute-start | bytes 2408456 | tf_op jit(solution)/shard_map/ppermute | solution.py:269
  5.2 0.2 collective-permute-start
  5.4 4.3 %collective-permute-start.3 = (bf16[49,64,128]{2,1,0:T(8,128)(2,1)S(1)}, bf16[49,64,128]{2,1,0:T(8,128)(2,1)S(1)}, u32[]{:S(2)}, u32[]{:S(2)}) collective-permute-start(bf16[49,64,128]{2,1,0:T(8,128)(2,1)S(1)} %get-tuple-element.45.fa), channel_id=1, source_target_pairs={{0,30},{2,0},{4,2},{6,4},{8,6},{10,8},{12,10},{14,12},{16,14},{18,... | collective-permute-start | bytes 2408456 | tf_op jit(solution)/shard_map/ppermute | solution.py:269
  9.7 0.7 add_select_fusion.index_rows
  10.4 0.6 copy-done.12
  11.0 0.6 fusion.6
  11.6 2.7 %slice_bitcast_fusion = (bf16[49,64,128]{2,1,0:T(8,128)(2,1)}, bf16[49,64,128]{2,1,0:T(8,128)(2,1)}) fusion(bf16[64,49,256]{2,0,1:T(8,128)(2,1)} %param.8), kind=kLoop, calls=%fused_computation.2 | loop fusion | bytes 3211264 | tf_op jit(solution)/shard_map/transpose | solution.py:319
  14.3 26.0 %collective-permute-done.2.flm = bf16[49,64,128]{2,1,0:T(8,128)(2,1)S(1)} collective-permute-done((bf16[49,64,128]{2,1,0:T(8,128)(2,1)S(1)}, bf16[49,64,128]{2,1,0:T(8,128)(2,1)S(1)}, u32[]{:S(2)}, u32[]{:S(2)}) %collective-permute-start.2) | collective-permute-done | bytes 802848 | tf_op jit(solution)/shard_map/ppermute | solution.py:269
  40.3 1.9 %collective-permute-done.3.frm = bf16[49,64,128]{2,1,0:T(8,128)(2,1)S(1)} collective-permute-done((bf16[49,64,128]{2,1,0:T(8,128)(2,1)S(1)}, bf16[49,64,128]{2,1,0:T(8,128)(2,1)S(1)}, u32[]{:S(2)}, u32[]{:S(2)}) %collective-permute-start.3) | collective-permute-done | bytes 802848 | tf_op jit(solution)/shard_map/ppermute | solution.py:269
  42.2 0.2 fusion.4
  42.5 1.0 maximum_select_fusion.1
  43.5 3.6 %collective-permute-start.7 = (s32[16,128]{1,0:T(8,128)}, s32[16,128]{1,0:T(8,128)S(1)}, u32[]{:S(2)}, u32[]{:S(2)}) collective-permute-start(s32[16,128]{1,0:T(8,128)} %get-tuple-element.58), channel_id=1, source_target_pairs={{0,30},{2,0},{4,2},{6,4},{8,6},{10,8},{12,10},{14,12},{16,14},{18,... | collective-permute-start | bytes 24584 | tf_op jit(solution)/shard_map/ppermute | solution.py:269
  47.1 0.8 copy.19.own_index
  47.8 0.8 copy.22.index_wide
  48.6 1.4 copy.20.left_index
  50.0 0.7 copy.21.right_index
  50.8 8.8 %shard_map.85 = (bf16[49,192,256]{2,1,0:T(8,128)(2,1)}, f32[8,256,256]{2,1,0:T(8,128)}, s32[2,3,128,128]{3,2,1,0:T(8,128)}, s32[128,128]{1,0:T(8,128)}, s32[128,128]{1,0:T(8,128)}) custom-call(bf16[49,64,128]{2,1,0:T(8,128)(2,1)} %copy-done.3, bf16[49,64,128]{2,1,0:T(8,128)(2,1)} %copy-done.2, bf16[49,64,128]{2,1,0:T(8,128)(2,1)} %collective-permute-done.oa, ...), custom_call_target="tpu_custom_call" | custom-call | flops 1438646272 | bytes 12632064 | tf_op jit(solution)/shard_map/pallas_call | solution.py:255
  59.6 8.8 %shard_map.86 = (bf16[49,192,256]{2,1,0:T(8,128)(2,1)}, f32[4,16,256]{2,1,0:T(8,128)}, bf16[256,128]{1,0:T(8,128)(2,1)}) custom-call(bf16[49,64,128]{2,1,0:T(8,128)(2,1)} %copy-done.6, bf16[49,64,128]{2,1,0:T(8,128)(2,1)} %collective-permute-done.4.flo, bf16[49,64,128]{2,1,0:T(8,128)(2,1)} %copy-done.7, bf16[49,64,128]{2,1,0:T(8,128)(2,1)} %collective-permute-done.5.fro, ...), custom_call_target="tpu_custom_call" | custom-call | flops 1027604480 | bytes 17252352 | tf_op jit(solution)/shard_map/pallas_call | solution.py:255
  68.4 13.2 %shard_map.87 = (bf16[49,64,256]{2,1,0:T(8,128)(2,1)}, f32[49,64,256]{2,1,0:T(8,128)}, f32[49,64,256]{2,1,0:T(8,128)}, f32[7,192,128]{2,1,0:T(8,128)}) custom-call(bf16[49,64,128]{2,1,0:T(8,128)(2,1)} %copy-done.3, bf16[49,64,128]{2,1,0:T(8,128)(2,1)} %copy-done.2, bf16[49,64,128]{2,1,0:T(8,128)(2,1)} %collective-permute-done.oa, ...), custom_call_target="tpu_custom_call" | custom-call | flops 3699376128 | bytes 26836992 | tf_op jit(solution)/shard_map/pallas_call | solution.py:255
  81.7 1.3 select_convert_fusion
  83.0 9.6 %collective-permute-done.13 = bf16[7,96,128]{2,1,0:T(8,128)(2,1)S(1)} collective-permute-done((bf16[7,96,128]{2,1,0:T(8,128)(2,1)S(1)}, bf16[7,96,128]{2,1,0:T(8,128)(2,1)S(1)}, u32[]{:S(2)}, u32[]{:S(2)}) %collective-permute-start.13) | collective-permute-done | bytes 172064 | tf_op jit(solution)/shard_map/ppermute | solution.py:289
  92.6 1.1 convert_add_fusion
  93.9 6.3 %collective-permute-done.14 = f32[7,48,128]{2,1,0:T(8,128)S(1)} collective-permute-done((f32[7,48,128]{2,1,0:T(8,128)S(1)}, f32[7,48,128]{2,1,0:T(8,128)S(1)}, u32[]{:S(2)}, u32[]{:S(2)}) %collective-permute-start.14) | collective-permute-done | bytes 172064 | tf_op jit(solution)/shard_map/ppermute | solution.py:289
  100.2 0.2 collective-permute-start.15
  100.4 4.4 %collective-permute-done.15 = f32[7,24,128]{2,1,0:T(8,128)S(1)} collective-permute-done((f32[7,24,128]{2,1,0:T(8,128)S(1)}, f32[7,24,128]{2,1,0:T(8,128)S(1)}, u32[]{:S(2)}, u32[]{:S(2)}) %collective-permute-start.15) | collective-permute-done | bytes 86048 | tf_op jit(solution)/shard_map/ppermute | solution.py:289
  104.9 1.0 copy.24.wc
  105.9 2.0 %collective-permute-start.8 = (bf16[49,64,128]{2,1,0:T(8,128)(2,1)S(1)}, bf16[49,64,128]{2,1,0:T(8,128)(2,1)S(1)}, u32[]{:S(2)}, u32[]{:S(2)}) collective-permute-start(bf16[49,64,128]{2,1,0:T(8,128)(2,1)S(1)} %copy-done.1), channel_id=1, source_target_pairs={{0,2},{2,4},{4,6},{6,8},{8,10},{10,12},{12,14},{14,16},{16,18},{18... | collective-permute-start | bytes 2408456 | tf_op jit(solution)/shard_map/ppermute | solution.py:269
  107.9 3.6 %collective-permute-start.9 = (bf16[49,64,128]{2,1,0:T(8,128)(2,1)S(1)}, bf16[49,64,128]{2,1,0:T(8,128)(2,1)S(1)}, u32[]{:S(2)}, u32[]{:S(2)}) collective-permute-start(bf16[49,64,128]{2,1,0:T(8,128)(2,1)S(1)} %copy-done), channel_id=1, source_target_pairs={{0,30},{2,0},{4,2},{6,4},{8,6},{10,8},{12,10},{14,12},{16,14},{18,... | collective-permute-start | bytes 2408456 | tf_op jit(solution)/shard_map/ppermute | solution.py:269
  111.6 16.4 %collective-permute-start.10 = (bf16[128,128]{1,0:T(8,128)(2,1)S(1)}, bf16[128,128]{1,0:T(8,128)(2,1)S(1)}, u32[]{:S(2)}, u32[]{:S(2)}) collective-permute-start(bf16[128,128]{1,0:T(8,128)(2,1)S(1)} %get-tuple-element.57), channel_id=1, source_target_pairs={{0,2},{2,4},{4,6},{6,8},{8,10},{10,12},{12,14},{14,16},{16,18},{18... | collective-permute-start | bytes 98312 | tf_op jit(solution)/shard_map/ppermute | solution.py:269
  128.0 2.5 %collective-permute-start.11 = (bf16[128,128]{1,0:T(8,128)(2,1)S(1)}, bf16[128,128]{1,0:T(8,128)(2,1)S(1)}, u32[]{:S(2)}, u32[]{:S(2)}) collective-permute-start(bf16[128,128]{1,0:T(8,128)(2,1)S(1)} %get-tuple-element.56), channel_id=1, source_target_pairs={{0,30},{2,0},{4,2},{6,4},{8,6},{10,8},{12,10},{14,12},{16,14},{18,... | collective-permute-start | bytes 98312 | tf_op jit(solution)/shard_map/ppermute | solution.py:269
  130.5 2.4 %collective-permute-start.18 = (bf16[7,48,128]{2,1,0:T(8,128)(2,1)S(1)}, bf16[7,48,128]{2,1,0:T(8,128)(2,1)S(1)}, u32[]{:S(2)}, u32[]{:S(2)}) collective-permute-start(bf16[7,48,128]{2,1,0:T(8,128)(2,1)S(1)} %pad_maximum_fusion.2), channel_id=1, source_target_pairs={{0,8},{2,10},{4,12},{6,14},{8,0},{10,2},{12,4},{14,6},{16,24},{18,... | collective-permute-start | bytes 258056 | tf_op jit(solution)/shard_map/ppermute | solution.py:296
  132.9 9.6 %collective-permute-done.10.coef_left = bf16[128,128]{1,0:T(8,128)(2,1)S(1)} collective-permute-done((bf16[128,128]{1,0:T(8,128)(2,1)S(1)}, bf16[128,128]{1,0:T(8,128)(2,1)S(1)}, u32[]{:S(2)}, u32[]{:S(2)}) %collective-permute-start.10) | collective-permute-done | bytes 32800 | tf_op jit(solution)/shard_map/ppermute | solution.py:269
  142.5 0.8 collective-permute-done.11.coef_right
  143.3 0.6 copy-done.14
  143.9 8.6 %shard_map.88.terms = f32[49,128,256]{2,1,0:T(8,128)} custom-call(bf16[49,64,256]{2,1,0:T(8,128)(2,1)} %get-tuple-element.33.grad_query, f32[49,64,256]{2,1,0:T(8,128)} %get-tuple-element.34.own_key, bf16[49,192,256]{2,1,0:T(8,128)(2,1)} %get-tuple-element.25.halo_qkv, bf16[128,128]{1,0:T(8,128)(2,1)} %copy-done.13, bf16[128,128]{1,0:T(8,128)(2,1)} %copy-done.14, ...), custom_call_target="tpu_custom_call" | custom-call | flops 822083584 | bytes 16596992 | tf_op jit(solution)/shard_map/pallas_call | solution.py:255
  152.5 0.9 copy-done.9
  153.3 0.3 copy-done.10
  153.6 8.6 %shard_map.89 = (f32[49,64,256]{2,1,0:T(8,128)}, bf16[49,64,256]{2,1,0:T(8,128)(2,1)}) custom-call(f32[49,64,256]{2,1,0:T(8,128)} %get-tuple-element.28.own_value, bf16[49,64,128]{2,1,0:T(8,128)(2,1)} %copy-done.9, bf16[49,64,128]{2,1,0:T(8,128)(2,1)} %copy-done.10, bf16[128,128]{1,0:T(8,128)(2,1)} %copy-done.13, bf16[128,128]{1,0:T(8,128)(2,1)} %copy-done.14, ...), custom_call_target="tpu_custom_call" | custom-call | flops 513802240 | bytes 16596992 | tf_op jit(solution)/shard_map/pallas_call | solution.py:255
  162.3 3.2 %collective-permute-start.19 = (bf16[7,96,128]{2,1,0:T(8,128)(2,1)S(1)}, bf16[7,96,128]{2,1,0:T(8,128)(2,1)S(1)}, u32[]{:S(2)}, u32[]{:S(2)}) collective-permute-start(bf16[7,96,128]{2,1,0:T(8,128)(2,1)S(1)} %pad_maximum_fusion.1), channel_id=1, source_target_pairs={{0,16},{2,18},{4,20},{6,22},{8,24},{10,26},{12,28},{14,30},{16,0},... | collective-permute-start | bytes 516104 | tf_op jit(solution)/shard_map/ppermute | solution.py:296
  165.5 8.7 %collective-permute-done.19 = bf16[7,96,128]{2,1,0:T(8,128)(2,1)S(1)} collective-permute-done((bf16[7,96,128]{2,1,0:T(8,128)(2,1)S(1)}, bf16[7,96,128]{2,1,0:T(8,128)(2,1)S(1)}, u32[]{:S(2)}, u32[]{:S(2)}) %collective-permute-start.19) | collective-permute-done | bytes 172064 | tf_op jit(solution)/shard_map/ppermute | solution.py:296
  174.2 0.1 broadcast_select_fusion.1
  174.4 0.3 fusion.3
  174.7 0.2 maximum_select_fusion
  174.9 0.9 copy.25
  175.9 1.0 copy-done.5
  176.9 1.7 fusion
  (66 shorter events, 0.7 us)
Async XLA Ops:
  2.1 40.3 %copy-start.2 = (bf16[49,64,128]{2,1,0:T(8,128)(2,1)}, bf16[49,64,128]{2,1,0:T(8,128)(2,1)S(1)}, u32[]{:S(2)}) copy-start(bf16[49,64,128]{2,1,0:T(8,128)(2,1)S(1)} %get-tuple-element.44.fb) | copy-start | bytes 2408452
  2.1 40.3 %copy-start.3 = (bf16[49,64,128]{2,1,0:T(8,128)(2,1)}, bf16[49,64,128]{2,1,0:T(8,128)(2,1)S(1)}, u32[]{:S(2)}) copy-start(bf16[49,64,128]{2,1,0:T(8,128)(2,1)S(1)} %get-tuple-element.45.fa) | copy-start | bytes 2408452
  2.2 40.1 %copy-start.8 = (bf16[3,7,128,64]{2,3,1,0:T(8,128)(2,1)S(1)}, bf16[3,7,128,64]{2,3,1,0:T(8,128)(2,1)}, u32[]{:S(2)}) copy-start(bf16[3,7,128,64]{2,3,1,0:T(8,128)(2,1)} %param.7) | copy-start | bytes 1032196
  2.2 48.6 %collective-permute-start.1 = (bf16[49,64,128]{2,1,0:T(8,128)(2,1)S(1)}, bf16[49,64,128]{2,1,0:T(8,128)(2,1)}, u32[]{:S(2)}, u32[]{:S(2)}) collective-permute-start(bf16[49,64,128]{2,1,0:T(8,128)(2,1)S(1)} %get-tuple-element.44.fb), channel_id=1, source_target_pairs={{0,1},{1,0},{2,3},{3,2},{4,5},{5,4},{6,7},{7,6},{8,9},{9,8},{10,11... | collective-permute-start | bytes 2408456 | tf_op jit(solution)/shard_map/ppermute | solution.py:269
  2.7 37.6 %collective-permute-start.2 = (bf16[49,64,128]{2,1,0:T(8,128)(2,1)S(1)}, bf16[49,64,128]{2,1,0:T(8,128)(2,1)S(1)}, u32[]{:S(2)}, u32[]{:S(2)}) collective-permute-start(bf16[49,64,128]{2,1,0:T(8,128)(2,1)S(1)} %get-tuple-element.44.fb), channel_id=1, source_target_pairs={{0,2},{2,4},{4,6},{6,8},{8,10},{10,12},{12,14},{14,16},{16,18},{18... | collective-permute-start | bytes 2408456 | tf_op jit(solution)/shard_map/ppermute | solution.py:269
  5.2 45.5 %collective-permute-start = (bf16[49,64,128]{2,1,0:T(8,128)(2,1)S(1)}, bf16[49,64,128]{2,1,0:T(8,128)(2,1)}, u32[]{:S(2)}, u32[]{:S(2)}) collective-permute-start(bf16[49,64,128]{2,1,0:T(8,128)(2,1)S(1)} %get-tuple-element.45.fa), channel_id=1, source_target_pairs={{0,1},{1,0},{2,3},{3,2},{4,5},{5,4},{6,7},{7,6},{8,9},{9,8},{10,11... | collective-permute-start | bytes 2408456 | tf_op jit(solution)/shard_map/ppermute | solution.py:269
  5.4 36.8 %collective-permute-start.3 = (bf16[49,64,128]{2,1,0:T(8,128)(2,1)S(1)}, bf16[49,64,128]{2,1,0:T(8,128)(2,1)S(1)}, u32[]{:S(2)}, u32[]{:S(2)}) collective-permute-start(bf16[49,64,128]{2,1,0:T(8,128)(2,1)S(1)} %get-tuple-element.45.fa), channel_id=1, source_target_pairs={{0,30},{2,0},{4,2},{6,4},{8,6},{10,8},{12,10},{14,12},{16,14},{18,... | collective-permute-start | bytes 2408456 | tf_op jit(solution)/shard_map/ppermute | solution.py:269
  9.7 1.9 %copy-start.16 = (s32[256]{0:T(256)}, s32[256]{0:T(256)S(1)}, u32[]{:S(2)}) copy-start(s32[256]{0:T(256)S(1)} %fusion.2) | copy-start | bytes 3076
  10.4 0.6 copy-start.12
  11.6 31.9 %collective-permute-start.6 = (s32[16,128]{1,0:T(8,128)}, s32[16,128]{1,0:T(8,128)}, u32[]{:S(2)}, u32[]{:S(2)}) collective-permute-start(s32[16,128]{1,0:T(8,128)} %get-tuple-element.59), channel_id=1, source_target_pairs={{0,2},{2,4},{4,6},{6,8},{8,10},{10,12},{12,14},{14,16},{16,18},{18... | collective-permute-start | bytes 24584 | tf_op jit(solution)/shard_map/ppermute | solution.py:269
  14.3 32.7 %copy-start.15 = (s32[16,256]{1,0:T(8,128)S(1)}, s32[16,256]{1,0:T(8,128)}, u32[]{:S(2)}) copy-start(s32[16,256]{1,0:T(8,128)} %param.10) | copy-start | bytes 49156
  14.3 32.7 %copy-start.17 = (s32[256]{0:T(256)S(1)}, s32[256]{0:T(256)}, u32[]{:S(2)}) copy-start(s32[256]{0:T(256)} %copy-done.16) | copy-start | bytes 3076
  40.3 19.3 %copy-start.6 = (bf16[49,64,128]{2,1,0:T(8,128)(2,1)}, bf16[49,64,128]{2,1,0:T(8,128)(2,1)S(1)}, u32[]{:S(2)}) copy-start(bf16[49,64,128]{2,1,0:T(8,128)(2,1)S(1)} %collective-permute-done.2.flm) | copy-start | bytes 2408452
  40.3 19.3 %collective-permute-start.4 = (bf16[49,64,128]{2,1,0:T(8,128)(2,1)S(1)}, bf16[49,64,128]{2,1,0:T(8,128)(2,1)}, u32[]{:S(2)}, u32[]{:S(2)}) collective-permute-start(bf16[49,64,128]{2,1,0:T(8,128)(2,1)S(1)} %collective-permute-done.2.flm), channel_id=1, source_target_pairs={{0,1},{1,0},{2,3},{3,2},{4,5},{5,4},{6,7},{7,6},{8,9},{9,8},{10,11... | collective-permute-start | bytes 2408456 | tf_op jit(solution)/shard_map/ppermute | solution.py:269
  42.2 17.4 %copy-start.7 = (bf16[49,64,128]{2,1,0:T(8,128)(2,1)}, bf16[49,64,128]{2,1,0:T(8,128)(2,1)S(1)}, u32[]{:S(2)}) copy-start(bf16[49,64,128]{2,1,0:T(8,128)(2,1)S(1)} %collective-permute-done.3.frm) | copy-start | bytes 2408452
  42.2 17.4 %collective-permute-start.5 = (bf16[49,64,128]{2,1,0:T(8,128)(2,1)S(1)}, bf16[49,64,128]{2,1,0:T(8,128)(2,1)}, u32[]{:S(2)}, u32[]{:S(2)}) collective-permute-start(bf16[49,64,128]{2,1,0:T(8,128)(2,1)S(1)} %collective-permute-done.3.frm), channel_id=1, source_target_pairs={{0,1},{1,0},{2,3},{3,2},{4,5},{5,4},{6,7},{7,6},{8,9},{9,8},{10,11... | collective-permute-start | bytes 2408456 | tf_op jit(solution)/shard_map/ppermute | solution.py:269
  43.5 6.5 %collective-permute-start.7 = (s32[16,128]{1,0:T(8,128)}, s32[16,128]{1,0:T(8,128)S(1)}, u32[]{:S(2)}, u32[]{:S(2)}) collective-permute-start(s32[16,128]{1,0:T(8,128)} %get-tuple-element.58), channel_id=1, source_target_pairs={{0,30},{2,0},{4,2},{6,4},{8,6},{10,8},{12,10},{14,12},{16,14},{18,... | collective-permute-start | bytes 24584 | tf_op jit(solution)/shard_map/ppermute | solution.py:269
  81.6 23.2 %copy-start.4 = (bf16[3,7,128,64]{2,3,0,1:T(8,128)(2,1)S(1)}, bf16[3,7,128,64]{2,3,0,1:T(8,128)(2,1)}, u32[]{:S(2)}) copy-start(bf16[3,7,128,64]{2,3,0,1:T(8,128)(2,1)} %maximum_select_fusion.1) | copy-start | bytes 1032196
  81.6 24.2 %copy-start.1 = (bf16[49,64,128]{2,1,0:T(8,128)(2,1)S(1)}, bf16[49,64,128]{2,1,0:T(8,128)(2,1)}, u32[]{:S(2)}) copy-start(bf16[49,64,128]{2,1,0:T(8,128)(2,1)} %get-tuple-element.29.cb) | copy-start | bytes 2408452
  81.7 26.2 %copy-start = (bf16[49,64,128]{2,1,0:T(8,128)(2,1)S(1)}, bf16[49,64,128]{2,1,0:T(8,128)(2,1)}, u32[]{:S(2)}) copy-start(bf16[49,64,128]{2,1,0:T(8,128)(2,1)} %get-tuple-element.30.ca) | copy-start | bytes 2408452
  82.9 28.7 %copy-start.11 = (bf16[256,128]{1,0:T(8,128)(2,1)S(1)}, bf16[256,128]{1,0:T(8,128)(2,1)}, u32[]{:S(2)}) copy-start(bf16[256,128]{1,0:T(8,128)(2,1)} %get-tuple-element.27.coef) | copy-start | bytes 196612
  82.9 9.7 %collective-permute-start.13 = (bf16[7,96,128]{2,1,0:T(8,128)(2,1)S(1)}, bf16[7,96,128]{2,1,0:T(8,128)(2,1)S(1)}, u32[]{:S(2)}, u32[]{:S(2)}) collective-permute-start(bf16[7,96,128]{2,1,0:T(8,128)(2,1)S(1)} %select_convert_fusion), channel_id=1, source_target_pairs={{0,16},{2,18},{4,20},{6,22},{8,24},{10,26},{12,28},{14,30},{16,0},... | collective-permute-start | bytes 516104 | tf_op jit(solution)/shard_map/ppermute | solution.py:289
  93.8 6.4 %collective-permute-start.14 = (f32[7,48,128]{2,1,0:T(8,128)S(1)}, f32[7,48,128]{2,1,0:T(8,128)S(1)}, u32[]{:S(2)}, u32[]{:S(2)}) collective-permute-start(f32[7,48,128]{2,1,0:T(8,128)S(1)} %slice_select_fusion), channel_id=1, source_target_pairs={{0,8},{2,10},{4,12},{6,14},{8,0},{10,2},{12,4},{14,6},{16,24},{18,... | collective-permute-start | bytes 516104 | tf_op jit(solution)/shard_map/ppermute | solution.py:289
  100.2 4.6 %collective-permute-start.15 = (f32[7,24,128]{2,1,0:T(8,128)S(1)}, f32[7,24,128]{2,1,0:T(8,128)S(1)}, u32[]{:S(2)}, u32[]{:S(2)}) collective-permute-start(f32[7,24,128]{2,1,0:T(8,128)S(1)} %slice_select_fusion.1), channel_id=1, source_target_pairs={{0,4},{2,6},{4,0},{6,2},{8,12},{10,14},{12,8},{14,10},{16,20},{18,... | collective-permute-start | bytes 258056 | tf_op jit(solution)/shard_map/ppermute | solution.py:289
  104.8 6.7 %collective-permute-start.16 = (f32[7,24,128]{2,1,0:T(8,128)S(1)}, f32[7,24,128]{2,1,0:T(8,128)S(1)}, u32[]{:S(2)}, u32[]{:S(2)}) collective-permute-start(f32[7,24,128]{2,1,0:T(8,128)S(1)} %select_add_fusion.1), channel_id=1, source_target_pairs={{0,2},{2,0},{4,6},{6,4},{8,10},{10,8},{12,14},{14,12},{16,18},{18,... | collective-permute-start | bytes 258056 | tf_op jit(solution)/shard_map/ppermute | solution.py:292
  105.9 46.6 %collective-permute-start.8 = (bf16[49,64,128]{2,1,0:T(8,128)(2,1)S(1)}, bf16[49,64,128]{2,1,0:T(8,128)(2,1)S(1)}, u32[]{:S(2)}, u32[]{:S(2)}) collective-permute-start(bf16[49,64,128]{2,1,0:T(8,128)(2,1)S(1)} %copy-done.1), channel_id=1, source_target_pairs={{0,2},{2,4},{4,6},{6,8},{8,10},{10,12},{12,14},{14,16},{16,18},{18... | collective-permute-start | bytes 2408456 | tf_op jit(solution)/shard_map/ppermute | solution.py:269
  107.9 44.6 %collective-permute-start.9 = (bf16[49,64,128]{2,1,0:T(8,128)(2,1)S(1)}, bf16[49,64,128]{2,1,0:T(8,128)(2,1)S(1)}, u32[]{:S(2)}, u32[]{:S(2)}) collective-permute-start(bf16[49,64,128]{2,1,0:T(8,128)(2,1)S(1)} %copy-done), channel_id=1, source_target_pairs={{0,30},{2,0},{4,2},{6,4},{8,6},{10,8},{12,10},{14,12},{16,14},{18,... | collective-permute-start | bytes 2408456 | tf_op jit(solution)/shard_map/ppermute | solution.py:269
  111.5 19.0 %collective-permute-start.17 = (bf16[7,24,128]{2,1,0:T(8,128)(2,1)S(1)}, bf16[7,24,128]{2,1,0:T(8,128)(2,1)S(1)}, u32[]{:S(2)}, u32[]{:S(2)}) collective-permute-start(bf16[7,24,128]{2,1,0:T(8,128)(2,1)S(1)} %add_convert_fusion.1), channel_id=1, source_target_pairs={{0,4},{2,6},{4,0},{6,2},{8,12},{10,14},{12,8},{14,10},{16,20},{18,... | collective-permute-start | bytes 129032 | tf_op jit(solution)/shard_map/ppermute | solution.py:296
  111.6 30.9 %collective-permute-start.10 = (bf16[128,128]{1,0:T(8,128)(2,1)S(1)}, bf16[128,128]{1,0:T(8,128)(2,1)S(1)}, u32[]{:S(2)}, u32[]{:S(2)}) collective-permute-start(bf16[128,128]{1,0:T(8,128)(2,1)S(1)} %get-tuple-element.57), channel_id=1, source_target_pairs={{0,2},{2,4},{4,6},{6,8},{8,10},{10,12},{12,14},{14,16},{16,18},{18... | collective-permute-start | bytes 98312 | tf_op jit(solution)/shard_map/ppermute | solution.py:269
  128.0 15.3 %collective-permute-start.11 = (bf16[128,128]{1,0:T(8,128)(2,1)S(1)}, bf16[128,128]{1,0:T(8,128)(2,1)S(1)}, u32[]{:S(2)}, u32[]{:S(2)}) collective-permute-start(bf16[128,128]{1,0:T(8,128)(2,1)S(1)} %get-tuple-element.56), channel_id=1, source_target_pairs={{0,30},{2,0},{4,2},{6,4},{8,6},{10,8},{12,10},{14,12},{16,14},{18,... | collective-permute-start | bytes 98312 | tf_op jit(solution)/shard_map/ppermute | solution.py:269
  130.5 31.7 %collective-permute-start.18 = (bf16[7,48,128]{2,1,0:T(8,128)(2,1)S(1)}, bf16[7,48,128]{2,1,0:T(8,128)(2,1)S(1)}, u32[]{:S(2)}, u32[]{:S(2)}) collective-permute-start(bf16[7,48,128]{2,1,0:T(8,128)(2,1)S(1)} %pad_maximum_fusion.2), channel_id=1, source_target_pairs={{0,8},{2,10},{4,12},{6,14},{8,0},{10,2},{12,4},{14,6},{16,24},{18,... | collective-permute-start | bytes 258056 | tf_op jit(solution)/shard_map/ppermute | solution.py:296
  142.5 0.8 copy-start.13
  143.3 0.6 copy-start.14
  152.5 0.9 copy-start.9
  152.5 1.2 copy-start.10
  162.3 13.6 %collective-permute-start.12 = (bf16[49,64,256]{2,1,0:T(8,128)(2,1)}, bf16[49,64,256]{2,1,0:T(8,128)(2,1)S(1)}, u32[]{:S(2)}, u32[]{:S(2)}) collective-permute-start(bf16[49,64,256]{2,1,0:T(8,128)(2,1)} %get-tuple-element.36), channel_id=1, source_target_pairs={{0,1},{1,0},{2,3},{3,2},{4,5},{5,4},{6,7},{7,6},{8,9},{9,8},{10,11... | collective-permute-start | bytes 4816904 | tf_op jit(solution)/shard_map/ppermute | solution.py:269
  162.3 11.9 %collective-permute-start.19 = (bf16[7,96,128]{2,1,0:T(8,128)(2,1)S(1)}, bf16[7,96,128]{2,1,0:T(8,128)(2,1)S(1)}, u32[]{:S(2)}, u32[]{:S(2)}) collective-permute-start(bf16[7,96,128]{2,1,0:T(8,128)(2,1)S(1)} %pad_maximum_fusion.1), channel_id=1, source_target_pairs={{0,16},{2,18},{4,20},{6,22},{8,24},{10,26},{12,28},{14,30},{16,0},... | collective-permute-start | bytes 516104 | tf_op jit(solution)/shard_map/ppermute | solution.py:296
  174.7 2.2 %copy-start.5 = (f32[49,64,256]{2,1,0:T(8,128)S(1)}, f32[49,64,256]{2,1,0:T(8,128)}, u32[]{:S(2)}) copy-start(f32[49,64,256]{2,1,0:T(8,128)} %get-tuple-element.35) | copy-start | bytes 9633796

commit v2 on v1

v2 whole, which is shorter than its diff:
```python
import functools
import math

import jax
import jax.numpy as jnp
from jax import lax
from jax.experimental import pallas as pl
from jax.experimental.pallas import tpu as pltpu
from jax.sharding import PartitionSpec as P

LMAX = 6
HALO = 128
SOFT_CAP = 10.0
F32 = jnp.float32
BF16 = jnp.bfloat16


def degree_of(comp):
    return math.isqrt(comp)


def nn(lhs, rhs):
    return lax.dot_general(lhs, rhs, (((1,), (0,)), ((), ())), preferred_element_type=F32)


def nt(lhs, rhs):
    return lax.dot_general(lhs, rhs, (((1,), (1,)), ((), ())), preferred_element_type=F32)


def tn(lhs, rhs):
    return lax.dot_general(lhs, rhs, (((0,), (0,)), ((), ())), preferred_element_type=F32)


def pick(table, index):
    return jnp.take_along_axis(table, index, axis=1, mode="promise_in_bounds")


def head_rows_of(ref, first_row, rows):
    block = ref[:, first_row : first_row + rows, :]
    return block.reshape(block.shape[0] * rows, block.shape[2])


def slot_tile(window_index, tile):
    atoms, slots = window_index.shape
    lane = lax.broadcasted_iota(jnp.int32, (atoms, HALO), 1) + tile * HALO
    found = jnp.full((atoms, HALO), -1, jnp.int32)
    for slot in range(slots):
        found = jnp.where(window_index[:, slot : slot + 1] == lane, slot, found)
    return found


def spread(slot, coef, quantity, slots):
    values = pick(coef, jnp.maximum(slot, 0) + quantity * slots)
    return jnp.where(slot >= 0, values, 0.0).astype(BF16)


def wide_transpose(rows):
    return jnp.concatenate([rows] * (HALO // rows.shape[0]), axis=0).T


def own_kernel(heads, total_atoms, place, fm, fo, cot, weights, neighbours,
               qkv, scores, slot_own, index_rows, index_wide, wp, wc):
    comps, chan_local = fm.shape[0], fm.shape[1]
    channels = weights.shape[3]
    rows = chan_local // heads
    slots = neighbours.shape[0]
    core, first_atom = place[0], place[1]
    for degree in range(LMAX + 1):
        mix = jnp.concatenate([weights[g, degree] for g in range(3)], axis=0).astype(F32)
        mix = jnp.where(core == 0, mix, pltpu.roll(mix, chan_local, 1))
        wp[degree] = mix.astype(BF16)
        padded = jnp.concatenate([mix, jnp.zeros((chan_local, channels), F32)], axis=0)
        wc[degree] = padded.T[:, : 3 * chan_local].astype(BF16)
    for comp in range(comps):
        feats = jnp.concatenate([fm[comp], fo[comp]], axis=0)
        qkv[comp] = nn(wp[degree_of(comp)], feats).astype(BF16)
    for head in range(heads):
        query = head_rows_of(qkv, head * rows, rows)
        key = head_rows_of(qkv, chan_local + head * rows, rows)
        value = head_rows_of(qkv, 2 * chan_local + head * rows, rows)
        scores[head] = tn(query, key)
        scores[heads + head] = tn(head_rows_of(cot, head * rows, rows), value)
    for half in range(2):
        span = slice(half * HALO, (half + 1) * HALO)
        index = neighbours[:, span] - (first_atom + (half - 1) * HALO)
        index = jnp.where(index < 0, index + total_atoms, index)
        index = jnp.where(index >= total_atoms, index - total_atoms, index)
        index_rows[:, span] = index
        wide = wide_transpose(index)
        index_wide[span, :] = wide
        for tile in range(3):
            slot_own[half, tile] = slot_tile(wide[:, :slots], tile)


def edge_kernel(heads, score_scale, flm, flo, frm, fro, wp, qkv, cot, scores, bias, valid,
                index_rows, index_wide, halo_qkv, grad_bias, message_a, message_b):
    comps, chan_local = flm.shape[0], flm.shape[1]
    rows = chan_local // heads
    slots = valid.shape[0]
    for comp in range(comps):
        feats = jnp.concatenate(
            [
                jnp.concatenate([flm[comp], frm[comp]], axis=1),
                jnp.concatenate([flo[comp], fro[comp]], axis=1),
            ],
            axis=0,
        )
        halo_qkv[comp] = nn(wp[degree_of(comp)], feats).astype(BF16)
    lane = lax.broadcasted_iota(jnp.int32, (HALO, 2 * heads * slots), 1)
    gathered = [jnp.zeros((HALO, 2 * heads * slots), F32) for _ in range(2)]
    for quantity in range(2 * heads):
        head = quantity % heads
        if quantity < heads:
            mine = head_rows_of(qkv, head * rows, rows)
            theirs = head_rows_of(halo_qkv, chan_local + head * rows, rows)
        else:
            mine = head_rows_of(cot, head * rows, rows)
            theirs = head_rows_of(halo_qkv, 2 * chan_local + head * rows, rows)
        left = tn(mine[:, :HALO], theirs[:, :HALO])
        right = tn(mine[:, HALO:], theirs[:, HALO:])
        for half in range(2):
            own = scores[quantity, half * HALO : (half + 1) * HALO, :]
            own = [own[:, :HALO], own[:, HALO:]]
            tiles = [left] + own if half == 0 else own + [right]
            index = index_wide[half * HALO : (half + 1) * HALO, :]
            inner, tile_of = index & (HALO - 1), index >> 7
            values = jnp.where(
                tile_of == 0,
                pick(tiles[0], inner),
                jnp.where(tile_of == 1, pick(tiles[1], inner), pick(tiles[2], inner)),
            )
            gathered[half] = jnp.where(lane // slots == quantity, values, gathered[half])
    for half, message in enumerate((message_a, message_b)):
        span = slice(half * HALO, (half + 1) * HALO)
        edges = gathered[half].T.reshape(2, heads, slots, HALO)
        squashed = jnp.tanh(edges[0] * (score_scale / SOFT_CAP))
        logits = SOFT_CAP * squashed + bias[:, :, span]
        live = valid[:, span][None] > 0
        weight = jnp.where(live, jnp.exp(logits), 0.0)
        attention = weight / jnp.sum(weight, axis=1, keepdims=True)
        grad_attn = edges[1]
        grad_logit = attention * (
            grad_attn - jnp.sum(attention * grad_attn, axis=1, keepdims=True)
        )
        grad_bias[:, :, span] = grad_logit
        grad_raw = score_scale * grad_logit * (1.0 - squashed * squashed)
        index = index_rows[:, span]
        both = jnp.stack([grad_raw, attention]).reshape(2 * heads, slots, HALO)
        merged = jnp.zeros_like(both)
        for slot in range(slots):
            same = (index == index[slot : slot + 1, :])[None]
            merged = merged + jnp.where(same, both[:, slot : slot + 1, :], 0.0)
        atom = lax.broadcasted_iota(jnp.int32, (slots, HALO), 1)
        message[: 2 * heads * slots, :] = merged.reshape(2 * heads * slots, HALO).astype(BF16)
        message[2 * heads * slots :, :] = (index - HALO - atom).astype(F32).astype(BF16)


def grads_kernel(heads, slots, place, fm, fo, flm, flo, frm, fro, qkv, halo_qkv, cot, slot_own,
                 message_a, message_b, grad_query, own_key, own_value, weight_terms, ext):
    comps, chan_local = fm.shape[0], fm.shape[1]
    rows = chan_local // heads
    atoms = 2 * HALO
    core = place[0]
    empty = jnp.zeros((HALO, HALO), BF16)
    coefs = [message[: 2 * heads * slots, :].astype(F32).T for message in (message_a, message_b)]
    for head in range(heads):
        tables = []
        for quantity in (head, heads + head):
            halves = []
            for half in range(2):
                tiles = [spread(slot_own[half, t], coefs[half], quantity, slots) for t in range(3)]
                tiles = tiles + [empty] if half == 0 else [empty] + tiles
                halves.append(jnp.concatenate(tiles, axis=1))
            tables.append(jnp.concatenate(halves, axis=0))
        raw_table, attn_table = tables
        query = head_rows_of(qkv, head * rows, rows)
        key = head_rows_of(qkv, chan_local + head * rows, rows)
        halo_key = head_rows_of(halo_qkv, chan_local + head * rows, rows)
        key_ext = jnp.concatenate([halo_key[:, :HALO], key, halo_key[:, HALO:]], axis=1)
        span = slice(head * rows, (head + 1) * rows)
        value_span = slice(chan_local + head * rows, chan_local + (head + 1) * rows)
        grad_query[:, span, :] = nt(key_ext, raw_table).astype(BF16).reshape(comps, rows, atoms)
        key_sums = nn(query, raw_table)
        own_key[:, span, :] = key_sums[:, HALO : HALO + atoms].reshape(comps, rows, atoms)
        ext[:, span, :] = key_sums.astype(BF16).reshape(comps, rows, atoms + 2 * HALO)
        value_sums = nn(head_rows_of(cot, head * rows, rows), attn_table)
        own_value[:, span, :] = value_sums[:, HALO : HALO + atoms].reshape(comps, rows, atoms)
        ext[:, value_span, :] = value_sums.astype(BF16).reshape(comps, rows, atoms + 2 * HALO)
    for degree in range(LMAX + 1):
        query_total = jnp.zeros((chan_local, 2 * chan_local), F32)
        keyval_total = jnp.zeros((2 * chan_local, 2 * chan_local), F32)
        for comp in range(degree * degree, (degree + 1) * (degree + 1)):
            own = jnp.concatenate([fm[comp], fo[comp]], axis=0)
            wide = jnp.concatenate(
                [
                    jnp.concatenate([flm[comp], fm[comp], frm[comp]], axis=1),
                    jnp.concatenate([flo[comp], fo[comp], fro[comp]], axis=1),
                ],
                axis=0,
            )
            query_total = query_total + nt(grad_query[comp], own)
            keyval_total = keyval_total + nt(ext[comp], wide)
        total = jnp.concatenate([query_total, keyval_total], axis=0)
        total = jnp.where(core == 0, total, pltpu.roll(total, chan_local, 1))
        for g in range(3):
            weight_terms[g, degree] = total[g * chan_local : (g + 1) * chan_local]


def halo_slots(message_left, message_right, quantities, slots):
    coefs, tables = [], []
    for message, tile in ((message_left, 2), (message_right, 0)):
        coefs.append(message[: quantities * slots, :].astype(F32).T)
        offset = message[quantities * slots :, :].astype(F32).astype(jnp.int32)
        atom = lax.broadcasted_iota(jnp.int32, offset.shape, 1)
        tables.append(slot_tile(wide_transpose(offset + HALO + atom)[:, :slots], tile))
    return coefs, tables


def key_kernel(heads, slots, grad_query, own_key, halo_qkv, message_left, message_right, wc,
               terms, grad):
    comps, chan_local = grad_query.shape[0], grad_query.shape[1]
    rows = chan_local // heads
    grad[:, :chan_local, :] = grad_query[...]
    coefs, tables = halo_slots(message_left, message_right, 2 * heads, slots)
    for head in range(heads):
        query = head_rows_of(halo_qkv, head * rows, rows)
        rim = jnp.concatenate(
            [
                nn(query[:, :HALO], spread(tables[0], coefs[0], head, slots)),
                nn(query[:, HALO:], spread(tables[1], coefs[1], head, slots)),
            ],
            axis=1,
        )
        total = head_rows_of(own_key, head * rows, rows) + rim
        span = slice(chan_local + head * rows, chan_local + (head + 1) * rows)
        grad[:, span, :] = total.astype(BF16).reshape(comps, rows, 2 * HALO)
    for comp in range(comps):
        terms[comp] = nn(wc[degree_of(comp)][:, : 2 * chan_local], grad[comp])


def value_kernel(heads, slots, start, own_value, cl, cr, message_left, message_right, wc, terms,
                 mine, theirs, grad):
    comps, chan_local = cl.shape[0], cl.shape[1]
    rows = chan_local // heads
    coefs, tables = halo_slots(message_left, message_right, 2 * heads, slots)
    for head in range(heads):
        span = slice(head * rows, (head + 1) * rows)
        rim = jnp.concatenate(
            [
                nn(head_rows_of(cl, head * rows, rows),
                   spread(tables[0], coefs[0], heads + head, slots)),
                nn(head_rows_of(cr, head * rows, rows),
                   spread(tables[1], coefs[1], heads + head, slots)),
            ],
            axis=1,
        )
        own = own_value[start : start + comps, span, :].reshape(comps * rows, 2 * HALO)
        grad[:, span, :] = (own + rim).astype(BF16).reshape(comps, rows, 2 * HALO)
    for comp in range(comps):
        mix = wc[degree_of(start + comp)][:, 2 * chan_local :]
        total = terms[start + comp] + nn(mix, grad[comp])
        mine[comp] = total[:chan_local]
        theirs[comp] = total[chan_local:].astype(BF16)


def finish_kernel(mine_a, theirs_a, mine_b, theirs_b, out):
    cut = mine_a.shape[0]
    out[:cut] = (mine_a[...] + theirs_a[...].astype(F32)).astype(BF16)
    out[cut:] = (mine_b[...] + theirs_b[...].astype(F32)).astype(BF16)


def call(kernel, args, outs, scratch=(), scalars=0, limit=24):
    whole = pl.BlockSpec(memory_space=pltpu.VMEM)
    small = pl.BlockSpec(memory_space=pltpu.SMEM)
    args = list(args)
    args[scalars:] = [pltpu.with_memory_space_constraint(a, pltpu.VMEM) for a in args[scalars:]]
    return pl.pallas_call(
        kernel,
        out_shape=tuple(outs),
        in_specs=[small] * scalars + [whole] * (len(args) - scalars),
        out_specs=tuple([whole] * len(outs)),
        scratch_shapes=list(scratch),
        compiler_params=pltpu.CompilerParams(vmem_limit_bytes=limit * 1024 * 1024),
        cost_estimate=pl.CostEstimate(flops=0, bytes_accessed=1024, transcendentals=0),
    )(*args)


def after(values, tokens):
    anywhere = pl.BlockSpec(memory_space=pl.ANY)
    count = len(values)

    def kernel(*refs):
        pass

    return pl.pallas_call(
        kernel,
        out_shape=tuple(jax.ShapeDtypeStruct(v.shape, v.dtype) for v in values),
        in_specs=[anywhere] * (count + len(tokens)),
        out_specs=tuple([anywhere] * count),
        input_output_aliases={i: i for i in range(count)},
        cost_estimate=pl.CostEstimate(flops=0, bytes_accessed=1024, transcendentals=0),
    )(*values, *tokens)


def shifted(value, axis, steps):
    count = lax.axis_size(axis)
    pairs = [(source, (source + steps) % count) for source in range(count)]
    return lax.ppermute(value, axis, pairs)


def summed_over(value, axis):
    count = lax.axis_size(axis)
    columns = value.shape[-1]
    flat = value.reshape(-1, columns)
    rows = -(-flat.shape[0] // count)
    padded = jnp.pad(flat, ((0, rows * count - flat.shape[0]), (0, 0)))
    pieces = padded.reshape(count, rows, columns).astype(BF16)
    pieces = lax.all_to_all(pieces, axis, 0, 0, tiled=True)
    piece = jnp.sum(pieces.astype(F32), axis=0).astype(BF16)
    every = lax.all_to_all(jnp.broadcast_to(piece[None], pieces.shape), axis, 0, 0, tiled=True)
    return every.astype(F32).reshape(rows * count, columns)[: flat.shape[0]].reshape(value.shape)


def on_device(features, weights, cotangent, edge_bias, neighbours, valid_mask):
    chan_local, comps, atoms_dev = features.shape
    heads, slots = edge_bias.shape[0], edge_bias.shape[1]
    channels = weights.shape[2]
    assert atoms_dev == 2 * HALO and channels == 2 * chan_local
    score_scale = 1.0 / math.sqrt(chan_local // heads * comps)
    total_atoms = atoms_dev * lax.axis_size("atom")
    place = jnp.stack([lax.axis_index("chan"), lax.axis_index("atom") * atoms_dev])
    place = place.astype(jnp.int32)
    cut = comps // 2

    def held(*dims, dtype=F32):
        return pltpu.VMEM(dims, dtype)

    def plain(*dims, dtype=F32):
        return jax.ShapeDtypeStruct(dims, dtype)

    fm = jnp.transpose(features, (1, 0, 2))
    cot = jnp.transpose(cotangent, (1, 0, 2))
    mix = jnp.transpose(weights, (0, 1, 3, 2))
    flm = shifted(fm[:, :, HALO:], "atom", 1)
    frm = shifted(fm[:, :, :HALO], "atom", -1)
    fo = shifted(fm, "chan", 1)
    rims = [cot[:cut, :, HALO:], cot[:cut, :, :HALO], cot[cut:, :, HALO:], cot[cut:, :, :HALO]]

    qkv, scores, slot_own, index_rows, index_wide, wp, wc = call(
        functools.partial(own_kernel, heads, total_atoms),
        (place, fm, fo, cot, mix, neighbours),
        (
            held(comps, 3 * chan_local, atoms_dev, dtype=BF16),
            held(2 * heads, atoms_dev, atoms_dev),
            held(2, 3, HALO, HALO, dtype=jnp.int32),
            held(slots, atoms_dev, dtype=jnp.int32),
            held(atoms_dev, HALO, dtype=jnp.int32),
            held(LMAX + 1, 3 * chan_local, channels, dtype=BF16),
            held(LMAX + 1, channels, 3 * chan_local, dtype=BF16),
        ),
        scalars=1,
    )
    flm, frm = after((flm, frm), (index_rows,))
    flo = shifted(flm, "chan", 1)
    fro = shifted(frm, "chan", 1)
    rims[:2] = after(rims[:2], (flm, frm))
    first = (shifted(rims[0], "atom", 1), shifted(rims[1], "atom", -1))
    halo_qkv, grad_bias, message_a, message_b = call(
        functools.partial(edge_kernel, heads, score_scale),
        (flm, flo, frm, fro, wp, qkv, cot, scores, edge_bias, valid_mask, index_rows, index_wide),
        (
            held(comps, 3 * chan_local, atoms_dev, dtype=BF16),
            plain(heads, slots, atoms_dev),
            held((2 * heads + 1) * slots, HALO, dtype=BF16),
            held((2 * heads + 1) * slots, HALO, dtype=BF16),
        ),
    )
    message_left = shifted(message_b, "atom", 1)
    message_right = shifted(message_a, "atom", -1)
    rims[2:] = after(rims[2:], (message_left, message_right))
    second = (shifted(rims[2], "atom", 1), shifted(rims[3], "atom", -1))
    grad_query, own_key, own_value, weight_terms = call(
        functools.partial(grads_kernel, heads, slots),
        (place, fm, fo, flm, flo, frm, fro, qkv, halo_qkv, cot, slot_own, message_a, message_b),
        (
            held(comps, chan_local, atoms_dev, dtype=BF16),
            held(comps, chan_local, atoms_dev),
            held(comps, chan_local, atoms_dev),
            held(3, LMAX + 1, chan_local, channels),
        ),
        scratch=[pltpu.VMEM((comps, 2 * chan_local, 2 * atoms_dev), BF16)],
        scalars=1,
    )
    grad_weights = summed_over(weight_terms, "atom")
    (terms,) = call(
        functools.partial(key_kernel, heads, slots),
        (grad_query, own_key, halo_qkv, message_left, message_right, wc),
        (held(comps, channels, atoms_dev),),
        scratch=[pltpu.VMEM((comps, 2 * chan_local, atoms_dev), BF16)],
    )
    parts = []
    for start, (cl, cr) in ((0, first), (cut, second)):
        count = cl.shape[0]
        mine, theirs = call(
            functools.partial(value_kernel, heads, slots, start),
            (own_value, cl, cr, message_left, message_right, wc, terms),
            (
                held(count, chan_local, atoms_dev),
                held(count, chan_local, atoms_dev, dtype=BF16),
            ),
            scratch=[pltpu.VMEM((count, chan_local, atoms_dev), BF16)],
        )
        parts += [mine, shifted(theirs, "chan", 1)]
    (out,) = call(finish_kernel, parts, (plain(comps, chan_local, atoms_dev, dtype=BF16),))
    grad_features = jnp.transpose(out, (1, 0, 2))
    grad_weights = jnp.transpose(grad_weights, (0, 1, 3, 2))
    return grad_features, grad_weights, grad_bias


def solution(mesh):
    in_specs = (
        P("chan", None, "atom"),
        P(None, None, None, "chan"),
        P("chan", None, "atom"),
        P("chan", None, "atom"),
        P(None, "atom"),
        P(None, "atom"),
    )
    out_specs = (P("chan", None, "atom"), P(None, None, None, "chan"), P("chan", None, "atom"))
    return jax.shard_map(
        on_device, mesh=mesh, in_specs=in_specs, out_specs=out_specs, check_vma=False
    )
```

time: 179 us -> 151 us (0.84)
  local copies, waits for them, and re-layouts: 14.2 us -> 36.3 us
  waiting for transfers between devices: 67.3 us -> 48.1 us
  Pallas kernels: 48.1 us -> 29.8 us
  starting transfers between devices: 41.6 us -> 33.7 us
  other arithmetic: 6.44 us -> 1.17 us
    ppermute x7 -> x0, waiting for transfers between devices: 29 us -> none  [the longest x3 20.3 us: summed_over(): value = keep + lax.ppermute(send, axis, pairs).astype(F32)]
    unnamed x37 -> x70, local copies, waits for them, and re-layouts: 4.3 us -> 28.6 us
    pallas_call x5 -> x10, Pallas kernels: 48.1 us -> 29.8 us  [the longest x7 29.8 us: call(): pl.pallas_call(kernel, out_shape=tuple(outs), in_specs=[small] * scalars...]
    ppermute x13, starting transfers between devices: 35.6 us -> 24.3 us  [shifted(): return lax.ppermute(value, axis, pairs)]
    all_to_all x0 -> x2, starting transfers between devices: none -> 9.41 us  [the longest x1 5.21 us: summed_over(): lax.all_to_all(jnp.broadcast_to(piece[None], pieces.shape), axis, 0, 0, t...]
    all_to_all x0 -> x2, waiting for transfers between devices: none -> 8.61 us  [the longest x1 8.6 us: summed_over(): lax.all_to_all(jnp.broadcast_to(piece[None], pieces.shape), axis, 0, 0, t...]
    transpose x5 -> x1, local copies, waits for them, and re-layouts: 7.09 us -> 0.91 us  [on_device(): grad_weights = jnp.transpose(grad_weights, (0, 1, 3, 2))]
    ppermute x7 -> x0, starting transfers between devices: 6.03 us -> none  [the longest x3 5.65 us: summed_over(): other = lax.ppermute(value, axis, pairs)]
  transfers between devices with their start and end apart: 20 -> 15, of which waited for: 8 -> 8; matrix products, arithmetic and copies ran while one was open for 6% -> 5% of each run, Pallas kernels for 15% -> 16%
where the time goes in v2:
time: 151 us; the launch traced here: 150 us
  waiting for transfers between devices  48.1 us (32%)
  local copies, waits for them, and re-layouts  36.3 us (24%)
  starting transfers between devices  33.7 us (22%)
  Pallas kernels  29.8 us (20%)
    ppermute x13, waiting for transfers between devices, shifted(): return lax.ppermute(value, axis, pairs)  39.5 us
    pallas_call x7, Pallas kernels, call(): pl.pallas_call(kernel, out_shape=tuple(outs), in_specs=[small] * scalars...  29.8 us
    unnamed x70, local copies, waits for them, and re-layouts  28.6 us
    ppermute x13, starting transfers between devices, shifted(): return lax.ppermute(value, axis, pairs)  24.3 us
    all_to_all x1, waiting for transfers between devices, summed_over(): lax.all_to_all(jnp.broadcast_to(piece[None], pieces.shape), axis, 0, 0, t...  8.6 us
    all_to_all x1, starting transfers between devices, summed_over(): lax.all_to_all(jnp.broadcast_to(piece[None], pieces.shape), axis, 0, 0, t...  5.21 us
    all_to_all x1, starting transfers between devices, summed_over(): pieces = lax.all_to_all(pieces, axis, 0, 0, tiled=True)  4.2 us
  transfers between devices with their start and end apart: 15, of which 8 were waited for; matrix products, arithmetic and copies ran while one was open for 5% of the time, Pallas kernels for 16%

profile of v2, /device:TPU:0, one launch (start us, length us, event | category | flops | bytes accessed | tf_op | source)
XLA Modules:
  0.0 150.0 jit_solution(9233582024132380877)
XLA Ops:
  1.2 2.9 %fusion.2 = (bf16[49,64,128]{2,1,0:T(8,128)(2,1)}, bf16[49,64,128]{2,1,0:T(8,128)(2,1)}) fusion(bf16[49,64,256]{2,1,0:T(8,128)(2,1)} %bitcast.15), kind=kLoop, calls=%fused_computation.3 | loop fusion | bytes 3211264 | tf_op jit(solution)/shard_map/slice | solution.py:345
  4.1 2.4 %collective-permute-start.1 = (bf16[49,64,128]{2,1,0:T(8,128)(2,1)}, bf16[49,64,128]{2,1,0:T(8,128)(2,1)}, u32[]{:S(2)}, u32[]{:S(2)}) collective-permute-start(bf16[49,64,128]{2,1,0:T(8,128)(2,1)} %get-tuple-element.58), channel_id=1, source_target_pairs={{0,2},{2,4},{4,6},{6,8},{8,10},{10,12},{12,14},{14,16},{16,18},{18... | collective-permute-start | bytes 2408456 | tf_op jit(solution)/shard_map/ppermute | solution.py:308
  6.5 4.0 %collective-permute-start.2 = (bf16[49,64,128]{2,1,0:T(8,128)(2,1)}, bf16[49,64,128]{2,1,0:T(8,128)(2,1)}, u32[]{:S(2)}, u32[]{:S(2)}) collective-permute-start(bf16[49,64,128]{2,1,0:T(8,128)(2,1)} %get-tuple-element.57), channel_id=1, source_target_pairs={{0,30},{2,0},{4,2},{6,4},{8,6},{10,8},{12,10},{14,12},{16,14},{18,... | collective-permute-start | bytes 2408456 | tf_op jit(solution)/shard_map/ppermute | solution.py:308
  10.6 1.0 copy-done.25
  12.3 4.4 %shard_map.85 = (bf16[49,192,256]{2,1,0:T(8,128)(2,1)S(1)}, f32[8,256,256]{2,1,0:T(8,128)S(1)}, s32[2,3,128,128]{3,2,1,0:T(8,128)S(1)}, s32[16,256]{1,0:T(8,128)...) custom-call(s32[2]{0:T(128)S(1)} %pad_add_fusion.place, ...), custom_call_target="tpu_custom_call" | custom-call | bytes 1024 | tf_op jit(solution)/shard_map/pallas_call | solution.py:277
  16.7 2.2 %copy-done.3 = bf16[49,192,256]{2,1,0:T(8,128)(2,1)} copy-done((bf16[49,192,256]{2,1,0:T(8,128)(2,1)}, bf16[49,192,256]{2,1,0:T(8,128)(2,1)S(1)}, u32[]{:S(2)}) %copy-start.3) | copy-done | bytes 4816920
  18.9 0.8 copy-done.9
  19.7 1.3 copy-done.13
  21.1 0.8 copy-done.23
  23.1 18.8 %collective-permute-done.1.refs_0_ = bf16[49,64,128]{2,1,0:T(8,128)(2,1)} collective-permute-done((bf16[49,64,128]{2,1,0:T(8,128)(2,1)}, bf16[49,64,128]{2,1,0:T(8,128)(2,1)}, u32[]{:S(2)}, u32[]{:S(2)}) %collective-permute-start.1) | collective-permute-done | bytes 802848 | tf_op jit(solution)/shard_map/ppermute | solution.py:308
  41.9 1.9 %collective-permute-done.2.refs_1_ = bf16[49,64,128]{2,1,0:T(8,128)(2,1)} collective-permute-done((bf16[49,64,128]{2,1,0:T(8,128)(2,1)}, bf16[49,64,128]{2,1,0:T(8,128)(2,1)}, u32[]{:S(2)}, u32[]{:S(2)}) %collective-permute-start.2) | collective-permute-done | bytes 802848 | tf_op jit(solution)/shard_map/ppermute | solution.py:308
  44.3 2.0 %collective-permute-done.3.flo = bf16[49,64,128]{2,1,0:T(8,128)(2,1)S(1)} collective-permute-done((bf16[49,64,128]{2,1,0:T(8,128)(2,1)}, bf16[49,64,128]{2,1,0:T(8,128)(2,1)S(1)}, u32[]{:S(2)}, u32[]{:S(2)}) %collective-permute-start.3) | collective-permute-done | bytes 802848 | tf_op jit(solution)/shard_map/ppermute | solution.py:308
  46.3 1.1 collective-permute-done.4.fro
  47.5 2.4 %copy-done.4 = bf16[49,192,256]{2,1,0:T(8,128)(2,1)S(1)} copy-done((bf16[49,192,256]{2,1,0:T(8,128)(2,1)S(1)}, bf16[49,192,256]{2,1,0:T(8,128)(2,1)}, u32[]{:S(2)}) %copy-start.4) | copy-done | bytes 4816920
  49.9 1.6 %copy-done.14 = f32[8,256,256]{2,1,0:T(8,128)S(1)} copy-done((f32[8,256,256]{2,1,0:T(8,128)S(1)}, f32[8,256,256]{2,1,0:T(8,128)}, u32[]{:S(2)}) %copy-start.14) | copy-done | bytes 2097176
  51.4 0.9 copy-done.27
  52.4 0.8 copy-done.28
  54.6 5.8 %shard_map.87 = (bf16[49,192,256]{2,1,0:T(8,128)(2,1)S(1)}, f32[4,16,256]{2,1,0:T(8,128)}, bf16[144,128]{1,0:T(8,128)(2,1)}, bf16[144,128]{1,0:T(8,128)(2,1)}) custom-call(bf16[49,64,128]{2,1,0:T(8,128)(2,1)} %get-tuple-element.29.flm.refs_2_, bf16[49,64,128]{2,1,0:T(8,128)(2,1)S(1)} %collective-permute-done.3.flo, ...), custom_call_target="tpu_custom_call" | custom-call | bytes 1024 | tf_op jit(solution)/shard_map/pallas_call | solution.py:277
  60.5 1.5 %collective-permute-start.7 = (bf16[144,128]{1,0:T(8,128)(2,1)}, bf16[144,128]{1,0:T(8,128)(2,1)S(1)}, u32[]{:S(2)}, u32[]{:S(2)}) collective-permute-start(bf16[144,128]{1,0:T(8,128)(2,1)} %get-tuple-element.38.message_b), channel_id=1, source_target_pairs={{0,2},{2,4},{4,6},{6,8},{8,10},{10,12},{12,14},{14,16},{16,18},{18... | collective-permute-start | bytes 110600 | tf_op jit(solution)/shard_map/ppermute | solution.py:308
  62.0 4.1 %collective-permute-start.8 = (bf16[144,128]{1,0:T(8,128)(2,1)}, bf16[144,128]{1,0:T(8,128)(2,1)S(1)}, u32[]{:S(2)}, u32[]{:S(2)}) collective-permute-start(bf16[144,128]{1,0:T(8,128)(2,1)} %get-tuple-element.37.message_a), channel_id=1, source_target_pairs={{0,30},{2,0},{4,2},{6,4},{8,6},{10,8},{12,10},{14,12},{16,14},{18,... | collective-permute-start | bytes 110600 | tf_op jit(solution)/shard_map/ppermute | solution.py:308
  66.1 1.1 fusion
  67.3 8.2 %shard_map.88 = (bf16[49,64,256]{2,1,0:T(8,128)(2,1)S(1)}, f32[49,64,256]{2,1,0:T(8,128)S(1)}, f32[49,64,256]{2,1,0:T(8,128)S(1)}, f32[3,7,64,128]{3,2,1,0:T(8,128)S(1)}) custom-call(s32[2]{0:T(128)S(1)} %copy-done.34, bf16[49,64,256]{2,1,0:T(8,128)(2,1)S(1)} %bitcast.17, bf16[49,64,256]{2,1,0:T(8,128)(2,1)} %collective-permute-done.fo, ...), custom_call_target="tpu_custom_call" | custom-call | bytes 1024 | tf_op jit(solution)/shard_map/pallas_call | solution.py:277
  75.5 1.7 %copy-done.7 = f32[49,64,256]{2,1,0:T(8,128)} copy-done((f32[49,64,256]{2,1,0:T(8,128)}, f32[49,64,256]{2,1,0:T(8,128)S(1)}, u32[]{:S(2)}) %copy-start.7) | copy-done | bytes 3211288
  77.2 1.6 %copy-done.11 = f32[49,64,256]{2,1,0:T(8,128)} copy-done((f32[49,64,256]{2,1,0:T(8,128)}, f32[49,64,256]{2,1,0:T(8,128)S(1)}, u32[]{:S(2)}) %copy-start.11) | copy-done | bytes 3211288
  78.8 1.2 copy-done.17
  80.0 0.8 convert_element_type.10
  80.9 4.2 %all-to-all-start = ((bf16[16,84,128]{2,1,0:T(8,128)(2,1)}), bf16[16,84,128]{2,1,0:T(8,128)(2,1)}, u32[]{:S(2)}, u32[]{:S(2)}) async-start(bf16[16,84,128]{2,1,0:T(8,128)(2,1)} %convert_element_type.10), calls=%async_computation | async-start | bytes 720896 | tf_op jit(solution)/shard_map/all_to_all | solution.py:318
  85.7 1.7 %collective-permute-start.10 = (bf16[25,64,128]{2,1,0:T(8,128)(2,1)}, bf16[25,64,128]{2,1,0:T(8,128)(2,1)S(1)}, u32[]{:S(2)}, u32[]{:S(2)}) collective-permute-start(bf16[25,64,128]{2,1,0:T(8,128)(2,1)} %get-tuple-element.47), channel_id=1, source_target_pairs={{0,2},{2,4},{4,6},{6,8},{8,10},{10,12},{12,14},{14,16},{16,18},{18... | collective-permute-start | bytes 1228808 | tf_op jit(solution)/shard_map/ppermute | solution.py:308
  87.5 3.9 %collective-permute-start.11 = (bf16[25,64,128]{2,1,0:T(8,128)(2,1)}, bf16[25,64,128]{2,1,0:T(8,128)(2,1)S(1)}, u32[]{:S(2)}, u32[]{:S(2)}) collective-permute-start(bf16[25,64,128]{2,1,0:T(8,128)(2,1)} %get-tuple-element.48), channel_id=1, source_target_pairs={{0,30},{2,0},{4,2},{6,4},{8,6},{10,8},{12,10},{14,12},{16,14},{18,... | collective-permute-start | bytes 1228808 | tf_op jit(solution)/shard_map/ppermute | solution.py:308
  91.3 1.1 fusion.1
  92.4 5.6 %collective-permute-start.6 = (bf16[24,64,128]{2,1,0:T(8,128)(2,1)}, bf16[24,64,128]{2,1,0:T(8,128)(2,1)S(1)}, u32[]{:S(2)}, u32[]{:S(2)}) collective-permute-start(bf16[24,64,128]{2,1,0:T(8,128)(2,1)} %get-tuple-element.41), channel_id=1, source_target_pairs={{0,30},{2,0},{4,2},{6,4},{8,6},{10,8},{12,10},{14,12},{16,14},{18,... | collective-permute-start | bytes 1179656 | tf_op jit(solution)/shard_map/ppermute | solution.py:308
  98.1 2.4 %copy-done.2 = bf16[49,192,256]{2,1,0:T(8,128)(2,1)S(1)} copy-done((bf16[49,192,256]{2,1,0:T(8,128)(2,1)S(1)}, bf16[49,192,256]{2,1,0:T(8,128)(2,1)}, u32[]{:S(2)}) %copy-start.2) | copy-done | bytes 4816920
  100.4 1.9 %copy-done.12 = f32[49,64,256]{2,1,0:T(8,128)S(1)} copy-done((f32[49,64,256]{2,1,0:T(8,128)S(1)}, f32[49,64,256]{2,1,0:T(8,128)}, u32[]{:S(2)}) %copy-start.12) | copy-done | bytes 3211288
  102.3 1.4 copy-done.18
  103.8 2.9 %shard_map.90.terms = f32[49,128,256]{2,1,0:T(8,128)S(1)} custom-call(bf16[49,64,256]{2,1,0:T(8,128)(2,1)S(1)} %copy-done.18, f32[49,64,256]{2,1,0:T(8,128)S(1)} %copy-done.12, bf16[49,192,256]{2,1,0:T(8,128)(2,1)S(1)} %copy-done.2, bf16[144,128]{1,0:T(8,128)(2,1)S(1)} %copy-done.20, bf16[144,128]{1,0:T(8,128)(2,1)S(1)} %copy-done.22, ...), custom_call_target="tpu_custom_call" | custom-call | bytes 1024 | tf_op jit(solution)/shard_map/pallas_call | solution.py:277
  106.7 10.5 %collective-permute-done.10.cl = bf16[25,64,128]{2,1,0:T(8,128)(2,1)S(1)} collective-permute-done((bf16[25,64,128]{2,1,0:T(8,128)(2,1)}, bf16[25,64,128]{2,1,0:T(8,128)(2,1)S(1)}, u32[]{:S(2)}, u32[]{:S(2)}) %collective-permute-start.10) | collective-permute-done | bytes 409632 | tf_op jit(solution)/shard_map/ppermute | solution.py:308
  117.2 3.0 %shard_map.93 = (f32[25,64,256]{2,1,0:T(8,128)S(1)}, bf16[25,64,256]{2,1,0:T(8,128)(2,1)}) custom-call(f32[49,64,256]{2,1,0:T(8,128)S(1)} %copy-done.8, bf16[25,64,128]{2,1,0:T(8,128)(2,1)S(1)} %collective-permute-done.10.cl, bf16[25,64,128]{2,1,0:T(8,128)(2,1)S(1)} %collective-permute-done.11.cr, bf16[144,128]{1,0:T(8,128)(2,1)S(1)} %copy-done.20, ...), custom_call_target="tpu_custom_call" | custom-call | bytes 1024 | tf_op jit(solution)/shard_map/pallas_call | solution.py:277
  120.2 1.2 copy-done.15
  121.4 2.7 %collective-permute-done.5.cl = bf16[24,64,128]{2,1,0:T(8,128)(2,1)S(1)} collective-permute-done((bf16[24,64,128]{2,1,0:T(8,128)(2,1)}, bf16[24,64,128]{2,1,0:T(8,128)(2,1)S(1)}, u32[]{:S(2)}, u32[]{:S(2)}) %collective-permute-start.5) | collective-permute-done | bytes 393248 | tf_op jit(solution)/shard_map/ppermute | solution.py:308
  124.1 2.4 %collective-permute-done.6.cr = bf16[24,64,128]{2,1,0:T(8,128)(2,1)S(1)} collective-permute-done((bf16[24,64,128]{2,1,0:T(8,128)(2,1)}, bf16[24,64,128]{2,1,0:T(8,128)(2,1)S(1)}, u32[]{:S(2)}, u32[]{:S(2)}) %collective-permute-start.6) | collective-permute-done | bytes 393248 | tf_op jit(solution)/shard_map/ppermute | solution.py:308
  126.5 2.9 %shard_map.91 = (f32[24,64,256]{2,1,0:T(8,128)S(1)}, bf16[24,64,256]{2,1,0:T(8,128)(2,1)}) custom-call(f32[49,64,256]{2,1,0:T(8,128)S(1)} %copy-done.8, bf16[24,64,128]{2,1,0:T(8,128)(2,1)S(1)} %collective-permute-done.5.cl, bf16[24,64,128]{2,1,0:T(8,128)(2,1)S(1)} %collective-permute-done.6.cr, bf16[144,128]{1,0:T(8,128)(2,1)S(1)} %copy-done.20, ...), custom_call_target="tpu_custom_call" | custom-call | bytes 1024 | tf_op jit(solution)/shard_map/pallas_call | solution.py:277
  129.4 1.0 reduce_sum.12
  130.5 0.8 broadcast_in_dim.2
  131.2 5.2 %all-to-all-start.1 = ((bf16[16,84,128]{2,1,0:T(8,128)(2,1)}), bf16[16,84,128]{2,1,0:T(8,128)(2,1)S(1)}, u32[]{:S(2)}, u32[]{:S(2)}) async-start(bf16[16,84,128]{2,1,0:T(8,128)(2,1)} %broadcast_in_dim.2), calls=%async_computation.1 | async-start | bytes 720896 | tf_op jit(solution)/shard_map/all_to_all | solution.py:320
  136.5 1.4 copy-done.16
  137.9 2.5 %shard_map.94 = bf16[49,64,256]{2,1,0:T(8,128)(2,1)} custom-call(f32[24,64,256]{2,1,0:T(8,128)S(1)} %get-tuple-element.45.mine_a, bf16[24,64,256]{2,1,0:T(8,128)(2,1)} %collective-permute-done.9.theirs_a, f32[25,64,256]{2,1,0:T(8,128)S(1)} %copy-done.16, bf16[25,64,256]{2,1,0:T(8,128)(2,1)S(1)} %collective-permute-done.12.theirs_b), custom_call_target="tpu_custom_call" | custom-call | bytes 1024 | tf_op jit(solution)/shard_map/pallas_call | solution.py:277
  140.5 8.6 %all-to-all-done.1 = bf16[16,84,128]{2,1,0:T(8,128)(2,1)S(1)} async-done(((bf16[16,84,128]{2,1,0:T(8,128)(2,1)}), bf16[16,84,128]{2,1,0:T(8,128)(2,1)S(1)}, u32[]{:S(2)}, u32[]{:S(2)}) %all-to-all-start.1) | async-done | bytes 344096 | tf_op jit(solution)/shard_map/all_to_all | solution.py:320
  149.1 0.9 reshape.11
  (71 shorter events, 5.3 us)
Async XLA Ops:
  0.6 9.9 %copy-start = (bf16[64,49,256]{2,0,1:T(8,128)(2,1)S(1)}, bf16[64,49,256]{2,0,1:T(8,128)(2,1)}, u32[]{:S(2)}) copy-start(bf16[64,49,256]{2,0,1:T(8,128)(2,1)} %param.8) | copy-start | bytes 4816900
  0.6 9.9 %copy-start.6 = (bf16[64,49,256]{2,0,1:T(8,128)(2,1)S(1)}, bf16[64,49,256]{2,0,1:T(8,128)(2,1)}, u32[]{:S(2)}) copy-start(bf16[64,49,256]{2,0,1:T(8,128)(2,1)} %param.6) | copy-start | bytes 4816900
  0.6 9.9 %collective-permute-start = (bf16[49,64,256]{2,1,0:T(8,128)(2,1)}, bf16[49,64,256]{2,1,0:T(8,128)(2,1)}, u32[]{:S(2)}, u32[]{:S(2)}) collective-permute-start(bf16[49,64,256]{2,1,0:T(8,128)(2,1)} %bitcast.14), channel_id=1, source_target_pairs={{0,1},{1,0},{2,3},{3,2},{4,5},{5,4},{6,7},{7,6},{8,9},{9,8},{10,11... | collective-permute-start | bytes 4816904 | tf_op jit(solution)/shard_map/ppermute | solution.py:308
  4.1 37.8 %collective-permute-start.1 = (bf16[49,64,128]{2,1,0:T(8,128)(2,1)}, bf16[49,64,128]{2,1,0:T(8,128)(2,1)}, u32[]{:S(2)}, u32[]{:S(2)}) collective-permute-start(bf16[49,64,128]{2,1,0:T(8,128)(2,1)} %get-tuple-element.58), channel_id=1, source_target_pairs={{0,2},{2,4},{4,6},{6,8},{8,10},{10,12},{12,14},{14,16},{16,18},{18... | collective-permute-start | bytes 2408456 | tf_op jit(solution)/shard_map/ppermute | solution.py:308
  6.5 37.3 %collective-permute-start.2 = (bf16[49,64,128]{2,1,0:T(8,128)(2,1)}, bf16[49,64,128]{2,1,0:T(8,128)(2,1)}, u32[]{:S(2)}, u32[]{:S(2)}) collective-permute-start(bf16[49,64,128]{2,1,0:T(8,128)(2,1)} %get-tuple-element.57), channel_id=1, source_target_pairs={{0,30},{2,0},{4,2},{6,4},{8,6},{10,8},{12,10},{14,12},{16,14},{18,... | collective-permute-start | bytes 2408456 | tf_op jit(solution)/shard_map/ppermute | solution.py:308
  10.6 6.2 %copy-start.33 = (s32[2]{0:T(128)}, s32[2]{0:T(128)S(1)}, u32[]{:S(2)}) copy-start(s32[2]{0:T(128)S(1)} %pad_add_fusion.place) | copy-start | bytes 28
  10.6 1.0 copy-start.25
  11.6 0.7 copy-start.31
  16.7 2.2 %copy-start.3 = (bf16[49,192,256]{2,1,0:T(8,128)(2,1)}, bf16[49,192,256]{2,1,0:T(8,128)(2,1)S(1)}, u32[]{:S(2)}) copy-start(bf16[49,192,256]{2,1,0:T(8,128)(2,1)S(1)} %get-tuple-element.31.qkv) | copy-start | bytes 14450692
  18.9 0.8 copy-start.9
  19.7 1.3 copy-start.13
  21.1 0.8 copy-start.23
  21.8 0.7 copy-start.26
  43.8 2.5 %collective-permute-start.3 = (bf16[49,64,128]{2,1,0:T(8,128)(2,1)}, bf16[49,64,128]{2,1,0:T(8,128)(2,1)S(1)}, u32[]{:S(2)}, u32[]{:S(2)}) collective-permute-start(bf16[49,64,128]{2,1,0:T(8,128)(2,1)} %get-tuple-element.29.flm.refs_2_), channel_id=1, source_target_pairs={{0,1},{1,0},{2,3},{3,2},{4,5},{5,4},{6,7},{7,6},{8,9},{9,8},{10,11... | collective-permute-start | bytes 2408456 | tf_op jit(solution)/shard_map/ppermute | solution.py:308
  43.8 3.7 %collective-permute-start.4 = (bf16[49,64,128]{2,1,0:T(8,128)(2,1)}, bf16[49,64,128]{2,1,0:T(8,128)(2,1)S(1)}, u32[]{:S(2)}, u32[]{:S(2)}) collective-permute-start(bf16[49,64,128]{2,1,0:T(8,128)(2,1)} %get-tuple-element.30.frm.refs_3_), channel_id=1, source_target_pairs={{0,1},{1,0},{2,3},{3,2},{4,5},{5,4},{6,7},{7,6},{8,9},{9,8},{10,11... | collective-permute-start | bytes 2408456 | tf_op jit(solution)/shard_map/ppermute | solution.py:308
  47.5 2.4 %copy-start.4 = (bf16[49,192,256]{2,1,0:T(8,128)(2,1)S(1)}, bf16[49,192,256]{2,1,0:T(8,128)(2,1)}, u32[]{:S(2)}) copy-start(bf16[49,192,256]{2,1,0:T(8,128)(2,1)} %copy-done.3) | copy-start | bytes 14450692
  49.9 1.6 %copy-start.14 = (f32[8,256,256]{2,1,0:T(8,128)S(1)}, f32[8,256,256]{2,1,0:T(8,128)}, u32[]{:S(2)}) copy-start(f32[8,256,256]{2,1,0:T(8,128)} %copy-done.13) | copy-start | bytes 6291460
  51.4 0.9 copy-start.27
  52.3 0.8 copy-start.28
  53.2 0.7 copy-start.30
  53.9 0.7 copy-start.32
  54.6 12.7 %copy-start.5 = (bf16[49,192,256]{2,1,0:T(8,128)(2,1)S(1)}, bf16[49,192,256]{2,1,0:T(8,128)(2,1)}, u32[]{:S(2)}) copy-start(bf16[49,192,256]{2,1,0:T(8,128)(2,1)} %copy-done.3) | copy-start | bytes 14450692
  60.5 15.0 %copy-start.1 = (bf16[49,192,256]{2,1,0:T(8,128)(2,1)}, bf16[49,192,256]{2,1,0:T(8,128)(2,1)S(1)}, u32[]{:S(2)}) copy-start(bf16[49,192,256]{2,1,0:T(8,128)(2,1)S(1)} %get-tuple-element.35.halo_qkv) | copy-start | bytes 14450692
  60.5 6.8 %copy-start.24 = (s32[2,3,128,128]{3,2,1,0:T(8,128)S(1)}, s32[2,3,128,128]{3,2,1,0:T(8,128)}, u32[]{:S(2)}) copy-start(s32[2,3,128,128]{3,2,1,0:T(8,128)} %copy-done.23) | copy-start | bytes 1179652
  60.5 6.8 %copy-start.34 = (s32[2]{0:T(128)S(1)}, s32[2]{0:T(128)}, u32[]{:S(2)}) copy-start(s32[2]{0:T(128)} %copy-done.33) | copy-start | bytes 28
  60.5 24.6 %collective-permute-start.7 = (bf16[144,128]{1,0:T(8,128)(2,1)}, bf16[144,128]{1,0:T(8,128)(2,1)S(1)}, u32[]{:S(2)}, u32[]{:S(2)}) collective-permute-start(bf16[144,128]{1,0:T(8,128)(2,1)} %get-tuple-element.38.message_b), channel_id=1, source_target_pairs={{0,2},{2,4},{4,6},{6,8},{8,10},{10,12},{12,14},{14,16},{16,18},{18... | collective-permute-start | bytes 110600 | tf_op jit(solution)/shard_map/ppermute | solution.py:308
  62.0 23.1 %collective-permute-start.8 = (bf16[144,128]{1,0:T(8,128)(2,1)}, bf16[144,128]{1,0:T(8,128)(2,1)S(1)}, u32[]{:S(2)}, u32[]{:S(2)}) collective-permute-start(bf16[144,128]{1,0:T(8,128)(2,1)} %get-tuple-element.37.message_a), channel_id=1, source_target_pairs={{0,30},{2,0},{4,2},{6,4},{8,6},{10,8},{12,10},{14,12},{16,14},{18,... | collective-permute-start | bytes 110600 | tf_op jit(solution)/shard_map/ppermute | solution.py:308
  75.5 1.7 %copy-start.7 = (f32[49,64,256]{2,1,0:T(8,128)}, f32[49,64,256]{2,1,0:T(8,128)S(1)}, u32[]{:S(2)}) copy-start(f32[49,64,256]{2,1,0:T(8,128)S(1)} %get-tuple-element.39.own_value) | copy-start | bytes 9633796
  77.2 1.6 %copy-start.11 = (f32[49,64,256]{2,1,0:T(8,128)}, f32[49,64,256]{2,1,0:T(8,128)S(1)}, u32[]{:S(2)}) copy-start(f32[49,64,256]{2,1,0:T(8,128)S(1)} %get-tuple-element.44.own_key) | copy-start | bytes 9633796
  78.8 1.2 copy-start.17
  80.9 48.6 %all-to-all-start = ((bf16[16,84,128]{2,1,0:T(8,128)(2,1)}), bf16[16,84,128]{2,1,0:T(8,128)(2,1)}, u32[]{:S(2)}, u32[]{:S(2)}) async-start(bf16[16,84,128]{2,1,0:T(8,128)(2,1)} %convert_element_type.10), calls=%async_computation | async-start | bytes 720896 | tf_op jit(solution)/shard_map/all_to_all | solution.py:318
  85.1 0.6 copy-start.21
  85.7 31.4 %collective-permute-start.10 = (bf16[25,64,128]{2,1,0:T(8,128)(2,1)}, bf16[25,64,128]{2,1,0:T(8,128)(2,1)S(1)}, u32[]{:S(2)}, u32[]{:S(2)}) collective-permute-start(bf16[25,64,128]{2,1,0:T(8,128)(2,1)} %get-tuple-element.47), channel_id=1, source_target_pairs={{0,2},{2,4},{4,6},{6,8},{8,10},{10,12},{12,14},{14,16},{16,18},{18... | collective-permute-start | bytes 1228808 | tf_op jit(solution)/shard_map/ppermute | solution.py:308
  87.5 10.6 %copy-start.10 = (bf16[7,128,192]{2,1,0:T(8,128)(2,1)S(1)}, bf16[7,128,192]{2,1,0:T(8,128)(2,1)}, u32[]{:S(2)}) copy-start(bf16[7,128,192]{2,1,0:T(8,128)(2,1)} %copy-done.9) | copy-start | bytes 1032196
  87.5 10.6 %copy-start.20 = (bf16[144,128]{1,0:T(8,128)(2,1)S(1)}, bf16[144,128]{1,0:T(8,128)(2,1)}, u32[]{:S(2)}) copy-start(bf16[144,128]{1,0:T(8,128)(2,1)} %copy-done.19) | copy-start | bytes 110596
  87.5 10.6 %copy-start.22 = (bf16[144,128]{1,0:T(8,128)(2,1)S(1)}, bf16[144,128]{1,0:T(8,128)(2,1)}, u32[]{:S(2)}) copy-start(bf16[144,128]{1,0:T(8,128)(2,1)} %copy-done.21) | copy-start | bytes 110596
  87.5 29.7 %collective-permute-start.11 = (bf16[25,64,128]{2,1,0:T(8,128)(2,1)}, bf16[25,64,128]{2,1,0:T(8,128)(2,1)S(1)}, u32[]{:S(2)}, u32[]{:S(2)}) collective-permute-start(bf16[25,64,128]{2,1,0:T(8,128)(2,1)} %get-tuple-element.48), channel_id=1, source_target_pairs={{0,30},{2,0},{4,2},{6,4},{8,6},{10,8},{12,10},{14,12},{16,14},{18,... | collective-permute-start | bytes 1228808 | tf_op jit(solution)/shard_map/ppermute | solution.py:308
  92.4 31.7 %collective-permute-start.5 = (bf16[24,64,128]{2,1,0:T(8,128)(2,1)}, bf16[24,64,128]{2,1,0:T(8,128)(2,1)S(1)}, u32[]{:S(2)}, u32[]{:S(2)}) collective-permute-start(bf16[24,64,128]{2,1,0:T(8,128)(2,1)} %get-tuple-element.40), channel_id=1, source_target_pairs={{0,2},{2,4},{4,6},{6,8},{8,10},{10,12},{12,14},{14,16},{16,18},{18... | collective-permute-start | bytes 1179656 | tf_op jit(solution)/shard_map/ppermute | solution.py:308
  92.4 34.1 %collective-permute-start.6 = (bf16[24,64,128]{2,1,0:T(8,128)(2,1)}, bf16[24,64,128]{2,1,0:T(8,128)(2,1)S(1)}, u32[]{:S(2)}, u32[]{:S(2)}) collective-permute-start(bf16[24,64,128]{2,1,0:T(8,128)(2,1)} %get-tuple-element.41), channel_id=1, source_target_pairs={{0,30},{2,0},{4,2},{6,4},{8,6},{10,8},{12,10},{14,12},{16,14},{18,... | collective-permute-start | bytes 1179656 | tf_op jit(solution)/shard_map/ppermute | solution.py:308
  98.1 2.4 %copy-start.2 = (bf16[49,192,256]{2,1,0:T(8,128)(2,1)S(1)}, bf16[49,192,256]{2,1,0:T(8,128)(2,1)}, u32[]{:S(2)}) copy-start(bf16[49,192,256]{2,1,0:T(8,128)(2,1)} %copy-done.1) | copy-start | bytes 14450692
  100.4 1.9 %copy-start.12 = (f32[49,64,256]{2,1,0:T(8,128)S(1)}, f32[49,64,256]{2,1,0:T(8,128)}, u32[]{:S(2)}) copy-start(f32[49,64,256]{2,1,0:T(8,128)} %copy-done.11) | copy-start | bytes 9633796
  102.3 1.4 copy-start.18
  103.8 13.4 %copy-start.8 = (f32[49,64,256]{2,1,0:T(8,128)S(1)}, f32[49,64,256]{2,1,0:T(8,128)}, u32[]{:S(2)}) copy-start(f32[49,64,256]{2,1,0:T(8,128)} %copy-done.7) | copy-start | bytes 9633796
  120.2 1.2 copy-start.15
  121.4 15.1 %collective-permute-start.12 = (bf16[25,64,256]{2,1,0:T(8,128)(2,1)}, bf16[25,64,256]{2,1,0:T(8,128)(2,1)S(1)}, u32[]{:S(2)}, u32[]{:S(2)}) collective-permute-start(bf16[25,64,256]{2,1,0:T(8,128)(2,1)} %get-tuple-element.50), channel_id=1, source_target_pairs={{0,1},{1,0},{2,3},{3,2},{4,5},{5,4},{6,7},{7,6},{8,9},{9,8},{10,11... | collective-permute-start | bytes 2457608 | tf_op jit(solution)/shard_map/ppermute | solution.py:308
  129.4 7.1 %collective-permute-start.9 = (bf16[24,64,256]{2,1,0:T(8,128)(2,1)}, bf16[24,64,256]{2,1,0:T(8,128)(2,1)}, u32[]{:S(2)}, u32[]{:S(2)}) collective-permute-start(bf16[24,64,256]{2,1,0:T(8,128)(2,1)} %get-tuple-element.46), channel_id=1, source_target_pairs={{0,1},{1,0},{2,3},{3,2},{4,5},{5,4},{6,7},{7,6},{8,9},{9,8},{10,11... | collective-permute-start | bytes 2359304 | tf_op jit(solution)/shard_map/ppermute | solution.py:308
  131.2 17.8 %all-to-all-start.1 = ((bf16[16,84,128]{2,1,0:T(8,128)(2,1)}), bf16[16,84,128]{2,1,0:T(8,128)(2,1)S(1)}, u32[]{:S(2)}, u32[]{:S(2)}) async-start(bf16[16,84,128]{2,1,0:T(8,128)(2,1)} %broadcast_in_dim.2), calls=%async_computation.1 | async-start | bytes 720896 | tf_op jit(solution)/shard_map/all_to_all | solution.py:320
  136.5 1.4 copy-start.16
  (2 other events, 1.2 us)

commit v3 on v2

--- a/solution.py
+++ b/solution.py
@@ -58,8 +58,25 @@
     return jnp.concatenate([rows] * (HALO // rows.shape[0]), axis=0).T
 
 
-def own_kernel(heads, total_atoms, place, fm, fo, cot, weights, neighbours,
-               qkv, scores, slot_own, index_rows, index_wide, wp, wc):
+def split_kernel(fm, low, high, sems):
+    copies = [
+        pltpu.make_async_copy(fm.at[:, :, pl.ds(at * HALO, HALO)], part, sems.at[at])
+        for at, part in enumerate((low, high))
+    ]
+    for copy in copies:
+        copy.start()
+    for copy in copies:
+        copy.wait()
+
+
+def own_kernel(heads, total_atoms, cut, place, fm, fo, cot, weights, neighbours,
+               qkv, scores, slot_own, index_rows, index_wide, wp, wc, rims_a, rims_b,
+               rims_c, rims_d, token):
+    token[...] = jnp.zeros_like(token)
+    rims_a[...] = cot[:cut, :, HALO:]
+    rims_b[...] = cot[:cut, :, :HALO]
+    rims_c[...] = cot[cut:, :, HALO:]
+    rims_d[...] = cot[cut:, :, :HALO]
     comps, chan_local = fm.shape[0], fm.shape[1]
     channels = weights.shape[3]
     rows = chan_local // heads
@@ -156,7 +173,8 @@
 
 
 def grads_kernel(heads, slots, place, fm, fo, flm, flo, frm, fro, qkv, halo_qkv, cot, slot_own,
-                 message_a, message_b, grad_query, own_key, own_value, weight_terms, ext):
+                 message_a, message_b, grad_query, own_key, own_value, kept, sent_1, sent_2,
+                 sent_3, ext, weight_terms):
     comps, chan_local = fm.shape[0], fm.shape[1]
     rows = chan_local // heads
     atoms = 2 * HALO
@@ -203,7 +221,12 @@
         total = jnp.concatenate([query_total, keyval_total], axis=0)
         total = jnp.where(core == 0, total, pltpu.roll(total, chan_local, 1))
         for g in range(3):
-            weight_terms[g, degree] = total[g * chan_local : (g + 1) * chan_local]
+            weight_terms[g * (LMAX + 1) + degree] = total[g * chan_local : (g + 1) * chan_local]
+    piece = chan_local // 4
+    spot = place[2]
+    for delta, part in enumerate((kept, sent_1, sent_2, sent_3)):
+        first = pl.multiple_of((spot ^ delta) * piece, piece)
+        part[...] = weight_terms[:, pl.ds(first, piece), :].astype(part.dtype)
 
 
 def halo_slots(message_left, message_right, quantities, slots):
@@ -239,7 +262,8 @@
 
 
 def value_kernel(heads, slots, start, own_value, cl, cr, message_left, message_right, wc, terms,
-                 mine, theirs, grad):
+                 mine, theirs, token, grad):
+    token[...] = jnp.zeros_like(token)
     comps, chan_local = cl.shape[0], cl.shape[1]
     rows = chan_local // heads
     coefs, tables = halo_slots(message_left, message_right, 2 * heads, slots)
@@ -269,20 +293,37 @@
     out[cut:] = (mine_b[...] + theirs_b[...].astype(F32)).astype(BF16)
 
 
-def call(kernel, args, outs, scratch=(), scalars=0, limit=24):
+def gather_kernel(place, part_0, part_1, part_2, part_3, out):
+    piece = part_0.shape[1]
+    spot = place[2]
+    for delta, part in enumerate((part_0, part_1, part_2, part_3)):
+        first = pl.multiple_of((spot ^ delta) * piece, piece)
+        out[:, pl.ds(first, piece), :] = part[...].astype(F32)
+
+
+def call(kernel, args, outs, scratch=(), scalars=0, limit=24, stay=(), tokens=()):
     whole = pl.BlockSpec(memory_space=pltpu.VMEM)
     small = pl.BlockSpec(memory_space=pltpu.SMEM)
-    args = list(args)
-    args[scalars:] = [pltpu.with_memory_space_constraint(a, pltpu.VMEM) for a in args[scalars:]]
+    args = [
+        pltpu.with_memory_space_constraint(a, pltpu.VMEM) if at in stay else a
+        for at, a in enumerate(args)
+    ]
+    count = len(args)
+
+    def body(*refs):
+        kernel(*refs[:count], *refs[count + len(tokens) :])
+
     return pl.pallas_call(
-        kernel,
+        body,
         out_shape=tuple(outs),
-        in_specs=[small] * scalars + [whole] * (len(args) - scalars),
+        in_specs=[small] * scalars
+        + [whole] * (count - scalars)
+        + [pl.BlockSpec(memory_space=pl.ANY)] * len(tokens),
         out_specs=tuple([whole] * len(outs)),
         scratch_shapes=list(scratch),
         compiler_params=pltpu.CompilerParams(vmem_limit_bytes=limit * 1024 * 1024),
         cost_estimate=pl.CostEstimate(flops=0, bytes_accessed=1024, transcendentals=0),
-    )(*args)
+    )(*args, *tokens)
 
 
 def after(values, tokens):
@@ -298,6 +339,7 @@
         in_specs=[anywhere] * (count + len(tokens)),
         out_specs=tuple([anywhere] * count),
         input_output_aliases={i: i for i in range(count)},
+        compiler_params=pltpu.CompilerParams(vmem_limit_bytes=1024 * 1024),
         cost_estimate=pl.CostEstimate(flops=0, bytes_accessed=1024, transcendentals=0),
     )(*values, *tokens)
 
@@ -308,17 +350,9 @@
     return lax.ppermute(value, axis, pairs)
 
 
-def summed_over(value, axis):
+def exchanged(value, axis, offset):
     count = lax.axis_size(axis)
-    columns = value.shape[-1]
-    flat = value.reshape(-1, columns)
-    rows = -(-flat.shape[0] // count)
-    padded = jnp.pad(flat, ((0, rows * count - flat.shape[0]), (0, 0)))
-    pieces = padded.reshape(count, rows, columns).astype(BF16)
-    pieces = lax.all_to_all(pieces, axis, 0, 0, tiled=True)
-    piece = jnp.sum(pieces.astype(F32), axis=0).astype(BF16)
-    every = lax.all_to_all(jnp.broadcast_to(piece[None], pieces.shape), axis, 0, 0, tiled=True)
-    return every.astype(F32).reshape(rows * count, columns)[: flat.shape[0]].reshape(value.shape)
+    return lax.ppermute(value, axis, [(source, source ^ offset) for source in range(count)])
 
 
 def on_device(features, weights, cotangent, edge_bias, neighbours, valid_mask):
@@ -328,7 +362,12 @@
     assert atoms_dev == 2 * HALO and channels == 2 * chan_local
     score_scale = 1.0 / math.sqrt(chan_local // heads * comps)
     total_atoms = atoms_dev * lax.axis_size("atom")
-    place = jnp.stack([lax.axis_index("chan"), lax.axis_index("atom") * atoms_dev])
+    count = lax.axis_size("atom")
+    assert count >= 4 and count & (count - 1) == 0
+    atom_place = lax.axis_index("atom")
+    cut_bits = (1, 2) if count >= 8 else (0, 1)
+    spot = (atom_place >> cut_bits[0]) & 3
+    place = jnp.stack([lax.axis_index("chan"), atom_place * atoms_dev, spot])
     place = place.astype(jnp.int32)
     cut = comps // 2
 
@@ -341,13 +380,21 @@
     fm = jnp.transpose(features, (1, 0, 2))
     cot = jnp.transpose(cotangent, (1, 0, 2))
     mix = jnp.transpose(weights, (0, 1, 3, 2))
-    flm = shifted(fm[:, :, HALO:], "atom", 1)
-    frm = shifted(fm[:, :, :HALO], "atom", -1)
+    anywhere = pl.BlockSpec(memory_space=pl.ANY)
+    low, high = pl.pallas_call(
+        split_kernel,
+        out_shape=(plain(comps, chan_local, HALO, dtype=BF16),) * 2,
+        in_specs=[anywhere],
+        out_specs=(anywhere, anywhere),
+        scratch_shapes=[pltpu.SemaphoreType.DMA((2,))],
+        compiler_params=pltpu.CompilerParams(vmem_limit_bytes=1024 * 1024),
+    )(fm)
+    flm = shifted(high, "atom", 1)
+    frm = shifted(low, "atom", -1)
     fo = shifted(fm, "chan", 1)
-    rims = [cot[:cut, :, HALO:], cot[:cut, :, :HALO], cot[cut:, :, HALO:], cot[cut:, :, :HALO]]
-
-    qkv, scores, slot_own, index_rows, index_wide, wp, wc = call(
-        functools.partial(own_kernel, heads, total_atoms),
+
+    qkv, scores, slot_own, index_rows, index_wide, wp, wc, *rims, token = call(
+        functools.partial(own_kernel, heads, total_atoms, cut),
         (place, fm, fo, cot, mix, neighbours),
         (
             held(comps, 3 * chan_local, atoms_dev, dtype=BF16),
@@ -357,10 +404,16 @@
             held(atoms_dev, HALO, dtype=jnp.int32),
             held(LMAX + 1, 3 * chan_local, channels, dtype=BF16),
             held(LMAX + 1, channels, 3 * chan_local, dtype=BF16),
+            plain(cut, chan_local, HALO, dtype=BF16),
+            plain(cut, chan_local, HALO, dtype=BF16),
+            plain(comps - cut, chan_local, HALO, dtype=BF16),
+            plain(comps - cut, chan_local, HALO, dtype=BF16),
+            plain(8, HALO),
         ),
         scalars=1,
-    )
-    flm, frm = after((flm, frm), (index_rows,))
+        stay=(1, 2, 3),
+    )
+    flm, frm = after((flm, frm), (token,))
     flo = shifted(flm, "chan", 1)
     fro = shifted(frm, "chan", 1)
     rims[:2] = after(rims[:2], (flm, frm))
@@ -374,45 +427,86 @@
             held((2 * heads + 1) * slots, HALO, dtype=BF16),
             held((2 * heads + 1) * slots, HALO, dtype=BF16),
         ),
+        stay=(0, 1, 2, 3, 4, 5, 6, 7, 10, 11),
     )
     message_left = shifted(message_b, "atom", 1)
     message_right = shifted(message_a, "atom", -1)
-    rims[2:] = after(rims[2:], (message_left, message_right))
-    second = (shifted(rims[2], "atom", 1), shifted(rims[3], "atom", -1))
-    grad_query, own_key, own_value, weight_terms = call(
+    piece = (3 * (LMAX + 1), chan_local // 4, channels)
+    grad_query, own_key, own_value, kept, *sent = call(
         functools.partial(grads_kernel, heads, slots),
         (place, fm, fo, flm, flo, frm, fro, qkv, halo_qkv, cot, slot_own, message_a, message_b),
         (
             held(comps, chan_local, atoms_dev, dtype=BF16),
             held(comps, chan_local, atoms_dev),
             held(comps, chan_local, atoms_dev),
-            held(3, LMAX + 1, chan_local, channels),
+            held(*piece),
+            held(*piece, dtype=BF16),
+            held(*piece, dtype=BF16),
+            held(*piece, dtype=BF16),
         ),
-        scratch=[pltpu.VMEM((comps, 2 * chan_local, 2 * atoms_dev), BF16)],
+        scratch=[
+            pltpu.VMEM((comps, 2 * chan_local, 2 * atoms_dev), BF16),
+            pltpu.VMEM((3 * (LMAX + 1), chan_local, channels), F32),
+        ],
         scalars=1,
-    )
-    grad_weights = summed_over(weight_terms, "atom")
+        stay=tuple(range(1, 13)),
+    )
+    arrived = [exchanged(sent[d - 1], "atom", d << cut_bits[0]) for d in range(1, 4)]
+    rims[2:] = after(rims[2:], (message_left, message_right, arrived[0], *first))
+    second = (shifted(rims[2], "atom", 1), shifted(rims[3], "atom", -1))
+    kept = kept + arrived[0].astype(F32) + arrived[1].astype(F32) + arrived[2].astype(F32)
+    rest = [bit for bit in range(count.bit_length() - 1) if bit not in cut_bits]
+    while rest:
+        group, rest = rest[:2], rest[2:]
+        rounded = kept.astype(BF16)
+        offsets = [1 << bit for bit in group]
+        for offset in offsets + [sum(offsets)] * (len(group) - 1):
+            kept = kept + exchanged(rounded, "atom", offset).astype(F32)
+    rounded = kept.astype(BF16)
+    pieces = [rounded] + [exchanged(rounded, "atom", d << cut_bits[0]) for d in range(1, 4)]
+    (grad_weights,) = call(
+        gather_kernel,
+        (place, *pieces),
+        (plain(3 * (LMAX + 1), chan_local, channels),),
+        scalars=1,
+        limit=8,
+    )
     (terms,) = call(
         functools.partial(key_kernel, heads, slots),
         (grad_query, own_key, halo_qkv, message_left, message_right, wc),
         (held(comps, channels, atoms_dev),),
         scratch=[pltpu.VMEM((comps, 2 * chan_local, atoms_dev), BF16)],
+        limit=16,
+        stay=(0, 1, 2, 5),
     )
     parts = []
+    tokens = ()
     for start, (cl, cr) in ((0, first), (cut, second)):
-        count = cl.shape[0]
-        mine, theirs = call(
+        size = cl.shape[0]
+        mine, theirs, token = call(
             functools.partial(value_kernel, heads, slots, start),
             (own_value, cl, cr, message_left, message_right, wc, terms),
             (
-                held(count, chan_local, atoms_dev),
-                held(count, chan_local, atoms_dev, dtype=BF16),
+                held(size, chan_local, atoms_dev),
+                held(size, chan_local, atoms_dev, dtype=BF16),
+                plain(8, HALO),
             ),
-            scratch=[pltpu.VMEM((count, chan_local, atoms_dev), BF16)],
+            scratch=[pltpu.VMEM((size, chan_local, atoms_dev), BF16)],
+            limit=16,
+            stay=(0, 5, 6),
+            tokens=tokens,
         )
+        tokens = (token, rounded)
         parts += [mine, shifted(theirs, "chan", 1)]
-    (out,) = call(finish_kernel, parts, (plain(comps, chan_local, atoms_dev, dtype=BF16),))
+    (out,) = call(
+        finish_kernel,
+        parts,
+        (plain(comps, chan_local, atoms_dev, dtype=BF16),),
+        limit=8,
+        stay=(0, 1, 2, 3),
+    )
     grad_features = jnp.transpose(out, (1, 0, 2))
+    grad_weights = grad_weights.reshape(3, LMAX + 1, chan_local, channels)
     grad_weights = jnp.transpose(grad_weights, (0, 1, 3, 2))
     return grad_features, grad_weights, grad_bias
 

time: 151 us -> 107 us (0.71)
  local copies, waits for them, and re-layouts: 36.3 us -> 3.83 us
  waiting for transfers between devices: 48.1 us -> 41.3 us
  Pallas kernels: 29.8 us -> 27.7 us
    unnamed x70 -> x14, local copies, waits for them, and re-layouts: 28.6 us -> 3.83 us
    ppermute x0 -> x9, starting transfers between devices: none -> 11.5 us  [exchanged(): lax.ppermute(value, axis, [(source, source ^ offset) for source in range(...]
    all_to_all x2 -> x0, starting transfers between devices: 9.41 us -> none  [the longest x1 5.21 us: summed_over(): lax.all_to_all(jnp.broadcast_to(piece[None], pieces.shape), axis, 0, 0, t...]
    all_to_all x2 -> x0, waiting for transfers between devices: 8.61 us -> none  [the longest x1 8.6 us: summed_over(): lax.all_to_all(jnp.broadcast_to(piece[None], pieces.shape), axis, 0, 0, t...]
    ppermute x0 -> x9, waiting for transfers between devices: none -> 8.48 us  [exchanged(): lax.ppermute(value, axis, [(source, source ^ offset) for source in range(...]
    ppermute x13, waiting for transfers between devices: 39.5 us -> 32.8 us  [shifted(): return lax.ppermute(value, axis, pairs)]
    slice x3 -> x0, local copies, waits for them, and re-layouts: 5.16 us -> none  [the longest x1 2.93 us: on_device(): frm = shifted(fm[:, :, :HALO], 'atom', -1)]
    ppermute x13, starting transfers between devices: 24.3 us -> 21.6 us  [shifted(): return lax.ppermute(value, axis, pairs)]
  transfers between devices with their start and end apart: 15 -> 22, of which waited for: 8 -> 9; matrix products, arithmetic and copies ran while one was open for 5% -> 0% of each run, Pallas kernels for 16% -> 22%
where the time goes in v3:
time: 107 us
  waiting for transfers between devices  41.3 us (39%)
  starting transfers between devices  33.1 us (31%)
  Pallas kernels  27.7 us (26%)
  local copies, waits for them, and re-layouts  3.83 us (4%)
    ppermute x13, waiting for transfers between devices, shifted(): return lax.ppermute(value, axis, pairs)  32.8 us
    pallas_call x8, Pallas kernels, call(): pl.pallas_call(body, out_shape=tuple(outs), in_specs=[small] * scalars +...  26.5 us
    ppermute x13, starting transfers between devices, shifted(): return lax.ppermute(value, axis, pairs)  21.6 us
    ppermute x9, starting transfers between devices, exchanged(): lax.ppermute(value, axis, [(source, source ^ offset) for source in range(...  11.5 us
    ppermute x9, waiting for transfers between devices, exchanged(): lax.ppermute(value, axis, [(source, source ^ offset) for source in range(...  8.48 us
    unnamed x14, local copies, waits for them, and re-layouts  3.83 us
  transfers between devices with their start and end apart: 22, of which 9 were waited for; matrix products, arithmetic and copies ran while one was open for 0% of the time, Pallas kernels for 22%

profile of v3, /device:TPU:0, one launch (start us, length us, event | category | flops | bytes accessed | tf_op | source)
XLA Modules:
  0.0 106.9 jit_solution(9421265946427458569)
XLA Ops:
  0.6 0.5 collective-permute-start
  1.2 1.4 %copy-done.1 = bf16[64,49,256]{2,0,1:T(8,128)(2,1)S(1)} copy-done((bf16[64,49,256]{2,0,1:T(8,128)(2,1)S(1)}, bf16[64,49,256]{2,0,1:T(8,128)(2,1)}, u32[]{:S(2)}) %copy-start.1) | copy-done | bytes 1605656
  2.6 1.2 %shard_map.85 = (bf16[49,64,128]{2,1,0:T(8,128)(2,1)}, bf16[49,64,128]{2,1,0:T(8,128)(2,1)}) custom-call(bf16[49,64,256]{2,1,0:T(8,128)(2,1)S(1)} %bitcast.14), custom_call_target="tpu_custom_call" | custom-call | tf_op jit(solution)/shard_map/pallas_call | solution.py:384
  3.8 2.7 %collective-permute-start.1 = (bf16[49,64,128]{2,1,0:T(8,128)(2,1)}, bf16[49,64,128]{2,1,0:T(8,128)(2,1)S(1)}, u32[]{:S(2)}, u32[]{:S(2)}) collective-permute-start(bf16[49,64,128]{2,1,0:T(8,128)(2,1)} %get-tuple-element.39), channel_id=1, source_target_pairs={{0,2},{2,4},{4,6},{6,8},{8,10},{10,12},{12,14},{14,16},{16,18},{18... | collective-permute-start | bytes 2408456 | tf_op jit(solution)/shard_map/ppermute | solution.py:350
  6.4 4.1 %collective-permute-start.2 = (bf16[49,64,128]{2,1,0:T(8,128)(2,1)}, bf16[49,64,128]{2,1,0:T(8,128)(2,1)S(1)}, u32[]{:S(2)}, u32[]{:S(2)}) collective-permute-start(bf16[49,64,128]{2,1,0:T(8,128)(2,1)} %get-tuple-element.40), channel_id=1, source_target_pairs={{0,30},{2,0},{4,2},{6,4},{8,6},{10,8},{12,10},{14,12},{16,14},{18,... | collective-permute-start | bytes 2408456 | tf_op jit(solution)/shard_map/ppermute | solution.py:350
  10.5 0.1 pad_add_fusion.refs_0_
  10.6 0.0 collective-permute-done.refs_2_
  10.6 0.0 copy-start.2
  10.6 1.4 %copy-done.2 = bf16[64,49,256]{2,0,1:T(8,128)(2,1)S(1)} copy-done((bf16[64,49,256]{2,0,1:T(8,128)(2,1)S(1)}, bf16[64,49,256]{2,0,1:T(8,128)(2,1)}, u32[]{:S(2)}) %copy-start.2) | copy-done | bytes 1605656
  12.0 1.0 copy-done.3
  13.0 4.6 %shard_map.86 = (bf16[49,192,256]{2,1,0:T(8,128)(2,1)S(1)}, f32[8,256,256]{2,1,0:T(8,128)S(1)}, s32[2,3,128,128]{3,2,1,0:T(8,128)S(1)}, s32[16,256]{1,0:T(8,128)...) custom-call(s32[3]{0:T(128)S(1)} %pad_add_fusion.refs_0_, ...), custom_call_target="tpu_custom_call" | custom-call | bytes 1024 | tf_op jit(solution)/shard_map/pallas_call | solution.py:316
  17.6 24.0 %collective-permute-done.1.refs_0_ = bf16[49,64,128]{2,1,0:T(8,128)(2,1)S(1)} collective-permute-done((bf16[49,64,128]{2,1,0:T(8,128)(2,1)}, bf16[49,64,128]{2,1,0:T(8,128)(2,1)S(1)}, u32[]{:S(2)}, u32[]{:S(2)}) %collective-permute-start.1) | collective-permute-done | bytes 802848 | tf_op jit(solution)/shard_map/ppermute | solution.py:350
  41.6 1.8 %collective-permute-done.2.refs_1_ = bf16[49,64,128]{2,1,0:T(8,128)(2,1)S(1)} collective-permute-done((bf16[49,64,128]{2,1,0:T(8,128)(2,1)}, bf16[49,64,128]{2,1,0:T(8,128)(2,1)S(1)}, u32[]{:S(2)}, u32[]{:S(2)}) %collective-permute-start.2) | collective-permute-done | bytes 802848 | tf_op jit(solution)/shard_map/ppermute | solution.py:350
  43.5 0.0 collective-permute-start.3
  43.5 0.5 collective-permute-start.4
  44.0 1.5 %collective-permute-start.5 = (bf16[24,64,128]{2,1,0:T(8,128)(2,1)S(1)}, bf16[24,64,128]{2,1,0:T(8,128)(2,1)S(1)}, u32[]{:S(2)}, u32[]{:S(2)}) collective-permute-start(bf16[24,64,128]{2,1,0:T(8,128)(2,1)S(1)} %get-tuple-element.56), channel_id=1, source_target_pairs={{0,2},{2,4},{4,6},{6,8},{8,10},{10,12},{12,14},{14,16},{16,18},{18... | collective-permute-start | bytes 1179656 | tf_op jit(solution)/shard_map/ppermute | solution.py:350
  45.5 4.1 %collective-permute-start.6 = (bf16[24,64,128]{2,1,0:T(8,128)(2,1)S(1)}, bf16[24,64,128]{2,1,0:T(8,128)(2,1)S(1)}, u32[]{:S(2)}, u32[]{:S(2)}) collective-permute-start(bf16[24,64,128]{2,1,0:T(8,128)(2,1)S(1)} %get-tuple-element.57), channel_id=1, source_target_pairs={{0,30},{2,0},{4,2},{6,4},{8,6},{10,8},{12,10},{14,12},{16,14},{18,... | collective-permute-start | bytes 1179656 | tf_op jit(solution)/shard_map/ppermute | solution.py:350
  49.6 0.0 collective-permute-done.3.refs_1_.refs_4_
  49.6 4.1 %shard_map.88 = (bf16[49,192,256]{2,1,0:T(8,128)(2,1)S(1)}, f32[4,16,256]{2,1,0:T(8,128)}, bf16[144,128]{1,0:T(8,128)(2,1)S(1)}, bf16[144,128]{1,0:T(8,128)(2,1)S(1)}) custom-call(bf16[49,64,128]{2,1,0:T(8,128)(2,1)S(1)} %get-tuple-element.42.refs_0_.refs_3_.refs_2_, bf16[49,64,128]{2,1,0:T(8,128)(2,1)S(1)} %collective-permute-done.3.refs_1_.refs_4_, ...), custom_call_target="tpu_custom_call" | custom-call | bytes 1024 | tf_op jit(solution)/shard_map/pallas_call | solution.py:316
  53.8 7.7 %shard_map.89 = (bf16[49,64,256]{2,1,0:T(8,128)(2,1)S(1)}, f32[49,64,256]{2,1,0:T(8,128)S(1)}, f32[49,64,256]{2,1,0:T(8,128)S(1)}, f32[21,16,128]{2,1,0:T(8,128)...) custom-call(s32[3]{0:T(128)S(1)} %pad_add_fusion.refs_0_, ...), custom_call_target="tpu_custom_call" | custom-call | bytes 1024 | tf_op jit(solution)/shard_map/pallas_call | solution.py:316
  61.4 0.1 collective-permute-start.10
  61.5 0.3 collective-permute-start.13
  61.8 3.2 %collective-permute-start.14 = (bf16[21,16,128]{2,1,0:T(8,128)(2,1)S(1)}, bf16[21,16,128]{2,1,0:T(8,128)(2,1)S(1)}, u32[]{:S(2)}, u32[]{:S(2)}) collective-permute-start(bf16[21,16,128]{2,1,0:T(8,128)(2,1)S(1)} %get-tuple-element.71), channel_id=1, source_target_pairs={{0,12},{2,14},{4,8},{6,10},{8,4},{10,6},{12,0},{14,2},{16,28},{18,... | collective-permute-start | bytes 258056 | tf_op jit(solution)/shard_map/ppermute | solution.py:355
  65.0 1.3 %collective-permute-start.8 = (bf16[144,128]{1,0:T(8,128)(2,1)S(1)}, bf16[144,128]{1,0:T(8,128)(2,1)S(1)}, u32[]{:S(2)}, u32[]{:S(2)}) collective-permute-start(bf16[144,128]{1,0:T(8,128)(2,1)S(1)} %get-tuple-element.51.refs_11_), channel_id=1, source_target_pairs={{0,30},{2,0},{4,2},{6,4},{8,6},{10,8},{12,10},{14,12},{16,14},{18,... | collective-permute-start | bytes 110600 | tf_op jit(solution)/shard_map/ppermute | solution.py:350
  66.3 0.7 collective-permute-start.7
  67.0 1.9 %collective-permute-done.8.refs_4_.refs_3_ = bf16[144,128]{1,0:T(8,128)(2,1)S(1)} collective-permute-done((bf16[144,128]{1,0:T(8,128)(2,1)S(1)}, bf16[144,128]{1,0:T(8,128)(2,1)S(1)}, u32[]{:S(2)}, u32[]{:S(2)}) %collective-permute-start.8) | collective-permute-done | bytes 36896 | tf_op jit(solution)/shard_map/ppermute | solution.py:350
  68.9 5.1 %collective-permute-done.7.refs_3_.refs_2_ = bf16[144,128]{1,0:T(8,128)(2,1)S(1)} collective-permute-done((bf16[144,128]{1,0:T(8,128)(2,1)S(1)}, bf16[144,128]{1,0:T(8,128)(2,1)S(1)}, u32[]{:S(2)}, u32[]{:S(2)}) %collective-permute-start.7) | collective-permute-done | bytes 36896 | tf_op jit(solution)/shard_map/ppermute | solution.py:350
  74.0 5.6 %collective-permute-start.12 = (bf16[25,64,128]{2,1,0:T(8,128)(2,1)S(1)}, bf16[25,64,128]{2,1,0:T(8,128)(2,1)S(1)}, u32[]{:S(2)}, u32[]{:S(2)}) collective-permute-start(bf16[25,64,128]{2,1,0:T(8,128)(2,1)S(1)} %get-tuple-element.67), channel_id=1, source_target_pairs={{0,30},{2,0},{4,2},{6,4},{8,6},{10,8},{12,10},{14,12},{16,14},{18,... | collective-permute-start | bytes 1228808 | tf_op jit(solution)/shard_map/ppermute | solution.py:350
  79.6 0.1 fusion
  79.7 0.1 collective-permute-start.17
  79.8 0.1 collective-permute-start.16
  79.8 4.3 %collective-permute-start.15 = (bf16[21,16,128]{2,1,0:T(8,128)(2,1)S(1)}, bf16[21,16,128]{2,1,0:T(8,128)(2,1)S(1)}, u32[]{:S(2)}, u32[]{:S(2)}) collective-permute-start(bf16[21,16,128]{2,1,0:T(8,128)(2,1)S(1)} %fusion), channel_id=1, source_target_pairs={{0,2},{2,0},{4,6},{6,4},{8,10},{10,8},{12,14},{14,12},{16,18},{18,... | collective-permute-start | bytes 258056 | tf_op jit(solution)/shard_map/ppermute | solution.py:355
  84.1 2.9 %shard_map.91.refs_6_ = f32[49,128,256]{2,1,0:T(8,128)S(1)} custom-call(bf16[49,64,256]{2,1,0:T(8,128)(2,1)S(1)} %get-tuple-element.59.refs_0_, f32[49,64,256]{2,1,0:T(8,128)S(1)} %get-tuple-element.60.refs_1_, bf16[49,192,256]{2,1,0:T(8,128)(2,1)S(1)} %get-tuple-element.49.refs_8_.refs_2_, bf16[144,128]{1,0:T(8,128)(2,1)S(1)} %collective-permute-done.7.refs_3_.refs_2_, ...), custom_call_target="tpu_custom_call" | custom-call | bytes 1024 | tf_op jit(solution)/shard_map/pallas_call | solution.py:316
  87.1 2.0 %shard_map.92 = (f32[24,64,256]{2,1,0:T(8,128)S(1)}, bf16[24,64,256]{2,1,0:T(8,128)(2,1)S(1)}, f32[8,128]{1,0:T(8,128)S(1)}) custom-call(f32[49,64,256]{2,1,0:T(8,128)S(1)} %get-tuple-element.53.refs_0_, bf16[24,64,128]{2,1,0:T(8,128)(2,1)S(1)} %collective-permute-done.5.refs_1_.refs_5_, bf16[24,64,128]{2,1,0:T(8,128)(2,1)S(1)} %collective-permute-done.6.refs_2_.refs_6_, ...), custom_call_target="tpu_custom_call" | custom-call | bytes 1024 | tf_op jit(solution)/shard_map/pallas_call | solution.py:316
  89.1 2.0 %collective-permute-done.16 = bf16[21,16,128]{2,1,0:T(8,128)(2,1)S(1)} collective-permute-done((bf16[21,16,128]{2,1,0:T(8,128)(2,1)S(1)}, bf16[21,16,128]{2,1,0:T(8,128)(2,1)S(1)}, u32[]{:S(2)}, u32[]{:S(2)}) %collective-permute-start.16) | collective-permute-done | bytes 86048 | tf_op jit(solution)/shard_map/ppermute | solution.py:355
  91.1 2.6 %collective-permute-done.15 = bf16[21,16,128]{2,1,0:T(8,128)(2,1)S(1)} collective-permute-done((bf16[21,16,128]{2,1,0:T(8,128)(2,1)S(1)}, bf16[21,16,128]{2,1,0:T(8,128)(2,1)S(1)}, u32[]{:S(2)}, u32[]{:S(2)}) %collective-permute-start.15) | collective-permute-done | bytes 86048 | tf_op jit(solution)/shard_map/ppermute | solution.py:355
  93.7 0.1 add_convert_fusion.refs_8_.refs_1_
  93.8 2.1 %shard_map.94 = (f32[25,64,256]{2,1,0:T(8,128)S(1)}, bf16[25,64,256]{2,1,0:T(8,128)(2,1)S(1)}, f32[8,128]{1,0:T(8,128)}) custom-call(f32[49,64,256]{2,1,0:T(8,128)S(1)} %get-tuple-element.53.refs_0_, bf16[25,64,128]{2,1,0:T(8,128)(2,1)S(1)} %collective-permute-done.11.refs_1_, bf16[25,64,128]{2,1,0:T(8,128)(2,1)S(1)} %collective-permute-done.12.refs_2_, ...), custom_call_target="tpu_custom_call" | custom-call | bytes 1024 | tf_op jit(solution)/shard_map/pallas_call | solution.py:316
  95.9 0.1 collective-permute-start.18
  96.0 0.5 collective-permute-start.9
  96.5 1.7 %collective-permute-start.21 = (bf16[21,16,128]{2,1,0:T(8,128)(2,1)S(1)}, bf16[21,16,128]{2,1,0:T(8,128)(2,1)S(1)}, u32[]{:S(2)}, u32[]{:S(2)}) collective-permute-start(bf16[21,16,128]{2,1,0:T(8,128)(2,1)S(1)} %add_convert_fusion.refs_8_.refs_1_), channel_id=1, source_target_pairs={{0,12},{2,14},{4,8},{6,10},{8,4},{10,6},{12,0},{14,2},{16,28},{18,... | collective-permute-start | bytes 258056 | tf_op jit(solution)/shard_map/ppermute | solution.py:355
  98.3 1.0 collective-permute-start.20
  99.2 0.8 collective-permute-start.19
  100.0 2.8 %collective-permute-done.21.refs_4_ = bf16[21,16,128]{2,1,0:T(8,128)(2,1)S(1)} collective-permute-done((bf16[21,16,128]{2,1,0:T(8,128)(2,1)S(1)}, bf16[21,16,128]{2,1,0:T(8,128)(2,1)S(1)}, u32[]{:S(2)}, u32[]{:S(2)}) %collective-permute-start.21) | collective-permute-done | bytes 86048 | tf_op jit(solution)/shard_map/ppermute | solution.py:355
  102.8 0.7 collective-permute-done.20.refs_3_
  103.6 0.4 collective-permute-done.19.refs_2_
  103.9 1.4 %shard_map.96 = f32[21,64,128]{2,1,0:T(8,128)} custom-call(s32[3]{0:T(128)S(1)} %pad_add_fusion.refs_0_, bf16[21,16,128]{2,1,0:T(8,128)(2,1)S(1)} %add_convert_fusion.refs_8_.refs_1_, bf16[21,16,128]{2,1,0:T(8,128)(2,1)S(1)} %collective-permute-done.19.refs_2_, bf16[21,16,128]{2,1,0:T(8,128)(2,1)S(1)} %collective-permute-done.20.refs_3_, ...), custom_call_target="tpu_custom_call" | custom-call | bytes 1024 | tf_op jit(solution)/shard_map/pallas_call | solution.py:316
  105.4 1.6 %shard_map.95 = bf16[49,64,256]{2,1,0:T(8,128)(2,1)} custom-call(f32[24,64,256]{2,1,0:T(8,128)S(1)} %get-tuple-element.61.refs_0_, bf16[24,64,256]{2,1,0:T(8,128)(2,1)S(1)} %collective-permute-done.9.refs_1_, f32[25,64,256]{2,1,0:T(8,128)S(1)} %get-tuple-element.72.refs_2_, bf16[25,64,256]{2,1,0:T(8,128)(2,1)S(1)} %collective-permute-done.18.refs_3_), custom_call_target="tpu_custom_call" | custom-call | bytes 1024 | tf_op jit(solution)/shard_map/pallas_call | solution.py:316
  (25 shorter events, 0.1 us)
Async XLA Ops:
  0.6 10.0 %copy-start = (bf16[64,49,256]{2,0,1:T(8,128)(2,1)S(1)}, bf16[64,49,256]{2,0,1:T(8,128)(2,1)}, u32[]{:S(2)}) copy-start(bf16[64,49,256]{2,0,1:T(8,128)(2,1)} %param.8) | copy-start | bytes 4816900
  0.6 9.9 %collective-permute-start = (bf16[49,64,256]{2,1,0:T(8,128)(2,1)}, bf16[49,64,256]{2,1,0:T(8,128)(2,1)}, u32[]{:S(2)}, u32[]{:S(2)}) collective-permute-start(bf16[49,64,256]{2,1,0:T(8,128)(2,1)} %bitcast.13), channel_id=1, source_target_pairs={{0,1},{1,0},{2,3},{3,2},{4,5},{5,4},{6,7},{7,6},{8,9},{9,8},{10,11... | collective-permute-start | bytes 4816904 | tf_op jit(solution)/shard_map/ppermute | solution.py:350
  1.2 1.4 %copy-start.1 = (bf16[64,49,256]{2,0,1:T(8,128)(2,1)S(1)}, bf16[64,49,256]{2,0,1:T(8,128)(2,1)}, u32[]{:S(2)}) copy-start(bf16[64,49,256]{2,0,1:T(8,128)(2,1)} %param.6) | copy-start | bytes 4816900
  2.6 8.0 %copy-start.5 = (s32[16,256]{1,0:T(8,128)S(1)}, s32[16,256]{1,0:T(8,128)}, u32[]{:S(2)}) copy-start(s32[16,256]{1,0:T(8,128)} %refs_5_.1) | copy-start | bytes 49156
  3.8 37.9 %collective-permute-start.1 = (bf16[49,64,128]{2,1,0:T(8,128)(2,1)}, bf16[49,64,128]{2,1,0:T(8,128)(2,1)S(1)}, u32[]{:S(2)}, u32[]{:S(2)}) collective-permute-start(bf16[49,64,128]{2,1,0:T(8,128)(2,1)} %get-tuple-element.39), channel_id=1, source_target_pairs={{0,2},{2,4},{4,6},{6,8},{8,10},{10,12},{12,14},{14,16},{16,18},{18... | collective-permute-start | bytes 2408456 | tf_op jit(solution)/shard_map/ppermute | solution.py:350
  6.4 37.0 %collective-permute-start.2 = (bf16[49,64,128]{2,1,0:T(8,128)(2,1)}, bf16[49,64,128]{2,1,0:T(8,128)(2,1)S(1)}, u32[]{:S(2)}, u32[]{:S(2)}) collective-permute-start(bf16[49,64,128]{2,1,0:T(8,128)(2,1)} %get-tuple-element.40), channel_id=1, source_target_pairs={{0,30},{2,0},{4,2},{6,4},{8,6},{10,8},{12,10},{14,12},{16,14},{18,... | collective-permute-start | bytes 2408456 | tf_op jit(solution)/shard_map/ppermute | solution.py:350
  10.6 1.4 %copy-start.2 = (bf16[64,49,256]{2,0,1:T(8,128)(2,1)S(1)}, bf16[64,49,256]{2,0,1:T(8,128)(2,1)}, u32[]{:S(2)}) copy-start(bf16[64,49,256]{2,0,1:T(8,128)(2,1)} %param.6) | copy-start | bytes 4816900
  12.0 1.0 copy-start.3
  43.5 6.1 %copy-start.4 = (f32[4,16,256]{2,1,0:T(8,128)S(1)}, f32[4,16,256]{2,1,0:T(8,128)}, u32[]{:S(2)}) copy-start(f32[4,16,256]{2,1,0:T(8,128)} %refs_8_.1) | copy-start | bytes 196612
  43.5 6.2 %copy-start.6 = (s32[16,256]{1,0:T(8,128)S(1)}, s32[16,256]{1,0:T(8,128)}, u32[]{:S(2)}) copy-start(s32[16,256]{1,0:T(8,128)} %refs_9_.1) | copy-start | bytes 49156
  43.5 6.1 %collective-permute-start.3 = (bf16[49,64,128]{2,1,0:T(8,128)(2,1)S(1)}, bf16[49,64,128]{2,1,0:T(8,128)(2,1)S(1)}, u32[]{:S(2)}, u32[]{:S(2)}) collective-permute-start(bf16[49,64,128]{2,1,0:T(8,128)(2,1)S(1)} %get-tuple-element.42.refs_0_.refs_3_.refs_2_), channel_id=1, source_target_pairs={{0,1},{1,0},{2,3},{3,2},{4,5},{5,4},{6,7},{7,6},{8,9},{9,8},{10,11... | collective-permute-start | bytes 2408456 | tf_op jit(solution)/shard_map/ppermute | solution.py:350
  43.5 6.1 %collective-permute-start.4 = (bf16[49,64,128]{2,1,0:T(8,128)(2,1)S(1)}, bf16[49,64,128]{2,1,0:T(8,128)(2,1)S(1)}, u32[]{:S(2)}, u32[]{:S(2)}) collective-permute-start(bf16[49,64,128]{2,1,0:T(8,128)(2,1)S(1)} %get-tuple-element.43.refs_2_.refs_5_.refs_3_), channel_id=1, source_target_pairs={{0,1},{1,0},{2,3},{3,2},{4,5},{5,4},{6,7},{7,6},{8,9},{9,8},{10,11... | collective-permute-start | bytes 2408456 | tf_op jit(solution)/shard_map/ppermute | solution.py:350
  44.0 21.0 %collective-permute-start.5 = (bf16[24,64,128]{2,1,0:T(8,128)(2,1)S(1)}, bf16[24,64,128]{2,1,0:T(8,128)(2,1)S(1)}, u32[]{:S(2)}, u32[]{:S(2)}) collective-permute-start(bf16[24,64,128]{2,1,0:T(8,128)(2,1)S(1)} %get-tuple-element.56), channel_id=1, source_target_pairs={{0,2},{2,4},{4,6},{6,8},{8,10},{10,12},{12,14},{14,16},{16,18},{18... | collective-permute-start | bytes 1179656 | tf_op jit(solution)/shard_map/ppermute | solution.py:350
  45.5 20.8 %collective-permute-start.6 = (bf16[24,64,128]{2,1,0:T(8,128)(2,1)S(1)}, bf16[24,64,128]{2,1,0:T(8,128)(2,1)S(1)}, u32[]{:S(2)}, u32[]{:S(2)}) collective-permute-start(bf16[24,64,128]{2,1,0:T(8,128)(2,1)S(1)} %get-tuple-element.57), channel_id=1, source_target_pairs={{0,30},{2,0},{4,2},{6,4},{8,6},{10,8},{12,10},{14,12},{16,14},{18,... | collective-permute-start | bytes 1179656 | tf_op jit(solution)/shard_map/ppermute | solution.py:350
  61.4 12.6 %collective-permute-start.10 = (bf16[21,16,128]{2,1,0:T(8,128)(2,1)S(1)}, bf16[21,16,128]{2,1,0:T(8,128)(2,1)S(1)}, u32[]{:S(2)}, u32[]{:S(2)}) collective-permute-start(bf16[21,16,128]{2,1,0:T(8,128)(2,1)S(1)} %get-tuple-element.65), channel_id=1, source_target_pairs={{0,4},{2,6},{4,0},{6,2},{8,12},{10,14},{12,8},{14,10},{16,20},{18,... | collective-permute-start | bytes 258056 | tf_op jit(solution)/shard_map/ppermute | solution.py:355
  61.5 18.1 %collective-permute-start.13 = (bf16[21,16,128]{2,1,0:T(8,128)(2,1)S(1)}, bf16[21,16,128]{2,1,0:T(8,128)(2,1)S(1)}, u32[]{:S(2)}, u32[]{:S(2)}) collective-permute-start(bf16[21,16,128]{2,1,0:T(8,128)(2,1)S(1)} %get-tuple-element.70), channel_id=1, source_target_pairs={{0,8},{2,10},{4,12},{6,14},{8,0},{10,2},{12,4},{14,6},{16,24},{18,... | collective-permute-start | bytes 258056 | tf_op jit(solution)/shard_map/ppermute | solution.py:355
  61.8 17.9 %collective-permute-start.14 = (bf16[21,16,128]{2,1,0:T(8,128)(2,1)S(1)}, bf16[21,16,128]{2,1,0:T(8,128)(2,1)S(1)}, u32[]{:S(2)}, u32[]{:S(2)}) collective-permute-start(bf16[21,16,128]{2,1,0:T(8,128)(2,1)S(1)} %get-tuple-element.71), channel_id=1, source_target_pairs={{0,12},{2,14},{4,8},{6,10},{8,4},{10,6},{12,0},{14,2},{16,28},{18,... | collective-permute-start | bytes 258056 | tf_op jit(solution)/shard_map/ppermute | solution.py:355
  65.0 4.0 %collective-permute-start.8 = (bf16[144,128]{1,0:T(8,128)(2,1)S(1)}, bf16[144,128]{1,0:T(8,128)(2,1)S(1)}, u32[]{:S(2)}, u32[]{:S(2)}) collective-permute-start(bf16[144,128]{1,0:T(8,128)(2,1)S(1)} %get-tuple-element.51.refs_11_), channel_id=1, source_target_pairs={{0,30},{2,0},{4,2},{6,4},{8,6},{10,8},{12,10},{14,12},{16,14},{18,... | collective-permute-start | bytes 110600 | tf_op jit(solution)/shard_map/ppermute | solution.py:350
  66.3 7.7 %collective-permute-start.7 = (bf16[144,128]{1,0:T(8,128)(2,1)S(1)}, bf16[144,128]{1,0:T(8,128)(2,1)S(1)}, u32[]{:S(2)}, u32[]{:S(2)}) collective-permute-start(bf16[144,128]{1,0:T(8,128)(2,1)S(1)} %get-tuple-element.52.refs_12_), channel_id=1, source_target_pairs={{0,2},{2,4},{4,6},{6,8},{8,10},{10,12},{12,14},{14,16},{16,18},{18... | collective-permute-start | bytes 110600 | tf_op jit(solution)/shard_map/ppermute | solution.py:350
  74.0 19.8 %collective-permute-start.11 = (bf16[25,64,128]{2,1,0:T(8,128)(2,1)S(1)}, bf16[25,64,128]{2,1,0:T(8,128)(2,1)S(1)}, u32[]{:S(2)}, u32[]{:S(2)}) collective-permute-start(bf16[25,64,128]{2,1,0:T(8,128)(2,1)S(1)} %get-tuple-element.66), channel_id=1, source_target_pairs={{0,2},{2,4},{4,6},{6,8},{8,10},{10,12},{12,14},{14,16},{16,18},{18... | collective-permute-start | bytes 1228808 | tf_op jit(solution)/shard_map/ppermute | solution.py:350
  74.0 19.8 %collective-permute-start.12 = (bf16[25,64,128]{2,1,0:T(8,128)(2,1)S(1)}, bf16[25,64,128]{2,1,0:T(8,128)(2,1)S(1)}, u32[]{:S(2)}, u32[]{:S(2)}) collective-permute-start(bf16[25,64,128]{2,1,0:T(8,128)(2,1)S(1)} %get-tuple-element.67), channel_id=1, source_target_pairs={{0,30},{2,0},{4,2},{6,4},{8,6},{10,8},{12,10},{14,12},{16,14},{18,... | collective-permute-start | bytes 1228808 | tf_op jit(solution)/shard_map/ppermute | solution.py:350
  79.7 9.4 %collective-permute-start.17 = (bf16[21,16,128]{2,1,0:T(8,128)(2,1)S(1)}, bf16[21,16,128]{2,1,0:T(8,128)(2,1)S(1)}, u32[]{:S(2)}, u32[]{:S(2)}) collective-permute-start(bf16[21,16,128]{2,1,0:T(8,128)(2,1)S(1)} %fusion), channel_id=1, source_target_pairs={{0,18},{2,16},{4,22},{6,20},{8,26},{10,24},{12,30},{14,28},{16,2},... | collective-permute-start | bytes 258056 | tf_op jit(solution)/shard_map/ppermute | solution.py:355
  79.8 11.3 %collective-permute-start.16 = (bf16[21,16,128]{2,1,0:T(8,128)(2,1)S(1)}, bf16[21,16,128]{2,1,0:T(8,128)(2,1)S(1)}, u32[]{:S(2)}, u32[]{:S(2)}) collective-permute-start(bf16[21,16,128]{2,1,0:T(8,128)(2,1)S(1)} %fusion), channel_id=1, source_target_pairs={{0,16},{2,18},{4,20},{6,22},{8,24},{10,26},{12,28},{14,30},{16,0},... | collective-permute-start | bytes 258056 | tf_op jit(solution)/shard_map/ppermute | solution.py:355
  79.8 13.8 %collective-permute-start.15 = (bf16[21,16,128]{2,1,0:T(8,128)(2,1)S(1)}, bf16[21,16,128]{2,1,0:T(8,128)(2,1)S(1)}, u32[]{:S(2)}, u32[]{:S(2)}) collective-permute-start(bf16[21,16,128]{2,1,0:T(8,128)(2,1)S(1)} %fusion), channel_id=1, source_target_pairs={{0,2},{2,0},{4,6},{6,4},{8,10},{10,8},{12,14},{14,12},{16,18},{18,... | collective-permute-start | bytes 258056 | tf_op jit(solution)/shard_map/ppermute | solution.py:355
  95.9 9.4 %collective-permute-start.18 = (bf16[25,64,256]{2,1,0:T(8,128)(2,1)S(1)}, bf16[25,64,256]{2,1,0:T(8,128)(2,1)S(1)}, u32[]{:S(2)}, u32[]{:S(2)}) collective-permute-start(bf16[25,64,256]{2,1,0:T(8,128)(2,1)S(1)} %get-tuple-element.73), channel_id=1, source_target_pairs={{0,1},{1,0},{2,3},{3,2},{4,5},{5,4},{6,7},{7,6},{8,9},{9,8},{10,11... | collective-permute-start | bytes 2457608 | tf_op jit(solution)/shard_map/ppermute | solution.py:350
  96.0 9.3 %collective-permute-start.9 = (bf16[24,64,256]{2,1,0:T(8,128)(2,1)S(1)}, bf16[24,64,256]{2,1,0:T(8,128)(2,1)S(1)}, u32[]{:S(2)}, u32[]{:S(2)}) collective-permute-start(bf16[24,64,256]{2,1,0:T(8,128)(2,1)S(1)} %get-tuple-element.62), channel_id=1, source_target_pairs={{0,1},{1,0},{2,3},{3,2},{4,5},{5,4},{6,7},{7,6},{8,9},{9,8},{10,11... | collective-permute-start | bytes 2359304 | tf_op jit(solution)/shard_map/ppermute | solution.py:350
  96.5 6.3 %collective-permute-start.21 = (bf16[21,16,128]{2,1,0:T(8,128)(2,1)S(1)}, bf16[21,16,128]{2,1,0:T(8,128)(2,1)S(1)}, u32[]{:S(2)}, u32[]{:S(2)}) collective-permute-start(bf16[21,16,128]{2,1,0:T(8,128)(2,1)S(1)} %add_convert_fusion.refs_8_.refs_1_), channel_id=1, source_target_pairs={{0,12},{2,14},{4,8},{6,10},{8,4},{10,6},{12,0},{14,2},{16,28},{18,... | collective-permute-start | bytes 258056 | tf_op jit(solution)/shard_map/ppermute | solution.py:355
  98.3 5.3 %collective-permute-start.20 = (bf16[21,16,128]{2,1,0:T(8,128)(2,1)S(1)}, bf16[21,16,128]{2,1,0:T(8,128)(2,1)S(1)}, u32[]{:S(2)}, u32[]{:S(2)}) collective-permute-start(bf16[21,16,128]{2,1,0:T(8,128)(2,1)S(1)} %add_convert_fusion.refs_8_.refs_1_), channel_id=1, source_target_pairs={{0,8},{2,10},{4,12},{6,14},{8,0},{10,2},{12,4},{14,6},{16,24},{18,... | collective-permute-start | bytes 258056 | tf_op jit(solution)/shard_map/ppermute | solution.py:355
  99.2 4.7 %collective-permute-start.19 = (bf16[21,16,128]{2,1,0:T(8,128)(2,1)S(1)}, bf16[21,16,128]{2,1,0:T(8,128)(2,1)S(1)}, u32[]{:S(2)}, u32[]{:S(2)}) collective-permute-start(bf16[21,16,128]{2,1,0:T(8,128)(2,1)S(1)} %add_convert_fusion.refs_8_.refs_1_), channel_id=1, source_target_pairs={{0,4},{2,6},{4,0},{6,2},{8,12},{10,14},{12,8},{14,10},{16,20},{18,... | collective-permute-start | bytes 258056 | tf_op jit(solution)/shard_map/ppermute | solution.py:355

commit v4 on v3

--- a/solution.py
+++ b/solution.py
@@ -58,10 +58,18 @@
     return jnp.concatenate([rows] * (HALO // rows.shape[0]), axis=0).T
 
 
-def split_kernel(fm, low, high, sems):
+def split_kernel(cut, fm, high_a, low_a, high_b, low_b, sems):
+    ranges = (
+        (high_a, 0, cut, HALO),
+        (low_a, 0, cut, 0),
+        (high_b, cut, fm.shape[0] - cut, HALO),
+        (low_b, cut, fm.shape[0] - cut, 0),
+    )
     copies = [
-        pltpu.make_async_copy(fm.at[:, :, pl.ds(at * HALO, HALO)], part, sems.at[at])
-        for at, part in enumerate((low, high))
+        pltpu.make_async_copy(
+            fm.at[pl.ds(start, size), :, pl.ds(atom, HALO)], part, sems.at[at]
+        )
+        for at, (part, start, size, atom) in enumerate(ranges)
     ]
     for copy in copies:
         copy.start()
@@ -69,14 +77,12 @@
         copy.wait()
 
 
-def own_kernel(heads, total_atoms, cut, place, fm, fo, cot, weights, neighbours,
-               qkv, scores, slot_own, index_rows, index_wide, wp, wc, rims_a, rims_b,
-               rims_c, rims_d, token):
+def own_kernel(heads, total_atoms, cuts, place, fm, fo, cot, weights, neighbours,
+               qkv, scores, slot_own, index_rows, index_wide, wp, wc, token, *rims):
     token[...] = jnp.zeros_like(token)
-    rims_a[...] = cot[:cut, :, HALO:]
-    rims_b[...] = cot[:cut, :, :HALO]
-    rims_c[...] = cot[cut:, :, HALO:]
-    rims_d[...] = cot[cut:, :, :HALO]
+    for at, (start, stop) in enumerate(cuts):
+        rims[2 * at][...] = cot[start:stop, :, HALO:]
+        rims[2 * at + 1][...] = cot[start:stop, :, :HALO]
     comps, chan_local = fm.shape[0], fm.shape[1]
     channels = weights.shape[3]
     rows = chan_local // heads
@@ -109,12 +115,8 @@
             slot_own[half, tile] = slot_tile(wide[:, :slots], tile)
 
 
-def edge_kernel(heads, score_scale, flm, flo, frm, fro, wp, qkv, cot, scores, bias, valid,
-                index_rows, index_wide, halo_qkv, grad_bias, message_a, message_b):
-    comps, chan_local = flm.shape[0], flm.shape[1]
-    rows = chan_local // heads
-    slots = valid.shape[0]
-    for comp in range(comps):
+def project_halo(start, flm, flo, frm, fro, wp, halo_qkv):
+    for comp in range(flm.shape[0]):
         feats = jnp.concatenate(
             [
                 jnp.concatenate([flm[comp], frm[comp]], axis=1),
@@ -122,19 +124,39 @@
             ],
             axis=0,
         )
-        halo_qkv[comp] = nn(wp[degree_of(comp)], feats).astype(BF16)
+        halo_qkv[comp] = nn(wp[degree_of(start + comp)], feats).astype(BF16)
+
+
+def halo_scores(heads, quantity, start, qkv, cot, halo_qkv):
+    size, chan_local = halo_qkv.shape[0], cot.shape[1]
+    rows = chan_local // heads
+    head = quantity % heads
+    first = (1 if quantity < heads else 2) * chan_local + head * rows
+    source = qkv if quantity < heads else cot
+    mine = source[start : start + size, head * rows : (head + 1) * rows, :]
+    mine = mine.reshape(size * rows, mine.shape[2])
+    theirs = head_rows_of(halo_qkv, first, rows)
+    return tn(mine[:, :HALO], theirs[:, :HALO]), tn(mine[:, HALO:], theirs[:, HALO:])
+
+
+def early_kernel(heads, flm, flo, frm, fro, wp, qkv, cot, halo_qkv, partial, token):
+    token[...] = jnp.zeros_like(token)
+    project_halo(0, flm, flo, frm, fro, wp, halo_qkv)
+    for quantity in range(2 * heads):
+        left, right = halo_scores(heads, quantity, 0, qkv, cot, halo_qkv)
+        partial[quantity, 0] = left
+        partial[quantity, 1] = right
+
+
+def edge_kernel(heads, score_scale, start, flm, flo, frm, fro, wp, qkv, cot, scores, partial, bias,
+                valid, index_rows, index_wide, halo_qkv, grad_bias, message_a, message_b):
+    slots = valid.shape[0]
+    project_halo(start, flm, flo, frm, fro, wp, halo_qkv)
     lane = lax.broadcasted_iota(jnp.int32, (HALO, 2 * heads * slots), 1)
     gathered = [jnp.zeros((HALO, 2 * heads * slots), F32) for _ in range(2)]
     for quantity in range(2 * heads):
-        head = quantity % heads
-        if quantity < heads:
-            mine = head_rows_of(qkv, head * rows, rows)
-            theirs = head_rows_of(halo_qkv, chan_local + head * rows, rows)
-        else:
-            mine = head_rows_of(cot, head * rows, rows)
-            theirs = head_rows_of(halo_qkv, 2 * chan_local + head * rows, rows)
-        left = tn(mine[:, :HALO], theirs[:, :HALO])
-        right = tn(mine[:, HALO:], theirs[:, HALO:])
+        left, right = halo_scores(heads, quantity, start, qkv, cot, halo_qkv)
+        left, right = left + partial[quantity, 0], right + partial[quantity, 1]
         for half in range(2):
             own = scores[quantity, half * HALO : (half + 1) * HALO, :]
             own = [own[:, :HALO], own[:, HALO:]]
@@ -172,13 +194,21 @@
         message[2 * heads * slots :, :] = (index - HALO - atom).astype(F32).astype(BF16)
 
 
-def grads_kernel(heads, slots, place, fm, fo, flm, flo, frm, fro, qkv, halo_qkv, cot, slot_own,
-                 message_a, message_b, grad_query, own_key, own_value, kept, sent_1, sent_2,
+def joined_rows(early, late, first_row, rows):
+    return jnp.concatenate(
+        [head_rows_of(early, first_row, rows), head_rows_of(late, first_row, rows)], axis=0
+    )
+
+
+def grads_kernel(heads, slots, place, fm, fo, flm_a, flo_a, frm_a, fro_a, flm_b, flo_b, frm_b,
+                 fro_b, qkv, halo_a, halo_b, cot, slot_own, message_a, message_b, grad_query, own_key, own_value, kept, sent_1, sent_2,
                  sent_3, ext, weight_terms):
     comps, chan_local = fm.shape[0], fm.shape[1]
     rows = chan_local // heads
     atoms = 2 * HALO
     core = place[0]
+    cut = flm_a.shape[0]
+    early, late = (flm_a, flo_a, frm_a, fro_a), (flm_b, flo_b, frm_b, fro_b)
     empty = jnp.zeros((HALO, HALO), BF16)
     coefs = [message[: 2 * heads * slots, :].astype(F32).T for message in (message_a, message_b)]
     for head in range(heads):
@@ -193,7 +223,7 @@
         raw_table, attn_table = tables
         query = head_rows_of(qkv, head * rows, rows)
         key = head_rows_of(qkv, chan_local + head * rows, rows)
-        halo_key = head_rows_of(halo_qkv, chan_local + head * rows, rows)
+        halo_key = joined_rows(halo_a, halo_b, chan_local + head * rows, rows)
         key_ext = jnp.concatenate([halo_key[:, :HALO], key, halo_key[:, HALO:]], axis=1)
         span = slice(head * rows, (head + 1) * rows)
         value_span = slice(chan_local + head * rows, chan_local + (head + 1) * rows)
@@ -209,10 +239,12 @@
         keyval_total = jnp.zeros((2 * chan_local, 2 * chan_local), F32)
         for comp in range(degree * degree, (degree + 1) * (degree + 1)):
             own = jnp.concatenate([fm[comp], fo[comp]], axis=0)
+            at = comp if comp < cut else comp - cut
+            flm, flo, frm, fro = early if comp < cut else late
             wide = jnp.concatenate(
                 [
-                    jnp.concatenate([flm[comp], fm[comp], frm[comp]], axis=1),
-                    jnp.concatenate([flo[comp], fo[comp], fro[comp]], axis=1),
+                    jnp.concatenate([flm[at], fm[comp], frm[at]], axis=1),
+                    jnp.concatenate([flo[at], fo[comp], fro[at]], axis=1),
                 ],
                 axis=0,
             )
@@ -239,14 +271,14 @@
     return coefs, tables
 
 
-def key_kernel(heads, slots, grad_query, own_key, halo_qkv, message_left, message_right, wc,
+def key_kernel(heads, slots, grad_query, own_key, halo_a, halo_b, message_left, message_right, wc,
                terms, grad):
     comps, chan_local = grad_query.shape[0], grad_query.shape[1]
     rows = chan_local // heads
     grad[:, :chan_local, :] = grad_query[...]
     coefs, tables = halo_slots(message_left, message_right, 2 * heads, slots)
     for head in range(heads):
-        query = head_rows_of(halo_qkv, head * rows, rows)
+        query = joined_rows(halo_a, halo_b, head * rows, rows)
         rim = jnp.concatenate(
             [
                 nn(query[:, :HALO], spread(tables[0], coefs[0], head, slots)),
@@ -262,7 +294,8 @@
 
 
 def value_kernel(heads, slots, start, own_value, cl, cr, message_left, message_right, wc, terms,
-                 mine, theirs, token, grad):
+                 mine, token, *theirs):
+    *theirs, grad = theirs
     token[...] = jnp.zeros_like(token)
     comps, chan_local = cl.shape[0], cl.shape[1]
     rows = chan_local // heads
@@ -284,13 +317,22 @@
         mix = wc[degree_of(start + comp)][:, 2 * chan_local :]
         total = terms[start + comp] + nn(mix, grad[comp])
         mine[comp] = total[:chan_local]
-        theirs[comp] = total[chan_local:].astype(BF16)
-
-
-def finish_kernel(mine_a, theirs_a, mine_b, theirs_b, out):
-    cut = mine_a.shape[0]
-    out[:cut] = (mine_a[...] + theirs_a[...].astype(F32)).astype(BF16)
-    out[cut:] = (mine_b[...] + theirs_b[...].astype(F32)).astype(BF16)
+        part = theirs[0].shape[0]
+        theirs[comp // part][comp % part] = total[chan_local:].astype(BF16)
+
+
+def finish_kernel(parts, *refs):
+    *refs, out = refs
+    start = 0
+    for count in parts:
+        mine, theirs, refs = refs[0], refs[1 : count + 1], refs[count + 1 :]
+        at = 0
+        for part in theirs:
+            size = part.shape[0]
+            total = mine[at : at + size] + part[...].astype(F32)
+            out[start + at : start + at + size] = total.astype(BF16)
+            at += size
+        start += at
 
 
 def gather_kernel(place, part_0, part_1, part_2, part_3, out):
@@ -301,7 +343,7 @@
         out[:, pl.ds(first, piece), :] = part[...].astype(F32)
 
 
-def call(kernel, args, outs, scratch=(), scalars=0, limit=24, stay=(), tokens=()):
+def call(kernel, args, outs, scratch=(), scalars=0, limit=24, stay=(), tokens=(), flops=0):
     whole = pl.BlockSpec(memory_space=pltpu.VMEM)
     small = pl.BlockSpec(memory_space=pltpu.SMEM)
     args = [
@@ -322,7 +364,7 @@
         out_specs=tuple([whole] * len(outs)),
         scratch_shapes=list(scratch),
         compiler_params=pltpu.CompilerParams(vmem_limit_bytes=limit * 1024 * 1024),
-        cost_estimate=pl.CostEstimate(flops=0, bytes_accessed=1024, transcendentals=0),
+        cost_estimate=pl.CostEstimate(flops=flops, bytes_accessed=1024, transcendentals=0),
     )(*args, *tokens)
 
 
@@ -369,7 +411,9 @@
     spot = (atom_place >> cut_bits[0]) & 3
     place = jnp.stack([lax.axis_index("chan"), atom_place * atoms_dev, spot])
     place = place.astype(jnp.int32)
-    cut = comps // 2
+    feature_cut = comps // 2
+    cotangent_cut = 2 * comps // 3
+    cuts = ((0, cotangent_cut), (cotangent_cut, comps))
 
     def held(*dims, dtype=F32):
         return pltpu.VMEM(dims, dtype)
@@ -381,20 +425,23 @@
     cot = jnp.transpose(cotangent, (1, 0, 2))
     mix = jnp.transpose(weights, (0, 1, 3, 2))
     anywhere = pl.BlockSpec(memory_space=pl.ANY)
-    low, high = pl.pallas_call(
-        split_kernel,
-        out_shape=(plain(comps, chan_local, HALO, dtype=BF16),) * 2,
+    sizes = (feature_cut, feature_cut, comps - feature_cut, comps - feature_cut)
+    high_a, low_a, high_b, low_b = pl.pallas_call(
+        functools.partial(split_kernel, feature_cut),
+        out_shape=tuple(held(size, chan_local, HALO, dtype=BF16) for size in sizes),
         in_specs=[anywhere],
-        out_specs=(anywhere, anywhere),
-        scratch_shapes=[pltpu.SemaphoreType.DMA((2,))],
-        compiler_params=pltpu.CompilerParams(vmem_limit_bytes=1024 * 1024),
-    )(fm)
-    flm = shifted(high, "atom", 1)
-    frm = shifted(low, "atom", -1)
+        out_specs=(pl.BlockSpec(memory_space=pltpu.VMEM),) * 4,
+        scratch_shapes=[pltpu.SemaphoreType.DMA((4,))],
+        compiler_params=pltpu.CompilerParams(vmem_limit_bytes=4 * 1024 * 1024),
+    )(pltpu.with_memory_space_constraint(fm, pltpu.HBM))
+    flm_a = shifted(high_a, "atom", 1)
+    frm_a = shifted(low_a, "atom", -1)
+    flm_b = shifted(high_b, "atom", 1)
+    frm_b = shifted(low_b, "atom", -1)
     fo = shifted(fm, "chan", 1)
 
-    qkv, scores, slot_own, index_rows, index_wide, wp, wc, *rims, token = call(
-        functools.partial(own_kernel, heads, total_atoms, cut),
+    qkv, scores, slot_own, index_rows, index_wide, wp, wc, token, *rims = call(
+        functools.partial(own_kernel, heads, total_atoms, cuts),
         (place, fm, fo, cot, mix, neighbours),
         (
             held(comps, 3 * chan_local, atoms_dev, dtype=BF16),
@@ -404,64 +451,82 @@
             held(atoms_dev, HALO, dtype=jnp.int32),
             held(LMAX + 1, 3 * chan_local, channels, dtype=BF16),
             held(LMAX + 1, channels, 3 * chan_local, dtype=BF16),
-            plain(cut, chan_local, HALO, dtype=BF16),
-            plain(cut, chan_local, HALO, dtype=BF16),
-            plain(comps - cut, chan_local, HALO, dtype=BF16),
-            plain(comps - cut, chan_local, HALO, dtype=BF16),
             plain(8, HALO),
+            *(
+                plain(stop - start, chan_local, HALO, dtype=BF16)
+                for start, stop in cuts
+                for _ in range(2)
+            ),
         ),
         scalars=1,
         stay=(1, 2, 3),
-    )
-    flm, frm = after((flm, frm), (token,))
-    flo = shifted(flm, "chan", 1)
-    fro = shifted(frm, "chan", 1)
-    rims[:2] = after(rims[:2], (flm, frm))
-    first = (shifted(rims[0], "atom", 1), shifted(rims[1], "atom", -1))
-    halo_qkv, grad_bias, message_a, message_b = call(
-        functools.partial(edge_kernel, heads, score_scale),
-        (flm, flo, frm, fro, wp, qkv, cot, scores, edge_bias, valid_mask, index_rows, index_wide),
+        flops=12 * 10**9,
+    )
+    flm_a, frm_a = after((flm_a, frm_a), (token,))
+    flo_a = shifted(flm_a, "chan", 1)
+    fro_a = shifted(frm_a, "chan", 1)
+    halo_a, partial, token = call(
+        functools.partial(early_kernel, heads),
+        (flm_a, flo_a, frm_a, fro_a, wp, qkv, cot),
         (
-            held(comps, 3 * chan_local, atoms_dev, dtype=BF16),
+            held(feature_cut, 3 * chan_local, atoms_dev, dtype=BF16),
+            held(2 * heads, 2, HALO, HALO),
+            plain(8, HALO),
+        ),
+        stay=tuple(range(7)),
+    )
+    rims[:2] = after(rims[:2], (token,))
+    flm_b, frm_b = after((flm_b, frm_b), (token,))
+    halos = [(shifted(rims[0], "atom", 1), shifted(rims[1], "atom", -1))]
+    flo_b = shifted(flm_b, "chan", 1)
+    fro_b = shifted(frm_b, "chan", 1)
+    halo_b, grad_bias, message_a, message_b = call(
+        functools.partial(edge_kernel, heads, score_scale, feature_cut),
+        (flm_b, flo_b, frm_b, fro_b, wp, qkv, cot, scores, partial, edge_bias, valid_mask,
+         index_rows, index_wide),
+        (
+            held(comps - feature_cut, 3 * chan_local, atoms_dev, dtype=BF16),
             plain(heads, slots, atoms_dev),
             held((2 * heads + 1) * slots, HALO, dtype=BF16),
             held((2 * heads + 1) * slots, HALO, dtype=BF16),
         ),
-        stay=(0, 1, 2, 3, 4, 5, 6, 7, 10, 11),
+        stay=(0, 1, 2, 3, 4, 5, 6, 7, 8, 11, 12),
     )
     message_left = shifted(message_b, "atom", 1)
     message_right = shifted(message_a, "atom", -1)
     piece = (3 * (LMAX + 1), chan_local // 4, channels)
     grad_query, own_key, own_value, kept, *sent = call(
         functools.partial(grads_kernel, heads, slots),
-        (place, fm, fo, flm, flo, frm, fro, qkv, halo_qkv, cot, slot_own, message_a, message_b),
+        (place, fm, fo, flm_a, flo_a, frm_a, fro_a, flm_b, flo_b, frm_b, fro_b, qkv, halo_a, halo_b,
+         cot, slot_own, message_a, message_b),
         (
             held(comps, chan_local, atoms_dev, dtype=BF16),
             held(comps, chan_local, atoms_dev),
             held(comps, chan_local, atoms_dev),
             held(*piece),
-            held(*piece, dtype=BF16),
-            held(*piece, dtype=BF16),
-            held(*piece, dtype=BF16),
+            plain(*piece, dtype=BF16),
+            plain(*piece, dtype=BF16),
+            plain(*piece, dtype=BF16),
         ),
         scratch=[
             pltpu.VMEM((comps, 2 * chan_local, 2 * atoms_dev), BF16),
             pltpu.VMEM((3 * (LMAX + 1), chan_local, channels), F32),
         ],
         scalars=1,
-        stay=tuple(range(1, 13)),
-    )
-    arrived = [exchanged(sent[d - 1], "atom", d << cut_bits[0]) for d in range(1, 4)]
-    rims[2:] = after(rims[2:], (message_left, message_right, arrived[0], *first))
-    second = (shifted(rims[2], "atom", 1), shifted(rims[3], "atom", -1))
-    kept = kept + arrived[0].astype(F32) + arrived[1].astype(F32) + arrived[2].astype(F32)
+        stay=tuple(range(1, 18)),
+    )
+    for delta, part in enumerate(sent, 1):
+        kept = kept + exchanged(part, "atom", delta << cut_bits[0]).astype(F32)
     rest = [bit for bit in range(count.bit_length() - 1) if bit not in cut_bits]
     while rest:
-        group, rest = rest[:2], rest[2:]
+        offsets = [1 << bit for bit in rest[:2]]
+        rest = rest[2:]
         rounded = kept.astype(BF16)
-        offsets = [1 << bit for bit in group]
-        for offset in offsets + [sum(offsets)] * (len(group) - 1):
-            kept = kept + exchanged(rounded, "atom", offset).astype(F32)
+        offsets += [sum(offsets)] * (len(offsets) - 1)
+        arrived = [exchanged(rounded, "atom", offset) for offset in offsets]
+        kept = functools.reduce(lambda total, part: total + part.astype(F32), arrived, kept)
+    rims[2:] = after(rims[2:], (*arrived, *halos[0]))
+    halos.append((shifted(rims[2], "atom", 1), shifted(rims[3], "atom", -1)))
     rounded = kept.astype(BF16)
     pieces = [rounded] + [exchanged(rounded, "atom", d << cut_bits[0]) for d in range(1, 4)]
     (grad_weights,) = call(
@@ -473,37 +538,41 @@
     )
     (terms,) = call(
         functools.partial(key_kernel, heads, slots),
-        (grad_query, own_key, halo_qkv, message_left, message_right, wc),
+        (grad_query, own_key, halo_a, halo_b, message_left, message_right, wc),
         (held(comps, channels, atoms_dev),),
         scratch=[pltpu.VMEM((comps, 2 * chan_local, atoms_dev), BF16)],
         limit=16,
-        stay=(0, 1, 2, 5),
-    )
-    parts = []
-    tokens = ()
-    for start, (cl, cr) in ((0, first), (cut, second)):
-        size = cl.shape[0]
-        mine, theirs, token = call(
+        stay=(0, 1, 2, 3, 6),
+        tokens=tuple(arrived),
+    )
+    parts, counts = [], []
+    tokens = tuple(arrived)
+    for (start, stop), (cl, cr) in zip(cuts, halos):
+        size = stop - start
+        part = -(-size // -(-size // (comps // 6)))
+        sizes = [min(part, size - at) for at in range(0, size, part)]
+        mine, token, *theirs = call(
             functools.partial(value_kernel, heads, slots, start),
             (own_value, cl, cr, message_left, message_right, wc, terms),
             (
                 held(size, chan_local, atoms_dev),
-                held(size, chan_local, atoms_dev, dtype=BF16),
                 plain(8, HALO),
+                *(held(some, chan_local, atoms_dev, dtype=BF16) for some in sizes),
             ),
             scratch=[pltpu.VMEM((size, chan_local, atoms_dev), BF16)],
             limit=16,
             stay=(0, 5, 6),
             tokens=tokens,
         )
-        tokens = (token, rounded)
-        parts += [mine, shifted(theirs, "chan", 1)]
+        tokens = (token, *pieces)
+        counts.append(len(sizes))
+        parts += [mine, *(shifted(some, "chan", 1) for some in theirs)]
     (out,) = call(
-        finish_kernel,
+        functools.partial(finish_kernel, counts),
         parts,
         (plain(comps, chan_local, atoms_dev, dtype=BF16),),
         limit=8,
-        stay=(0, 1, 2, 3),
+        stay=tuple(range(len(parts))),
     )
     grad_features = jnp.transpose(out, (1, 0, 2))
     grad_weights = grad_weights.reshape(3, LMAX + 1, chan_local, channels)

time: 107 us -> 120 us (1.12)
  starting transfers between devices: 33.1 us -> 45.4 us
    ppermute x13 -> x22, waiting for transfers between devices: 32.8 us -> 20.4 us  [shifted(): return lax.ppermute(value, axis, pairs)]
    ppermute x9, waiting for transfers between devices: 8.48 us -> 20.3 us  [exchanged(): lax.ppermute(value, axis, [(source, source ^ offset) for source in range(...]
    ppermute x13 -> x22, starting transfers between devices: 21.6 us -> 32.2 us  [shifted(): return lax.ppermute(value, axis, pairs)]
    ppermute x9, starting transfers between devices: 11.5 us -> 13.2 us  [exchanged(): lax.ppermute(value, axis, [(source, source ^ offset) for source in range(...]
    pallas_call x1, Pallas kernels: 1.17 us -> 2.54 us  [on_device(): pl.pallas_call(functools.partial(split_kernel, feature_cut), out_shape=tu...]
    unnamed x14 -> x12, local copies, waits for them, and re-layouts: 3.83 us -> 4.54 us
    pallas_call x8 -> x9, Pallas kernels: 26.5 us -> 25.9 us  [call(): pl.pallas_call(body, out_shape=tuple(outs), in_specs=[small] * scalars +...]
  transfers between devices with their start and end apart: 22 -> 31, of which waited for: 9 -> 12; matrix products, arithmetic and copies ran while one was open for 0% -> 0% of each run, Pallas kernels for 22% -> 22%
where the time goes in v4:
time: 120 us
  starting transfers between devices  45.4 us (38%)
  waiting for transfers between devices  40.7 us (34%)
  Pallas kernels  28.4 us (24%)
  local copies, waits for them, and re-layouts  4.54 us (4%)
    ppermute x22, starting transfers between devices, shifted(): return lax.ppermute(value, axis, pairs)  32.2 us
    pallas_call x9, Pallas kernels, call(): pl.pallas_call(body, out_shape=tuple(outs), in_specs=[small] * scalars +...  25.9 us
    ppermute x22, waiting for transfers between devices, shifted(): return lax.ppermute(value, axis, pairs)  20.4 us
    ppermute x9, waiting for transfers between devices, exchanged(): lax.ppermute(value, axis, [(source, source ^ offset) for source in range(...  20.3 us
    ppermute x9, starting transfers between devices, exchanged(): lax.ppermute(value, axis, [(source, source ^ offset) for source in range(...  13.2 us
    unnamed x12, local copies, waits for them, and re-layouts  4.54 us
    pallas_call x1, Pallas kernels, on_device(): pl.pallas_call(functools.partial(split_kernel, feature_cut), out_shape=tu...  2.54 us
  transfers between devices with their start and end apart: 31, of which 12 were waited for; matrix products, arithmetic and copies ran while one was open for 0% of the time, Pallas kernels for 22%

profile of v4, /device:TPU:0, one launch (start us, length us, event | category | flops | bytes accessed | tf_op | source)
XLA Modules:
  0.0 120.1 jit_solution(9375284982163790855)
XLA Ops:
  0.6 0.5 collective-permute-start
  1.1 2.5 %shard_map.85 = (bf16[24,64,128]{2,1,0:T(8,128)(2,1)}, bf16[24,64,128]{2,1,0:T(8,128)(2,1)}, bf16[25,64,128]{2,1,0:T(8,128)(2,1)}, bf16[25,64,128]{2,1,0:T(8,128)(2,1)}) custom-call(bf16[49,64,256]{2,1,0:T(8,128)(2,1)} %bitcast.15), custom_call_target="tpu_custom_call" | custom-call | tf_op jit(solution)/shard_map/pallas_call | solution.py:429
  3.7 2.6 %collective-permute-start.1 = (bf16[24,64,128]{2,1,0:T(8,128)(2,1)}, bf16[24,64,128]{2,1,0:T(8,128)(2,1)S(1)}, u32[]{:S(2)}, u32[]{:S(2)}) collective-permute-start(bf16[24,64,128]{2,1,0:T(8,128)(2,1)} %get-tuple-element.51), channel_id=1, source_target_pairs={{0,2},{2,4},{4,6},{6,8},{8,10},{10,12},{12,14},{14,16},{16,18},{18... | collective-permute-start | bytes 1179656 | tf_op jit(solution)/shard_map/ppermute | solution.py:392
  6.3 4.1 %collective-permute-start.2 = (bf16[24,64,128]{2,1,0:T(8,128)(2,1)}, bf16[24,64,128]{2,1,0:T(8,128)(2,1)S(1)}, u32[]{:S(2)}, u32[]{:S(2)}) collective-permute-start(bf16[24,64,128]{2,1,0:T(8,128)(2,1)} %get-tuple-element.52), channel_id=1, source_target_pairs={{0,30},{2,0},{4,2},{6,4},{8,6},{10,8},{12,10},{14,12},{16,14},{18,... | collective-permute-start | bytes 1179656 | tf_op jit(solution)/shard_map/ppermute | solution.py:392
  10.3 5.6 %collective-permute-start.6 = (bf16[25,64,128]{2,1,0:T(8,128)(2,1)}, bf16[25,64,128]{2,1,0:T(8,128)(2,1)S(1)}, u32[]{:S(2)}, u32[]{:S(2)}) collective-permute-start(bf16[25,64,128]{2,1,0:T(8,128)(2,1)} %get-tuple-element.57), channel_id=1, source_target_pairs={{0,30},{2,0},{4,2},{6,4},{8,6},{10,8},{12,10},{14,12},{16,14},{18,... | collective-permute-start | bytes 1228808 | tf_op jit(solution)/shard_map/ppermute | solution.py:392
  15.9 0.1 pad_add_fusion.refs_0_
  16.0 1.4 %copy-done = bf16[64,49,256]{2,0,1:T(8,128)(2,1)S(1)} copy-done((bf16[64,49,256]{2,0,1:T(8,128)(2,1)S(1)}, bf16[64,49,256]{2,0,1:T(8,128)(2,1)}, u32[]{:S(2)}) %copy-start) | copy-done | bytes 1605656
  17.4 1.4 %copy-done.1 = bf16[64,49,256]{2,0,1:T(8,128)(2,1)S(1)} copy-done((bf16[64,49,256]{2,0,1:T(8,128)(2,1)S(1)}, bf16[64,49,256]{2,0,1:T(8,128)(2,1)}, u32[]{:S(2)}) %copy-start.1) | copy-done | bytes 1605656
  18.9 1.0 copy-done.4
  19.8 0.7 copy-done.5
  20.6 3.8 %shard_map.86 = (bf16[49,192,256]{2,1,0:T(8,128)(2,1)S(1)}, f32[8,256,256]{2,1,0:T(8,128)S(1)}, s32[2,3,128,128]{3,2,1,0:T(8,128)S(1)}, s32[16,256]{1,0:T(8,128)...) custom-call(s32[3]{0:T(128)S(1)} %pad_add_fusion.refs_0_, ...), custom_call_target="tpu_custom_call" | custom-call | flops 12000000000 | bytes 1024 | tf_op jit(solution)/shard_map/pallas_call | solution.py:358
  24.3 8.9 %collective-permute-done.1.refs_0_ = bf16[24,64,128]{2,1,0:T(8,128)(2,1)S(1)} collective-permute-done((bf16[24,64,128]{2,1,0:T(8,128)(2,1)}, bf16[24,64,128]{2,1,0:T(8,128)(2,1)S(1)}, u32[]{:S(2)}, u32[]{:S(2)}) %collective-permute-start.1) | collective-permute-done | bytes 393248 | tf_op jit(solution)/shard_map/ppermute | solution.py:392
  33.2 0.5 collective-permute-start.4
  33.7 1.2 %collective-permute-done.3.refs_1_.refs_4_ = bf16[24,64,128]{2,1,0:T(8,128)(2,1)S(1)} collective-permute-done((bf16[24,64,128]{2,1,0:T(8,128)(2,1)S(1)}, bf16[24,64,128]{2,1,0:T(8,128)(2,1)S(1)}, u32[]{:S(2)}, u32[]{:S(2)}) %collective-permute-start.3) | collective-permute-done | bytes 393248 | tf_op jit(solution)/shard_map/ppermute | solution.py:392
  34.9 0.6 collective-permute-done.4.refs_3_.refs_6_
  35.5 1.3 %shard_map.88 = (bf16[24,192,256]{2,1,0:T(8,128)(2,1)S(1)}, f32[8,2,128,128]{3,2,1,0:T(8,128)S(1)}, f32[8,128]{1,0:T(8,128)S(1)}) custom-call(bf16[24,64,128]{2,1,0:T(8,128)(2,1)S(1)} %get-tuple-element.54.refs_0_.refs_3_, bf16[24,64,128]{2,1,0:T(8,128)(2,1)S(1)} %collective-permute-done.3.refs_1_.refs_4_, ...), custom_call_target="tpu_custom_call" | custom-call | bytes 1024 | tf_op jit(solution)/shard_map/pallas_call | solution.py:358
  36.8 4.8 %collective-permute-done.5.refs_0_ = bf16[25,64,128]{2,1,0:T(8,128)(2,1)S(1)} collective-permute-done((bf16[25,64,128]{2,1,0:T(8,128)(2,1)}, bf16[25,64,128]{2,1,0:T(8,128)(2,1)S(1)}, u32[]{:S(2)}, u32[]{:S(2)}) %collective-permute-start.5) | collective-permute-done | bytes 409632 | tf_op jit(solution)/shard_map/ppermute | solution.py:392
  41.6 1.8 %collective-permute-done.6.refs_1_ = bf16[25,64,128]{2,1,0:T(8,128)(2,1)S(1)} collective-permute-done((bf16[25,64,128]{2,1,0:T(8,128)(2,1)}, bf16[25,64,128]{2,1,0:T(8,128)(2,1)S(1)}, u32[]{:S(2)}, u32[]{:S(2)}) %collective-permute-start.6) | collective-permute-done | bytes 409632 | tf_op jit(solution)/shard_map/ppermute | solution.py:392
  43.4 0.5 collective-permute-start.8
  43.9 1.5 %collective-permute-start.9 = (bf16[32,64,128]{2,1,0:T(8,128)(2,1)S(1)}, bf16[32,64,128]{2,1,0:T(8,128)(2,1)S(1)}, u32[]{:S(2)}, u32[]{:S(2)}) collective-permute-start(bf16[32,64,128]{2,1,0:T(8,128)(2,1)S(1)} %get-tuple-element.75), channel_id=1, source_target_pairs={{0,2},{2,4},{4,6},{6,8},{8,10},{10,12},{12,14},{14,16},{16,18},{18... | collective-permute-start | bytes 1572872 | tf_op jit(solution)/shard_map/ppermute | solution.py:392
  45.4 4.1 %collective-permute-start.10 = (bf16[32,64,128]{2,1,0:T(8,128)(2,1)S(1)}, bf16[32,64,128]{2,1,0:T(8,128)(2,1)S(1)}, u32[]{:S(2)}, u32[]{:S(2)}) collective-permute-start(bf16[32,64,128]{2,1,0:T(8,128)(2,1)S(1)} %get-tuple-element.76), channel_id=1, source_target_pairs={{0,30},{2,0},{4,2},{6,4},{8,6},{10,8},{12,10},{14,12},{16,14},{18,... | collective-permute-start | bytes 1572872 | tf_op jit(solution)/shard_map/ppermute | solution.py:392
  49.6 3.8 %shard_map.90 = (bf16[25,192,256]{2,1,0:T(8,128)(2,1)S(1)}, f32[4,16,256]{2,1,0:T(8,128)}, bf16[144,128]{1,0:T(8,128)(2,1)S(1)}, bf16[144,128]{1,0:T(8,128)(2,1)S(1)}) custom-call(bf16[25,64,128]{2,1,0:T(8,128)(2,1)S(1)} %get-tuple-element.61.refs_0_.refs_7_, bf16[25,64,128]{2,1,0:T(8,128)(2,1)S(1)} %collective-permute-done.7.refs_1_.refs_8_, ...), custom_call_target="tpu_custom_call" | custom-call | bytes 1024 | tf_op jit(solution)/shard_map/pallas_call | solution.py:358
  53.4 6.8 %shard_map.91 = (bf16[49,64,256]{2,1,0:T(8,128)(2,1)S(1)}, f32[49,64,256]{2,1,0:T(8,128)S(1)}, f32[49,64,256]{2,1,0:T(8,128)S(1)}, f32[21,16,128]{2,1,0:T(8,128)...) custom-call(s32[3]{0:T(128)S(1)} %pad_add_fusion.refs_0_, ...), custom_call_target="tpu_custom_call" | custom-call | bytes 1024 | tf_op jit(solution)/shard_map/pallas_call | solution.py:358
  60.2 0.1 collective-permute-start.13
  60.3 0.3 collective-permute-start.14
  60.5 3.2 %collective-permute-start.15 = (bf16[21,16,128]{2,1,0:T(8,128)(2,1)S(1)}, bf16[21,16,128]{2,1,0:T(8,128)(2,1)S(1)}, u32[]{:S(2)}, u32[]{:S(2)}) collective-permute-start(bf16[21,16,128]{2,1,0:T(8,128)(2,1)S(1)} %get-tuple-element.83), channel_id=1, source_target_pairs={{0,12},{2,14},{4,8},{6,10},{8,4},{10,6},{12,0},{14,2},{16,28},{18,... | collective-permute-start | bytes 258056 | tf_op jit(solution)/shard_map/ppermute | solution.py:397
  63.7 1.9 %collective-permute-done.13 = bf16[21,16,128]{2,1,0:T(8,128)(2,1)S(1)} collective-permute-done((bf16[21,16,128]{2,1,0:T(8,128)(2,1)S(1)}, bf16[21,16,128]{2,1,0:T(8,128)(2,1)S(1)}, u32[]{:S(2)}, u32[]{:S(2)}) %collective-permute-start.13) | collective-permute-done | bytes 86048 | tf_op jit(solution)/shard_map/ppermute | solution.py:397
  65.7 1.5 %collective-permute-done.15 = bf16[21,16,128]{2,1,0:T(8,128)(2,1)S(1)} collective-permute-done((bf16[21,16,128]{2,1,0:T(8,128)(2,1)S(1)}, bf16[21,16,128]{2,1,0:T(8,128)(2,1)S(1)}, u32[]{:S(2)}, u32[]{:S(2)}) %collective-permute-start.15) | collective-permute-done | bytes 86048 | tf_op jit(solution)/shard_map/ppermute | solution.py:397
  67.2 8.8 %collective-permute-start.18 = (bf16[21,16,128]{2,1,0:T(8,128)(2,1)S(1)}, bf16[21,16,128]{2,1,0:T(8,128)(2,1)S(1)}, u32[]{:S(2)}, u32[]{:S(2)}) collective-permute-start(bf16[21,16,128]{2,1,0:T(8,128)(2,1)S(1)} %fusion), channel_id=1, source_target_pairs={{0,18},{2,16},{4,22},{6,20},{8,26},{10,24},{12,30},{14,28},{16,2},... | collective-permute-start | bytes 258056 | tf_op jit(solution)/shard_map/ppermute | solution.py:397
  76.0 0.7 collective-permute-start.17
  76.7 6.3 %collective-permute-done.18.refs_9_.refs_4_ = bf16[21,16,128]{2,1,0:T(8,128)(2,1)S(1)} collective-permute-done((bf16[21,16,128]{2,1,0:T(8,128)(2,1)S(1)}, bf16[21,16,128]{2,1,0:T(8,128)(2,1)S(1)}, u32[]{:S(2)}, u32[]{:S(2)}) %collective-permute-start.18) | collective-permute-done | bytes 86048 | tf_op jit(solution)/shard_map/ppermute | solution.py:397
  83.0 1.6 %collective-permute-done.17.refs_8_.refs_3_ = bf16[21,16,128]{2,1,0:T(8,128)(2,1)S(1)} collective-permute-done((bf16[21,16,128]{2,1,0:T(8,128)(2,1)S(1)}, bf16[21,16,128]{2,1,0:T(8,128)(2,1)S(1)}, u32[]{:S(2)}, u32[]{:S(2)}) %collective-permute-start.17) | collective-permute-done | bytes 86048 | tf_op jit(solution)/shard_map/ppermute | solution.py:397
  84.6 0.4 collective-permute-start.23
  85.1 0.1 add_convert_fusion.refs_8_.refs_1_
  85.3 5.2 %collective-permute-start.12 = (bf16[144,128]{1,0:T(8,128)(2,1)S(1)}, bf16[144,128]{1,0:T(8,128)(2,1)S(1)}, u32[]{:S(2)}, u32[]{:S(2)}) collective-permute-start(bf16[144,128]{1,0:T(8,128)(2,1)S(1)} %get-tuple-element.70.refs_16_), channel_id=1, source_target_pairs={{0,30},{2,0},{4,2},{6,4},{8,6},{10,8},{12,10},{14,12},{16,14},{18,... | collective-permute-start | bytes 110600 | tf_op jit(solution)/shard_map/ppermute | solution.py:392
  90.5 5.6 %collective-permute-start.24 = (bf16[17,64,128]{2,1,0:T(8,128)(2,1)S(1)}, bf16[17,64,128]{2,1,0:T(8,128)(2,1)S(1)}, u32[]{:S(2)}, u32[]{:S(2)}) collective-permute-start(bf16[17,64,128]{2,1,0:T(8,128)(2,1)S(1)} %get-tuple-element.92), channel_id=1, source_target_pairs={{0,30},{2,0},{4,2},{6,4},{8,6},{10,8},{12,10},{14,12},{16,14},{18,... | collective-permute-start | bytes 835592 | tf_op jit(solution)/shard_map/ppermute | solution.py:392
  96.1 3.1 %collective-permute-done.11.refs_4_.refs_3_ = bf16[144,128]{1,0:T(8,128)(2,1)S(1)} collective-permute-done((bf16[144,128]{1,0:T(8,128)(2,1)S(1)}, bf16[144,128]{1,0:T(8,128)(2,1)S(1)}, u32[]{:S(2)}, u32[]{:S(2)}) %collective-permute-start.11) | collective-permute-done | bytes 36896 | tf_op jit(solution)/shard_map/ppermute | solution.py:392
  99.2 2.9 %shard_map.93.refs_6_ = f32[49,128,256]{2,1,0:T(8,128)S(1)} custom-call(bf16[49,64,256]{2,1,0:T(8,128)(2,1)S(1)} %get-tuple-element.78.refs_0_, f32[49,64,256]{2,1,0:T(8,128)S(1)} %get-tuple-element.79.refs_1_, bf16[24,192,256]{2,1,0:T(8,128)(2,1)S(1)} %get-tuple-element.63.refs_12_.refs_2_, bf16[25,192,256]{2,1,0:T(8,128)(2,1)S(1)} %get-tuple-element.68.refs_13_.refs_3_, ...), custom_call_target="tpu_custom_call" | custom-call | bytes 1024 | tf_op jit(solution)/shard_map/pallas_call | solution.py:358
  102.1 2.2 %shard_map.94 = (f32[32,64,256]{2,1,0:T(8,128)S(1)}, f32[8,128]{1,0:T(8,128)S(1)}, bf16[8,64,256]{2,1,0:T(8,128)(2,1)S(1)}, bf16[8,64,256]{2,1,0:T(8,128)(2,1)S(...) custom-call(f32[49,64,256]{2,1,0:T(8,128)S(1)} %get-tuple-element.72.refs_0_, ...), custom_call_target="tpu_custom_call" | custom-call | bytes 1024 | tf_op jit(solution)/shard_map/pallas_call | solution.py:358
  104.4 0.1 collective-permute-start.26
  104.5 0.4 collective-permute-start.20
  104.9 4.4 %collective-permute-done.26.refs_10_.refs_3_ = bf16[21,16,128]{2,1,0:T(8,128)(2,1)S(1)} collective-permute-done((bf16[21,16,128]{2,1,0:T(8,128)(2,1)S(1)}, bf16[21,16,128]{2,1,0:T(8,128)(2,1)S(1)}, u32[]{:S(2)}, u32[]{:S(2)}) %collective-permute-start.26) | collective-permute-done | bytes 86048 | tf_op jit(solution)/shard_map/ppermute | solution.py:397
  109.4 4.5 %collective-permute-done.25.refs_9_.refs_2_ = bf16[21,16,128]{2,1,0:T(8,128)(2,1)S(1)} collective-permute-done((bf16[21,16,128]{2,1,0:T(8,128)(2,1)S(1)}, bf16[21,16,128]{2,1,0:T(8,128)(2,1)S(1)}, u32[]{:S(2)}, u32[]{:S(2)}) %collective-permute-start.25) | collective-permute-done | bytes 86048 | tf_op jit(solution)/shard_map/ppermute | solution.py:397
  113.8 0.5 collective-permute-start.22
  114.4 2.1 %shard_map.96 = (f32[17,64,256]{2,1,0:T(8,128)S(1)}, f32[8,128]{1,0:T(8,128)}, bf16[6,64,256]{2,1,0:T(8,128)(2,1)S(1)}, bf16[6,64,256]{2,1,0:T(8,128)(2,1)S(1)}, bf16[5,64,256]{2,1,0:T(8,128)(2,1)S(1)}) custom-call(f32[49,64,256]{2,1,0:T(8,128)S(1)} %get-tuple-element.72.refs_0_, bf16[17,64,128]{2,1,0:T(8,128)(2,1)S(1)} %collective-permute-done.23.refs_1_, ...), custom_call_target="tpu_custom_call" | custom-call | bytes 1024 | tf_op jit(solution)/shard_map/pallas_call | solution.py:358
  116.5 0.5 collective-permute-start.29
  117.1 1.4 %shard_map.98 = f32[21,64,128]{2,1,0:T(8,128)} custom-call(s32[3]{0:T(128)S(1)} %pad_add_fusion.refs_0_, bf16[21,16,128]{2,1,0:T(8,128)(2,1)S(1)} %add_convert_fusion.refs_8_.refs_1_, bf16[21,16,128]{2,1,0:T(8,128)(2,1)S(1)} %collective-permute-done.25.refs_9_.refs_2_, bf16[21,16,128]{2,1,0:T(8,128)(2,1)S(1)} %collective-permute-done.26.refs_10_.refs_3_, ...), custom_call_target="tpu_custom_call" | custom-call | bytes 1024 | tf_op jit(solution)/shard_map/pallas_call | solution.py:358
  118.5 1.5 %shard_map.97 = bf16[49,64,256]{2,1,0:T(8,128)(2,1)} custom-call(f32[32,64,256]{2,1,0:T(8,128)S(1)} %get-tuple-element.84.refs_0_, bf16[8,64,256]{2,1,0:T(8,128)(2,1)S(1)} %collective-permute-done.19.refs_1_, bf16[8,64,256]{2,1,0:T(8,128)(2,1)S(1)} %collective-permute-done.20.refs_2_, bf16[8,64,256]{2,1,0:T(8,128)(2,1)S(1)} %collective-permute-done.21.refs_3_, ...), custom_call_target="tpu_custom_call" | custom-call | bytes 1024 | tf_op jit(solution)/shard_map/pallas_call | solution.py:358
  (43 shorter events, 0.4 us)
Async XLA Ops:
  0.6 15.4 %collective-permute-start = (bf16[49,64,256]{2,1,0:T(8,128)(2,1)}, bf16[49,64,256]{2,1,0:T(8,128)(2,1)S(1)}, u32[]{:S(2)}, u32[]{:S(2)}) collective-permute-start(bf16[49,64,256]{2,1,0:T(8,128)(2,1)} %bitcast.14), channel_id=1, source_target_pairs={{0,1},{1,0},{2,3},{3,2},{4,5},{5,4},{6,7},{7,6},{8,9},{9,8},{10,11... | collective-permute-start | bytes 4816904 | tf_op jit(solution)/shard_map/ppermute | solution.py:392
  3.7 29.5 %collective-permute-start.1 = (bf16[24,64,128]{2,1,0:T(8,128)(2,1)}, bf16[24,64,128]{2,1,0:T(8,128)(2,1)S(1)}, u32[]{:S(2)}, u32[]{:S(2)}) collective-permute-start(bf16[24,64,128]{2,1,0:T(8,128)(2,1)} %get-tuple-element.51), channel_id=1, source_target_pairs={{0,2},{2,4},{4,6},{6,8},{8,10},{10,12},{12,14},{14,16},{16,18},{18... | collective-permute-start | bytes 1179656 | tf_op jit(solution)/shard_map/ppermute | solution.py:392
  6.3 27.0 %collective-permute-start.2 = (bf16[24,64,128]{2,1,0:T(8,128)(2,1)}, bf16[24,64,128]{2,1,0:T(8,128)(2,1)S(1)}, u32[]{:S(2)}, u32[]{:S(2)}) collective-permute-start(bf16[24,64,128]{2,1,0:T(8,128)(2,1)} %get-tuple-element.52), channel_id=1, source_target_pairs={{0,30},{2,0},{4,2},{6,4},{8,6},{10,8},{12,10},{14,12},{16,14},{18,... | collective-permute-start | bytes 1179656 | tf_op jit(solution)/shard_map/ppermute | solution.py:392
  10.3 31.3 %collective-permute-start.5 = (bf16[25,64,128]{2,1,0:T(8,128)(2,1)}, bf16[25,64,128]{2,1,0:T(8,128)(2,1)S(1)}, u32[]{:S(2)}, u32[]{:S(2)}) collective-permute-start(bf16[25,64,128]{2,1,0:T(8,128)(2,1)} %get-tuple-element.56), channel_id=1, source_target_pairs={{0,2},{2,4},{4,6},{6,8},{8,10},{10,12},{12,14},{14,16},{16,18},{18... | collective-permute-start | bytes 1228808 | tf_op jit(solution)/shard_map/ppermute | solution.py:392
  10.3 33.1 %collective-permute-start.6 = (bf16[25,64,128]{2,1,0:T(8,128)(2,1)}, bf16[25,64,128]{2,1,0:T(8,128)(2,1)S(1)}, u32[]{:S(2)}, u32[]{:S(2)}) collective-permute-start(bf16[25,64,128]{2,1,0:T(8,128)(2,1)} %get-tuple-element.57), channel_id=1, source_target_pairs={{0,30},{2,0},{4,2},{6,4},{8,6},{10,8},{12,10},{14,12},{16,14},{18,... | collective-permute-start | bytes 1228808 | tf_op jit(solution)/shard_map/ppermute | solution.py:392
  16.0 1.4 %copy-start = (bf16[64,49,256]{2,0,1:T(8,128)(2,1)S(1)}, bf16[64,49,256]{2,0,1:T(8,128)(2,1)}, u32[]{:S(2)}) copy-start(bf16[64,49,256]{2,0,1:T(8,128)(2,1)} %param.8) | copy-start | bytes 4816900
  17.4 1.4 %copy-start.1 = (bf16[64,49,256]{2,0,1:T(8,128)(2,1)S(1)}, bf16[64,49,256]{2,0,1:T(8,128)(2,1)}, u32[]{:S(2)}) copy-start(bf16[64,49,256]{2,0,1:T(8,128)(2,1)} %param.6) | copy-start | bytes 4816900
  18.9 1.0 copy-start.4
  19.8 0.7 copy-start.5
  33.2 1.7 %collective-permute-start.3 = (bf16[24,64,128]{2,1,0:T(8,128)(2,1)S(1)}, bf16[24,64,128]{2,1,0:T(8,128)(2,1)S(1)}, u32[]{:S(2)}, u32[]{:S(2)}) collective-permute-start(bf16[24,64,128]{2,1,0:T(8,128)(2,1)S(1)} %get-tuple-element.54.refs_0_.refs_3_), channel_id=1, source_target_pairs={{0,1},{1,0},{2,3},{3,2},{4,5},{5,4},{6,7},{7,6},{8,9},{9,8},{10,11... | collective-permute-start | bytes 1179656 | tf_op jit(solution)/shard_map/ppermute | solution.py:392
  33.2 2.3 %collective-permute-start.4 = (bf16[24,64,128]{2,1,0:T(8,128)(2,1)S(1)}, bf16[24,64,128]{2,1,0:T(8,128)(2,1)S(1)}, u32[]{:S(2)}, u32[]{:S(2)}) collective-permute-start(bf16[24,64,128]{2,1,0:T(8,128)(2,1)S(1)} %get-tuple-element.55.refs_2_.refs_5_), channel_id=1, source_target_pairs={{0,1},{1,0},{2,3},{3,2},{4,5},{5,4},{6,7},{7,6},{8,9},{9,8},{10,11... | collective-permute-start | bytes 1179656 | tf_op jit(solution)/shard_map/ppermute | solution.py:392
  35.5 14.1 %copy-start.2 = (f32[4,16,256]{2,1,0:T(8,128)S(1)}, f32[4,16,256]{2,1,0:T(8,128)}, u32[]{:S(2)}) copy-start(f32[4,16,256]{2,1,0:T(8,128)} %refs_9_.1) | copy-start | bytes 196612
  35.5 14.1 %copy-start.3 = (s32[16,256]{1,0:T(8,128)S(1)}, s32[16,256]{1,0:T(8,128)}, u32[]{:S(2)}) copy-start(s32[16,256]{1,0:T(8,128)} %refs_10_.1) | copy-start | bytes 49156
  43.4 6.1 %collective-permute-start.7 = (bf16[25,64,128]{2,1,0:T(8,128)(2,1)S(1)}, bf16[25,64,128]{2,1,0:T(8,128)(2,1)S(1)}, u32[]{:S(2)}, u32[]{:S(2)}) collective-permute-start(bf16[25,64,128]{2,1,0:T(8,128)(2,1)S(1)} %get-tuple-element.61.refs_0_.refs_7_), channel_id=1, source_target_pairs={{0,1},{1,0},{2,3},{3,2},{4,5},{5,4},{6,7},{7,6},{8,9},{9,8},{10,11... | collective-permute-start | bytes 1228808 | tf_op jit(solution)/shard_map/ppermute | solution.py:392
  43.4 6.1 %collective-permute-start.8 = (bf16[25,64,128]{2,1,0:T(8,128)(2,1)S(1)}, bf16[25,64,128]{2,1,0:T(8,128)(2,1)S(1)}, u32[]{:S(2)}, u32[]{:S(2)}) collective-permute-start(bf16[25,64,128]{2,1,0:T(8,128)(2,1)S(1)} %get-tuple-element.62.refs_2_.refs_9_), channel_id=1, source_target_pairs={{0,1},{1,0},{2,3},{3,2},{4,5},{5,4},{6,7},{7,6},{8,9},{9,8},{10,11... | collective-permute-start | bytes 1228808 | tf_op jit(solution)/shard_map/ppermute | solution.py:392
  43.9 32.8 %collective-permute-start.9 = (bf16[32,64,128]{2,1,0:T(8,128)(2,1)S(1)}, bf16[32,64,128]{2,1,0:T(8,128)(2,1)S(1)}, u32[]{:S(2)}, u32[]{:S(2)}) collective-permute-start(bf16[32,64,128]{2,1,0:T(8,128)(2,1)S(1)} %get-tuple-element.75), channel_id=1, source_target_pairs={{0,2},{2,4},{4,6},{6,8},{8,10},{10,12},{12,14},{14,16},{16,18},{18... | collective-permute-start | bytes 1572872 | tf_op jit(solution)/shard_map/ppermute | solution.py:392
  45.4 31.3 %collective-permute-start.10 = (bf16[32,64,128]{2,1,0:T(8,128)(2,1)S(1)}, bf16[32,64,128]{2,1,0:T(8,128)(2,1)S(1)}, u32[]{:S(2)}, u32[]{:S(2)}) collective-permute-start(bf16[32,64,128]{2,1,0:T(8,128)(2,1)S(1)} %get-tuple-element.76), channel_id=1, source_target_pairs={{0,30},{2,0},{4,2},{6,4},{8,6},{10,8},{12,10},{14,12},{16,14},{18,... | collective-permute-start | bytes 1572872 | tf_op jit(solution)/shard_map/ppermute | solution.py:392
  60.2 5.5 %collective-permute-start.13 = (bf16[21,16,128]{2,1,0:T(8,128)(2,1)S(1)}, bf16[21,16,128]{2,1,0:T(8,128)(2,1)S(1)}, u32[]{:S(2)}, u32[]{:S(2)}) collective-permute-start(bf16[21,16,128]{2,1,0:T(8,128)(2,1)S(1)} %get-tuple-element.81), channel_id=1, source_target_pairs={{0,4},{2,6},{4,0},{6,2},{8,12},{10,14},{12,8},{14,10},{16,20},{18,... | collective-permute-start | bytes 258056 | tf_op jit(solution)/shard_map/ppermute | solution.py:397
  60.3 5.4 %collective-permute-start.14 = (bf16[21,16,128]{2,1,0:T(8,128)(2,1)S(1)}, bf16[21,16,128]{2,1,0:T(8,128)(2,1)S(1)}, u32[]{:S(2)}, u32[]{:S(2)}) collective-permute-start(bf16[21,16,128]{2,1,0:T(8,128)(2,1)S(1)} %get-tuple-element.82), channel_id=1, source_target_pairs={{0,8},{2,10},{4,12},{6,14},{8,0},{10,2},{12,4},{14,6},{16,24},{18,... | collective-permute-start | bytes 258056 | tf_op jit(solution)/shard_map/ppermute | solution.py:397
  60.5 6.6 %collective-permute-start.15 = (bf16[21,16,128]{2,1,0:T(8,128)(2,1)S(1)}, bf16[21,16,128]{2,1,0:T(8,128)(2,1)S(1)}, u32[]{:S(2)}, u32[]{:S(2)}) collective-permute-start(bf16[21,16,128]{2,1,0:T(8,128)(2,1)S(1)} %get-tuple-element.83), channel_id=1, source_target_pairs={{0,12},{2,14},{4,8},{6,10},{8,4},{10,6},{12,0},{14,2},{16,28},{18,... | collective-permute-start | bytes 258056 | tf_op jit(solution)/shard_map/ppermute | solution.py:397
  67.2 15.8 %collective-permute-start.18 = (bf16[21,16,128]{2,1,0:T(8,128)(2,1)S(1)}, bf16[21,16,128]{2,1,0:T(8,128)(2,1)S(1)}, u32[]{:S(2)}, u32[]{:S(2)}) collective-permute-start(bf16[21,16,128]{2,1,0:T(8,128)(2,1)S(1)} %fusion), channel_id=1, source_target_pairs={{0,18},{2,16},{4,22},{6,20},{8,26},{10,24},{12,30},{14,28},{16,2},... | collective-permute-start | bytes 258056 | tf_op jit(solution)/shard_map/ppermute | solution.py:397
  76.0 8.6 %collective-permute-start.17 = (bf16[21,16,128]{2,1,0:T(8,128)(2,1)S(1)}, bf16[21,16,128]{2,1,0:T(8,128)(2,1)S(1)}, u32[]{:S(2)}, u32[]{:S(2)}) collective-permute-start(bf16[21,16,128]{2,1,0:T(8,128)(2,1)S(1)} %fusion), channel_id=1, source_target_pairs={{0,16},{2,18},{4,20},{6,22},{8,24},{10,26},{12,28},{14,30},{16,0},... | collective-permute-start | bytes 258056 | tf_op jit(solution)/shard_map/ppermute | solution.py:397
  76.7 8.0 %collective-permute-start.16 = (bf16[21,16,128]{2,1,0:T(8,128)(2,1)S(1)}, bf16[21,16,128]{2,1,0:T(8,128)(2,1)S(1)}, u32[]{:S(2)}, u32[]{:S(2)}) collective-permute-start(bf16[21,16,128]{2,1,0:T(8,128)(2,1)S(1)} %fusion), channel_id=1, source_target_pairs={{0,2},{2,0},{4,6},{6,4},{8,10},{10,8},{12,14},{14,12},{16,18},{18,... | collective-permute-start | bytes 258056 | tf_op jit(solution)/shard_map/ppermute | solution.py:397
  84.6 29.2 %collective-permute-start.23 = (bf16[17,64,128]{2,1,0:T(8,128)(2,1)S(1)}, bf16[17,64,128]{2,1,0:T(8,128)(2,1)S(1)}, u32[]{:S(2)}, u32[]{:S(2)}) collective-permute-start(bf16[17,64,128]{2,1,0:T(8,128)(2,1)S(1)} %get-tuple-element.91), channel_id=1, source_target_pairs={{0,2},{2,4},{4,6},{6,8},{8,10},{10,12},{12,14},{14,16},{16,18},{18... | collective-permute-start | bytes 835592 | tf_op jit(solution)/shard_map/ppermute | solution.py:392
  85.2 19.3 %collective-permute-start.27 = (bf16[21,16,128]{2,1,0:T(8,128)(2,1)S(1)}, bf16[21,16,128]{2,1,0:T(8,128)(2,1)S(1)}, u32[]{:S(2)}, u32[]{:S(2)}) collective-permute-start(bf16[21,16,128]{2,1,0:T(8,128)(2,1)S(1)} %add_convert_fusion.refs_8_.refs_1_), channel_id=1, source_target_pairs={{0,12},{2,14},{4,8},{6,10},{8,4},{10,6},{12,0},{14,2},{16,28},{18,... | collective-permute-start | bytes 258056 | tf_op jit(solution)/shard_map/ppermute | solution.py:397
  85.3 10.9 %collective-permute-start.12 = (bf16[144,128]{1,0:T(8,128)(2,1)S(1)}, bf16[144,128]{1,0:T(8,128)(2,1)S(1)}, u32[]{:S(2)}, u32[]{:S(2)}) collective-permute-start(bf16[144,128]{1,0:T(8,128)(2,1)S(1)} %get-tuple-element.70.refs_16_), channel_id=1, source_target_pairs={{0,30},{2,0},{4,2},{6,4},{8,6},{10,8},{12,10},{14,12},{16,14},{18,... | collective-permute-start | bytes 110600 | tf_op jit(solution)/shard_map/ppermute | solution.py:392
  90.5 8.7 %collective-permute-start.11 = (bf16[144,128]{1,0:T(8,128)(2,1)S(1)}, bf16[144,128]{1,0:T(8,128)(2,1)S(1)}, u32[]{:S(2)}, u32[]{:S(2)}) collective-permute-start(bf16[144,128]{1,0:T(8,128)(2,1)S(1)} %get-tuple-element.71.refs_17_), channel_id=1, source_target_pairs={{0,2},{2,4},{4,6},{6,8},{8,10},{10,12},{12,14},{14,16},{16,18},{18... | collective-permute-start | bytes 110600 | tf_op jit(solution)/shard_map/ppermute | solution.py:392
  90.5 23.9 %collective-permute-start.24 = (bf16[17,64,128]{2,1,0:T(8,128)(2,1)S(1)}, bf16[17,64,128]{2,1,0:T(8,128)(2,1)S(1)}, u32[]{:S(2)}, u32[]{:S(2)}) collective-permute-start(bf16[17,64,128]{2,1,0:T(8,128)(2,1)S(1)} %get-tuple-element.92), channel_id=1, source_target_pairs={{0,30},{2,0},{4,2},{6,4},{8,6},{10,8},{12,10},{14,12},{16,14},{18,... | collective-permute-start | bytes 835592 | tf_op jit(solution)/shard_map/ppermute | solution.py:392
  104.3 12.2 %collective-permute-start.19 = (bf16[8,64,256]{2,1,0:T(8,128)(2,1)S(1)}, bf16[8,64,256]{2,1,0:T(8,128)(2,1)S(1)}, u32[]{:S(2)}, u32[]{:S(2)}) collective-permute-start(bf16[8,64,256]{2,1,0:T(8,128)(2,1)S(1)} %get-tuple-element.85), channel_id=1, source_target_pairs={{0,1},{1,0},{2,3},{3,2},{4,5},{5,4},{6,7},{7,6},{8,9},{9,8},{10,11... | collective-permute-start | bytes 786440 | tf_op jit(solution)/shard_map/ppermute | solution.py:392
  104.4 4.9 %collective-permute-start.26 = (bf16[21,16,128]{2,1,0:T(8,128)(2,1)S(1)}, bf16[21,16,128]{2,1,0:T(8,128)(2,1)S(1)}, u32[]{:S(2)}, u32[]{:S(2)}) collective-permute-start(bf16[21,16,128]{2,1,0:T(8,128)(2,1)S(1)} %add_convert_fusion.refs_8_.refs_1_), channel_id=1, source_target_pairs={{0,8},{2,10},{4,12},{6,14},{8,0},{10,2},{12,4},{14,6},{16,24},{18,... | collective-permute-start | bytes 258056 | tf_op jit(solution)/shard_map/ppermute | solution.py:397
  104.5 12.5 %collective-permute-start.20 = (bf16[8,64,256]{2,1,0:T(8,128)(2,1)S(1)}, bf16[8,64,256]{2,1,0:T(8,128)(2,1)S(1)}, u32[]{:S(2)}, u32[]{:S(2)}) collective-permute-start(bf16[8,64,256]{2,1,0:T(8,128)(2,1)S(1)} %get-tuple-element.86), channel_id=1, source_target_pairs={{0,1},{1,0},{2,3},{3,2},{4,5},{5,4},{6,7},{7,6},{8,9},{9,8},{10,11... | collective-permute-start | bytes 786440 | tf_op jit(solution)/shard_map/ppermute | solution.py:392
  109.3 4.5 %collective-permute-start.25 = (bf16[21,16,128]{2,1,0:T(8,128)(2,1)S(1)}, bf16[21,16,128]{2,1,0:T(8,128)(2,1)S(1)}, u32[]{:S(2)}, u32[]{:S(2)}) collective-permute-start(bf16[21,16,128]{2,1,0:T(8,128)(2,1)S(1)} %add_convert_fusion.refs_8_.refs_1_), channel_id=1, source_target_pairs={{0,4},{2,6},{4,0},{6,2},{8,12},{10,14},{12,8},{14,10},{16,20},{18,... | collective-permute-start | bytes 258056 | tf_op jit(solution)/shard_map/ppermute | solution.py:397
  113.8 4.7 %collective-permute-start.21 = (bf16[8,64,256]{2,1,0:T(8,128)(2,1)S(1)}, bf16[8,64,256]{2,1,0:T(8,128)(2,1)S(1)}, u32[]{:S(2)}, u32[]{:S(2)}) collective-permute-start(bf16[8,64,256]{2,1,0:T(8,128)(2,1)S(1)} %get-tuple-element.87), channel_id=1, source_target_pairs={{0,1},{1,0},{2,3},{3,2},{4,5},{5,4},{6,7},{7,6},{8,9},{9,8},{10,11... | collective-permute-start | bytes 786440 | tf_op jit(solution)/shard_map/ppermute | solution.py:392
  113.8 4.7 %collective-permute-start.22 = (bf16[8,64,256]{2,1,0:T(8,128)(2,1)S(1)}, bf16[8,64,256]{2,1,0:T(8,128)(2,1)S(1)}, u32[]{:S(2)}, u32[]{:S(2)}) collective-permute-start(bf16[8,64,256]{2,1,0:T(8,128)(2,1)S(1)} %get-tuple-element.88), channel_id=1, source_target_pairs={{0,1},{1,0},{2,3},{3,2},{4,5},{5,4},{6,7},{7,6},{8,9},{9,8},{10,11... | collective-permute-start | bytes 786440 | tf_op jit(solution)/shard_map/ppermute | solution.py:392
  116.5 2.0 %collective-permute-start.28 = (bf16[6,64,256]{2,1,0:T(8,128)(2,1)S(1)}, bf16[6,64,256]{2,1,0:T(8,128)(2,1)S(1)}, u32[]{:S(2)}, u32[]{:S(2)}) collective-permute-start(bf16[6,64,256]{2,1,0:T(8,128)(2,1)S(1)} %get-tuple-element.95), channel_id=1, source_target_pairs={{0,1},{1,0},{2,3},{3,2},{4,5},{5,4},{6,7},{7,6},{8,9},{9,8},{10,11... | collective-permute-start | bytes 589832 | tf_op jit(solution)/shard_map/ppermute | solution.py:392
  116.5 2.0 %collective-permute-start.29 = (bf16[6,64,256]{2,1,0:T(8,128)(2,1)S(1)}, bf16[6,64,256]{2,1,0:T(8,128)(2,1)S(1)}, u32[]{:S(2)}, u32[]{:S(2)}) collective-permute-start(bf16[6,64,256]{2,1,0:T(8,128)(2,1)S(1)} %get-tuple-element.96), channel_id=1, source_target_pairs={{0,1},{1,0},{2,3},{3,2},{4,5},{5,4},{6,7},{7,6},{8,9},{9,8},{10,11... | collective-permute-start | bytes 589832 | tf_op jit(solution)/shard_map/ppermute | solution.py:392
  117.0 1.5 %collective-permute-start.30 = (bf16[5,64,256]{2,1,0:T(8,128)(2,1)S(1)}, bf16[5,64,256]{2,1,0:T(8,128)(2,1)S(1)}, u32[]{:S(2)}, u32[]{:S(2)}) collective-permute-start(bf16[5,64,256]{2,1,0:T(8,128)(2,1)S(1)} %get-tuple-element.97), channel_id=1, source_target_pairs={{0,1},{1,0},{2,3},{3,2},{4,5},{5,4},{6,7},{7,6},{8,9},{9,8},{10,11... | collective-permute-start | bytes 491528 | tf_op jit(solution)/shard_map/ppermute | solution.py:392

commit v5 on v4

--- a/solution.py
+++ b/solution.py
@@ -335,7 +335,8 @@
         start += at
 
 
-def gather_kernel(place, part_0, part_1, part_2, part_3, out):
+def gather_kernel(place, part_0, part_1, part_2, part_3, out, token):
+    token[...] = jnp.zeros_like(token)
     piece = part_0.shape[1]
     spot = place[2]
     for delta, part in enumerate((part_0, part_1, part_2, part_3)):
@@ -412,7 +413,7 @@
     place = jnp.stack([lax.axis_index("chan"), atom_place * atoms_dev, spot])
     place = place.astype(jnp.int32)
     feature_cut = comps // 2
-    cotangent_cut = 2 * comps // 3
+    cotangent_cut = comps - feature_cut + 2
     cuts = ((0, cotangent_cut), (cotangent_cut, comps))
 
     def held(*dims, dtype=F32):
@@ -515,6 +516,9 @@
         scalars=1,
         stay=tuple(range(1, 18)),
     )
+    (token,) = after((token,), halos[0])
+    rims[2:] = after(rims[2:], (sent[0], shifted(token, "chan", 1)))
+    halos.append((shifted(rims[2], "atom", 1), shifted(rims[3], "atom", -1)))
     for delta, part in enumerate(sent, 1):
         kept = kept + exchanged(part, "atom", delta << cut_bits[0]).astype(F32)
     rest = [bit for bit in range(count.bit_length() - 1) if bit not in cut_bits]
@@ -525,16 +529,15 @@
         offsets += [sum(offsets)] * (len(offsets) - 1)
         arrived = [exchanged(rounded, "atom", offset) for offset in offsets]
         kept = functools.reduce(lambda total, part: total + part.astype(F32), arrived, kept)
-    rims[2:] = after(rims[2:], (*arrived, *halos[0]))
-    halos.append((shifted(rims[2], "atom", 1), shifted(rims[3], "atom", -1)))
     rounded = kept.astype(BF16)
     pieces = [rounded] + [exchanged(rounded, "atom", d << cut_bits[0]) for d in range(1, 4)]
-    (grad_weights,) = call(
+    grad_weights, gathered = call(
         gather_kernel,
         (place, *pieces),
-        (plain(3 * (LMAX + 1), chan_local, channels),),
+        (plain(3 * (LMAX + 1), chan_local, channels), plain(8, HALO)),
         scalars=1,
         limit=8,
+        flops=20 * 10**9,
     )
     (terms,) = call(
         functools.partial(key_kernel, heads, slots),
@@ -543,10 +546,9 @@
         scratch=[pltpu.VMEM((comps, 2 * chan_local, atoms_dev), BF16)],
         limit=16,
         stay=(0, 1, 2, 3, 6),
-        tokens=tuple(arrived),
     )
     parts, counts = [], []
-    tokens = tuple(arrived)
+    tokens = ()
     for (start, stop), (cl, cr) in zip(cuts, halos):
         size = stop - start
         part = -(-size // -(-size // (comps // 6)))
@@ -564,7 +566,7 @@
             stay=(0, 5, 6),
             tokens=tokens,
         )
-        tokens = (token, *pieces)
+        tokens = (token, rounded)
         counts.append(len(sizes))
         parts += [mine, *(shifted(some, "chan", 1) for some in theirs)]
     (out,) = call(
@@ -573,6 +575,7 @@
         (plain(comps, chan_local, atoms_dev, dtype=BF16),),
         limit=8,
         stay=tuple(range(len(parts))),
+        tokens=(gathered,),
     )
     grad_features = jnp.transpose(out, (1, 0, 2))
     grad_weights = grad_weights.reshape(3, LMAX + 1, chan_local, channels)

time: 120 us -> 105 us (0.88)
  waiting for transfers between devices: 40.7 us -> 29.5 us
  starting transfers between devices: 45.4 us -> 40.4 us
    ppermute x9, waiting for transfers between devices: 20.3 us -> 8.59 us  [exchanged(): lax.ppermute(value, axis, [(source, source ^ offset) for source in range(...]
    ppermute x22 -> x23, starting transfers between devices: 32.2 us -> 29.4 us  [shifted(): return lax.ppermute(value, axis, pairs)]
    ppermute x9, starting transfers between devices: 13.2 us -> 11 us  [exchanged(): lax.ppermute(value, axis, [(source, source ^ offset) for source in range(...]
    ppermute x22 -> x23, waiting for transfers between devices: 20.4 us -> 20.9 us  [shifted(): return lax.ppermute(value, axis, pairs)]
  transfers between devices with their start and end apart: 31 -> 32, of which waited for: 12 -> 13; matrix products, arithmetic and copies ran while one was open for 0% -> 0% of each run, Pallas kernels for 22% -> 26%
where the time goes in v5:
time: 105 us; the launch traced here: 104 us
  starting transfers between devices  40.4 us (38%)
  waiting for transfers between devices  29.5 us (28%)
  Pallas kernels  28.9 us (28%)
  local copies, waits for them, and re-layouts  4.54 us (4%)
    ppermute x23, starting transfers between devices, shifted(): return lax.ppermute(value, axis, pairs)  29.4 us
    pallas_call x9, Pallas kernels, call(): pl.pallas_call(body, out_shape=tuple(outs), in_specs=[small] * scalars +...  26.4 us
    ppermute x23, waiting for transfers between devices, shifted(): return lax.ppermute(value, axis, pairs)  20.9 us
    ppermute x9, starting transfers between devices, exchanged(): lax.ppermute(value, axis, [(source, source ^ offset) for source in range(...  11 us
    ppermute x9, waiting for transfers between devices, exchanged(): lax.ppermute(value, axis, [(source, source ^ offset) for source in range(...  8.59 us
    unnamed x12, local copies, waits for them, and re-layouts  4.54 us
    pallas_call x1, Pallas kernels, on_device(): pl.pallas_call(functools.partial(split_kernel, feature_cut), out_shape=tu...  2.54 us
  transfers between devices with their start and end apart: 32, of which 13 were waited for; matrix products, arithmetic and copies ran while one was open for 0% of the time, Pallas kernels for 26%

profile of v5, /device:TPU:0, one launch (start us, length us, event | category | flops | bytes accessed | tf_op | source)
XLA Modules:
  0.0 104.3 jit_solution(8227149337426322641)
XLA Ops:
  0.6 0.5 collective-permute-start
  1.1 2.5 %shard_map.85 = (bf16[24,64,128]{2,1,0:T(8,128)(2,1)}, bf16[24,64,128]{2,1,0:T(8,128)(2,1)}, bf16[25,64,128]{2,1,0:T(8,128)(2,1)}, bf16[25,64,128]{2,1,0:T(8,128)(2,1)}) custom-call(bf16[49,64,256]{2,1,0:T(8,128)(2,1)} %bitcast.15), custom_call_target="tpu_custom_call" | custom-call | tf_op jit(solution)/shard_map/pallas_call | solution.py:430
  3.7 2.6 %collective-permute-start.1 = (bf16[24,64,128]{2,1,0:T(8,128)(2,1)}, bf16[24,64,128]{2,1,0:T(8,128)(2,1)S(1)}, u32[]{:S(2)}, u32[]{:S(2)}) collective-permute-start(bf16[24,64,128]{2,1,0:T(8,128)(2,1)} %get-tuple-element.53), channel_id=1, source_target_pairs={{0,2},{2,4},{4,6},{6,8},{8,10},{10,12},{12,14},{14,16},{16,18},{18... | collective-permute-start | bytes 1179656 | tf_op jit(solution)/shard_map/ppermute | solution.py:393
  6.3 4.1 %collective-permute-start.2 = (bf16[24,64,128]{2,1,0:T(8,128)(2,1)}, bf16[24,64,128]{2,1,0:T(8,128)(2,1)S(1)}, u32[]{:S(2)}, u32[]{:S(2)}) collective-permute-start(bf16[24,64,128]{2,1,0:T(8,128)(2,1)} %get-tuple-element.54), channel_id=1, source_target_pairs={{0,30},{2,0},{4,2},{6,4},{8,6},{10,8},{12,10},{14,12},{16,14},{18,... | collective-permute-start | bytes 1179656 | tf_op jit(solution)/shard_map/ppermute | solution.py:393
  10.3 5.6 %collective-permute-start.6 = (bf16[25,64,128]{2,1,0:T(8,128)(2,1)}, bf16[25,64,128]{2,1,0:T(8,128)(2,1)S(1)}, u32[]{:S(2)}, u32[]{:S(2)}) collective-permute-start(bf16[25,64,128]{2,1,0:T(8,128)(2,1)} %get-tuple-element.59), channel_id=1, source_target_pairs={{0,30},{2,0},{4,2},{6,4},{8,6},{10,8},{12,10},{14,12},{16,14},{18,... | collective-permute-start | bytes 1228808 | tf_op jit(solution)/shard_map/ppermute | solution.py:393
  16.0 1.4 %copy-done = bf16[64,49,256]{2,0,1:T(8,128)(2,1)S(1)} copy-done((bf16[64,49,256]{2,0,1:T(8,128)(2,1)S(1)}, bf16[64,49,256]{2,0,1:T(8,128)(2,1)}, u32[]{:S(2)}) %copy-start) | copy-done | bytes 1605656
  17.4 1.4 %copy-done.1 = bf16[64,49,256]{2,0,1:T(8,128)(2,1)S(1)} copy-done((bf16[64,49,256]{2,0,1:T(8,128)(2,1)S(1)}, bf16[64,49,256]{2,0,1:T(8,128)(2,1)}, u32[]{:S(2)}) %copy-start.1) | copy-done | bytes 1605656
  18.9 1.0 copy-done.4
  19.8 0.7 copy-done.5
  20.6 3.8 %shard_map.86 = (bf16[49,192,256]{2,1,0:T(8,128)(2,1)S(1)}, f32[8,256,256]{2,1,0:T(8,128)S(1)}, s32[2,3,128,128]{3,2,1,0:T(8,128)S(1)}, s32[16,256]{1,0:T(8,128)...) custom-call(s32[3]{0:T(128)S(1)} %pad_add_fusion.refs_0_, ...), custom_call_target="tpu_custom_call" | custom-call | flops 12000000000 | bytes 1024 | tf_op jit(solution)/shard_map/pallas_call | solution.py:359
  24.3 8.9 %collective-permute-done.1.refs_0_ = bf16[24,64,128]{2,1,0:T(8,128)(2,1)S(1)} collective-permute-done((bf16[24,64,128]{2,1,0:T(8,128)(2,1)}, bf16[24,64,128]{2,1,0:T(8,128)(2,1)S(1)}, u32[]{:S(2)}, u32[]{:S(2)}) %collective-permute-start.1) | collective-permute-done | bytes 393248 | tf_op jit(solution)/shard_map/ppermute | solution.py:393
  33.2 0.5 collective-permute-start.4
  33.7 1.2 %collective-permute-done.3.refs_1_.refs_4_ = bf16[24,64,128]{2,1,0:T(8,128)(2,1)S(1)} collective-permute-done((bf16[24,64,128]{2,1,0:T(8,128)(2,1)S(1)}, bf16[24,64,128]{2,1,0:T(8,128)(2,1)S(1)}, u32[]{:S(2)}, u32[]{:S(2)}) %collective-permute-start.3) | collective-permute-done | bytes 393248 | tf_op jit(solution)/shard_map/ppermute | solution.py:393
  34.9 0.6 collective-permute-done.4.refs_3_.refs_6_
  35.5 1.3 %shard_map.88 = (bf16[24,192,256]{2,1,0:T(8,128)(2,1)S(1)}, f32[8,2,128,128]{3,2,1,0:T(8,128)S(1)}, f32[8,128]{1,0:T(8,128)S(1)}) custom-call(bf16[24,64,128]{2,1,0:T(8,128)(2,1)S(1)} %get-tuple-element.56.refs_0_.refs_3_, bf16[24,64,128]{2,1,0:T(8,128)(2,1)S(1)} %collective-permute-done.3.refs_1_.refs_4_, ...), custom_call_target="tpu_custom_call" | custom-call | bytes 1024 | tf_op jit(solution)/shard_map/pallas_call | solution.py:359
  36.8 4.8 %collective-permute-done.5.refs_0_ = bf16[25,64,128]{2,1,0:T(8,128)(2,1)S(1)} collective-permute-done((bf16[25,64,128]{2,1,0:T(8,128)(2,1)}, bf16[25,64,128]{2,1,0:T(8,128)(2,1)S(1)}, u32[]{:S(2)}, u32[]{:S(2)}) %collective-permute-start.5) | collective-permute-done | bytes 409632 | tf_op jit(solution)/shard_map/ppermute | solution.py:393
  41.6 1.8 %collective-permute-done.6.refs_1_ = bf16[25,64,128]{2,1,0:T(8,128)(2,1)S(1)} collective-permute-done((bf16[25,64,128]{2,1,0:T(8,128)(2,1)}, bf16[25,64,128]{2,1,0:T(8,128)(2,1)S(1)}, u32[]{:S(2)}, u32[]{:S(2)}) %collective-permute-start.6) | collective-permute-done | bytes 409632 | tf_op jit(solution)/shard_map/ppermute | solution.py:393
  43.4 0.5 collective-permute-start.8
  43.9 1.5 %collective-permute-start.9 = (bf16[27,64,128]{2,1,0:T(8,128)(2,1)S(1)}, bf16[27,64,128]{2,1,0:T(8,128)(2,1)S(1)}, u32[]{:S(2)}, u32[]{:S(2)}) collective-permute-start(bf16[27,64,128]{2,1,0:T(8,128)(2,1)S(1)} %get-tuple-element.77), channel_id=1, source_target_pairs={{0,2},{2,4},{4,6},{6,8},{8,10},{10,12},{12,14},{14,16},{16,18},{18... | collective-permute-start | bytes 1327112 | tf_op jit(solution)/shard_map/ppermute | solution.py:393
  45.4 4.1 %collective-permute-start.10 = (bf16[27,64,128]{2,1,0:T(8,128)(2,1)S(1)}, bf16[27,64,128]{2,1,0:T(8,128)(2,1)S(1)}, u32[]{:S(2)}, u32[]{:S(2)}) collective-permute-start(bf16[27,64,128]{2,1,0:T(8,128)(2,1)S(1)} %get-tuple-element.78), channel_id=1, source_target_pairs={{0,30},{2,0},{4,2},{6,4},{8,6},{10,8},{12,10},{14,12},{16,14},{18,... | collective-permute-start | bytes 1327112 | tf_op jit(solution)/shard_map/ppermute | solution.py:393
  49.6 3.8 %shard_map.90 = (bf16[25,192,256]{2,1,0:T(8,128)(2,1)S(1)}, f32[4,16,256]{2,1,0:T(8,128)}, bf16[144,128]{1,0:T(8,128)(2,1)S(1)}, bf16[144,128]{1,0:T(8,128)(2,1)S(1)}) custom-call(bf16[25,64,128]{2,1,0:T(8,128)(2,1)S(1)} %get-tuple-element.63.refs_0_.refs_7_, bf16[25,64,128]{2,1,0:T(8,128)(2,1)S(1)} %collective-permute-done.7.refs_1_.refs_8_, ...), custom_call_target="tpu_custom_call" | custom-call | bytes 1024 | tf_op jit(solution)/shard_map/pallas_call | solution.py:359
  53.4 6.8 %shard_map.91 = (bf16[49,64,256]{2,1,0:T(8,128)(2,1)S(1)}, f32[49,64,256]{2,1,0:T(8,128)S(1)}, f32[49,64,256]{2,1,0:T(8,128)S(1)}, f32[21,16,128]{2,1,0:T(8,128)...) custom-call(s32[3]{0:T(128)S(1)} %pad_add_fusion.refs_0_, ...), custom_call_target="tpu_custom_call" | custom-call | bytes 1024 | tf_op jit(solution)/shard_map/pallas_call | solution.py:359
  60.3 0.5 collective-permute-start.22
  60.8 2.9 %collective-permute-start.20 = (bf16[21,16,128]{2,1,0:T(8,128)(2,1)S(1)}, bf16[21,16,128]{2,1,0:T(8,128)(2,1)S(1)}, u32[]{:S(2)}, u32[]{:S(2)}) collective-permute-start(bf16[21,16,128]{2,1,0:T(8,128)(2,1)S(1)} %get-tuple-element.89.refs_2_), channel_id=1, source_target_pairs={{0,4},{2,6},{4,0},{6,2},{8,12},{10,14},{12,8},{14,10},{16,20},{18,... | collective-permute-start | bytes 258056 | tf_op jit(solution)/shard_map/ppermute | solution.py:398
  63.7 0.8 collective-permute-done.9.refs_1_
  64.5 2.2 %collective-permute-done.10.refs_2_ = bf16[27,64,128]{2,1,0:T(8,128)(2,1)S(1)} collective-permute-done((bf16[27,64,128]{2,1,0:T(8,128)(2,1)S(1)}, bf16[27,64,128]{2,1,0:T(8,128)(2,1)S(1)}, u32[]{:S(2)}, u32[]{:S(2)}) %collective-permute-start.10) | collective-permute-done | bytes 442400 | tf_op jit(solution)/shard_map/ppermute | solution.py:393
  66.7 2.3 %collective-permute-start.12 = (bf16[144,128]{1,0:T(8,128)(2,1)S(1)}, bf16[144,128]{1,0:T(8,128)(2,1)S(1)}, u32[]{:S(2)}, u32[]{:S(2)}) collective-permute-start(bf16[144,128]{1,0:T(8,128)(2,1)S(1)} %get-tuple-element.72.refs_16_), channel_id=1, source_target_pairs={{0,30},{2,0},{4,2},{6,4},{8,6},{10,8},{12,10},{14,12},{16,14},{18,... | collective-permute-start | bytes 110600 | tf_op jit(solution)/shard_map/ppermute | solution.py:393
  69.0 1.1 %collective-permute-start.11 = (bf16[144,128]{1,0:T(8,128)(2,1)S(1)}, bf16[144,128]{1,0:T(8,128)(2,1)S(1)}, u32[]{:S(2)}, u32[]{:S(2)}) collective-permute-start(bf16[144,128]{1,0:T(8,128)(2,1)S(1)} %get-tuple-element.73.refs_17_), channel_id=1, source_target_pairs={{0,2},{2,4},{4,6},{6,8},{8,10},{10,12},{12,14},{14,16},{16,18},{18... | collective-permute-start | bytes 110600 | tf_op jit(solution)/shard_map/ppermute | solution.py:393
  70.1 1.8 %collective-permute-start.18 = (bf16[22,64,128]{2,1,0:T(8,128)(2,1)S(1)}, bf16[22,64,128]{2,1,0:T(8,128)(2,1)S(1)}, u32[]{:S(2)}, u32[]{:S(2)}) collective-permute-start(bf16[22,64,128]{2,1,0:T(8,128)(2,1)S(1)} %get-tuple-element.90), channel_id=1, source_target_pairs={{0,2},{2,4},{4,6},{6,8},{8,10},{10,12},{12,14},{14,16},{16,18},{18... | collective-permute-start | bytes 1081352 | tf_op jit(solution)/shard_map/ppermute | solution.py:393
  71.9 3.9 %collective-permute-start.19 = (bf16[22,64,128]{2,1,0:T(8,128)(2,1)S(1)}, bf16[22,64,128]{2,1,0:T(8,128)(2,1)S(1)}, u32[]{:S(2)}, u32[]{:S(2)}) collective-permute-start(bf16[22,64,128]{2,1,0:T(8,128)(2,1)S(1)} %get-tuple-element.91), channel_id=1, source_target_pairs={{0,30},{2,0},{4,2},{6,4},{8,6},{10,8},{12,10},{14,12},{16,14},{18,... | collective-permute-start | bytes 1081352 | tf_op jit(solution)/shard_map/ppermute | solution.py:393
  75.9 0.5 collective-permute-start.24
  76.4 0.6 collective-permute-done.11.refs_4_.refs_3_
  77.0 3.2 %collective-permute-start.23 = (bf16[21,16,128]{2,1,0:T(8,128)(2,1)S(1)}, bf16[21,16,128]{2,1,0:T(8,128)(2,1)S(1)}, u32[]{:S(2)}, u32[]{:S(2)}) collective-permute-start(bf16[21,16,128]{2,1,0:T(8,128)(2,1)S(1)} %fusion), channel_id=1, source_target_pairs={{0,2},{2,0},{4,6},{6,4},{8,10},{10,8},{12,14},{14,12},{16,18},{18,... | collective-permute-start | bytes 258056 | tf_op jit(solution)/shard_map/ppermute | solution.py:398
  80.3 2.9 %shard_map.93.refs_6_ = f32[49,128,256]{2,1,0:T(8,128)S(1)} custom-call(bf16[49,64,256]{2,1,0:T(8,128)(2,1)S(1)} %get-tuple-element.80.refs_0_, f32[49,64,256]{2,1,0:T(8,128)S(1)} %get-tuple-element.81.refs_1_, bf16[24,192,256]{2,1,0:T(8,128)(2,1)S(1)} %get-tuple-element.65.refs_12_.refs_2_, bf16[25,192,256]{2,1,0:T(8,128)(2,1)S(1)} %get-tuple-element.70.refs_13_.refs_3_, ...), custom_call_target="tpu_custom_call" | custom-call | bytes 1024 | tf_op jit(solution)/shard_map/pallas_call | solution.py:359
  83.2 2.2 %shard_map.94 = (f32[27,64,256]{2,1,0:T(8,128)S(1)}, f32[8,128]{1,0:T(8,128)S(1)}, bf16[7,64,256]{2,1,0:T(8,128)(2,1)S(1)}, bf16[7,64,256]{2,1,0:T(8,128)(2,1)S(...) custom-call(f32[49,64,256]{2,1,0:T(8,128)S(1)} %get-tuple-element.74.refs_0_, ...), custom_call_target="tpu_custom_call" | custom-call | bytes 1024 | tf_op jit(solution)/shard_map/pallas_call | solution.py:359
  85.4 0.6 collective-permute-done.25
  86.0 5.5 %collective-permute-done.24 = bf16[21,16,128]{2,1,0:T(8,128)(2,1)S(1)} collective-permute-done((bf16[21,16,128]{2,1,0:T(8,128)(2,1)S(1)}, bf16[21,16,128]{2,1,0:T(8,128)(2,1)S(1)}, u32[]{:S(2)}, u32[]{:S(2)}) %collective-permute-start.24) | collective-permute-done | bytes 86048 | tf_op jit(solution)/shard_map/ppermute | solution.py:398
  91.5 1.1 %collective-permute-done.23 = bf16[21,16,128]{2,1,0:T(8,128)(2,1)S(1)} collective-permute-done((bf16[21,16,128]{2,1,0:T(8,128)(2,1)S(1)}, bf16[21,16,128]{2,1,0:T(8,128)(2,1)S(1)}, u32[]{:S(2)}, u32[]{:S(2)}) %collective-permute-start.23) | collective-permute-done | bytes 86048 | tf_op jit(solution)/shard_map/ppermute | solution.py:398
  92.6 0.1 add_convert_fusion.refs_8_.refs_1_
  92.7 2.2 %collective-permute-start.31 = (bf16[21,16,128]{2,1,0:T(8,128)(2,1)S(1)}, bf16[21,16,128]{2,1,0:T(8,128)(2,1)S(1)}, u32[]{:S(2)}, u32[]{:S(2)}) collective-permute-start(bf16[21,16,128]{2,1,0:T(8,128)(2,1)S(1)} %add_convert_fusion.refs_8_.refs_1_), channel_id=1, source_target_pairs={{0,12},{2,14},{4,8},{6,10},{8,4},{10,6},{12,0},{14,2},{16,28},{18,... | collective-permute-start | bytes 258056 | tf_op jit(solution)/shard_map/ppermute | solution.py:398
  94.9 1.4 %collective-permute-start.30 = (bf16[21,16,128]{2,1,0:T(8,128)(2,1)S(1)}, bf16[21,16,128]{2,1,0:T(8,128)(2,1)S(1)}, u32[]{:S(2)}, u32[]{:S(2)}) collective-permute-start(bf16[21,16,128]{2,1,0:T(8,128)(2,1)S(1)} %add_convert_fusion.refs_8_.refs_1_), channel_id=1, source_target_pairs={{0,8},{2,10},{4,12},{6,14},{8,0},{10,2},{12,4},{14,6},{16,24},{18,... | collective-permute-start | bytes 258056 | tf_op jit(solution)/shard_map/ppermute | solution.py:398
  96.3 2.6 %shard_map.97 = (f32[22,64,256]{2,1,0:T(8,128)S(1)}, f32[8,128]{1,0:T(8,128)}, bf16[8,64,256]{2,1,0:T(8,128)(2,1)S(1)}, bf16[8,64,256]{2,1,0:T(8,128)(2,1)S(1)}, bf16[6,64,256]{2,1,0:T(8,128)(2,1)S(1)}) custom-call(f32[49,64,256]{2,1,0:T(8,128)S(1)} %get-tuple-element.74.refs_0_, bf16[22,64,128]{2,1,0:T(8,128)(2,1)S(1)} %collective-permute-done.18.refs_1_, ...), custom_call_target="tpu_custom_call" | custom-call | bytes 1024 | tf_op jit(solution)/shard_map/pallas_call | solution.py:359
  98.9 0.5 collective-permute-start.15
  99.4 0.6 collective-permute-done.30.refs_3_
  100.0 0.8 collective-permute-done.29.refs_2_
  100.8 0.5 collective-permute-start.27
  101.3 1.4 %shard_map.98 = (f32[21,64,128]{2,1,0:T(8,128)}, f32[8,128]{1,0:T(8,128)S(1)}) custom-call(s32[3]{0:T(128)S(1)} %pad_add_fusion.refs_0_, bf16[21,16,128]{2,1,0:T(8,128)(2,1)S(1)} %add_convert_fusion.refs_8_.refs_1_, bf16[21,16,128]{2,1,0:T(8,128)(2,1)S(1)} %collective-permute-done.29.refs_2_, bf16[21,16,128]{2,1,0:T(8,128)(2,1)S(1)} %collective-permute-done.30.refs_3_, ...), custom_call_target="tpu_custom_call" | custom-call | flops 20000000000 | bytes 1024 | tf_op jit(solution)/shard_map/pallas_call | solution.py:359
  102.8 1.6 %shard_map.99 = bf16[49,64,256]{2,1,0:T(8,128)(2,1)} custom-call(f32[27,64,256]{2,1,0:T(8,128)S(1)} %get-tuple-element.82.refs_0_, bf16[7,64,256]{2,1,0:T(8,128)(2,1)S(1)} %collective-permute-done.13.refs_1_, bf16[7,64,256]{2,1,0:T(8,128)(2,1)S(1)} %collective-permute-done.14.refs_2_, bf16[7,64,256]{2,1,0:T(8,128)(2,1)S(1)} %collective-permute-done.15.refs_3_, ...), custom_call_target="tpu_custom_call" | custom-call | bytes 1024 | tf_op jit(solution)/shard_map/pallas_call | solution.py:359
  (46 shorter events, 0.4 us)
Async XLA Ops:
  0.6 15.4 %collective-permute-start = (bf16[49,64,256]{2,1,0:T(8,128)(2,1)}, bf16[49,64,256]{2,1,0:T(8,128)(2,1)S(1)}, u32[]{:S(2)}, u32[]{:S(2)}) collective-permute-start(bf16[49,64,256]{2,1,0:T(8,128)(2,1)} %bitcast.14), channel_id=1, source_target_pairs={{0,1},{1,0},{2,3},{3,2},{4,5},{5,4},{6,7},{7,6},{8,9},{9,8},{10,11... | collective-permute-start | bytes 4816904 | tf_op jit(solution)/shard_map/ppermute | solution.py:393
  3.7 29.5 %collective-permute-start.1 = (bf16[24,64,128]{2,1,0:T(8,128)(2,1)}, bf16[24,64,128]{2,1,0:T(8,128)(2,1)S(1)}, u32[]{:S(2)}, u32[]{:S(2)}) collective-permute-start(bf16[24,64,128]{2,1,0:T(8,128)(2,1)} %get-tuple-element.53), channel_id=1, source_target_pairs={{0,2},{2,4},{4,6},{6,8},{8,10},{10,12},{12,14},{14,16},{16,18},{18... | collective-permute-start | bytes 1179656 | tf_op jit(solution)/shard_map/ppermute | solution.py:393
  6.3 27.0 %collective-permute-start.2 = (bf16[24,64,128]{2,1,0:T(8,128)(2,1)}, bf16[24,64,128]{2,1,0:T(8,128)(2,1)S(1)}, u32[]{:S(2)}, u32[]{:S(2)}) collective-permute-start(bf16[24,64,128]{2,1,0:T(8,128)(2,1)} %get-tuple-element.54), channel_id=1, source_target_pairs={{0,30},{2,0},{4,2},{6,4},{8,6},{10,8},{12,10},{14,12},{16,14},{18,... | collective-permute-start | bytes 1179656 | tf_op jit(solution)/shard_map/ppermute | solution.py:393
  10.3 31.3 %collective-permute-start.5 = (bf16[25,64,128]{2,1,0:T(8,128)(2,1)}, bf16[25,64,128]{2,1,0:T(8,128)(2,1)S(1)}, u32[]{:S(2)}, u32[]{:S(2)}) collective-permute-start(bf16[25,64,128]{2,1,0:T(8,128)(2,1)} %get-tuple-element.58), channel_id=1, source_target_pairs={{0,2},{2,4},{4,6},{6,8},{8,10},{10,12},{12,14},{14,16},{16,18},{18... | collective-permute-start | bytes 1228808 | tf_op jit(solution)/shard_map/ppermute | solution.py:393
  10.3 33.1 %collective-permute-start.6 = (bf16[25,64,128]{2,1,0:T(8,128)(2,1)}, bf16[25,64,128]{2,1,0:T(8,128)(2,1)S(1)}, u32[]{:S(2)}, u32[]{:S(2)}) collective-permute-start(bf16[25,64,128]{2,1,0:T(8,128)(2,1)} %get-tuple-element.59), channel_id=1, source_target_pairs={{0,30},{2,0},{4,2},{6,4},{8,6},{10,8},{12,10},{14,12},{16,14},{18,... | collective-permute-start | bytes 1228808 | tf_op jit(solution)/shard_map/ppermute | solution.py:393
  16.0 1.4 %copy-start = (bf16[64,49,256]{2,0,1:T(8,128)(2,1)S(1)}, bf16[64,49,256]{2,0,1:T(8,128)(2,1)}, u32[]{:S(2)}) copy-start(bf16[64,49,256]{2,0,1:T(8,128)(2,1)} %param.8) | copy-start | bytes 4816900
  17.4 1.4 %copy-start.1 = (bf16[64,49,256]{2,0,1:T(8,128)(2,1)S(1)}, bf16[64,49,256]{2,0,1:T(8,128)(2,1)}, u32[]{:S(2)}) copy-start(bf16[64,49,256]{2,0,1:T(8,128)(2,1)} %param.6) | copy-start | bytes 4816900
  18.9 1.0 copy-start.4
  19.8 0.7 copy-start.5
  33.2 1.7 %collective-permute-start.3 = (bf16[24,64,128]{2,1,0:T(8,128)(2,1)S(1)}, bf16[24,64,128]{2,1,0:T(8,128)(2,1)S(1)}, u32[]{:S(2)}, u32[]{:S(2)}) collective-permute-start(bf16[24,64,128]{2,1,0:T(8,128)(2,1)S(1)} %get-tuple-element.56.refs_0_.refs_3_), channel_id=1, source_target_pairs={{0,1},{1,0},{2,3},{3,2},{4,5},{5,4},{6,7},{7,6},{8,9},{9,8},{10,11... | collective-permute-start | bytes 1179656 | tf_op jit(solution)/shard_map/ppermute | solution.py:393
  33.2 2.3 %collective-permute-start.4 = (bf16[24,64,128]{2,1,0:T(8,128)(2,1)S(1)}, bf16[24,64,128]{2,1,0:T(8,128)(2,1)S(1)}, u32[]{:S(2)}, u32[]{:S(2)}) collective-permute-start(bf16[24,64,128]{2,1,0:T(8,128)(2,1)S(1)} %get-tuple-element.57.refs_2_.refs_5_), channel_id=1, source_target_pairs={{0,1},{1,0},{2,3},{3,2},{4,5},{5,4},{6,7},{7,6},{8,9},{9,8},{10,11... | collective-permute-start | bytes 1179656 | tf_op jit(solution)/shard_map/ppermute | solution.py:393
  35.5 14.1 %copy-start.2 = (f32[4,16,256]{2,1,0:T(8,128)S(1)}, f32[4,16,256]{2,1,0:T(8,128)}, u32[]{:S(2)}) copy-start(f32[4,16,256]{2,1,0:T(8,128)} %refs_9_.1) | copy-start | bytes 196612
  35.5 14.1 %copy-start.3 = (s32[16,256]{1,0:T(8,128)S(1)}, s32[16,256]{1,0:T(8,128)}, u32[]{:S(2)}) copy-start(s32[16,256]{1,0:T(8,128)} %refs_10_.1) | copy-start | bytes 49156
  43.4 6.1 %collective-permute-start.7 = (bf16[25,64,128]{2,1,0:T(8,128)(2,1)S(1)}, bf16[25,64,128]{2,1,0:T(8,128)(2,1)S(1)}, u32[]{:S(2)}, u32[]{:S(2)}) collective-permute-start(bf16[25,64,128]{2,1,0:T(8,128)(2,1)S(1)} %get-tuple-element.63.refs_0_.refs_7_), channel_id=1, source_target_pairs={{0,1},{1,0},{2,3},{3,2},{4,5},{5,4},{6,7},{7,6},{8,9},{9,8},{10,11... | collective-permute-start | bytes 1228808 | tf_op jit(solution)/shard_map/ppermute | solution.py:393
  43.4 6.1 %collective-permute-start.8 = (bf16[25,64,128]{2,1,0:T(8,128)(2,1)S(1)}, bf16[25,64,128]{2,1,0:T(8,128)(2,1)S(1)}, u32[]{:S(2)}, u32[]{:S(2)}) collective-permute-start(bf16[25,64,128]{2,1,0:T(8,128)(2,1)S(1)} %get-tuple-element.64.refs_2_.refs_9_), channel_id=1, source_target_pairs={{0,1},{1,0},{2,3},{3,2},{4,5},{5,4},{6,7},{7,6},{8,9},{9,8},{10,11... | collective-permute-start | bytes 1228808 | tf_op jit(solution)/shard_map/ppermute | solution.py:393
  43.9 20.6 %collective-permute-start.9 = (bf16[27,64,128]{2,1,0:T(8,128)(2,1)S(1)}, bf16[27,64,128]{2,1,0:T(8,128)(2,1)S(1)}, u32[]{:S(2)}, u32[]{:S(2)}) collective-permute-start(bf16[27,64,128]{2,1,0:T(8,128)(2,1)S(1)} %get-tuple-element.77), channel_id=1, source_target_pairs={{0,2},{2,4},{4,6},{6,8},{8,10},{10,12},{12,14},{14,16},{16,18},{18... | collective-permute-start | bytes 1327112 | tf_op jit(solution)/shard_map/ppermute | solution.py:393
  45.4 21.3 %collective-permute-start.10 = (bf16[27,64,128]{2,1,0:T(8,128)(2,1)S(1)}, bf16[27,64,128]{2,1,0:T(8,128)(2,1)S(1)}, u32[]{:S(2)}, u32[]{:S(2)}) collective-permute-start(bf16[27,64,128]{2,1,0:T(8,128)(2,1)S(1)} %get-tuple-element.78), channel_id=1, source_target_pairs={{0,30},{2,0},{4,2},{6,4},{8,6},{10,8},{12,10},{14,12},{16,14},{18,... | collective-permute-start | bytes 1327112 | tf_op jit(solution)/shard_map/ppermute | solution.py:393
  60.2 9.9 %collective-permute-start.21 = (bf16[21,16,128]{2,1,0:T(8,128)(2,1)S(1)}, bf16[21,16,128]{2,1,0:T(8,128)(2,1)S(1)}, u32[]{:S(2)}, u32[]{:S(2)}) collective-permute-start(bf16[21,16,128]{2,1,0:T(8,128)(2,1)S(1)} %get-tuple-element.94), channel_id=1, source_target_pairs={{0,8},{2,10},{4,12},{6,14},{8,0},{10,2},{12,4},{14,6},{16,24},{18,... | collective-permute-start | bytes 258056 | tf_op jit(solution)/shard_map/ppermute | solution.py:398
  60.3 11.6 %collective-permute-start.22 = (bf16[21,16,128]{2,1,0:T(8,128)(2,1)S(1)}, bf16[21,16,128]{2,1,0:T(8,128)(2,1)S(1)}, u32[]{:S(2)}, u32[]{:S(2)}) collective-permute-start(bf16[21,16,128]{2,1,0:T(8,128)(2,1)S(1)} %get-tuple-element.95), channel_id=1, source_target_pairs={{0,12},{2,14},{4,8},{6,10},{8,4},{10,6},{12,0},{14,2},{16,28},{18,... | collective-permute-start | bytes 258056 | tf_op jit(solution)/shard_map/ppermute | solution.py:398
  60.8 14.9 %collective-permute-start.20 = (bf16[21,16,128]{2,1,0:T(8,128)(2,1)S(1)}, bf16[21,16,128]{2,1,0:T(8,128)(2,1)S(1)}, u32[]{:S(2)}, u32[]{:S(2)}) collective-permute-start(bf16[21,16,128]{2,1,0:T(8,128)(2,1)S(1)} %get-tuple-element.89.refs_2_), channel_id=1, source_target_pairs={{0,4},{2,6},{4,0},{6,2},{8,12},{10,14},{12,8},{14,10},{16,20},{18,... | collective-permute-start | bytes 258056 | tf_op jit(solution)/shard_map/ppermute | solution.py:398
  66.7 2.3 %collective-permute-start.17 = (f32[8,128]{1,0:T(8,128)S(1)}, f32[8,128]{1,0:T(8,128)S(1)}, u32[]{:S(2)}, u32[]{:S(2)}) collective-permute-start(f32[8,128]{1,0:T(8,128)S(1)} %shard_map.95), channel_id=1, source_target_pairs={{0,1},{1,0},{2,3},{3,2},{4,5},{5,4},{6,7},{7,6},{8,9},{9,8},{10,11... | collective-permute-start | bytes 12296 | tf_op jit(solution)/shard_map/ppermute | solution.py:393
  66.7 9.2 %collective-permute-start.12 = (bf16[144,128]{1,0:T(8,128)(2,1)S(1)}, bf16[144,128]{1,0:T(8,128)(2,1)S(1)}, u32[]{:S(2)}, u32[]{:S(2)}) collective-permute-start(bf16[144,128]{1,0:T(8,128)(2,1)S(1)} %get-tuple-element.72.refs_16_), channel_id=1, source_target_pairs={{0,30},{2,0},{4,2},{6,4},{8,6},{10,8},{12,10},{14,12},{16,14},{18,... | collective-permute-start | bytes 110600 | tf_op jit(solution)/shard_map/ppermute | solution.py:393
  69.0 8.0 %collective-permute-start.11 = (bf16[144,128]{1,0:T(8,128)(2,1)S(1)}, bf16[144,128]{1,0:T(8,128)(2,1)S(1)}, u32[]{:S(2)}, u32[]{:S(2)}) collective-permute-start(bf16[144,128]{1,0:T(8,128)(2,1)S(1)} %get-tuple-element.73.refs_17_), channel_id=1, source_target_pairs={{0,2},{2,4},{4,6},{6,8},{8,10},{10,12},{12,14},{14,16},{16,18},{18... | collective-permute-start | bytes 110600 | tf_op jit(solution)/shard_map/ppermute | solution.py:393
  70.1 24.8 %collective-permute-start.18 = (bf16[22,64,128]{2,1,0:T(8,128)(2,1)S(1)}, bf16[22,64,128]{2,1,0:T(8,128)(2,1)S(1)}, u32[]{:S(2)}, u32[]{:S(2)}) collective-permute-start(bf16[22,64,128]{2,1,0:T(8,128)(2,1)S(1)} %get-tuple-element.90), channel_id=1, source_target_pairs={{0,2},{2,4},{4,6},{6,8},{8,10},{10,12},{12,14},{14,16},{16,18},{18... | collective-permute-start | bytes 1081352 | tf_op jit(solution)/shard_map/ppermute | solution.py:393
  71.9 24.4 %collective-permute-start.19 = (bf16[22,64,128]{2,1,0:T(8,128)(2,1)S(1)}, bf16[22,64,128]{2,1,0:T(8,128)(2,1)S(1)}, u32[]{:S(2)}, u32[]{:S(2)}) collective-permute-start(bf16[22,64,128]{2,1,0:T(8,128)(2,1)S(1)} %get-tuple-element.91), channel_id=1, source_target_pairs={{0,30},{2,0},{4,2},{6,4},{8,6},{10,8},{12,10},{14,12},{16,14},{18,... | collective-permute-start | bytes 1081352 | tf_op jit(solution)/shard_map/ppermute | solution.py:393
  75.8 10.2 %collective-permute-start.25 = (bf16[21,16,128]{2,1,0:T(8,128)(2,1)S(1)}, bf16[21,16,128]{2,1,0:T(8,128)(2,1)S(1)}, u32[]{:S(2)}, u32[]{:S(2)}) collective-permute-start(bf16[21,16,128]{2,1,0:T(8,128)(2,1)S(1)} %fusion), channel_id=1, source_target_pairs={{0,18},{2,16},{4,22},{6,20},{8,26},{10,24},{12,30},{14,28},{16,2},... | collective-permute-start | bytes 258056 | tf_op jit(solution)/shard_map/ppermute | solution.py:398
  75.9 15.6 %collective-permute-start.24 = (bf16[21,16,128]{2,1,0:T(8,128)(2,1)S(1)}, bf16[21,16,128]{2,1,0:T(8,128)(2,1)S(1)}, u32[]{:S(2)}, u32[]{:S(2)}) collective-permute-start(bf16[21,16,128]{2,1,0:T(8,128)(2,1)S(1)} %fusion), channel_id=1, source_target_pairs={{0,16},{2,18},{4,20},{6,22},{8,24},{10,26},{12,28},{14,30},{16,0},... | collective-permute-start | bytes 258056 | tf_op jit(solution)/shard_map/ppermute | solution.py:398
  77.0 15.5 %collective-permute-start.23 = (bf16[21,16,128]{2,1,0:T(8,128)(2,1)S(1)}, bf16[21,16,128]{2,1,0:T(8,128)(2,1)S(1)}, u32[]{:S(2)}, u32[]{:S(2)}) collective-permute-start(bf16[21,16,128]{2,1,0:T(8,128)(2,1)S(1)} %fusion), channel_id=1, source_target_pairs={{0,2},{2,0},{4,6},{6,4},{8,10},{10,8},{12,14},{14,12},{16,18},{18,... | collective-permute-start | bytes 258056 | tf_op jit(solution)/shard_map/ppermute | solution.py:398
  86.0 12.9 %collective-permute-start.16 = (bf16[6,64,256]{2,1,0:T(8,128)(2,1)S(1)}, bf16[6,64,256]{2,1,0:T(8,128)(2,1)S(1)}, u32[]{:S(2)}, u32[]{:S(2)}) collective-permute-start(bf16[6,64,256]{2,1,0:T(8,128)(2,1)S(1)} %get-tuple-element.86), channel_id=1, source_target_pairs={{0,1},{1,0},{2,3},{3,2},{4,5},{5,4},{6,7},{7,6},{8,9},{9,8},{10,11... | collective-permute-start | bytes 589832 | tf_op jit(solution)/shard_map/ppermute | solution.py:393
  91.5 9.3 %collective-permute-start.13 = (bf16[7,64,256]{2,1,0:T(8,128)(2,1)S(1)}, bf16[7,64,256]{2,1,0:T(8,128)(2,1)S(1)}, u32[]{:S(2)}, u32[]{:S(2)}) collective-permute-start(bf16[7,64,256]{2,1,0:T(8,128)(2,1)S(1)} %get-tuple-element.83), channel_id=1, source_target_pairs={{0,1},{1,0},{2,3},{3,2},{4,5},{5,4},{6,7},{7,6},{8,9},{9,8},{10,11... | collective-permute-start | bytes 688136 | tf_op jit(solution)/shard_map/ppermute | solution.py:393
  92.7 6.2 %collective-permute-start.31 = (bf16[21,16,128]{2,1,0:T(8,128)(2,1)S(1)}, bf16[21,16,128]{2,1,0:T(8,128)(2,1)S(1)}, u32[]{:S(2)}, u32[]{:S(2)}) collective-permute-start(bf16[21,16,128]{2,1,0:T(8,128)(2,1)S(1)} %add_convert_fusion.refs_8_.refs_1_), channel_id=1, source_target_pairs={{0,12},{2,14},{4,8},{6,10},{8,4},{10,6},{12,0},{14,2},{16,28},{18,... | collective-permute-start | bytes 258056 | tf_op jit(solution)/shard_map/ppermute | solution.py:398
  94.9 5.1 %collective-permute-start.30 = (bf16[21,16,128]{2,1,0:T(8,128)(2,1)S(1)}, bf16[21,16,128]{2,1,0:T(8,128)(2,1)S(1)}, u32[]{:S(2)}, u32[]{:S(2)}) collective-permute-start(bf16[21,16,128]{2,1,0:T(8,128)(2,1)S(1)} %add_convert_fusion.refs_8_.refs_1_), channel_id=1, source_target_pairs={{0,8},{2,10},{4,12},{6,14},{8,0},{10,2},{12,4},{14,6},{16,24},{18,... | collective-permute-start | bytes 258056 | tf_op jit(solution)/shard_map/ppermute | solution.py:398
  96.3 4.5 %collective-permute-start.29 = (bf16[21,16,128]{2,1,0:T(8,128)(2,1)S(1)}, bf16[21,16,128]{2,1,0:T(8,128)(2,1)S(1)}, u32[]{:S(2)}, u32[]{:S(2)}) collective-permute-start(bf16[21,16,128]{2,1,0:T(8,128)(2,1)S(1)} %add_convert_fusion.refs_8_.refs_1_), channel_id=1, source_target_pairs={{0,4},{2,6},{4,0},{6,2},{8,12},{10,14},{12,8},{14,10},{16,20},{18,... | collective-permute-start | bytes 258056 | tf_op jit(solution)/shard_map/ppermute | solution.py:398
  98.9 3.9 %collective-permute-start.14 = (bf16[7,64,256]{2,1,0:T(8,128)(2,1)S(1)}, bf16[7,64,256]{2,1,0:T(8,128)(2,1)S(1)}, u32[]{:S(2)}, u32[]{:S(2)}) collective-permute-start(bf16[7,64,256]{2,1,0:T(8,128)(2,1)S(1)} %get-tuple-element.84), channel_id=1, source_target_pairs={{0,1},{1,0},{2,3},{3,2},{4,5},{5,4},{6,7},{7,6},{8,9},{9,8},{10,11... | collective-permute-start | bytes 688136 | tf_op jit(solution)/shard_map/ppermute | solution.py:393
  98.9 3.9 %collective-permute-start.15 = (bf16[7,64,256]{2,1,0:T(8,128)(2,1)S(1)}, bf16[7,64,256]{2,1,0:T(8,128)(2,1)S(1)}, u32[]{:S(2)}, u32[]{:S(2)}) collective-permute-start(bf16[7,64,256]{2,1,0:T(8,128)(2,1)S(1)} %get-tuple-element.85), channel_id=1, source_target_pairs={{0,1},{1,0},{2,3},{3,2},{4,5},{5,4},{6,7},{7,6},{8,9},{9,8},{10,11... | collective-permute-start | bytes 688136 | tf_op jit(solution)/shard_map/ppermute | solution.py:393
  100.0 2.7 %collective-permute-start.28 = (bf16[6,64,256]{2,1,0:T(8,128)(2,1)S(1)}, bf16[6,64,256]{2,1,0:T(8,128)(2,1)S(1)}, u32[]{:S(2)}, u32[]{:S(2)}) collective-permute-start(bf16[6,64,256]{2,1,0:T(8,128)(2,1)S(1)} %get-tuple-element.99), channel_id=1, source_target_pairs={{0,1},{1,0},{2,3},{3,2},{4,5},{5,4},{6,7},{7,6},{8,9},{9,8},{10,11... | collective-permute-start | bytes 589832 | tf_op jit(solution)/shard_map/ppermute | solution.py:393
  100.8 2.0 %collective-permute-start.26 = (bf16[8,64,256]{2,1,0:T(8,128)(2,1)S(1)}, bf16[8,64,256]{2,1,0:T(8,128)(2,1)S(1)}, u32[]{:S(2)}, u32[]{:S(2)}) collective-permute-start(bf16[8,64,256]{2,1,0:T(8,128)(2,1)S(1)} %get-tuple-element.97), channel_id=1, source_target_pairs={{0,1},{1,0},{2,3},{3,2},{4,5},{5,4},{6,7},{7,6},{8,9},{9,8},{10,11... | collective-permute-start | bytes 786440 | tf_op jit(solution)/shard_map/ppermute | solution.py:393
  100.8 2.0 %collective-permute-start.27 = (bf16[8,64,256]{2,1,0:T(8,128)(2,1)S(1)}, bf16[8,64,256]{2,1,0:T(8,128)(2,1)S(1)}, u32[]{:S(2)}, u32[]{:S(2)}) collective-permute-start(bf16[8,64,256]{2,1,0:T(8,128)(2,1)S(1)} %get-tuple-element.98), channel_id=1, source_target_pairs={{0,1},{1,0},{2,3},{3,2},{4,5},{5,4},{6,7},{7,6},{8,9},{9,8},{10,11... | collective-permute-start | bytes 786440 | tf_op jit(solution)/shard_map/ppermute | solution.py:393

commit v6 on v5

--- a/solution.py
+++ b/solution.py
@@ -1,5 +1,6 @@
 import functools
 import math
+import operator
 
 import jax
 import jax.numpy as jnp
@@ -58,31 +59,28 @@
     return jnp.concatenate([rows] * (HALO // rows.shape[0]), axis=0).T
 
 
-def split_kernel(cut, fm, high_a, low_a, high_b, low_b, sems):
-    ranges = (
-        (high_a, 0, cut, HALO),
-        (low_a, 0, cut, 0),
-        (high_b, cut, fm.shape[0] - cut, HALO),
-        (low_b, cut, fm.shape[0] - cut, 0),
-    )
-    copies = [
-        pltpu.make_async_copy(
-            fm.at[pl.ds(start, size), :, pl.ds(atom, HALO)], part, sems.at[at]
+def split_kernel(cuts, fm, *refs):
+    *parts, sems = refs
+    copies = []
+    for at, part in enumerate(parts):
+        start, stop = cuts[at // 2]
+        atom = HALO if at % 2 == 0 else 0
+        copies.append(
+            pltpu.make_async_copy(
+                fm.at[pl.ds(start, stop - start), :, pl.ds(atom, HALO)], part, sems.at[at]
+            )
         )
-        for at, (part, start, size, atom) in enumerate(ranges)
-    ]
     for copy in copies:
         copy.start()
     for copy in copies:
         copy.wait()
 
 
-def own_kernel(heads, total_atoms, cuts, place, fm, fo, cot, weights, neighbours,
+def own_kernel(heads, total_atoms, place, fm, fo, cot, weights, neighbours,
                qkv, scores, slot_own, index_rows, index_wide, wp, wc, token, *rims):
     token[...] = jnp.zeros_like(token)
-    for at, (start, stop) in enumerate(cuts):
-        rims[2 * at][...] = cot[start:stop, :, HALO:]
-        rims[2 * at + 1][...] = cot[start:stop, :, :HALO]
+    rims[0][...] = cot[:, :, HALO:]
+    rims[1][...] = cot[:, :, :HALO]
     comps, chan_local = fm.shape[0], fm.shape[1]
     channels = weights.shape[3]
     rows = chan_local // heads
@@ -115,16 +113,19 @@
             slot_own[half, tile] = slot_tile(wide[:, :slots], tile)
 
 
-def project_halo(start, flm, flo, frm, fro, wp, halo_qkv):
-    for comp in range(flm.shape[0]):
-        feats = jnp.concatenate(
-            [
-                jnp.concatenate([flm[comp], frm[comp]], axis=1),
-                jnp.concatenate([flo[comp], fro[comp]], axis=1),
-            ],
-            axis=0,
-        )
-        halo_qkv[comp] = nn(wp[degree_of(start + comp)], feats).astype(BF16)
+def project_halo(start, chunks, wp, halo_qkv):
+    at = 0
+    for flm, flo, frm, fro in chunks:
+        for comp in range(flm.shape[0]):
+            feats = jnp.concatenate(
+                [
+                    jnp.concatenate([flm[comp], frm[comp]], axis=1),
+                    jnp.concatenate([flo[comp], fro[comp]], axis=1),
+                ],
+                axis=0,
+            )
+            halo_qkv[at] = nn(wp[degree_of(start + at)], feats).astype(BF16)
+            at += 1
 
 
 def halo_scores(heads, quantity, start, qkv, cot, halo_qkv):
@@ -141,17 +142,19 @@
 
 def early_kernel(heads, flm, flo, frm, fro, wp, qkv, cot, halo_qkv, partial, token):
     token[...] = jnp.zeros_like(token)
-    project_halo(0, flm, flo, frm, fro, wp, halo_qkv)
+    project_halo(0, [(flm, flo, frm, fro)], wp, halo_qkv)
     for quantity in range(2 * heads):
         left, right = halo_scores(heads, quantity, 0, qkv, cot, halo_qkv)
         partial[quantity, 0] = left
         partial[quantity, 1] = right
 
 
-def edge_kernel(heads, score_scale, start, flm, flo, frm, fro, wp, qkv, cot, scores, partial, bias,
-                valid, index_rows, index_wide, halo_qkv, grad_bias, message_a, message_b):
+def edge_kernel(heads, score_scale, start, late, *refs):
+    chunks = [refs[at : at + 4] for at in range(0, 4 * late, 4)]
+    (wp, qkv, cot, scores, partial, bias, valid, index_rows, index_wide,
+     halo_qkv, grad_bias, message_a, message_b) = refs[4 * late :]
     slots = valid.shape[0]
-    project_halo(start, flm, flo, frm, fro, wp, halo_qkv)
+    project_halo(start, chunks, wp, halo_qkv)
     lane = lax.broadcasted_iota(jnp.int32, (HALO, 2 * heads * slots), 1)
     gathered = [jnp.zeros((HALO, 2 * heads * slots), F32) for _ in range(2)]
     for quantity in range(2 * heads):
@@ -200,15 +203,15 @@
     )
 
 
-def grads_kernel(heads, slots, place, fm, fo, flm_a, flo_a, frm_a, fro_a, flm_b, flo_b, frm_b,
-                 fro_b, qkv, halo_a, halo_b, cot, slot_own, message_a, message_b, grad_query, own_key, own_value, kept, sent_1, sent_2,
-                 sent_3, ext, weight_terms):
+def grads_kernel(heads, slots, pieces, place, fm, fo, *refs):
+    chunks = [refs[at : at + 4] for at in range(0, 4 * pieces, 4)]
+    (qkv, halo_a, halo_b, cot, slot_own, message_a, message_b, grad_query, own_key, own_value, kept,
+     sent_1, sent_2, sent_3, ext, weight_terms) = refs[4 * pieces :]
+    places = [(chunk, at) for chunk in chunks for at in range(chunk[0].shape[0])]
     comps, chan_local = fm.shape[0], fm.shape[1]
     rows = chan_local // heads
     atoms = 2 * HALO
     core = place[0]
-    cut = flm_a.shape[0]
-    early, late = (flm_a, flo_a, frm_a, fro_a), (flm_b, flo_b, frm_b, fro_b)
     empty = jnp.zeros((HALO, HALO), BF16)
     coefs = [message[: 2 * heads * slots, :].astype(F32).T for message in (message_a, message_b)]
     for head in range(heads):
@@ -239,8 +242,7 @@
         keyval_total = jnp.zeros((2 * chan_local, 2 * chan_local), F32)
         for comp in range(degree * degree, (degree + 1) * (degree + 1)):
             own = jnp.concatenate([fm[comp], fo[comp]], axis=0)
-            at = comp if comp < cut else comp - cut
-            flm, flo, frm, fro = early if comp < cut else late
+            (flm, flo, frm, fro), at = places[comp]
             wide = jnp.concatenate(
                 [
                     jnp.concatenate([flm[at], fm[comp], frm[at]], axis=1),
@@ -272,7 +274,8 @@
 
 
 def key_kernel(heads, slots, grad_query, own_key, halo_a, halo_b, message_left, message_right, wc,
-               terms, grad):
+               terms, token, grad):
+    token[...] = jnp.zeros_like(token)
     comps, chan_local = grad_query.shape[0], grad_query.shape[1]
     rows = chan_local // heads
     grad[:, :chan_local, :] = grad_query[...]
@@ -293,25 +296,25 @@
         terms[comp] = nn(wc[degree_of(comp)][:, : 2 * chan_local], grad[comp])
 
 
-def value_kernel(heads, slots, start, own_value, cl, cr, message_left, message_right, wc, terms,
+def value_kernel(heads, slots, start, stop, own_value, cl, cr, message_left, message_right, wc, terms,
                  mine, token, *theirs):
     *theirs, grad = theirs
     token[...] = jnp.zeros_like(token)
-    comps, chan_local = cl.shape[0], cl.shape[1]
+    comps, chan_local = stop - start, cl.shape[1]
     rows = chan_local // heads
     coefs, tables = halo_slots(message_left, message_right, 2 * heads, slots)
     for head in range(heads):
         span = slice(head * rows, (head + 1) * rows)
         rim = jnp.concatenate(
             [
-                nn(head_rows_of(cl, head * rows, rows),
+                nn(cl[start:stop, span, :].reshape(comps * rows, HALO),
                    spread(tables[0], coefs[0], heads + head, slots)),
-                nn(head_rows_of(cr, head * rows, rows),
+                nn(cr[start:stop, span, :].reshape(comps * rows, HALO),
                    spread(tables[1], coefs[1], heads + head, slots)),
             ],
             axis=1,
         )
-        own = own_value[start : start + comps, span, :].reshape(comps * rows, 2 * HALO)
+        own = own_value[start:stop, span, :].reshape(comps * rows, 2 * HALO)
         grad[:, span, :] = (own + rim).astype(BF16).reshape(comps, rows, 2 * HALO)
     for comp in range(comps):
         mix = wc[degree_of(start + comp)][:, 2 * chan_local :]
@@ -396,6 +399,12 @@
 def exchanged(value, axis, offset):
     count = lax.axis_size(axis)
     return lax.ppermute(value, axis, [(source, source ^ offset) for source in range(count)])
+
+
+def crossed(value, target):
+    count = lax.axis_size("atom")
+    pairs = [(2 * at + core, 2 * target(at) + 1 - core) for at in range(count) for core in range(2)]
+    return shifted(lax.ppermute(value, ("atom", "chan"), pairs), "chan", 1)
 
 
 def on_device(features, weights, cotangent, edge_bias, neighbours, valid_mask):
@@ -413,8 +422,9 @@
     place = jnp.stack([lax.axis_index("chan"), atom_place * atoms_dev, spot])
     place = place.astype(jnp.int32)
     feature_cut = comps // 2
-    cotangent_cut = comps - feature_cut + 2
-    cuts = ((0, cotangent_cut), (cotangent_cut, comps))
+    value_cut = comps // 2
+    feature_cuts = ((0, feature_cut), (feature_cut, comps))
+    cuts = ((0, value_cut), (value_cut, comps))
 
     def held(*dims, dtype=F32):
         return pltpu.VMEM(dims, dtype)
@@ -426,23 +436,26 @@
     cot = jnp.transpose(cotangent, (1, 0, 2))
     mix = jnp.transpose(weights, (0, 1, 3, 2))
     anywhere = pl.BlockSpec(memory_space=pl.ANY)
-    sizes = (feature_cut, feature_cut, comps - feature_cut, comps - feature_cut)
-    high_a, low_a, high_b, low_b = pl.pallas_call(
-        functools.partial(split_kernel, feature_cut),
-        out_shape=tuple(held(size, chan_local, HALO, dtype=BF16) for size in sizes),
+    rim_count = 2 * len(feature_cuts)
+    feature_rims = pl.pallas_call(
+        functools.partial(split_kernel, feature_cuts),
+        out_shape=tuple(
+            held(stop - start, chan_local, HALO, dtype=BF16)
+            for start, stop in feature_cuts
+            for _ in range(2)
+        ),
         in_specs=[anywhere],
-        out_specs=(pl.BlockSpec(memory_space=pltpu.VMEM),) * 4,
-        scratch_shapes=[pltpu.SemaphoreType.DMA((4,))],
+        out_specs=(pl.BlockSpec(memory_space=pltpu.VMEM),) * rim_count,
+        scratch_shapes=[pltpu.SemaphoreType.DMA((rim_count,))],
         compiler_params=pltpu.CompilerParams(vmem_limit_bytes=4 * 1024 * 1024),
     )(pltpu.with_memory_space_constraint(fm, pltpu.HBM))
-    flm_a = shifted(high_a, "atom", 1)
-    frm_a = shifted(low_a, "atom", -1)
-    flm_b = shifted(high_b, "atom", 1)
-    frm_b = shifted(low_b, "atom", -1)
+    from_sides = [
+        shifted(rim, "atom", 1 if at % 2 == 0 else -1) for at, rim in enumerate(feature_rims)
+    ]
     fo = shifted(fm, "chan", 1)
 
     qkv, scores, slot_own, index_rows, index_wide, wp, wc, token, *rims = call(
-        functools.partial(own_kernel, heads, total_atoms, cuts),
+        functools.partial(own_kernel, heads, total_atoms),
         (place, fm, fo, cot, mix, neighbours),
         (
             held(comps, 3 * chan_local, atoms_dev, dtype=BF16),
@@ -454,21 +467,18 @@
             held(LMAX + 1, channels, 3 * chan_local, dtype=BF16),
             plain(8, HALO),
             *(
-                plain(stop - start, chan_local, HALO, dtype=BF16)
-                for start, stop in cuts
-                for _ in range(2)
+                plain(comps, chan_local, HALO, dtype=BF16) for _ in range(2)
             ),
         ),
         scalars=1,
         stay=(1, 2, 3),
         flops=12 * 10**9,
     )
-    flm_a, frm_a = after((flm_a, frm_a), (token,))
-    flo_a = shifted(flm_a, "chan", 1)
-    fro_a = shifted(frm_a, "chan", 1)
+    flm, frm = after(from_sides[:2], (token,))
+    early_chunk = (flm, shifted(flm, "chan", 1), frm, shifted(frm, "chan", 1))
     halo_a, partial, token = call(
         functools.partial(early_kernel, heads),
-        (flm_a, flo_a, frm_a, fro_a, wp, qkv, cot),
+        (*early_chunk, wp, qkv, cot),
         (
             held(feature_cut, 3 * chan_local, atoms_dev, dtype=BF16),
             held(2 * heads, 2, HALO, HALO),
@@ -476,30 +486,30 @@
         ),
         stay=tuple(range(7)),
     )
-    rims[:2] = after(rims[:2], (token,))
-    flm_b, frm_b = after((flm_b, frm_b), (token,))
-    halos = [(shifted(rims[0], "atom", 1), shifted(rims[1], "atom", -1))]
-    flo_b = shifted(flm_b, "chan", 1)
-    fro_b = shifted(frm_b, "chan", 1)
+    rims = after(rims, (token,))
+    late_sides = after(from_sides[2:], (token,))
+    late_chunks = []
+    for flm, frm in zip(late_sides[::2], late_sides[1::2]):
+        late_chunks += [flm, shifted(flm, "chan", 1), frm, shifted(frm, "chan", 1)]
+    from_left, from_right = shifted(rims[0], "atom", 1), shifted(rims[1], "atom", -1)
     halo_b, grad_bias, message_a, message_b = call(
-        functools.partial(edge_kernel, heads, score_scale, feature_cut),
-        (flm_b, flo_b, frm_b, fro_b, wp, qkv, cot, scores, partial, edge_bias, valid_mask,
-         index_rows, index_wide),
+        functools.partial(edge_kernel, heads, score_scale, feature_cut, len(late_chunks) // 4),
+        (*late_chunks, wp, qkv, cot, scores, partial, edge_bias, valid_mask, index_rows, index_wide),
         (
             held(comps - feature_cut, 3 * chan_local, atoms_dev, dtype=BF16),
             plain(heads, slots, atoms_dev),
             held((2 * heads + 1) * slots, HALO, dtype=BF16),
             held((2 * heads + 1) * slots, HALO, dtype=BF16),
         ),
-        stay=(0, 1, 2, 3, 4, 5, 6, 7, 8, 11, 12),
-    )
-    message_left = shifted(message_b, "atom", 1)
-    message_right = shifted(message_a, "atom", -1)
+        stay=(*range(len(late_chunks) + 5), len(late_chunks) + 7, len(late_chunks) + 8),
+    )
+    message_left = crossed(message_b, lambda at: (at + 1) % count)
+    message_right = crossed(message_a, lambda at: (at - 1) % count)
     piece = (3 * (LMAX + 1), chan_local // 4, channels)
     grad_query, own_key, own_value, kept, *sent = call(
-        functools.partial(grads_kernel, heads, slots),
-        (place, fm, fo, flm_a, flo_a, frm_a, fro_a, flm_b, flo_b, frm_b, fro_b, qkv, halo_a, halo_b,
-         cot, slot_own, message_a, message_b),
+        functools.partial(grads_kernel, heads, slots, len(feature_cuts)),
+        (place, fm, fo, *early_chunk, *late_chunks, qkv, halo_a, halo_b, cot, slot_own, message_a,
+         message_b),
         (
             held(comps, chan_local, atoms_dev, dtype=BF16),
             held(comps, chan_local, atoms_dev),
@@ -514,11 +524,8 @@
             pltpu.VMEM((3 * (LMAX + 1), chan_local, channels), F32),
         ],
         scalars=1,
-        stay=tuple(range(1, 18)),
-    )
-    (token,) = after((token,), halos[0])
-    rims[2:] = after(rims[2:], (sent[0], shifted(token, "chan", 1)))
-    halos.append((shifted(rims[2], "atom", 1), shifted(rims[3], "atom", -1)))
+        stay=tuple(range(1, 10 + 4 * len(feature_cuts))),
+    )
     for delta, part in enumerate(sent, 1):
         kept = kept + exchanged(part, "atom", delta << cut_bits[0]).astype(F32)
     rest = [bit for bit in range(count.bit_length() - 1) if bit not in cut_bits]
@@ -527,9 +534,22 @@
         rest = rest[2:]
         rounded = kept.astype(BF16)
         offsets += [sum(offsets)] * (len(offsets) - 1)
-        arrived = [exchanged(rounded, "atom", offset) for offset in offsets]
+        arrived = [
+            crossed(rounded, functools.partial(operator.xor, offset))
+            if offset == 1
+            else exchanged(rounded, "atom", offset)
+            for offset in offsets
+        ]
         kept = functools.reduce(lambda total, part: total + part.astype(F32), arrived, kept)
-    rounded = kept.astype(BF16)
+    terms, token = call(
+        functools.partial(key_kernel, heads, slots),
+        (grad_query, own_key, halo_a, halo_b, message_left, message_right, wc),
+        (held(comps, channels, atoms_dev), plain(8, HALO)),
+        scratch=[pltpu.VMEM((comps, 2 * chan_local, atoms_dev), BF16)],
+        limit=16,
+        stay=(0, 1, 2, 3, 6),
+    )
+    from_left, from_right, rounded = after((from_left, from_right, kept.astype(BF16)), (token,))
     pieces = [rounded] + [exchanged(rounded, "atom", d << cut_bits[0]) for d in range(1, 4)]
     grad_weights, gathered = call(
         gather_kernel,
@@ -539,23 +559,14 @@
         limit=8,
         flops=20 * 10**9,
     )
-    (terms,) = call(
-        functools.partial(key_kernel, heads, slots),
-        (grad_query, own_key, halo_a, halo_b, message_left, message_right, wc),
-        (held(comps, channels, atoms_dev),),
-        scratch=[pltpu.VMEM((comps, 2 * chan_local, atoms_dev), BF16)],
-        limit=16,
-        stay=(0, 1, 2, 3, 6),
-    )
     parts, counts = [], []
     tokens = ()
-    for (start, stop), (cl, cr) in zip(cuts, halos):
+    for start, stop in cuts:
         size = stop - start
-        part = -(-size // -(-size // (comps // 6)))
-        sizes = [min(part, size - at) for at in range(0, size, part)]
+        sizes = [size]
         mine, token, *theirs = call(
-            functools.partial(value_kernel, heads, slots, start),
-            (own_value, cl, cr, message_left, message_right, wc, terms),
+            functools.partial(value_kernel, heads, slots, start, stop),
+            (own_value, from_left, from_right, message_left, message_right, wc, terms),
             (
                 held(size, chan_local, atoms_dev),
                 plain(8, HALO),
@@ -563,10 +574,10 @@
             ),
             scratch=[pltpu.VMEM((size, chan_local, atoms_dev), BF16)],
             limit=16,
-            stay=(0, 5, 6),
+            stay=(0, 1, 2, 5, 6),
             tokens=tokens,
         )
-        tokens = (token, rounded)
+        tokens = (token, pieces[2])
         counts.append(len(sizes))
         parts += [mine, *(shifted(some, "chan", 1) for some in theirs)]
     (out,) = call(

time: 105 us -> 111 us (1.057)
  waiting for transfers between devices: 29.5 us -> 38.7 us
  starting transfers between devices: 40.4 us -> 38 us
    ppermute x23 -> x16, starting transfers between devices: 29.4 us -> 21.2 us  [shifted(): return lax.ppermute(value, axis, pairs)]
    ppermute x0 -> x3, waiting for transfers between devices: none -> 7.02 us  [crossed(): return shifted(lax.ppermute(value, ('atom', 'chan'), pairs), 'chan', 1)]
    ppermute x0 -> x3, starting transfers between devices: none -> 5.34 us  [crossed(): return shifted(lax.ppermute(value, ('atom', 'chan'), pairs), 'chan', 1)]
    ppermute x9 -> x8, waiting for transfers between devices: 8.59 us -> 13 us  [exchanged(): lax.ppermute(value, axis, [(source, source ^ offset) for source in range(...]
    ppermute x23 -> x16, waiting for transfers between devices: 20.9 us -> 18.6 us  [shifted(): return lax.ppermute(value, axis, pairs)]
    ppermute x9 -> x8, starting transfers between devices: 11 us -> 11.5 us  [exchanged(): lax.ppermute(value, axis, [(source, source ^ offset) for source in range(...]
  transfers between devices with their start and end apart: 32 -> 27, of which waited for: 13 -> 12; matrix products, arithmetic and copies ran while one was open for 0% -> 0% of each run, Pallas kernels for 26% -> 24%
where the time goes in v6:
time: 111 us; the launch traced here: 110 us
  waiting for transfers between devices  38.7 us (35%)
  starting transfers between devices  38 us (34%)
  Pallas kernels  28.2 us (25%)
  local copies, waits for them, and re-layouts  4.55 us (4%)
    pallas_call x9, Pallas kernels, call(): pl.pallas_call(body, out_shape=tuple(outs), in_specs=[small] * scalars +...  25.7 us
    ppermute x16, starting transfers between devices, shifted(): return lax.ppermute(value, axis, pairs)  21.2 us
    ppermute x16, waiting for transfers between devices, shifted(): return lax.ppermute(value, axis, pairs)  18.6 us
    ppermute x8, waiting for transfers between devices, exchanged(): lax.ppermute(value, axis, [(source, source ^ offset) for source in range(...  13 us
    ppermute x8, starting transfers between devices, exchanged(): lax.ppermute(value, axis, [(source, source ^ offset) for source in range(...  11.5 us
    ppermute x3, waiting for transfers between devices, crossed(): return shifted(lax.ppermute(value, ('atom', 'chan'), pairs), 'chan', 1)  7.02 us
    ppermute x3, starting transfers between devices, crossed(): return shifted(lax.ppermute(value, ('atom', 'chan'), pairs), 'chan', 1)  5.34 us
    unnamed x12, local copies, waits for them, and re-layouts  4.55 us
  transfers between devices with their start and end apart: 27, of which 12 were waited for; matrix products, arithmetic and copies ran while one was open for 0% of the time, Pallas kernels for 24%

profile of v6, /device:TPU:0, one launch (start us, length us, event | category | flops | bytes accessed | tf_op | source)
XLA Modules:
  0.0 110.5 jit_solution(2286743408114026965)
XLA Ops:
  0.6 0.5 collective-permute-start
  1.1 2.5 %shard_map.85 = (bf16[24,64,128]{2,1,0:T(8,128)(2,1)}, bf16[24,64,128]{2,1,0:T(8,128)(2,1)}, bf16[25,64,128]{2,1,0:T(8,128)(2,1)}, bf16[25,64,128]{2,1,0:T(8,128)(2,1)}) custom-call(bf16[49,64,256]{2,1,0:T(8,128)(2,1)} %bitcast.15), custom_call_target="tpu_custom_call" | custom-call | tf_op jit(solution)/shard_map/pallas_call | solution.py:440
  3.7 2.6 %collective-permute-start.1 = (bf16[24,64,128]{2,1,0:T(8,128)(2,1)}, bf16[24,64,128]{2,1,0:T(8,128)(2,1)S(1)}, u32[]{:S(2)}, u32[]{:S(2)}) collective-permute-start(bf16[24,64,128]{2,1,0:T(8,128)(2,1)} %get-tuple-element.49), channel_id=1, source_target_pairs={{0,2},{2,4},{4,6},{6,8},{8,10},{10,12},{12,14},{14,16},{16,18},{18... | collective-permute-start | bytes 1179656 | tf_op jit(solution)/shard_map/ppermute | solution.py:396
  6.3 4.1 %collective-permute-start.2 = (bf16[24,64,128]{2,1,0:T(8,128)(2,1)}, bf16[24,64,128]{2,1,0:T(8,128)(2,1)S(1)}, u32[]{:S(2)}, u32[]{:S(2)}) collective-permute-start(bf16[24,64,128]{2,1,0:T(8,128)(2,1)} %get-tuple-element.50), channel_id=1, source_target_pairs={{0,30},{2,0},{4,2},{6,4},{8,6},{10,8},{12,10},{14,12},{16,14},{18,... | collective-permute-start | bytes 1179656 | tf_op jit(solution)/shard_map/ppermute | solution.py:396
  10.3 5.6 %collective-permute-start.6 = (bf16[25,64,128]{2,1,0:T(8,128)(2,1)}, bf16[25,64,128]{2,1,0:T(8,128)(2,1)S(1)}, u32[]{:S(2)}, u32[]{:S(2)}) collective-permute-start(bf16[25,64,128]{2,1,0:T(8,128)(2,1)} %get-tuple-element.55), channel_id=1, source_target_pairs={{0,30},{2,0},{4,2},{6,4},{8,6},{10,8},{12,10},{14,12},{16,14},{18,... | collective-permute-start | bytes 1228808 | tf_op jit(solution)/shard_map/ppermute | solution.py:396
  15.9 0.1 pad_add_fusion.refs_0_
  16.0 1.4 %copy-done = bf16[64,49,256]{2,0,1:T(8,128)(2,1)S(1)} copy-done((bf16[64,49,256]{2,0,1:T(8,128)(2,1)S(1)}, bf16[64,49,256]{2,0,1:T(8,128)(2,1)}, u32[]{:S(2)}) %copy-start) | copy-done | bytes 1605656
  17.4 1.4 %copy-done.1 = bf16[64,49,256]{2,0,1:T(8,128)(2,1)S(1)} copy-done((bf16[64,49,256]{2,0,1:T(8,128)(2,1)S(1)}, bf16[64,49,256]{2,0,1:T(8,128)(2,1)}, u32[]{:S(2)}) %copy-start.1) | copy-done | bytes 1605656
  18.9 1.0 copy-done.4
  19.8 0.7 copy-done.5
  20.6 3.8 %shard_map.86 = (bf16[49,192,256]{2,1,0:T(8,128)(2,1)S(1)}, f32[8,256,256]{2,1,0:T(8,128)S(1)}, s32[2,3,128,128]{3,2,1,0:T(8,128)S(1)}, s32[16,256]{1,0:T(8,128)...) custom-call(s32[3]{0:T(128)S(1)} %pad_add_fusion.refs_0_, ...), custom_call_target="tpu_custom_call" | custom-call | flops 12000000000 | bytes 1024 | tf_op jit(solution)/shard_map/pallas_call | solution.py:362
  24.4 8.9 %collective-permute-done.1.refs_0_ = bf16[24,64,128]{2,1,0:T(8,128)(2,1)S(1)} collective-permute-done((bf16[24,64,128]{2,1,0:T(8,128)(2,1)}, bf16[24,64,128]{2,1,0:T(8,128)(2,1)S(1)}, u32[]{:S(2)}, u32[]{:S(2)}) %collective-permute-start.1) | collective-permute-done | bytes 393248 | tf_op jit(solution)/shard_map/ppermute | solution.py:396
  33.2 0.5 collective-permute-start.4
  33.7 1.2 %collective-permute-done.3.refs_1_.refs_4_ = bf16[24,64,128]{2,1,0:T(8,128)(2,1)S(1)} collective-permute-done((bf16[24,64,128]{2,1,0:T(8,128)(2,1)S(1)}, bf16[24,64,128]{2,1,0:T(8,128)(2,1)S(1)}, u32[]{:S(2)}, u32[]{:S(2)}) %collective-permute-start.3) | collective-permute-done | bytes 393248 | tf_op jit(solution)/shard_map/ppermute | solution.py:396
  34.9 0.6 collective-permute-done.4.refs_3_.refs_6_
  35.5 1.3 %shard_map.88 = (bf16[24,192,256]{2,1,0:T(8,128)(2,1)S(1)}, f32[8,2,128,128]{3,2,1,0:T(8,128)S(1)}, f32[8,128]{1,0:T(8,128)S(1)}) custom-call(bf16[24,64,128]{2,1,0:T(8,128)(2,1)S(1)} %get-tuple-element.52.refs_0_.refs_3_, bf16[24,64,128]{2,1,0:T(8,128)(2,1)S(1)} %collective-permute-done.3.refs_1_.refs_4_, ...), custom_call_target="tpu_custom_call" | custom-call | bytes 1024 | tf_op jit(solution)/shard_map/pallas_call | solution.py:362
  36.8 4.8 %collective-permute-done.5.refs_0_ = bf16[25,64,128]{2,1,0:T(8,128)(2,1)S(1)} collective-permute-done((bf16[25,64,128]{2,1,0:T(8,128)(2,1)}, bf16[25,64,128]{2,1,0:T(8,128)(2,1)S(1)}, u32[]{:S(2)}, u32[]{:S(2)}) %collective-permute-start.5) | collective-permute-done | bytes 409632 | tf_op jit(solution)/shard_map/ppermute | solution.py:396
  41.6 1.8 %collective-permute-done.6.refs_1_ = bf16[25,64,128]{2,1,0:T(8,128)(2,1)S(1)} collective-permute-done((bf16[25,64,128]{2,1,0:T(8,128)(2,1)}, bf16[25,64,128]{2,1,0:T(8,128)(2,1)S(1)}, u32[]{:S(2)}, u32[]{:S(2)}) %collective-permute-start.6) | collective-permute-done | bytes 409632 | tf_op jit(solution)/shard_map/ppermute | solution.py:396
  43.4 0.5 collective-permute-start.8
  43.9 1.5 %collective-permute-start.9 = (bf16[49,64,128]{2,1,0:T(8,128)(2,1)S(1)}, bf16[49,64,128]{2,1,0:T(8,128)(2,1)S(1)}, u32[]{:S(2)}, u32[]{:S(2)}) collective-permute-start(bf16[49,64,128]{2,1,0:T(8,128)(2,1)S(1)} %get-tuple-element.73), channel_id=1, source_target_pairs={{0,2},{2,4},{4,6},{6,8},{8,10},{10,12},{12,14},{14,16},{16,18},{18... | collective-permute-start | bytes 2408456 | tf_op jit(solution)/shard_map/ppermute | solution.py:396
  45.4 4.1 %collective-permute-start.10 = (bf16[49,64,128]{2,1,0:T(8,128)(2,1)S(1)}, bf16[49,64,128]{2,1,0:T(8,128)(2,1)S(1)}, u32[]{:S(2)}, u32[]{:S(2)}) collective-permute-start(bf16[49,64,128]{2,1,0:T(8,128)(2,1)S(1)} %get-tuple-element.74), channel_id=1, source_target_pairs={{0,30},{2,0},{4,2},{6,4},{8,6},{10,8},{12,10},{14,12},{16,14},{18,... | collective-permute-start | bytes 2408456 | tf_op jit(solution)/shard_map/ppermute | solution.py:396
  49.6 3.8 %shard_map.90 = (bf16[25,192,256]{2,1,0:T(8,128)(2,1)S(1)}, f32[4,16,256]{2,1,0:T(8,128)}, bf16[144,128]{1,0:T(8,128)(2,1)S(1)}, bf16[144,128]{1,0:T(8,128)(2,1)S(1)}) custom-call(bf16[25,64,128]{2,1,0:T(8,128)(2,1)S(1)} %get-tuple-element.59.refs_0_.refs_7_, bf16[25,64,128]{2,1,0:T(8,128)(2,1)S(1)} %collective-permute-done.7.refs_1_.refs_8_, ...), custom_call_target="tpu_custom_call" | custom-call | bytes 1024 | tf_op jit(solution)/shard_map/pallas_call | solution.py:362
  53.4 6.8 %shard_map.91 = (bf16[49,64,256]{2,1,0:T(8,128)(2,1)S(1)}, f32[49,64,256]{2,1,0:T(8,128)S(1)}, f32[49,64,256]{2,1,0:T(8,128)S(1)}, f32[21,16,128]{2,1,0:T(8,128)...) custom-call(s32[3]{0:T(128)S(1)} %pad_add_fusion.refs_0_, ...), custom_call_target="tpu_custom_call" | custom-call | bytes 1024 | tf_op jit(solution)/shard_map/pallas_call | solution.py:362
  60.2 0.1 collective-permute-start.11
  60.3 0.3 collective-permute-start.12
  60.6 3.2 %collective-permute-start.13 = (bf16[21,16,128]{2,1,0:T(8,128)(2,1)S(1)}, bf16[21,16,128]{2,1,0:T(8,128)(2,1)S(1)}, u32[]{:S(2)}, u32[]{:S(2)}) collective-permute-start(bf16[21,16,128]{2,1,0:T(8,128)(2,1)S(1)} %get-tuple-element.78), channel_id=1, source_target_pairs={{0,12},{2,14},{4,8},{6,10},{8,4},{10,6},{12,0},{14,2},{16,28},{18,... | collective-permute-start | bytes 258056 | tf_op jit(solution)/shard_map/ppermute | solution.py:401
  63.8 7.4 %collective-permute-done.11 = bf16[21,16,128]{2,1,0:T(8,128)(2,1)S(1)} collective-permute-done((bf16[21,16,128]{2,1,0:T(8,128)(2,1)S(1)}, bf16[21,16,128]{2,1,0:T(8,128)(2,1)S(1)}, u32[]{:S(2)}, u32[]{:S(2)}) %collective-permute-start.11) | collective-permute-done | bytes 86048 | tf_op jit(solution)/shard_map/ppermute | solution.py:401
  71.2 0.2 collective-permute-done.13
  71.5 1.3 %collective-permute-start.14 = (bf16[21,16,128]{2,1,0:T(8,128)(2,1)S(1)}, bf16[21,16,128]{2,1,0:T(8,128)(2,1)S(1)}, u32[]{:S(2)}, u32[]{:S(2)}) collective-permute-start(bf16[21,16,128]{2,1,0:T(8,128)(2,1)S(1)} %fusion), channel_id=1, source_target_pairs={{0,3},{1,2},{2,1},{3,0},{4,7},{5,6},{6,5},{7,4},{8,11},{9,10},{10,... | collective-permute-start | bytes 258056 | tf_op jit(solution)/shard_map/ppermute | solution.py:407
  72.8 4.0 %collective-permute-start.20 = (bf16[144,128]{1,0:T(8,128)(2,1)S(1)}, bf16[144,128]{1,0:T(8,128)(2,1)S(1)}, u32[]{:S(2)}, u32[]{:S(2)}) collective-permute-start(bf16[144,128]{1,0:T(8,128)(2,1)S(1)} %get-tuple-element.68.refs_16_), channel_id=1, source_target_pairs={{0,31},{1,30},{2,1},{3,0},{4,3},{5,2},{6,5},{7,4},{8,7},{9,6},{10,... | collective-permute-start | bytes 110600 | tf_op jit(solution)/shard_map/ppermute | solution.py:407
  76.9 7.0 %collective-permute-done.20 = bf16[144,128]{1,0:T(8,128)(2,1)S(1)} collective-permute-done((bf16[144,128]{1,0:T(8,128)(2,1)S(1)}, bf16[144,128]{1,0:T(8,128)(2,1)S(1)}, u32[]{:S(2)}, u32[]{:S(2)}) %collective-permute-start.20) | collective-permute-done | bytes 36896 | tf_op jit(solution)/shard_map/ppermute | solution.py:407
  83.9 1.2 %collective-permute-start.21 = (bf16[144,128]{1,0:T(8,128)(2,1)S(1)}, bf16[144,128]{1,0:T(8,128)(2,1)S(1)}, u32[]{:S(2)}, u32[]{:S(2)}) collective-permute-start(bf16[144,128]{1,0:T(8,128)(2,1)S(1)} %collective-permute-done.20), channel_id=1, source_target_pairs={{0,1},{1,0},{2,3},{3,2},{4,5},{5,4},{6,7},{7,6},{8,9},{9,8},{10,11... | collective-permute-start | bytes 110600 | tf_op jit(solution)/shard_map/ppermute | solution.py:396
  85.1 0.9 collective-permute-done.21.refs_5_.refs_4_
  85.9 3.7 %collective-permute-start.17 = (bf16[21,16,128]{2,1,0:T(8,128)(2,1)S(1)}, bf16[21,16,128]{2,1,0:T(8,128)(2,1)S(1)}, u32[]{:S(2)}, u32[]{:S(2)}) collective-permute-start(bf16[21,16,128]{2,1,0:T(8,128)(2,1)S(1)} %fusion), channel_id=1, source_target_pairs={{0,18},{2,16},{4,22},{6,20},{8,26},{10,24},{12,30},{14,28},{16,2},... | collective-permute-start | bytes 258056 | tf_op jit(solution)/shard_map/ppermute | solution.py:401
  89.6 0.7 collective-permute-start.16
  90.3 2.9 %shard_map.93 = (f32[49,128,256]{2,1,0:T(8,128)S(1)}, f32[8,128]{1,0:T(8,128)S(1)}) custom-call(bf16[49,64,256]{2,1,0:T(8,128)(2,1)S(1)} %get-tuple-element.79.refs_0_, f32[49,64,256]{2,1,0:T(8,128)S(1)} %get-tuple-element.80.refs_1_, bf16[24,192,256]{2,1,0:T(8,128)(2,1)S(1)} %get-tuple-element.61.refs_12_.refs_2_, ...), custom_call_target="tpu_custom_call" | custom-call | bytes 1024 | tf_op jit(solution)/shard_map/pallas_call | solution.py:362
  93.2 3.5 %collective-permute-done.17 = bf16[21,16,128]{2,1,0:T(8,128)(2,1)S(1)} collective-permute-done((bf16[21,16,128]{2,1,0:T(8,128)(2,1)S(1)}, bf16[21,16,128]{2,1,0:T(8,128)(2,1)S(1)}, u32[]{:S(2)}, u32[]{:S(2)}) %collective-permute-start.17) | collective-permute-done | bytes 86048 | tf_op jit(solution)/shard_map/ppermute | solution.py:401
  96.7 1.9 %collective-permute-done.16 = bf16[21,16,128]{2,1,0:T(8,128)(2,1)S(1)} collective-permute-done((bf16[21,16,128]{2,1,0:T(8,128)(2,1)S(1)}, bf16[21,16,128]{2,1,0:T(8,128)(2,1)S(1)}, u32[]{:S(2)}, u32[]{:S(2)}) %collective-permute-start.16) | collective-permute-done | bytes 86048 | tf_op jit(solution)/shard_map/ppermute | solution.py:401
  98.6 0.1 add_convert_fusion.refs_2_
  98.7 0.4 collective-permute-start.23
  99.1 1.3 %collective-permute-start.26 = (bf16[21,16,128]{2,1,0:T(8,128)(2,1)S(1)}, bf16[21,16,128]{2,1,0:T(8,128)(2,1)S(1)}, u32[]{:S(2)}, u32[]{:S(2)}) collective-permute-start(bf16[21,16,128]{2,1,0:T(8,128)(2,1)S(1)} %get-tuple-element.89.refs_1_), channel_id=1, source_target_pairs={{0,12},{2,14},{4,8},{6,10},{8,4},{10,6},{12,0},{14,2},{16,28},{18,... | collective-permute-start | bytes 258056 | tf_op jit(solution)/shard_map/ppermute | solution.py:401
  100.5 1.8 %collective-permute-start.25 = (bf16[21,16,128]{2,1,0:T(8,128)(2,1)S(1)}, bf16[21,16,128]{2,1,0:T(8,128)(2,1)S(1)}, u32[]{:S(2)}, u32[]{:S(2)}) collective-permute-start(bf16[21,16,128]{2,1,0:T(8,128)(2,1)S(1)} %get-tuple-element.89.refs_1_), channel_id=1, source_target_pairs={{0,4},{2,6},{4,0},{6,2},{8,12},{10,14},{12,8},{14,10},{16,20},{18,... | collective-permute-start | bytes 258056 | tf_op jit(solution)/shard_map/ppermute | solution.py:401
  102.3 2.0 %shard_map.95 = (f32[24,64,256]{2,1,0:T(8,128)S(1)}, f32[8,128]{1,0:T(8,128)S(1)}, bf16[24,64,256]{2,1,0:T(8,128)(2,1)S(1)}) custom-call(f32[49,64,256]{2,1,0:T(8,128)S(1)} %get-tuple-element.70.refs_0_, bf16[49,64,128]{2,1,0:T(8,128)(2,1)S(1)} %get-tuple-element.83.refs_1_, bf16[49,64,128]{2,1,0:T(8,128)(2,1)S(1)} %get-tuple-element.84.refs_2_, ...), custom_call_target="tpu_custom_call" | custom-call | bytes 1024 | tf_op jit(solution)/shard_map/pallas_call | solution.py:362
  104.4 2.1 %shard_map.96 = (f32[25,64,256]{2,1,0:T(8,128)S(1)}, f32[8,128]{1,0:T(8,128)}, bf16[25,64,256]{2,1,0:T(8,128)(2,1)S(1)}) custom-call(f32[49,64,256]{2,1,0:T(8,128)S(1)} %get-tuple-element.70.refs_0_, bf16[49,64,128]{2,1,0:T(8,128)(2,1)S(1)} %get-tuple-element.83.refs_1_, bf16[49,64,128]{2,1,0:T(8,128)(2,1)S(1)} %get-tuple-element.84.refs_2_, ...), custom_call_target="tpu_custom_call" | custom-call | bytes 1024 | tf_op jit(solution)/shard_map/pallas_call | solution.py:362
  106.5 0.6 collective-permute-start.24
  107.1 1.4 %shard_map.97 = (f32[21,64,128]{2,1,0:T(8,128)}, f32[8,128]{1,0:T(8,128)S(1)}) custom-call(s32[3]{0:T(128)S(1)} %pad_add_fusion.refs_0_, bf16[21,16,128]{2,1,0:T(8,128)(2,1)S(1)} %get-tuple-element.89.refs_1_, bf16[21,16,128]{2,1,0:T(8,128)(2,1)S(1)} %collective-permute-done.25.refs_2_, bf16[21,16,128]{2,1,0:T(8,128)(2,1)S(1)} %collective-permute-done.23.refs_8_.refs_3_, ...), custom_call_target="tpu_custom_call" | custom-call | flops 20000000000 | bytes 1024 | tf_op jit(solution)/shard_map/pallas_call | solution.py:362
  108.5 0.5 collective-permute-done.24.refs_3_
  109.0 1.4 %shard_map.98 = bf16[49,64,256]{2,1,0:T(8,128)(2,1)} custom-call(f32[24,64,256]{2,1,0:T(8,128)S(1)} %get-tuple-element.86.refs_0_, bf16[24,64,256]{2,1,0:T(8,128)(2,1)S(1)} %collective-permute-done.22.refs_1_, f32[25,64,256]{2,1,0:T(8,128)S(1)} %get-tuple-element.90.refs_2_, bf16[25,64,256]{2,1,0:T(8,128)(2,1)S(1)} %collective-permute-done.24.refs_3_, ...), custom_call_target="tpu_custom_call" | custom-call | bytes 1024 | tf_op jit(solution)/shard_map/pallas_call | solution.py:362
  (35 shorter events, 0.2 us)
Async XLA Ops:
  0.6 15.4 %collective-permute-start = (bf16[49,64,256]{2,1,0:T(8,128)(2,1)}, bf16[49,64,256]{2,1,0:T(8,128)(2,1)S(1)}, u32[]{:S(2)}, u32[]{:S(2)}) collective-permute-start(bf16[49,64,256]{2,1,0:T(8,128)(2,1)} %bitcast.14), channel_id=1, source_target_pairs={{0,1},{1,0},{2,3},{3,2},{4,5},{5,4},{6,7},{7,6},{8,9},{9,8},{10,11... | collective-permute-start | bytes 4816904 | tf_op jit(solution)/shard_map/ppermute | solution.py:396
  3.7 29.5 %collective-permute-start.1 = (bf16[24,64,128]{2,1,0:T(8,128)(2,1)}, bf16[24,64,128]{2,1,0:T(8,128)(2,1)S(1)}, u32[]{:S(2)}, u32[]{:S(2)}) collective-permute-start(bf16[24,64,128]{2,1,0:T(8,128)(2,1)} %get-tuple-element.49), channel_id=1, source_target_pairs={{0,2},{2,4},{4,6},{6,8},{8,10},{10,12},{12,14},{14,16},{16,18},{18... | collective-permute-start | bytes 1179656 | tf_op jit(solution)/shard_map/ppermute | solution.py:396
  6.3 27.0 %collective-permute-start.2 = (bf16[24,64,128]{2,1,0:T(8,128)(2,1)}, bf16[24,64,128]{2,1,0:T(8,128)(2,1)S(1)}, u32[]{:S(2)}, u32[]{:S(2)}) collective-permute-start(bf16[24,64,128]{2,1,0:T(8,128)(2,1)} %get-tuple-element.50), channel_id=1, source_target_pairs={{0,30},{2,0},{4,2},{6,4},{8,6},{10,8},{12,10},{14,12},{16,14},{18,... | collective-permute-start | bytes 1179656 | tf_op jit(solution)/shard_map/ppermute | solution.py:396
  10.3 31.3 %collective-permute-start.5 = (bf16[25,64,128]{2,1,0:T(8,128)(2,1)}, bf16[25,64,128]{2,1,0:T(8,128)(2,1)S(1)}, u32[]{:S(2)}, u32[]{:S(2)}) collective-permute-start(bf16[25,64,128]{2,1,0:T(8,128)(2,1)} %get-tuple-element.54), channel_id=1, source_target_pairs={{0,2},{2,4},{4,6},{6,8},{8,10},{10,12},{12,14},{14,16},{16,18},{18... | collective-permute-start | bytes 1228808 | tf_op jit(solution)/shard_map/ppermute | solution.py:396
  10.3 33.1 %collective-permute-start.6 = (bf16[25,64,128]{2,1,0:T(8,128)(2,1)}, bf16[25,64,128]{2,1,0:T(8,128)(2,1)S(1)}, u32[]{:S(2)}, u32[]{:S(2)}) collective-permute-start(bf16[25,64,128]{2,1,0:T(8,128)(2,1)} %get-tuple-element.55), channel_id=1, source_target_pairs={{0,30},{2,0},{4,2},{6,4},{8,6},{10,8},{12,10},{14,12},{16,14},{18,... | collective-permute-start | bytes 1228808 | tf_op jit(solution)/shard_map/ppermute | solution.py:396
  16.0 1.4 %copy-start = (bf16[64,49,256]{2,0,1:T(8,128)(2,1)S(1)}, bf16[64,49,256]{2,0,1:T(8,128)(2,1)}, u32[]{:S(2)}) copy-start(bf16[64,49,256]{2,0,1:T(8,128)(2,1)} %param.8) | copy-start | bytes 4816900
  17.4 1.4 %copy-start.1 = (bf16[64,49,256]{2,0,1:T(8,128)(2,1)S(1)}, bf16[64,49,256]{2,0,1:T(8,128)(2,1)}, u32[]{:S(2)}) copy-start(bf16[64,49,256]{2,0,1:T(8,128)(2,1)} %param.6) | copy-start | bytes 4816900
  18.9 1.0 copy-start.4
  19.8 0.7 copy-start.5
  33.2 1.7 %collective-permute-start.3 = (bf16[24,64,128]{2,1,0:T(8,128)(2,1)S(1)}, bf16[24,64,128]{2,1,0:T(8,128)(2,1)S(1)}, u32[]{:S(2)}, u32[]{:S(2)}) collective-permute-start(bf16[24,64,128]{2,1,0:T(8,128)(2,1)S(1)} %get-tuple-element.52.refs_0_.refs_3_), channel_id=1, source_target_pairs={{0,1},{1,0},{2,3},{3,2},{4,5},{5,4},{6,7},{7,6},{8,9},{9,8},{10,11... | collective-permute-start | bytes 1179656 | tf_op jit(solution)/shard_map/ppermute | solution.py:396
  33.2 2.3 %collective-permute-start.4 = (bf16[24,64,128]{2,1,0:T(8,128)(2,1)S(1)}, bf16[24,64,128]{2,1,0:T(8,128)(2,1)S(1)}, u32[]{:S(2)}, u32[]{:S(2)}) collective-permute-start(bf16[24,64,128]{2,1,0:T(8,128)(2,1)S(1)} %get-tuple-element.53.refs_2_.refs_5_), channel_id=1, source_target_pairs={{0,1},{1,0},{2,3},{3,2},{4,5},{5,4},{6,7},{7,6},{8,9},{9,8},{10,11... | collective-permute-start | bytes 1179656 | tf_op jit(solution)/shard_map/ppermute | solution.py:396
  36.8 12.8 %copy-start.2 = (f32[4,16,256]{2,1,0:T(8,128)S(1)}, f32[4,16,256]{2,1,0:T(8,128)}, u32[]{:S(2)}) copy-start(f32[4,16,256]{2,1,0:T(8,128)} %refs_9_.1) | copy-start | bytes 196612
  36.8 12.8 %copy-start.3 = (s32[16,256]{1,0:T(8,128)S(1)}, s32[16,256]{1,0:T(8,128)}, u32[]{:S(2)}) copy-start(s32[16,256]{1,0:T(8,128)} %refs_10_.1) | copy-start | bytes 49156
  43.4 6.1 %collective-permute-start.7 = (bf16[25,64,128]{2,1,0:T(8,128)(2,1)S(1)}, bf16[25,64,128]{2,1,0:T(8,128)(2,1)S(1)}, u32[]{:S(2)}, u32[]{:S(2)}) collective-permute-start(bf16[25,64,128]{2,1,0:T(8,128)(2,1)S(1)} %get-tuple-element.59.refs_0_.refs_7_), channel_id=1, source_target_pairs={{0,1},{1,0},{2,3},{3,2},{4,5},{5,4},{6,7},{7,6},{8,9},{9,8},{10,11... | collective-permute-start | bytes 1228808 | tf_op jit(solution)/shard_map/ppermute | solution.py:396
  43.4 6.1 %collective-permute-start.8 = (bf16[25,64,128]{2,1,0:T(8,128)(2,1)S(1)}, bf16[25,64,128]{2,1,0:T(8,128)(2,1)S(1)}, u32[]{:S(2)}, u32[]{:S(2)}) collective-permute-start(bf16[25,64,128]{2,1,0:T(8,128)(2,1)S(1)} %get-tuple-element.60.refs_2_.refs_9_), channel_id=1, source_target_pairs={{0,1},{1,0},{2,3},{3,2},{4,5},{5,4},{6,7},{7,6},{8,9},{9,8},{10,11... | collective-permute-start | bytes 1228808 | tf_op jit(solution)/shard_map/ppermute | solution.py:396
  43.9 54.8 %collective-permute-start.9 = (bf16[49,64,128]{2,1,0:T(8,128)(2,1)S(1)}, bf16[49,64,128]{2,1,0:T(8,128)(2,1)S(1)}, u32[]{:S(2)}, u32[]{:S(2)}) collective-permute-start(bf16[49,64,128]{2,1,0:T(8,128)(2,1)S(1)} %get-tuple-element.73), channel_id=1, source_target_pairs={{0,2},{2,4},{4,6},{6,8},{8,10},{10,12},{12,14},{14,16},{16,18},{18... | collective-permute-start | bytes 2408456 | tf_op jit(solution)/shard_map/ppermute | solution.py:396
  45.4 53.3 %collective-permute-start.10 = (bf16[49,64,128]{2,1,0:T(8,128)(2,1)S(1)}, bf16[49,64,128]{2,1,0:T(8,128)(2,1)S(1)}, u32[]{:S(2)}, u32[]{:S(2)}) collective-permute-start(bf16[49,64,128]{2,1,0:T(8,128)(2,1)S(1)} %get-tuple-element.74), channel_id=1, source_target_pairs={{0,30},{2,0},{4,2},{6,4},{8,6},{10,8},{12,10},{14,12},{16,14},{18,... | collective-permute-start | bytes 2408456 | tf_op jit(solution)/shard_map/ppermute | solution.py:396
  60.2 11.0 %collective-permute-start.11 = (bf16[21,16,128]{2,1,0:T(8,128)(2,1)S(1)}, bf16[21,16,128]{2,1,0:T(8,128)(2,1)S(1)}, u32[]{:S(2)}, u32[]{:S(2)}) collective-permute-start(bf16[21,16,128]{2,1,0:T(8,128)(2,1)S(1)} %get-tuple-element.76), channel_id=1, source_target_pairs={{0,4},{2,6},{4,0},{6,2},{8,12},{10,14},{12,8},{14,10},{16,20},{18,... | collective-permute-start | bytes 258056 | tf_op jit(solution)/shard_map/ppermute | solution.py:401
  60.3 10.9 %collective-permute-start.12 = (bf16[21,16,128]{2,1,0:T(8,128)(2,1)S(1)}, bf16[21,16,128]{2,1,0:T(8,128)(2,1)S(1)}, u32[]{:S(2)}, u32[]{:S(2)}) collective-permute-start(bf16[21,16,128]{2,1,0:T(8,128)(2,1)S(1)} %get-tuple-element.77), channel_id=1, source_target_pairs={{0,8},{2,10},{4,12},{6,14},{8,0},{10,2},{12,4},{14,6},{16,24},{18,... | collective-permute-start | bytes 258056 | tf_op jit(solution)/shard_map/ppermute | solution.py:401
  60.6 10.9 %collective-permute-start.13 = (bf16[21,16,128]{2,1,0:T(8,128)(2,1)S(1)}, bf16[21,16,128]{2,1,0:T(8,128)(2,1)S(1)}, u32[]{:S(2)}, u32[]{:S(2)}) collective-permute-start(bf16[21,16,128]{2,1,0:T(8,128)(2,1)S(1)} %get-tuple-element.78), channel_id=1, source_target_pairs={{0,12},{2,14},{4,8},{6,10},{8,4},{10,6},{12,0},{14,2},{16,28},{18,... | collective-permute-start | bytes 258056 | tf_op jit(solution)/shard_map/ppermute | solution.py:401
  71.5 18.8 %collective-permute-start.14 = (bf16[21,16,128]{2,1,0:T(8,128)(2,1)S(1)}, bf16[21,16,128]{2,1,0:T(8,128)(2,1)S(1)}, u32[]{:S(2)}, u32[]{:S(2)}) collective-permute-start(bf16[21,16,128]{2,1,0:T(8,128)(2,1)S(1)} %fusion), channel_id=1, source_target_pairs={{0,3},{1,2},{2,1},{3,0},{4,7},{5,6},{6,5},{7,4},{8,11},{9,10},{10,... | collective-permute-start | bytes 258056 | tf_op jit(solution)/shard_map/ppermute | solution.py:407
  72.8 11.0 %collective-permute-start.20 = (bf16[144,128]{1,0:T(8,128)(2,1)S(1)}, bf16[144,128]{1,0:T(8,128)(2,1)S(1)}, u32[]{:S(2)}, u32[]{:S(2)}) collective-permute-start(bf16[144,128]{1,0:T(8,128)(2,1)S(1)} %get-tuple-element.68.refs_16_), channel_id=1, source_target_pairs={{0,31},{1,30},{2,1},{3,0},{4,3},{5,2},{6,5},{7,4},{8,7},{9,6},{10,... | collective-permute-start | bytes 110600 | tf_op jit(solution)/shard_map/ppermute | solution.py:407
  76.8 8.2 %collective-permute-start.18 = (bf16[144,128]{1,0:T(8,128)(2,1)S(1)}, bf16[144,128]{1,0:T(8,128)(2,1)S(1)}, u32[]{:S(2)}, u32[]{:S(2)}) collective-permute-start(bf16[144,128]{1,0:T(8,128)(2,1)S(1)} %get-tuple-element.69.refs_17_), channel_id=1, source_target_pairs={{0,3},{1,2},{2,5},{3,4},{4,7},{5,6},{6,9},{7,8},{8,11},{9,10},{10,... | collective-permute-start | bytes 110600 | tf_op jit(solution)/shard_map/ppermute | solution.py:407
  83.9 2.0 %collective-permute-start.21 = (bf16[144,128]{1,0:T(8,128)(2,1)S(1)}, bf16[144,128]{1,0:T(8,128)(2,1)S(1)}, u32[]{:S(2)}, u32[]{:S(2)}) collective-permute-start(bf16[144,128]{1,0:T(8,128)(2,1)S(1)} %collective-permute-done.20), channel_id=1, source_target_pairs={{0,1},{1,0},{2,3},{3,2},{4,5},{5,4},{6,7},{7,6},{8,9},{9,8},{10,11... | collective-permute-start | bytes 110600 | tf_op jit(solution)/shard_map/ppermute | solution.py:396
  85.0 4.6 %collective-permute-start.19 = (bf16[144,128]{1,0:T(8,128)(2,1)S(1)}, bf16[144,128]{1,0:T(8,128)(2,1)S(1)}, u32[]{:S(2)}, u32[]{:S(2)}) collective-permute-start(bf16[144,128]{1,0:T(8,128)(2,1)S(1)} %collective-permute-done.18), channel_id=1, source_target_pairs={{0,1},{1,0},{2,3},{3,2},{4,5},{5,4},{6,7},{7,6},{8,9},{9,8},{10,11... | collective-permute-start | bytes 110600 | tf_op jit(solution)/shard_map/ppermute | solution.py:396
  85.9 10.8 %collective-permute-start.17 = (bf16[21,16,128]{2,1,0:T(8,128)(2,1)S(1)}, bf16[21,16,128]{2,1,0:T(8,128)(2,1)S(1)}, u32[]{:S(2)}, u32[]{:S(2)}) collective-permute-start(bf16[21,16,128]{2,1,0:T(8,128)(2,1)S(1)} %fusion), channel_id=1, source_target_pairs={{0,18},{2,16},{4,22},{6,20},{8,26},{10,24},{12,30},{14,28},{16,2},... | collective-permute-start | bytes 258056 | tf_op jit(solution)/shard_map/ppermute | solution.py:401
  89.6 8.9 %collective-permute-start.16 = (bf16[21,16,128]{2,1,0:T(8,128)(2,1)S(1)}, bf16[21,16,128]{2,1,0:T(8,128)(2,1)S(1)}, u32[]{:S(2)}, u32[]{:S(2)}) collective-permute-start(bf16[21,16,128]{2,1,0:T(8,128)(2,1)S(1)} %fusion), channel_id=1, source_target_pairs={{0,16},{2,18},{4,20},{6,22},{8,24},{10,26},{12,28},{14,30},{16,0},... | collective-permute-start | bytes 258056 | tf_op jit(solution)/shard_map/ppermute | solution.py:401
  90.3 8.3 %collective-permute-start.15 = (bf16[21,16,128]{2,1,0:T(8,128)(2,1)S(1)}, bf16[21,16,128]{2,1,0:T(8,128)(2,1)S(1)}, u32[]{:S(2)}, u32[]{:S(2)}) collective-permute-start(bf16[21,16,128]{2,1,0:T(8,128)(2,1)S(1)} %collective-permute-done.14), channel_id=1, source_target_pairs={{0,1},{1,0},{2,3},{3,2},{4,5},{5,4},{6,7},{7,6},{8,9},{9,8},{10,11... | collective-permute-start | bytes 258056 | tf_op jit(solution)/shard_map/ppermute | solution.py:396
  98.7 5.7 %collective-permute-start.23 = (bf16[21,16,128]{2,1,0:T(8,128)(2,1)S(1)}, bf16[21,16,128]{2,1,0:T(8,128)(2,1)S(1)}, u32[]{:S(2)}, u32[]{:S(2)}) collective-permute-start(bf16[21,16,128]{2,1,0:T(8,128)(2,1)S(1)} %get-tuple-element.89.refs_1_), channel_id=1, source_target_pairs={{0,8},{2,10},{4,12},{6,14},{8,0},{10,2},{12,4},{14,6},{16,24},{18,... | collective-permute-start | bytes 258056 | tf_op jit(solution)/shard_map/ppermute | solution.py:401
  99.1 7.9 %collective-permute-start.26 = (bf16[21,16,128]{2,1,0:T(8,128)(2,1)S(1)}, bf16[21,16,128]{2,1,0:T(8,128)(2,1)S(1)}, u32[]{:S(2)}, u32[]{:S(2)}) collective-permute-start(bf16[21,16,128]{2,1,0:T(8,128)(2,1)S(1)} %get-tuple-element.89.refs_1_), channel_id=1, source_target_pairs={{0,12},{2,14},{4,8},{6,10},{8,4},{10,6},{12,0},{14,2},{16,28},{18,... | collective-permute-start | bytes 258056 | tf_op jit(solution)/shard_map/ppermute | solution.py:401
  100.5 6.6 %collective-permute-start.25 = (bf16[21,16,128]{2,1,0:T(8,128)(2,1)S(1)}, bf16[21,16,128]{2,1,0:T(8,128)(2,1)S(1)}, u32[]{:S(2)}, u32[]{:S(2)}) collective-permute-start(bf16[21,16,128]{2,1,0:T(8,128)(2,1)S(1)} %get-tuple-element.89.refs_1_), channel_id=1, source_target_pairs={{0,4},{2,6},{4,0},{6,2},{8,12},{10,14},{12,8},{14,10},{16,20},{18,... | collective-permute-start | bytes 258056 | tf_op jit(solution)/shard_map/ppermute | solution.py:401
  104.3 4.2 %collective-permute-start.22 = (bf16[24,64,256]{2,1,0:T(8,128)(2,1)S(1)}, bf16[24,64,256]{2,1,0:T(8,128)(2,1)S(1)}, u32[]{:S(2)}, u32[]{:S(2)}) collective-permute-start(bf16[24,64,256]{2,1,0:T(8,128)(2,1)S(1)} %get-tuple-element.87), channel_id=1, source_target_pairs={{0,1},{1,0},{2,3},{3,2},{4,5},{5,4},{6,7},{7,6},{8,9},{9,8},{10,11... | collective-permute-start | bytes 2359304 | tf_op jit(solution)/shard_map/ppermute | solution.py:396
  106.5 2.5 %collective-permute-start.24 = (bf16[25,64,256]{2,1,0:T(8,128)(2,1)S(1)}, bf16[25,64,256]{2,1,0:T(8,128)(2,1)S(1)}, u32[]{:S(2)}, u32[]{:S(2)}) collective-permute-start(bf16[25,64,256]{2,1,0:T(8,128)(2,1)S(1)} %get-tuple-element.91), channel_id=1, source_target_pairs={{0,1},{1,0},{2,3},{3,2},{4,5},{5,4},{6,7},{7,6},{8,9},{9,8},{10,11... | collective-permute-start | bytes 2457608 | tf_op jit(solution)/shard_map/ppermute | solution.py:396

commit v7 on v6

--- a/solution.py
+++ b/solution.py
@@ -1,6 +1,5 @@
 import functools
 import math
-import operator
 
 import jax
 import jax.numpy as jnp
@@ -193,8 +192,10 @@
             same = (index == index[slot : slot + 1, :])[None]
             merged = merged + jnp.where(same, both[:, slot : slot + 1, :], 0.0)
         atom = lax.broadcasted_iota(jnp.int32, (slots, HALO), 1)
-        message[: 2 * heads * slots, :] = merged.reshape(2 * heads * slots, HALO).astype(BF16)
-        message[2 * heads * slots :, :] = (index - HALO - atom).astype(F32).astype(BF16)
+        edge_rows = 2 * heads * slots
+        message[:edge_rows, :] = merged.reshape(edge_rows, HALO)
+        message[edge_rows : edge_rows + slots, :] = (index - HALO - atom).astype(F32)
+        message[edge_rows + slots :, :] = jnp.zeros_like(message[edge_rows + slots :, :])
 
 
 def joined_rows(early, late, first_row, rows):
@@ -213,7 +214,7 @@
     atoms = 2 * HALO
     core = place[0]
     empty = jnp.zeros((HALO, HALO), BF16)
-    coefs = [message[: 2 * heads * slots, :].astype(F32).T for message in (message_a, message_b)]
+    coefs = [message[: 2 * heads * slots, :].T for message in (message_a, message_b)]
     for head in range(heads):
         tables = []
         for quantity in (head, heads + head):
@@ -266,80 +267,57 @@
 def halo_slots(message_left, message_right, quantities, slots):
     coefs, tables = [], []
     for message, tile in ((message_left, 2), (message_right, 0)):
-        coefs.append(message[: quantities * slots, :].astype(F32).T)
-        offset = message[quantities * slots :, :].astype(F32).astype(jnp.int32)
+        coefs.append(message[: quantities * slots, :].T)
+        offset = message[quantities * slots : (quantities + 1) * slots, :].astype(jnp.int32)
         atom = lax.broadcasted_iota(jnp.int32, offset.shape, 1)
         tables.append(slot_tile(wide_transpose(offset + HALO + atom)[:, :slots], tile))
     return coefs, tables
 
 
-def key_kernel(heads, slots, grad_query, own_key, halo_a, halo_b, message_left, message_right, wc,
-               terms, token, grad):
+def final_kernel(heads, slots, start, grad_query, own_key, own_value, halo_qkv, cl, cr,
+                 message_left, message_right, wc, mine, theirs, token, grad):
     token[...] = jnp.zeros_like(token)
-    comps, chan_local = grad_query.shape[0], grad_query.shape[1]
+    comps, chan_local = halo_qkv.shape[0], cl.shape[1]
     rows = chan_local // heads
-    grad[:, :chan_local, :] = grad_query[...]
-    coefs, tables = halo_slots(message_left, message_right, 2 * heads, slots)
-    for head in range(heads):
-        query = joined_rows(halo_a, halo_b, head * rows, rows)
-        rim = jnp.concatenate(
-            [
-                nn(query[:, :HALO], spread(tables[0], coefs[0], head, slots)),
-                nn(query[:, HALO:], spread(tables[1], coefs[1], head, slots)),
-            ],
-            axis=1,
-        )
-        total = head_rows_of(own_key, head * rows, rows) + rim
-        span = slice(chan_local + head * rows, chan_local + (head + 1) * rows)
-        grad[:, span, :] = total.astype(BF16).reshape(comps, rows, 2 * HALO)
-    for comp in range(comps):
-        terms[comp] = nn(wc[degree_of(comp)][:, : 2 * chan_local], grad[comp])
-
-
-def value_kernel(heads, slots, start, stop, own_value, cl, cr, message_left, message_right, wc, terms,
-                 mine, token, *theirs):
-    *theirs, grad = theirs
-    token[...] = jnp.zeros_like(token)
-    comps, chan_local = stop - start, cl.shape[1]
-    rows = chan_local // heads
+    stop = start + comps
+    grad[:, :chan_local, :] = grad_query[start:stop]
     coefs, tables = halo_slots(message_left, message_right, 2 * heads, slots)
     for head in range(heads):
         span = slice(head * rows, (head + 1) * rows)
-        rim = jnp.concatenate(
-            [
-                nn(cl[start:stop, span, :].reshape(comps * rows, HALO),
-                   spread(tables[0], coefs[0], heads + head, slots)),
-                nn(cr[start:stop, span, :].reshape(comps * rows, HALO),
-                   spread(tables[1], coefs[1], heads + head, slots)),
-            ],
-            axis=1,
+        query = head_rows_of(halo_qkv, head * rows, rows)
+        sides = (
+            (own_key, chan_local, head, (query[:, :HALO], query[:, HALO:])),
+            (
+                own_value,
+                2 * chan_local,
+                heads + head,
+                tuple(side[start:stop, span, :].reshape(comps * rows, HALO) for side in (cl, cr)),
+            ),
         )
-        own = own_value[start:stop, span, :].reshape(comps * rows, 2 * HALO)
-        grad[:, span, :] = (own + rim).astype(BF16).reshape(comps, rows, 2 * HALO)
+        for own, first, quantity, outer in sides:
+            rim = [
+                nn(outer[at], spread(tables[at], coefs[at], quantity, slots)) for at in range(2)
+            ]
+            total = own[start:stop, span, :].reshape(comps * rows, 2 * HALO)
+            total = total + jnp.concatenate(rim, axis=1)
+            grad[:, first + head * rows : first + (head + 1) * rows, :] = (
+                total.astype(BF16).reshape(comps, rows, 2 * HALO)
+            )
     for comp in range(comps):
-        mix = wc[degree_of(start + comp)][:, 2 * chan_local :]
-        total = terms[start + comp] + nn(mix, grad[comp])
+        total = nn(wc[degree_of(start + comp)], grad[comp])
         mine[comp] = total[:chan_local]
-        part = theirs[0].shape[0]
-        theirs[comp // part][comp % part] = total[chan_local:].astype(BF16)
-
-
-def finish_kernel(parts, *refs):
-    *refs, out = refs
-    start = 0
-    for count in parts:
-        mine, theirs, refs = refs[0], refs[1 : count + 1], refs[count + 1 :]
-        at = 0
-        for part in theirs:
-            size = part.shape[0]
-            total = mine[at : at + size] + part[...].astype(F32)
-            out[start + at : start + at + size] = total.astype(BF16)
-            at += size
-        start += at
-
-
-def gather_kernel(place, part_0, part_1, part_2, part_3, out, token):
-    token[...] = jnp.zeros_like(token)
+        theirs[comp] = total[chan_local:].astype(BF16)
+
+
+def finish_kernel(*refs):
+    out, start = refs[-1], 0
+    for mine, theirs in zip(refs[:-1:2], refs[1:-1:2]):
+        stop = start + mine.shape[0]
+        out[start:stop] = (mine[...] + theirs[...].astype(F32)).astype(BF16)
+        start = stop
+
+
+def gather_kernel(place, part_0, part_1, part_2, part_3, out):
     piece = part_0.shape[1]
     spot = place[2]
     for delta, part in enumerate((part_0, part_1, part_2, part_3)):
@@ -399,12 +377,6 @@
 def exchanged(value, axis, offset):
     count = lax.axis_size(axis)
     return lax.ppermute(value, axis, [(source, source ^ offset) for source in range(count)])
-
-
-def crossed(value, target):
-    count = lax.axis_size("atom")
-    pairs = [(2 * at + core, 2 * target(at) + 1 - core) for at in range(count) for core in range(2)]
-    return shifted(lax.ppermute(value, ("atom", "chan"), pairs), "chan", 1)
 
 
 def on_device(features, weights, cotangent, edge_bias, neighbours, valid_mask):
@@ -422,9 +394,7 @@
     place = jnp.stack([lax.axis_index("chan"), atom_place * atoms_dev, spot])
     place = place.astype(jnp.int32)
     feature_cut = comps // 2
-    value_cut = comps // 2
     feature_cuts = ((0, feature_cut), (feature_cut, comps))
-    cuts = ((0, value_cut), (value_cut, comps))
 
     def held(*dims, dtype=F32):
         return pltpu.VMEM(dims, dtype)
@@ -498,13 +468,13 @@
         (
             held(comps - feature_cut, 3 * chan_local, atoms_dev, dtype=BF16),
             plain(heads, slots, atoms_dev),
-            held((2 * heads + 1) * slots, HALO, dtype=BF16),
-            held((2 * heads + 1) * slots, HALO, dtype=BF16),
+            held((2 * heads + 3) * slots, HALO),
+            held((2 * heads + 3) * slots, HALO),
         ),
         stay=(*range(len(late_chunks) + 5), len(late_chunks) + 7, len(late_chunks) + 8),
     )
-    message_left = crossed(message_b, lambda at: (at + 1) % count)
-    message_right = crossed(message_a, lambda at: (at - 1) % count)
+    message_left = shifted(message_b, "atom", 1)
+    message_right = shifted(message_a, "atom", -1)
     piece = (3 * (LMAX + 1), chan_local // 4, channels)
     grad_query, own_key, own_value, kept, *sent = call(
         functools.partial(grads_kernel, heads, slots, len(feature_cuts)),
@@ -528,65 +498,49 @@
     )
     for delta, part in enumerate(sent, 1):
         kept = kept + exchanged(part, "atom", delta << cut_bits[0]).astype(F32)
-    rest = [bit for bit in range(count.bit_length() - 1) if bit not in cut_bits]
-    while rest:
-        offsets = [1 << bit for bit in rest[:2]]
-        rest = rest[2:]
-        rounded = kept.astype(BF16)
-        offsets += [sum(offsets)] * (len(offsets) - 1)
-        arrived = [
-            crossed(rounded, functools.partial(operator.xor, offset))
-            if offset == 1
-            else exchanged(rounded, "atom", offset)
-            for offset in offsets
-        ]
-        kept = functools.reduce(lambda total, part: total + part.astype(F32), arrived, kept)
-    terms, token = call(
-        functools.partial(key_kernel, heads, slots),
-        (grad_query, own_key, halo_a, halo_b, message_left, message_right, wc),
-        (held(comps, channels, atoms_dev), plain(8, HALO)),
-        scratch=[pltpu.VMEM((comps, 2 * chan_local, atoms_dev), BF16)],
-        limit=16,
-        stay=(0, 1, 2, 3, 6),
-    )
-    from_left, from_right, rounded = after((from_left, from_right, kept.astype(BF16)), (token,))
+    rest = [bit for bit in reversed(range(count.bit_length() - 1)) if bit not in cut_bits]
+    for bit in rest:
+        arrived = exchanged(kept.astype(BF16), "atom", 1 << bit)
+        if bit == rest[-1]:
+            from_left, from_right, message_left, message_right, arrived = after(
+                (from_left, from_right, message_left, message_right, arrived), ()
+            )
+        kept = kept + arrived.astype(F32)
+    rounded = kept.astype(BF16)
     pieces = [rounded] + [exchanged(rounded, "atom", d << cut_bits[0]) for d in range(1, 4)]
-    grad_weights, gathered = call(
+    (grad_weights,) = call(
         gather_kernel,
         (place, *pieces),
-        (plain(3 * (LMAX + 1), chan_local, channels), plain(8, HALO)),
+        (plain(3 * (LMAX + 1), chan_local, channels),),
         scalars=1,
         limit=8,
         flops=20 * 10**9,
     )
-    parts, counts = [], []
-    tokens = ()
-    for start, stop in cuts:
+    parts, tokens = [], ()
+    for (start, stop), halo_qkv in zip(feature_cuts, (halo_a, halo_b)):
         size = stop - start
-        sizes = [size]
-        mine, token, *theirs = call(
-            functools.partial(value_kernel, heads, slots, start, stop),
-            (own_value, from_left, from_right, message_left, message_right, wc, terms),
+        mine, theirs, token = call(
+            functools.partial(final_kernel, heads, slots, start),
+            (grad_query, own_key, own_value, halo_qkv, from_left, from_right, message_left,
+             message_right, wc),
             (
                 held(size, chan_local, atoms_dev),
+                held(size, chan_local, atoms_dev, dtype=BF16),
                 plain(8, HALO),
-                *(held(some, chan_local, atoms_dev, dtype=BF16) for some in sizes),
             ),
-            scratch=[pltpu.VMEM((size, chan_local, atoms_dev), BF16)],
+            scratch=[pltpu.VMEM((size, 3 * chan_local, atoms_dev), BF16)],
             limit=16,
-            stay=(0, 1, 2, 5, 6),
+            stay=(0, 1, 2, 3, 4, 5, 8),
             tokens=tokens,
         )
+        parts += [mine, shifted(theirs, "chan", 1)]
         tokens = (token, pieces[2])
-        counts.append(len(sizes))
-        parts += [mine, *(shifted(some, "chan", 1) for some in theirs)]
     (out,) = call(
-        functools.partial(finish_kernel, counts),
+        finish_kernel,
         parts,
         (plain(comps, chan_local, atoms_dev, dtype=BF16),),
         limit=8,
         stay=tuple(range(len(parts))),
-        tokens=(gathered,),
     )
     grad_features = jnp.transpose(out, (1, 0, 2))
     grad_weights = grad_weights.reshape(3, LMAX + 1, chan_local, channels)

time: 111 us -> 101 us (0.910)
  waiting for transfers between devices: 38.7 us -> 34.4 us
  starting transfers between devices: 38 us -> 34.8 us
  local copies, waits for them, and re-layouts: 4.55 us -> 2.41 us
    ppermute x3 -> x0, waiting for transfers between devices: 7.02 us -> none  [crossed(): return shifted(lax.ppermute(value, ('atom', 'chan'), pairs), 'chan', 1)]
    ppermute x16 -> x15, waiting for transfers between devices: 18.6 us -> 24 us  [shifted(): return lax.ppermute(value, axis, pairs)]
    ppermute x3 -> x0, starting transfers between devices: 5.34 us -> none  [crossed(): return shifted(lax.ppermute(value, ('atom', 'chan'), pairs), 'chan', 1)]
    ppermute x8, waiting for transfers between devices: 13 us -> 10.4 us  [exchanged(): lax.ppermute(value, axis, [(source, source ^ offset) for source in range(...]
    ppermute x16 -> x15, starting transfers between devices: 21.2 us -> 23.6 us  [shifted(): return lax.ppermute(value, axis, pairs)]
    unnamed x12, local copies, waits for them, and re-layouts: 4.55 us -> 2.41 us
    pallas_call x9 -> x8, Pallas kernels: 25.7 us -> 25.6 us  [call(): pl.pallas_call(body, out_shape=tuple(outs), in_specs=[small] * scalars +...]
  transfers between devices with their start and end apart: 27 -> 23, of which waited for: 12 -> 10; matrix products, arithmetic and copies ran while one was open for 0% -> 0% of each run, Pallas kernels for 24% -> 26%
where the time goes in v7:
time: 101 us
  starting transfers between devices  34.8 us (34%)
  waiting for transfers between devices  34.4 us (34%)
  Pallas kernels  28.1 us (28%)
  local copies, waits for them, and re-layouts  2.41 us (2%)
    pallas_call x8, Pallas kernels, call(): pl.pallas_call(body, out_shape=tuple(outs), in_specs=[small] * scalars +...  25.6 us
    ppermute x15, waiting for transfers between devices, shifted(): return lax.ppermute(value, axis, pairs)  24 us
    ppermute x15, starting transfers between devices, shifted(): return lax.ppermute(value, axis, pairs)  23.6 us
    ppermute x8, starting transfers between devices, exchanged(): lax.ppermute(value, axis, [(source, source ^ offset) for source in range(...  11.2 us
    ppermute x8, waiting for transfers between devices, exchanged(): lax.ppermute(value, axis, [(source, source ^ offset) for source in range(...  10.4 us
    pallas_call x1, Pallas kernels, on_device(): pl.pallas_call(functools.partial(split_kernel, feature_cuts), out_shape=t...  2.54 us
    unnamed x12, local copies, waits for them, and re-layouts  2.41 us
  transfers between devices with their start and end apart: 23, of which 10 were waited for; matrix products, arithmetic and copies ran while one was open for 0% of the time, Pallas kernels for 26%

profile of v7, /device:TPU:0, one launch (start us, length us, event | category | flops | bytes accessed | tf_op | source)
XLA Modules:
  0.0 100.7 jit_solution(2734443905502810122)
XLA Ops:
  0.7 0.5 collective-permute-start
  1.2 2.5 %shard_map.85 = (bf16[24,64,128]{2,1,0:T(8,128)(2,1)}, bf16[24,64,128]{2,1,0:T(8,128)(2,1)}, bf16[25,64,128]{2,1,0:T(8,128)(2,1)}, bf16[25,64,128]{2,1,0:T(8,128)(2,1)}) custom-call(bf16[49,64,256]{2,1,0:T(8,128)(2,1)} %bitcast.15), custom_call_target="tpu_custom_call" | custom-call | tf_op jit(solution)/shard_map/pallas_call | solution.py:410
  3.7 2.7 %collective-permute-start.1 = (bf16[24,64,128]{2,1,0:T(8,128)(2,1)}, bf16[24,64,128]{2,1,0:T(8,128)(2,1)S(1)}, u32[]{:S(2)}, u32[]{:S(2)}) collective-permute-start(bf16[24,64,128]{2,1,0:T(8,128)(2,1)} %get-tuple-element.47), channel_id=1, source_target_pairs={{0,2},{2,4},{4,6},{6,8},{8,10},{10,12},{12,14},{14,16},{16,18},{18... | collective-permute-start | bytes 1179656 | tf_op jit(solution)/shard_map/ppermute | solution.py:374
  6.4 4.1 %collective-permute-start.2 = (bf16[24,64,128]{2,1,0:T(8,128)(2,1)}, bf16[24,64,128]{2,1,0:T(8,128)(2,1)S(1)}, u32[]{:S(2)}, u32[]{:S(2)}) collective-permute-start(bf16[24,64,128]{2,1,0:T(8,128)(2,1)} %get-tuple-element.48), channel_id=1, source_target_pairs={{0,30},{2,0},{4,2},{6,4},{8,6},{10,8},{12,10},{14,12},{16,14},{18,... | collective-permute-start | bytes 1179656 | tf_op jit(solution)/shard_map/ppermute | solution.py:374
  10.5 0.0 collective-permute-start.5
  10.5 5.6 %collective-permute-start.6 = (bf16[25,64,128]{2,1,0:T(8,128)(2,1)}, bf16[25,64,128]{2,1,0:T(8,128)(2,1)S(1)}, u32[]{:S(2)}, u32[]{:S(2)}) collective-permute-start(bf16[25,64,128]{2,1,0:T(8,128)(2,1)} %get-tuple-element.53), channel_id=1, source_target_pairs={{0,30},{2,0},{4,2},{6,4},{8,6},{10,8},{12,10},{14,12},{16,14},{18,... | collective-permute-start | bytes 1228808 | tf_op jit(solution)/shard_map/ppermute | solution.py:374
  16.1 0.1 pad_add_fusion.refs_0_
  16.2 0.0 collective-permute-done.refs_2_
  16.2 0.0 copy-start.1
  16.2 1.4 %copy-done.1 = bf16[64,49,256]{2,0,1:T(8,128)(2,1)S(1)} copy-done((bf16[64,49,256]{2,0,1:T(8,128)(2,1)S(1)}, bf16[64,49,256]{2,0,1:T(8,128)(2,1)}, u32[]{:S(2)}) %copy-start.1) | copy-done | bytes 1605656
  17.6 1.0 copy-done.4
  18.6 4.7 %shard_map.86 = (bf16[49,192,256]{2,1,0:T(8,128)(2,1)S(1)}, f32[8,256,256]{2,1,0:T(8,128)S(1)}, s32[2,3,128,128]{3,2,1,0:T(8,128)S(1)}, s32[16,256]{1,0:T(8,128)...) custom-call(s32[3]{0:T(128)S(1)} %pad_add_fusion.refs_0_, ...), custom_call_target="tpu_custom_call" | custom-call | flops 12000000000 | bytes 1024 | tf_op jit(solution)/shard_map/pallas_call | solution.py:340
  23.3 10.1 %collective-permute-done.1.refs_0_ = bf16[24,64,128]{2,1,0:T(8,128)(2,1)S(1)} collective-permute-done((bf16[24,64,128]{2,1,0:T(8,128)(2,1)}, bf16[24,64,128]{2,1,0:T(8,128)(2,1)S(1)}, u32[]{:S(2)}, u32[]{:S(2)}) %collective-permute-start.1) | collective-permute-done | bytes 393248 | tf_op jit(solution)/shard_map/ppermute | solution.py:374
  33.4 0.5 collective-permute-start.4
  33.9 1.2 %collective-permute-done.3.refs_1_.refs_4_ = bf16[24,64,128]{2,1,0:T(8,128)(2,1)S(1)} collective-permute-done((bf16[24,64,128]{2,1,0:T(8,128)(2,1)S(1)}, bf16[24,64,128]{2,1,0:T(8,128)(2,1)S(1)}, u32[]{:S(2)}, u32[]{:S(2)}) %collective-permute-start.3) | collective-permute-done | bytes 393248 | tf_op jit(solution)/shard_map/ppermute | solution.py:374
  35.1 0.6 collective-permute-done.4.refs_3_.refs_6_
  35.7 1.3 %shard_map.88 = (bf16[24,192,256]{2,1,0:T(8,128)(2,1)S(1)}, f32[8,2,128,128]{3,2,1,0:T(8,128)S(1)}, f32[8,128]{1,0:T(8,128)S(1)}) custom-call(bf16[24,64,128]{2,1,0:T(8,128)(2,1)S(1)} %get-tuple-element.50.refs_0_.refs_3_, bf16[24,64,128]{2,1,0:T(8,128)(2,1)S(1)} %collective-permute-done.3.refs_1_.refs_4_, ...), custom_call_target="tpu_custom_call" | custom-call | bytes 1024 | tf_op jit(solution)/shard_map/pallas_call | solution.py:340
  37.0 0.0 copy-start.2
  37.0 0.0 copy-start.3
  37.0 4.6 %collective-permute-done.5.refs_0_ = bf16[25,64,128]{2,1,0:T(8,128)(2,1)S(1)} collective-permute-done((bf16[25,64,128]{2,1,0:T(8,128)(2,1)}, bf16[25,64,128]{2,1,0:T(8,128)(2,1)S(1)}, u32[]{:S(2)}, u32[]{:S(2)}) %collective-permute-start.5) | collective-permute-done | bytes 409632 | tf_op jit(solution)/shard_map/ppermute | solution.py:374
  41.6 1.8 %collective-permute-done.6.refs_1_ = bf16[25,64,128]{2,1,0:T(8,128)(2,1)S(1)} collective-permute-done((bf16[25,64,128]{2,1,0:T(8,128)(2,1)}, bf16[25,64,128]{2,1,0:T(8,128)(2,1)S(1)}, u32[]{:S(2)}, u32[]{:S(2)}) %collective-permute-start.6) | collective-permute-done | bytes 409632 | tf_op jit(solution)/shard_map/ppermute | solution.py:374
  43.4 0.5 collective-permute-start.8
  44.0 1.5 %collective-permute-start.9 = (bf16[49,64,128]{2,1,0:T(8,128)(2,1)S(1)}, bf16[49,64,128]{2,1,0:T(8,128)(2,1)S(1)}, u32[]{:S(2)}, u32[]{:S(2)}) collective-permute-start(bf16[49,64,128]{2,1,0:T(8,128)(2,1)S(1)} %get-tuple-element.73), channel_id=1, source_target_pairs={{0,2},{2,4},{4,6},{6,8},{8,10},{10,12},{12,14},{14,16},{16,18},{18... | collective-permute-start | bytes 2408456 | tf_op jit(solution)/shard_map/ppermute | solution.py:374
  45.4 4.1 %collective-permute-start.10 = (bf16[49,64,128]{2,1,0:T(8,128)(2,1)S(1)}, bf16[49,64,128]{2,1,0:T(8,128)(2,1)S(1)}, u32[]{:S(2)}, u32[]{:S(2)}) collective-permute-start(bf16[49,64,128]{2,1,0:T(8,128)(2,1)S(1)} %get-tuple-element.74), channel_id=1, source_target_pairs={{0,30},{2,0},{4,2},{6,4},{8,6},{10,8},{12,10},{14,12},{16,14},{18,... | collective-permute-start | bytes 2408456 | tf_op jit(solution)/shard_map/ppermute | solution.py:374
  49.6 3.8 %shard_map.90 = (bf16[25,192,256]{2,1,0:T(8,128)(2,1)S(1)}, f32[4,16,256]{2,1,0:T(8,128)}, f32[176,128]{1,0:T(8,128)S(1)}, f32[176,128]{1,0:T(8,128)S(1)}) custom-call(bf16[25,64,128]{2,1,0:T(8,128)(2,1)S(1)} %get-tuple-element.57.refs_0_.refs_7_, bf16[25,64,128]{2,1,0:T(8,128)(2,1)S(1)} %collective-permute-done.7.refs_1_.refs_8_, ...), custom_call_target="tpu_custom_call" | custom-call | bytes 1024 | tf_op jit(solution)/shard_map/pallas_call | solution.py:340
  53.4 7.7 %shard_map.91 = (bf16[49,64,256]{2,1,0:T(8,128)(2,1)S(1)}, f32[49,64,256]{2,1,0:T(8,128)S(1)}, f32[49,64,256]{2,1,0:T(8,128)S(1)}, f32[21,16,128]{2,1,0:T(8,128)...) custom-call(s32[3]{0:T(128)S(1)} %pad_add_fusion.refs_0_, ...), custom_call_target="tpu_custom_call" | custom-call | bytes 1024 | tf_op jit(solution)/shard_map/pallas_call | solution.py:340
  61.2 0.1 collective-permute-start.13
  61.2 0.3 collective-permute-start.14
  61.5 3.2 %collective-permute-start.15 = (bf16[21,16,128]{2,1,0:T(8,128)(2,1)S(1)}, bf16[21,16,128]{2,1,0:T(8,128)(2,1)S(1)}, u32[]{:S(2)}, u32[]{:S(2)}) collective-permute-start(bf16[21,16,128]{2,1,0:T(8,128)(2,1)S(1)} %get-tuple-element.78), channel_id=1, source_target_pairs={{0,12},{2,14},{4,8},{6,10},{8,4},{10,6},{12,0},{14,2},{16,28},{18,... | collective-permute-start | bytes 258056 | tf_op jit(solution)/shard_map/ppermute | solution.py:379
  64.7 6.5 %collective-permute-done.13 = bf16[21,16,128]{2,1,0:T(8,128)(2,1)S(1)} collective-permute-done((bf16[21,16,128]{2,1,0:T(8,128)(2,1)S(1)}, bf16[21,16,128]{2,1,0:T(8,128)(2,1)S(1)}, u32[]{:S(2)}, u32[]{:S(2)}) %collective-permute-start.13) | collective-permute-done | bytes 86048 | tf_op jit(solution)/shard_map/ppermute | solution.py:379
  71.2 0.1 fusion.1
  71.3 1.9 %collective-permute-start.16 = (bf16[21,16,128]{2,1,0:T(8,128)(2,1)S(1)}, bf16[21,16,128]{2,1,0:T(8,128)(2,1)S(1)}, u32[]{:S(2)}, u32[]{:S(2)}) collective-permute-start(bf16[21,16,128]{2,1,0:T(8,128)(2,1)S(1)} %get-tuple-element.91), channel_id=1, source_target_pairs={{0,16},{2,18},{4,20},{6,22},{8,24},{10,26},{12,28},{14,30},{16,0},... | collective-permute-start | bytes 258056 | tf_op jit(solution)/shard_map/ppermute | solution.py:379
  73.2 3.5 %collective-permute-start.12 = (f32[176,128]{1,0:T(8,128)S(1)}, f32[176,128]{1,0:T(8,128)S(1)}, u32[]{:S(2)}, u32[]{:S(2)}) collective-permute-start(f32[176,128]{1,0:T(8,128)S(1)} %get-tuple-element.66.refs_16_), channel_id=1, source_target_pairs={{0,30},{2,0},{4,2},{6,4},{8,6},{10,8},{12,10},{14,12},{16,14},{18,... | collective-permute-start | bytes 270344 | tf_op jit(solution)/shard_map/ppermute | solution.py:374
  76.7 0.0 collective-permute-start.11
  76.7 1.0 %collective-permute-done.16 = bf16[21,16,128]{2,1,0:T(8,128)(2,1)S(1)} collective-permute-done((bf16[21,16,128]{2,1,0:T(8,128)(2,1)S(1)}, bf16[21,16,128]{2,1,0:T(8,128)(2,1)S(1)}, u32[]{:S(2)}, u32[]{:S(2)}) %collective-permute-start.16) | collective-permute-done | bytes 86048 | tf_op jit(solution)/shard_map/ppermute | solution.py:379
  77.7 2.2 %collective-permute-start.17 = (bf16[21,16,128]{2,1,0:T(8,128)(2,1)S(1)}, bf16[21,16,128]{2,1,0:T(8,128)(2,1)S(1)}, u32[]{:S(2)}, u32[]{:S(2)}) collective-permute-start(bf16[21,16,128]{2,1,0:T(8,128)(2,1)S(1)} %fusion), channel_id=1, source_target_pairs={{0,2},{2,0},{4,6},{6,4},{8,10},{10,8},{12,14},{14,12},{16,18},{18,... | collective-permute-start | bytes 258056 | tf_op jit(solution)/shard_map/ppermute | solution.py:379
  79.9 5.2 %collective-permute-done.12.refs_3_ = f32[176,128]{1,0:T(8,128)S(1)} collective-permute-done((f32[176,128]{1,0:T(8,128)S(1)}, f32[176,128]{1,0:T(8,128)S(1)}, u32[]{:S(2)}, u32[]{:S(2)}) %collective-permute-start.12) | collective-permute-done | bytes 90144 | tf_op jit(solution)/shard_map/ppermute | solution.py:374
  85.1 2.8 %collective-permute-done.17.refs_4_ = bf16[21,16,128]{2,1,0:T(8,128)(2,1)S(1)} collective-permute-done((bf16[21,16,128]{2,1,0:T(8,128)(2,1)S(1)}, bf16[21,16,128]{2,1,0:T(8,128)(2,1)S(1)}, u32[]{:S(2)}, u32[]{:S(2)}) %collective-permute-start.17) | collective-permute-done | bytes 86048 | tf_op jit(solution)/shard_map/ppermute | solution.py:379
  88.0 1.3 %collective-permute-start.19 = (bf16[21,16,128]{2,1,0:T(8,128)(2,1)S(1)}, bf16[21,16,128]{2,1,0:T(8,128)(2,1)S(1)}, u32[]{:S(2)}, u32[]{:S(2)}) collective-permute-start(bf16[21,16,128]{2,1,0:T(8,128)(2,1)S(1)} %add_convert_fusion.refs_1_), channel_id=1, source_target_pairs={{0,8},{2,10},{4,12},{6,14},{8,0},{10,2},{12,4},{14,6},{16,24},{18,... | collective-permute-start | bytes 258056 | tf_op jit(solution)/shard_map/ppermute | solution.py:379
  89.3 1.5 %collective-permute-start.22 = (bf16[21,16,128]{2,1,0:T(8,128)(2,1)S(1)}, bf16[21,16,128]{2,1,0:T(8,128)(2,1)S(1)}, u32[]{:S(2)}, u32[]{:S(2)}) collective-permute-start(bf16[21,16,128]{2,1,0:T(8,128)(2,1)S(1)} %add_convert_fusion.refs_1_), channel_id=1, source_target_pairs={{0,12},{2,14},{4,8},{6,10},{8,4},{10,6},{12,0},{14,2},{16,28},{18,... | collective-permute-start | bytes 258056 | tf_op jit(solution)/shard_map/ppermute | solution.py:379
  90.7 0.8 collective-permute-start.21
  91.5 2.5 %shard_map.94 = (f32[24,64,256]{2,1,0:T(8,128)S(1)}, bf16[24,64,256]{2,1,0:T(8,128)(2,1)S(1)}, f32[8,128]{1,0:T(8,128)S(1)}) custom-call(bf16[49,64,256]{2,1,0:T(8,128)(2,1)S(1)} %get-tuple-element.68.refs_0_, f32[49,64,256]{2,1,0:T(8,128)S(1)} %get-tuple-element.69.refs_1_, f32[49,64,256]{2,1,0:T(8,128)S(1)} %get-tuple-element.70.refs_2_, ...), custom_call_target="tpu_custom_call" | custom-call | bytes 1024 | tf_op jit(solution)/shard_map/pallas_call | solution.py:340
  94.1 0.1 collective-permute-start.18
  94.2 2.6 %shard_map.95 = (f32[25,64,256]{2,1,0:T(8,128)S(1)}, bf16[25,64,256]{2,1,0:T(8,128)(2,1)S(1)}, f32[8,128]{1,0:T(8,128)}) custom-call(bf16[49,64,256]{2,1,0:T(8,128)(2,1)S(1)} %get-tuple-element.68.refs_0_, f32[49,64,256]{2,1,0:T(8,128)S(1)} %get-tuple-element.69.refs_1_, f32[49,64,256]{2,1,0:T(8,128)S(1)} %get-tuple-element.70.refs_2_, ...), custom_call_target="tpu_custom_call" | custom-call | bytes 1024 | tf_op jit(solution)/shard_map/pallas_call | solution.py:340
  96.7 0.6 collective-permute-start.20
  97.3 1.4 %shard_map.97 = f32[21,64,128]{2,1,0:T(8,128)} custom-call(s32[3]{0:T(128)S(1)} %pad_add_fusion.refs_0_, bf16[21,16,128]{2,1,0:T(8,128)(2,1)S(1)} %add_convert_fusion.refs_1_, bf16[21,16,128]{2,1,0:T(8,128)(2,1)S(1)} %collective-permute-done.21.refs_2_, bf16[21,16,128]{2,1,0:T(8,128)(2,1)S(1)} %collective-permute-done.19.refs_10_.refs_3_, ...), custom_call_target="tpu_custom_call" | custom-call | flops 20000000000 | bytes 1024 | tf_op jit(solution)/shard_map/pallas_call | solution.py:340
  98.7 0.5 collective-permute-done.20.refs_3_
  99.2 1.5 %shard_map.96 = bf16[49,64,256]{2,1,0:T(8,128)(2,1)} custom-call(f32[24,64,256]{2,1,0:T(8,128)S(1)} %get-tuple-element.84.refs_0_, bf16[24,64,256]{2,1,0:T(8,128)(2,1)S(1)} %collective-permute-done.18.refs_1_, f32[25,64,256]{2,1,0:T(8,128)S(1)} %get-tuple-element.88.refs_2_, bf16[25,64,256]{2,1,0:T(8,128)(2,1)S(1)} %collective-permute-done.20.refs_3_), custom_call_target="tpu_custom_call" | custom-call | bytes 1024 | tf_op jit(solution)/shard_map/pallas_call | solution.py:340
  (27 shorter events, 0.1 us)
Async XLA Ops:
  0.6 15.5 %copy-start.5 = (s32[16,256]{1,0:T(8,128)S(1)}, s32[16,256]{1,0:T(8,128)}, u32[]{:S(2)}) copy-start(s32[16,256]{1,0:T(8,128)} %refs_5_.1) | copy-start | bytes 49156
  0.6 15.5 %copy-start = (bf16[64,49,256]{2,0,1:T(8,128)(2,1)S(1)}, bf16[64,49,256]{2,0,1:T(8,128)(2,1)}, u32[]{:S(2)}) copy-start(bf16[64,49,256]{2,0,1:T(8,128)(2,1)} %param.8) | copy-start | bytes 4816900
  0.7 15.5 %collective-permute-start = (bf16[49,64,256]{2,1,0:T(8,128)(2,1)}, bf16[49,64,256]{2,1,0:T(8,128)(2,1)}, u32[]{:S(2)}, u32[]{:S(2)}) collective-permute-start(bf16[49,64,256]{2,1,0:T(8,128)(2,1)} %bitcast.14), channel_id=1, source_target_pairs={{0,1},{1,0},{2,3},{3,2},{4,5},{5,4},{6,7},{7,6},{8,9},{9,8},{10,11... | collective-permute-start | bytes 4816904 | tf_op jit(solution)/shard_map/ppermute | solution.py:374
  3.7 29.7 %collective-permute-start.1 = (bf16[24,64,128]{2,1,0:T(8,128)(2,1)}, bf16[24,64,128]{2,1,0:T(8,128)(2,1)S(1)}, u32[]{:S(2)}, u32[]{:S(2)}) collective-permute-start(bf16[24,64,128]{2,1,0:T(8,128)(2,1)} %get-tuple-element.47), channel_id=1, source_target_pairs={{0,2},{2,4},{4,6},{6,8},{8,10},{10,12},{12,14},{14,16},{16,18},{18... | collective-permute-start | bytes 1179656 | tf_op jit(solution)/shard_map/ppermute | solution.py:374
  6.4 27.0 %collective-permute-start.2 = (bf16[24,64,128]{2,1,0:T(8,128)(2,1)}, bf16[24,64,128]{2,1,0:T(8,128)(2,1)S(1)}, u32[]{:S(2)}, u32[]{:S(2)}) collective-permute-start(bf16[24,64,128]{2,1,0:T(8,128)(2,1)} %get-tuple-element.48), channel_id=1, source_target_pairs={{0,30},{2,0},{4,2},{6,4},{8,6},{10,8},{12,10},{14,12},{16,14},{18,... | collective-permute-start | bytes 1179656 | tf_op jit(solution)/shard_map/ppermute | solution.py:374
  10.5 31.1 %collective-permute-start.5 = (bf16[25,64,128]{2,1,0:T(8,128)(2,1)}, bf16[25,64,128]{2,1,0:T(8,128)(2,1)S(1)}, u32[]{:S(2)}, u32[]{:S(2)}) collective-permute-start(bf16[25,64,128]{2,1,0:T(8,128)(2,1)} %get-tuple-element.52), channel_id=1, source_target_pairs={{0,2},{2,4},{4,6},{6,8},{8,10},{10,12},{12,14},{14,16},{16,18},{18... | collective-permute-start | bytes 1228808 | tf_op jit(solution)/shard_map/ppermute | solution.py:374
  10.5 33.0 %collective-permute-start.6 = (bf16[25,64,128]{2,1,0:T(8,128)(2,1)}, bf16[25,64,128]{2,1,0:T(8,128)(2,1)S(1)}, u32[]{:S(2)}, u32[]{:S(2)}) collective-permute-start(bf16[25,64,128]{2,1,0:T(8,128)(2,1)} %get-tuple-element.53), channel_id=1, source_target_pairs={{0,30},{2,0},{4,2},{6,4},{8,6},{10,8},{12,10},{14,12},{16,14},{18,... | collective-permute-start | bytes 1228808 | tf_op jit(solution)/shard_map/ppermute | solution.py:374
  16.2 1.4 %copy-start.1 = (bf16[64,49,256]{2,0,1:T(8,128)(2,1)S(1)}, bf16[64,49,256]{2,0,1:T(8,128)(2,1)}, u32[]{:S(2)}) copy-start(bf16[64,49,256]{2,0,1:T(8,128)(2,1)} %param.6) | copy-start | bytes 4816900
  17.6 1.0 copy-start.4
  33.4 1.7 %collective-permute-start.3 = (bf16[24,64,128]{2,1,0:T(8,128)(2,1)S(1)}, bf16[24,64,128]{2,1,0:T(8,128)(2,1)S(1)}, u32[]{:S(2)}, u32[]{:S(2)}) collective-permute-start(bf16[24,64,128]{2,1,0:T(8,128)(2,1)S(1)} %get-tuple-element.50.refs_0_.refs_3_), channel_id=1, source_target_pairs={{0,1},{1,0},{2,3},{3,2},{4,5},{5,4},{6,7},{7,6},{8,9},{9,8},{10,11... | collective-permute-start | bytes 1179656 | tf_op jit(solution)/shard_map/ppermute | solution.py:374
  33.4 2.3 %collective-permute-start.4 = (bf16[24,64,128]{2,1,0:T(8,128)(2,1)S(1)}, bf16[24,64,128]{2,1,0:T(8,128)(2,1)S(1)}, u32[]{:S(2)}, u32[]{:S(2)}) collective-permute-start(bf16[24,64,128]{2,1,0:T(8,128)(2,1)S(1)} %get-tuple-element.51.refs_2_.refs_5_), channel_id=1, source_target_pairs={{0,1},{1,0},{2,3},{3,2},{4,5},{5,4},{6,7},{7,6},{8,9},{9,8},{10,11... | collective-permute-start | bytes 1179656 | tf_op jit(solution)/shard_map/ppermute | solution.py:374
  37.0 12.6 %copy-start.2 = (f32[4,16,256]{2,1,0:T(8,128)S(1)}, f32[4,16,256]{2,1,0:T(8,128)}, u32[]{:S(2)}) copy-start(f32[4,16,256]{2,1,0:T(8,128)} %refs_9_.1) | copy-start | bytes 196612
  37.0 12.6 %copy-start.3 = (s32[16,256]{1,0:T(8,128)S(1)}, s32[16,256]{1,0:T(8,128)}, u32[]{:S(2)}) copy-start(s32[16,256]{1,0:T(8,128)} %refs_10_.1) | copy-start | bytes 49156
  43.4 6.1 %collective-permute-start.7 = (bf16[25,64,128]{2,1,0:T(8,128)(2,1)S(1)}, bf16[25,64,128]{2,1,0:T(8,128)(2,1)S(1)}, u32[]{:S(2)}, u32[]{:S(2)}) collective-permute-start(bf16[25,64,128]{2,1,0:T(8,128)(2,1)S(1)} %get-tuple-element.57.refs_0_.refs_7_), channel_id=1, source_target_pairs={{0,1},{1,0},{2,3},{3,2},{4,5},{5,4},{6,7},{7,6},{8,9},{9,8},{10,11... | collective-permute-start | bytes 1228808 | tf_op jit(solution)/shard_map/ppermute | solution.py:374
  43.4 6.1 %collective-permute-start.8 = (bf16[25,64,128]{2,1,0:T(8,128)(2,1)S(1)}, bf16[25,64,128]{2,1,0:T(8,128)(2,1)S(1)}, u32[]{:S(2)}, u32[]{:S(2)}) collective-permute-start(bf16[25,64,128]{2,1,0:T(8,128)(2,1)S(1)} %get-tuple-element.58.refs_2_.refs_9_), channel_id=1, source_target_pairs={{0,1},{1,0},{2,3},{3,2},{4,5},{5,4},{6,7},{7,6},{8,9},{9,8},{10,11... | collective-permute-start | bytes 1228808 | tf_op jit(solution)/shard_map/ppermute | solution.py:374
  44.0 44.0 %collective-permute-start.9 = (bf16[49,64,128]{2,1,0:T(8,128)(2,1)S(1)}, bf16[49,64,128]{2,1,0:T(8,128)(2,1)S(1)}, u32[]{:S(2)}, u32[]{:S(2)}) collective-permute-start(bf16[49,64,128]{2,1,0:T(8,128)(2,1)S(1)} %get-tuple-element.73), channel_id=1, source_target_pairs={{0,2},{2,4},{4,6},{6,8},{8,10},{10,12},{12,14},{14,16},{16,18},{18... | collective-permute-start | bytes 2408456 | tf_op jit(solution)/shard_map/ppermute | solution.py:374
  45.4 42.5 %collective-permute-start.10 = (bf16[49,64,128]{2,1,0:T(8,128)(2,1)S(1)}, bf16[49,64,128]{2,1,0:T(8,128)(2,1)S(1)}, u32[]{:S(2)}, u32[]{:S(2)}) collective-permute-start(bf16[49,64,128]{2,1,0:T(8,128)(2,1)S(1)} %get-tuple-element.74), channel_id=1, source_target_pairs={{0,30},{2,0},{4,2},{6,4},{8,6},{10,8},{12,10},{14,12},{16,14},{18,... | collective-permute-start | bytes 2408456 | tf_op jit(solution)/shard_map/ppermute | solution.py:374
  61.2 10.1 %collective-permute-start.13 = (bf16[21,16,128]{2,1,0:T(8,128)(2,1)S(1)}, bf16[21,16,128]{2,1,0:T(8,128)(2,1)S(1)}, u32[]{:S(2)}, u32[]{:S(2)}) collective-permute-start(bf16[21,16,128]{2,1,0:T(8,128)(2,1)S(1)} %get-tuple-element.76), channel_id=1, source_target_pairs={{0,4},{2,6},{4,0},{6,2},{8,12},{10,14},{12,8},{14,10},{16,20},{18,... | collective-permute-start | bytes 258056 | tf_op jit(solution)/shard_map/ppermute | solution.py:379
  61.2 10.0 %collective-permute-start.14 = (bf16[21,16,128]{2,1,0:T(8,128)(2,1)S(1)}, bf16[21,16,128]{2,1,0:T(8,128)(2,1)S(1)}, u32[]{:S(2)}, u32[]{:S(2)}) collective-permute-start(bf16[21,16,128]{2,1,0:T(8,128)(2,1)S(1)} %get-tuple-element.77), channel_id=1, source_target_pairs={{0,8},{2,10},{4,12},{6,14},{8,0},{10,2},{12,4},{14,6},{16,24},{18,... | collective-permute-start | bytes 258056 | tf_op jit(solution)/shard_map/ppermute | solution.py:379
  61.5 9.7 %collective-permute-start.15 = (bf16[21,16,128]{2,1,0:T(8,128)(2,1)S(1)}, bf16[21,16,128]{2,1,0:T(8,128)(2,1)S(1)}, u32[]{:S(2)}, u32[]{:S(2)}) collective-permute-start(bf16[21,16,128]{2,1,0:T(8,128)(2,1)S(1)} %get-tuple-element.78), channel_id=1, source_target_pairs={{0,12},{2,14},{4,8},{6,10},{8,4},{10,6},{12,0},{14,2},{16,28},{18,... | collective-permute-start | bytes 258056 | tf_op jit(solution)/shard_map/ppermute | solution.py:379
  71.3 6.4 %collective-permute-start.16 = (bf16[21,16,128]{2,1,0:T(8,128)(2,1)S(1)}, bf16[21,16,128]{2,1,0:T(8,128)(2,1)S(1)}, u32[]{:S(2)}, u32[]{:S(2)}) collective-permute-start(bf16[21,16,128]{2,1,0:T(8,128)(2,1)S(1)} %get-tuple-element.91), channel_id=1, source_target_pairs={{0,16},{2,18},{4,20},{6,22},{8,24},{10,26},{12,28},{14,30},{16,0},... | collective-permute-start | bytes 258056 | tf_op jit(solution)/shard_map/ppermute | solution.py:379
  73.2 11.9 %collective-permute-start.12 = (f32[176,128]{1,0:T(8,128)S(1)}, f32[176,128]{1,0:T(8,128)S(1)}, u32[]{:S(2)}, u32[]{:S(2)}) collective-permute-start(f32[176,128]{1,0:T(8,128)S(1)} %get-tuple-element.66.refs_16_), channel_id=1, source_target_pairs={{0,30},{2,0},{4,2},{6,4},{8,6},{10,8},{12,10},{14,12},{16,14},{18,... | collective-permute-start | bytes 270344 | tf_op jit(solution)/shard_map/ppermute | solution.py:374
  76.7 8.4 %collective-permute-start.11 = (f32[176,128]{1,0:T(8,128)S(1)}, f32[176,128]{1,0:T(8,128)S(1)}, u32[]{:S(2)}, u32[]{:S(2)}) collective-permute-start(f32[176,128]{1,0:T(8,128)S(1)} %get-tuple-element.67.refs_17_), channel_id=1, source_target_pairs={{0,2},{2,4},{4,6},{6,8},{8,10},{10,12},{12,14},{14,16},{16,18},{18... | collective-permute-start | bytes 270344 | tf_op jit(solution)/shard_map/ppermute | solution.py:374
  77.7 10.2 %collective-permute-start.17 = (bf16[21,16,128]{2,1,0:T(8,128)(2,1)S(1)}, bf16[21,16,128]{2,1,0:T(8,128)(2,1)S(1)}, u32[]{:S(2)}, u32[]{:S(2)}) collective-permute-start(bf16[21,16,128]{2,1,0:T(8,128)(2,1)S(1)} %fusion), channel_id=1, source_target_pairs={{0,2},{2,0},{4,6},{6,4},{8,10},{10,8},{12,14},{14,12},{16,18},{18,... | collective-permute-start | bytes 258056 | tf_op jit(solution)/shard_map/ppermute | solution.py:379
  88.0 6.2 %collective-permute-start.19 = (bf16[21,16,128]{2,1,0:T(8,128)(2,1)S(1)}, bf16[21,16,128]{2,1,0:T(8,128)(2,1)S(1)}, u32[]{:S(2)}, u32[]{:S(2)}) collective-permute-start(bf16[21,16,128]{2,1,0:T(8,128)(2,1)S(1)} %add_convert_fusion.refs_1_), channel_id=1, source_target_pairs={{0,8},{2,10},{4,12},{6,14},{8,0},{10,2},{12,4},{14,6},{16,24},{18,... | collective-permute-start | bytes 258056 | tf_op jit(solution)/shard_map/ppermute | solution.py:379
  89.3 8.0 %collective-permute-start.22 = (bf16[21,16,128]{2,1,0:T(8,128)(2,1)S(1)}, bf16[21,16,128]{2,1,0:T(8,128)(2,1)S(1)}, u32[]{:S(2)}, u32[]{:S(2)}) collective-permute-start(bf16[21,16,128]{2,1,0:T(8,128)(2,1)S(1)} %add_convert_fusion.refs_1_), channel_id=1, source_target_pairs={{0,12},{2,14},{4,8},{6,10},{8,4},{10,6},{12,0},{14,2},{16,28},{18,... | collective-permute-start | bytes 258056 | tf_op jit(solution)/shard_map/ppermute | solution.py:379
  90.7 6.6 %collective-permute-start.21 = (bf16[21,16,128]{2,1,0:T(8,128)(2,1)S(1)}, bf16[21,16,128]{2,1,0:T(8,128)(2,1)S(1)}, u32[]{:S(2)}, u32[]{:S(2)}) collective-permute-start(bf16[21,16,128]{2,1,0:T(8,128)(2,1)S(1)} %add_convert_fusion.refs_1_), channel_id=1, source_target_pairs={{0,4},{2,6},{4,0},{6,2},{8,12},{10,14},{12,8},{14,10},{16,20},{18,... | collective-permute-start | bytes 258056 | tf_op jit(solution)/shard_map/ppermute | solution.py:379
  94.1 4.7 %collective-permute-start.18 = (bf16[24,64,256]{2,1,0:T(8,128)(2,1)S(1)}, bf16[24,64,256]{2,1,0:T(8,128)(2,1)S(1)}, u32[]{:S(2)}, u32[]{:S(2)}) collective-permute-start(bf16[24,64,256]{2,1,0:T(8,128)(2,1)S(1)} %get-tuple-element.85), channel_id=1, source_target_pairs={{0,1},{1,0},{2,3},{3,2},{4,5},{5,4},{6,7},{7,6},{8,9},{9,8},{10,11... | collective-permute-start | bytes 2359304 | tf_op jit(solution)/shard_map/ppermute | solution.py:374
  96.7 2.5 %collective-permute-start.20 = (bf16[25,64,256]{2,1,0:T(8,128)(2,1)S(1)}, bf16[25,64,256]{2,1,0:T(8,128)(2,1)S(1)}, u32[]{:S(2)}, u32[]{:S(2)}) collective-permute-start(bf16[25,64,256]{2,1,0:T(8,128)(2,1)S(1)} %get-tuple-element.89), channel_id=1, source_target_pairs={{0,1},{1,0},{2,3},{3,2},{4,5},{5,4},{6,7},{7,6},{8,9},{9,8},{10,11... | collective-permute-start | bytes 2457608 | tf_op jit(solution)/shard_map/ppermute | solution.py:374

commit v8 on v7

--- a/solution.py
+++ b/solution.py
@@ -325,6 +325,15 @@
         out[:, pl.ds(first, piece), :] = part[...].astype(F32)
 
 
+def add_kernel(*refs):
+    *parts, total, rounded = refs
+    value = parts[0][...]
+    for part in parts[1:]:
+        value = value + part[...].astype(F32)
+    total[...] = value
+    rounded[...] = value.astype(BF16)
+
+
 def call(kernel, args, outs, scratch=(), scalars=0, limit=24, stay=(), tokens=(), flops=0):
     whole = pl.BlockSpec(memory_space=pltpu.VMEM)
     small = pl.BlockSpec(memory_space=pltpu.SMEM)
@@ -393,7 +402,7 @@
     spot = (atom_place >> cut_bits[0]) & 3
     place = jnp.stack([lax.axis_index("chan"), atom_place * atoms_dev, spot])
     place = place.astype(jnp.int32)
-    feature_cut = comps // 2
+    feature_cut = comps // 2 - 6
     feature_cuts = ((0, feature_cut), (feature_cut, comps))
 
     def held(*dims, dtype=F32):
@@ -496,27 +505,19 @@
         scalars=1,
         stay=tuple(range(1, 10 + 4 * len(feature_cuts))),
     )
-    for delta, part in enumerate(sent, 1):
-        kept = kept + exchanged(part, "atom", delta << cut_bits[0]).astype(F32)
+    def summed(kept, parts):
+        return call(
+            add_kernel, (kept, *parts), (held(*piece), plain(*piece, dtype=BF16)), limit=8, stay=(0,)
+        )
+
+    kept, rounded = summed(
+        kept, [exchanged(part, "atom", delta << cut_bits[0]) for delta, part in enumerate(sent, 1)]
+    )
     rest = [bit for bit in reversed(range(count.bit_length() - 1)) if bit not in cut_bits]
-    for bit in rest:
-        arrived = exchanged(kept.astype(BF16), "atom", 1 << bit)
-        if bit == rest[-1]:
-            from_left, from_right, message_left, message_right, arrived = after(
-                (from_left, from_right, message_left, message_right, arrived), ()
-            )
-        kept = kept + arrived.astype(F32)
-    rounded = kept.astype(BF16)
-    pieces = [rounded] + [exchanged(rounded, "atom", d << cut_bits[0]) for d in range(1, 4)]
-    (grad_weights,) = call(
-        gather_kernel,
-        (place, *pieces),
-        (plain(3 * (LMAX + 1), chan_local, channels),),
-        scalars=1,
-        limit=8,
-        flops=20 * 10**9,
-    )
-    parts, tokens = [], ()
+    for bit in rest[:-1]:
+        kept, rounded = summed(kept, [exchanged(rounded, "atom", 1 << bit)])
+    last = exchanged(rounded, "atom", 1 << rest[-1])
+    parts, tokens = [], (rounded,)
     for (start, stop), halo_qkv in zip(feature_cuts, (halo_a, halo_b)):
         size = stop - start
         mine, theirs, token = call(
@@ -534,7 +535,16 @@
             tokens=tokens,
         )
         parts += [mine, shifted(theirs, "chan", 1)]
-        tokens = (token, pieces[2])
+        tokens = (token, last)
+    kept, rounded = summed(kept, after((last,), (token,)))
+    pieces = [rounded] + [exchanged(rounded, "atom", d << cut_bits[0]) for d in range(1, 4)]
+    (grad_weights,) = call(
+        gather_kernel,
+        (place, *pieces),
+        (plain(3 * (LMAX + 1), chan_local, channels),),
+        scalars=1,
+        limit=8,
+    )
     (out,) = call(
         finish_kernel,
         parts,

time: 101 us -> 111 us (1.099)
  waiting for transfers between devices: 34.4 us -> 44 us
  local copies, waits for them, and re-layouts: 2.41 us -> 4.55 us
    ppermute x15, waiting for transfers between devices: 24 us -> 33.1 us  [shifted(): return lax.ppermute(value, axis, pairs)]
    unnamed x12, local copies, waits for them, and re-layouts: 2.41 us -> 4.55 us
    ppermute x15, starting transfers between devices: 23.6 us -> 22 us  [shifted(): return lax.ppermute(value, axis, pairs)]
    pallas_call x8 -> x11, Pallas kernels: 25.6 us -> 24.6 us  [call(): pl.pallas_call(body, out_shape=tuple(outs), in_specs=[small] * scalars +...]
  transfers between devices with their start and end apart: 23 -> 23, of which waited for: 10 -> 14; matrix products, arithmetic and copies ran while one was open for 0% -> 0% of each run, Pallas kernels for 26% -> 21%
where the time goes in v8:
time: 111 us
  waiting for transfers between devices  44 us (40%)
  starting transfers between devices  34.2 us (31%)
  Pallas kernels  27.1 us (24%)
  local copies, waits for them, and re-layouts  4.55 us (4%)
    ppermute x15, waiting for transfers between devices, shifted(): return lax.ppermute(value, axis, pairs)  33.1 us
    pallas_call x11, Pallas kernels, call(): pl.pallas_call(body, out_shape=tuple(outs), in_specs=[small] * scalars +...  24.6 us
    ppermute x15, starting transfers between devices, shifted(): return lax.ppermute(value, axis, pairs)  22 us
    ppermute x8, starting transfers between devices, exchanged(): lax.ppermute(value, axis, [(source, source ^ offset) for source in range(...  12.2 us
    ppermute x8, waiting for transfers between devices, exchanged(): lax.ppermute(value, axis, [(source, source ^ offset) for source in range(...  10.9 us
    unnamed x12, local copies, waits for them, and re-layouts  4.55 us
    pallas_call x1, Pallas kernels, on_device(): pl.pallas_call(functools.partial(split_kernel, feature_cuts), out_shape=t...  2.45 us
  transfers between devices with their start and end apart: 23, of which 14 were waited for; matrix products, arithmetic and copies ran while one was open for 0% of the time, Pallas kernels for 21%

profile of v8, /device:TPU:0, one launch (start us, length us, event | category | flops | bytes accessed | tf_op | source)
XLA Modules:
  0.0 110.7 jit_solution(11505874930084196002)
XLA Ops:
  0.6 0.5 collective-permute-start
  1.1 2.4 %shard_map.85 = (bf16[18,64,128]{2,1,0:T(8,128)(2,1)}, bf16[18,64,128]{2,1,0:T(8,128)(2,1)S(1)}, bf16[31,64,128]{2,1,0:T(8,128)(2,1)}, bf16[31,64,128]{2,1,0:T(8,128)(2,1)}) custom-call(bf16[49,64,256]{2,1,0:T(8,128)(2,1)} %bitcast.15), custom_call_target="tpu_custom_call" | custom-call | tf_op jit(solution)/shard_map/pallas_call | solution.py:419
  3.6 2.6 %collective-permute-start.1 = (bf16[18,64,128]{2,1,0:T(8,128)(2,1)}, bf16[18,64,128]{2,1,0:T(8,128)(2,1)S(1)}, u32[]{:S(2)}, u32[]{:S(2)}) collective-permute-start(bf16[18,64,128]{2,1,0:T(8,128)(2,1)} %get-tuple-element.48), channel_id=1, source_target_pairs={{0,2},{2,4},{4,6},{6,8},{8,10},{10,12},{12,14},{14,16},{16,18},{18... | collective-permute-start | bytes 884744 | tf_op jit(solution)/shard_map/ppermute | solution.py:383
  6.2 4.1 %collective-permute-start.2 = (bf16[18,64,128]{2,1,0:T(8,128)(2,1)S(1)}, bf16[18,64,128]{2,1,0:T(8,128)(2,1)S(1)}, u32[]{:S(2)}, u32[]{:S(2)}) collective-permute-start(bf16[18,64,128]{2,1,0:T(8,128)(2,1)S(1)} %get-tuple-element.49), channel_id=1, source_target_pairs={{0,30},{2,0},{4,2},{6,4},{8,6},{10,8},{12,10},{14,12},{16,14},{18,... | collective-permute-start | bytes 884744 | tf_op jit(solution)/shard_map/ppermute | solution.py:383
  10.2 5.6 %collective-permute-start.6 = (bf16[31,64,128]{2,1,0:T(8,128)(2,1)}, bf16[31,64,128]{2,1,0:T(8,128)(2,1)S(1)}, u32[]{:S(2)}, u32[]{:S(2)}) collective-permute-start(bf16[31,64,128]{2,1,0:T(8,128)(2,1)} %get-tuple-element.54), channel_id=1, source_target_pairs={{0,30},{2,0},{4,2},{6,4},{8,6},{10,8},{12,10},{14,12},{16,14},{18,... | collective-permute-start | bytes 1523720 | tf_op jit(solution)/shard_map/ppermute | solution.py:383
  15.8 0.1 pad_add_fusion.refs_0_
  15.9 1.4 %copy-done = bf16[64,49,256]{2,0,1:T(8,128)(2,1)S(1)} copy-done((bf16[64,49,256]{2,0,1:T(8,128)(2,1)S(1)}, bf16[64,49,256]{2,0,1:T(8,128)(2,1)}, u32[]{:S(2)}) %copy-start) | copy-done | bytes 1605656
  17.3 1.4 %copy-done.1 = bf16[64,49,256]{2,0,1:T(8,128)(2,1)S(1)} copy-done((bf16[64,49,256]{2,0,1:T(8,128)(2,1)S(1)}, bf16[64,49,256]{2,0,1:T(8,128)(2,1)}, u32[]{:S(2)}) %copy-start.1) | copy-done | bytes 1605656
  18.8 1.0 copy-done.4
  19.7 0.7 copy-done.5
  20.5 3.8 %shard_map.86 = (bf16[49,192,256]{2,1,0:T(8,128)(2,1)S(1)}, f32[8,256,256]{2,1,0:T(8,128)S(1)}, s32[2,3,128,128]{3,2,1,0:T(8,128)S(1)}, s32[16,256]{1,0:T(8,128)...) custom-call(s32[3]{0:T(128)S(1)} %pad_add_fusion.refs_0_, ...), custom_call_target="tpu_custom_call" | custom-call | flops 12000000000 | bytes 1024 | tf_op jit(solution)/shard_map/pallas_call | solution.py:349
  24.3 6.7 %collective-permute-done.1.refs_0_ = bf16[18,64,128]{2,1,0:T(8,128)(2,1)S(1)} collective-permute-done((bf16[18,64,128]{2,1,0:T(8,128)(2,1)}, bf16[18,64,128]{2,1,0:T(8,128)(2,1)S(1)}, u32[]{:S(2)}, u32[]{:S(2)}) %collective-permute-start.1) | collective-permute-done | bytes 294944 | tf_op jit(solution)/shard_map/ppermute | solution.py:383
  31.0 0.5 collective-permute-start.4
  31.5 1.1 collective-permute-done.3.refs_1_.refs_4_
  32.6 0.4 collective-permute-done.4.refs_3_.refs_6_
  33.0 1.1 %shard_map.88 = (bf16[18,192,256]{2,1,0:T(8,128)(2,1)S(1)}, f32[8,2,128,128]{3,2,1,0:T(8,128)S(1)}, f32[8,128]{1,0:T(8,128)S(1)}) custom-call(bf16[18,64,128]{2,1,0:T(8,128)(2,1)S(1)} %get-tuple-element.51.refs_0_.refs_3_, bf16[18,64,128]{2,1,0:T(8,128)(2,1)S(1)} %collective-permute-done.3.refs_1_.refs_4_, ...), custom_call_target="tpu_custom_call" | custom-call | bytes 1024 | tf_op jit(solution)/shard_map/pallas_call | solution.py:349
  34.2 2.4 %collective-permute-start.9 = (bf16[49,64,128]{2,1,0:T(8,128)(2,1)S(1)}, bf16[49,64,128]{2,1,0:T(8,128)(2,1)S(1)}, u32[]{:S(2)}, u32[]{:S(2)}) collective-permute-start(bf16[49,64,128]{2,1,0:T(8,128)(2,1)S(1)} %get-tuple-element.74), channel_id=1, source_target_pairs={{0,2},{2,4},{4,6},{6,8},{8,10},{10,12},{12,14},{14,16},{16,18},{18... | collective-permute-start | bytes 2408456 | tf_op jit(solution)/shard_map/ppermute | solution.py:383
  36.6 3.2 %collective-permute-start.10 = (bf16[49,64,128]{2,1,0:T(8,128)(2,1)S(1)}, bf16[49,64,128]{2,1,0:T(8,128)(2,1)S(1)}, u32[]{:S(2)}, u32[]{:S(2)}) collective-permute-start(bf16[49,64,128]{2,1,0:T(8,128)(2,1)S(1)} %get-tuple-element.75), channel_id=1, source_target_pairs={{0,30},{2,0},{4,2},{6,4},{8,6},{10,8},{12,10},{14,12},{16,14},{18,... | collective-permute-start | bytes 2408456 | tf_op jit(solution)/shard_map/ppermute | solution.py:383
  39.9 19.2 %collective-permute-done.5.refs_0_ = bf16[31,64,128]{2,1,0:T(8,128)(2,1)S(1)} collective-permute-done((bf16[31,64,128]{2,1,0:T(8,128)(2,1)}, bf16[31,64,128]{2,1,0:T(8,128)(2,1)S(1)}, u32[]{:S(2)}, u32[]{:S(2)}) %collective-permute-start.5) | collective-permute-done | bytes 507936 | tf_op jit(solution)/shard_map/ppermute | solution.py:383
  59.1 0.5 collective-permute-start.8
  59.6 1.4 %collective-permute-done.7.refs_1_.refs_8_ = bf16[31,64,128]{2,1,0:T(8,128)(2,1)S(1)} collective-permute-done((bf16[31,64,128]{2,1,0:T(8,128)(2,1)S(1)}, bf16[31,64,128]{2,1,0:T(8,128)(2,1)S(1)}, u32[]{:S(2)}, u32[]{:S(2)}) %collective-permute-start.7) | collective-permute-done | bytes 507936 | tf_op jit(solution)/shard_map/ppermute | solution.py:383
  61.0 0.7 collective-permute-done.8.refs_3_.refs_10_
  61.7 3.8 %shard_map.90 = (bf16[31,192,256]{2,1,0:T(8,128)(2,1)S(1)}, f32[4,16,256]{2,1,0:T(8,128)}, f32[176,128]{1,0:T(8,128)S(1)}, f32[176,128]{1,0:T(8,128)S(1)}) custom-call(bf16[31,64,128]{2,1,0:T(8,128)(2,1)S(1)} %get-tuple-element.58.refs_0_.refs_7_, bf16[31,64,128]{2,1,0:T(8,128)(2,1)S(1)} %collective-permute-done.7.refs_1_.refs_8_, ...), custom_call_target="tpu_custom_call" | custom-call | bytes 1024 | tf_op jit(solution)/shard_map/pallas_call | solution.py:349
  65.5 6.9 %shard_map.91 = (bf16[49,64,256]{2,1,0:T(8,128)(2,1)S(1)}, f32[49,64,256]{2,1,0:T(8,128)S(1)}, f32[49,64,256]{2,1,0:T(8,128)S(1)}, f32[21,16,128]{2,1,0:T(8,128)...) custom-call(s32[3]{0:T(128)S(1)} %pad_add_fusion.refs_0_, ...), custom_call_target="tpu_custom_call" | custom-call | bytes 1024 | tf_op jit(solution)/shard_map/pallas_call | solution.py:349
  72.4 3.8 %collective-permute-start.13 = (bf16[21,16,128]{2,1,0:T(8,128)(2,1)S(1)}, bf16[21,16,128]{2,1,0:T(8,128)(2,1)S(1)}, u32[]{:S(2)}, u32[]{:S(2)}) collective-permute-start(bf16[21,16,128]{2,1,0:T(8,128)(2,1)S(1)} %get-tuple-element.78), channel_id=1, source_target_pairs={{0,4},{2,6},{4,0},{6,2},{8,12},{10,14},{12,8},{14,10},{16,20},{18,... | collective-permute-start | bytes 258056 | tf_op jit(solution)/shard_map/ppermute | solution.py:388
  76.2 0.8 collective-permute-start.14
  77.0 0.8 collective-permute-start.15
  77.7 1.3 %collective-permute-done.13.refs_1_ = bf16[21,16,128]{2,1,0:T(8,128)(2,1)S(1)} collective-permute-done((bf16[21,16,128]{2,1,0:T(8,128)(2,1)S(1)}, bf16[21,16,128]{2,1,0:T(8,128)(2,1)S(1)}, u32[]{:S(2)}, u32[]{:S(2)}) %collective-permute-start.13) | collective-permute-done | bytes 86048 | tf_op jit(solution)/shard_map/ppermute | solution.py:388
  79.0 2.4 %collective-permute-done.14.refs_2_ = bf16[21,16,128]{2,1,0:T(8,128)(2,1)S(1)} collective-permute-done((bf16[21,16,128]{2,1,0:T(8,128)(2,1)S(1)}, bf16[21,16,128]{2,1,0:T(8,128)(2,1)S(1)}, u32[]{:S(2)}, u32[]{:S(2)}) %collective-permute-start.14) | collective-permute-done | bytes 86048 | tf_op jit(solution)/shard_map/ppermute | solution.py:388
  81.4 0.9 collective-permute-done.15.refs_3_
  82.4 2.7 %collective-permute-start.16 = (bf16[21,16,128]{2,1,0:T(8,128)(2,1)S(1)}, bf16[21,16,128]{2,1,0:T(8,128)(2,1)S(1)}, u32[]{:S(2)}, u32[]{:S(2)}) collective-permute-start(bf16[21,16,128]{2,1,0:T(8,128)(2,1)S(1)} %get-tuple-element.82), channel_id=1, source_target_pairs={{0,16},{2,18},{4,20},{6,22},{8,24},{10,26},{12,28},{14,30},{16,0},... | collective-permute-start | bytes 258056 | tf_op jit(solution)/shard_map/ppermute | solution.py:388
  85.1 0.7 collective-permute-start.12
  85.8 1.3 %collective-permute-start.11 = (f32[176,128]{1,0:T(8,128)S(1)}, f32[176,128]{1,0:T(8,128)S(1)}, u32[]{:S(2)}, u32[]{:S(2)}) collective-permute-start(f32[176,128]{1,0:T(8,128)S(1)} %get-tuple-element.68.refs_17_), channel_id=1, source_target_pairs={{0,2},{2,4},{4,6},{6,8},{8,10},{10,12},{12,14},{14,16},{16,18},{18... | collective-permute-start | bytes 270344 | tf_op jit(solution)/shard_map/ppermute | solution.py:383
  87.1 2.5 %collective-permute-done.16.refs_1_ = bf16[21,16,128]{2,1,0:T(8,128)(2,1)S(1)} collective-permute-done((bf16[21,16,128]{2,1,0:T(8,128)(2,1)S(1)}, bf16[21,16,128]{2,1,0:T(8,128)(2,1)S(1)}, u32[]{:S(2)}, u32[]{:S(2)}) %collective-permute-start.16) | collective-permute-done | bytes 86048 | tf_op jit(solution)/shard_map/ppermute | solution.py:388
  89.7 0.7 collective-permute-start.18
  90.4 0.2 collective-permute-done.12.refs_7_
  90.6 3.4 %collective-permute-done.11.refs_6_ = f32[176,128]{1,0:T(8,128)S(1)} collective-permute-done((f32[176,128]{1,0:T(8,128)S(1)}, f32[176,128]{1,0:T(8,128)S(1)}, u32[]{:S(2)}, u32[]{:S(2)}) %collective-permute-start.11) | collective-permute-done | bytes 90144 | tf_op jit(solution)/shard_map/ppermute | solution.py:383
  93.9 2.4 %shard_map.95 = (f32[18,64,256]{2,1,0:T(8,128)S(1)}, bf16[18,64,256]{2,1,0:T(8,128)(2,1)S(1)}, f32[8,128]{1,0:T(8,128)S(1)}) custom-call(bf16[49,64,256]{2,1,0:T(8,128)(2,1)S(1)} %get-tuple-element.69.refs_0_, f32[49,64,256]{2,1,0:T(8,128)S(1)} %get-tuple-element.70.refs_1_, f32[49,64,256]{2,1,0:T(8,128)S(1)} %get-tuple-element.71.refs_2_, ...), custom_call_target="tpu_custom_call" | custom-call | bytes 1024 | tf_op jit(solution)/shard_map/pallas_call | solution.py:349
  96.3 2.9 %shard_map.96 = (f32[31,64,256]{2,1,0:T(8,128)S(1)}, bf16[31,64,256]{2,1,0:T(8,128)(2,1)S(1)}, f32[8,128]{1,0:T(8,128)S(1)}) custom-call(bf16[49,64,256]{2,1,0:T(8,128)(2,1)S(1)} %get-tuple-element.69.refs_0_, f32[49,64,256]{2,1,0:T(8,128)S(1)} %get-tuple-element.70.refs_1_, f32[49,64,256]{2,1,0:T(8,128)S(1)} %get-tuple-element.71.refs_2_, ...), custom_call_target="tpu_custom_call" | custom-call | bytes 1024 | tf_op jit(solution)/shard_map/pallas_call | solution.py:349
  99.2 0.1 collective-permute-start.19
  99.3 0.5 collective-permute-start.17
  99.8 0.7 shard_map.99
  100.5 1.4 %collective-permute-start.21 = (bf16[21,16,128]{2,1,0:T(8,128)(2,1)S(1)}, bf16[21,16,128]{2,1,0:T(8,128)(2,1)S(1)}, u32[]{:S(2)}, u32[]{:S(2)}) collective-permute-start(bf16[21,16,128]{2,1,0:T(8,128)(2,1)S(1)} %get-tuple-element.91.refs_1_), channel_id=1, source_target_pairs={{0,8},{2,10},{4,12},{6,14},{8,0},{10,2},{12,4},{14,6},{16,24},{18,... | collective-permute-start | bytes 258056 | tf_op jit(solution)/shard_map/ppermute | solution.py:388
  101.9 2.1 %collective-permute-start.20 = (bf16[21,16,128]{2,1,0:T(8,128)(2,1)S(1)}, bf16[21,16,128]{2,1,0:T(8,128)(2,1)S(1)}, u32[]{:S(2)}, u32[]{:S(2)}) collective-permute-start(bf16[21,16,128]{2,1,0:T(8,128)(2,1)S(1)} %get-tuple-element.91.refs_1_), channel_id=1, source_target_pairs={{0,4},{2,6},{4,0},{6,2},{8,12},{10,14},{12,8},{14,10},{16,20},{18,... | collective-permute-start | bytes 258056 | tf_op jit(solution)/shard_map/ppermute | solution.py:388
  104.0 2.8 %collective-permute-done.22.refs_4_ = bf16[21,16,128]{2,1,0:T(8,128)(2,1)S(1)} collective-permute-done((bf16[21,16,128]{2,1,0:T(8,128)(2,1)S(1)}, bf16[21,16,128]{2,1,0:T(8,128)(2,1)S(1)}, u32[]{:S(2)}, u32[]{:S(2)}) %collective-permute-start.22) | collective-permute-done | bytes 86048 | tf_op jit(solution)/shard_map/ppermute | solution.py:388
  106.8 1.0 collective-permute-done.20.refs_2_
  107.8 1.4 %shard_map.100 = f32[21,64,128]{2,1,0:T(8,128)} custom-call(s32[3]{0:T(128)S(1)} %pad_add_fusion.refs_0_, bf16[21,16,128]{2,1,0:T(8,128)(2,1)S(1)} %get-tuple-element.91.refs_1_, bf16[21,16,128]{2,1,0:T(8,128)(2,1)S(1)} %collective-permute-done.20.refs_2_, bf16[21,16,128]{2,1,0:T(8,128)(2,1)S(1)} %collective-permute-done.21.refs_3_, ...), custom_call_target="tpu_custom_call" | custom-call | bytes 1024 | tf_op jit(solution)/shard_map/pallas_call | solution.py:349
  109.2 1.5 %shard_map.97 = bf16[49,64,256]{2,1,0:T(8,128)(2,1)} custom-call(f32[18,64,256]{2,1,0:T(8,128)S(1)} %get-tuple-element.84.refs_0_, bf16[18,64,256]{2,1,0:T(8,128)(2,1)S(1)} %collective-permute-done.17.refs_1_, f32[31,64,256]{2,1,0:T(8,128)S(1)} %get-tuple-element.87.refs_2_, bf16[31,64,256]{2,1,0:T(8,128)(2,1)S(1)} %collective-permute-done.19.refs_3_), custom_call_target="tpu_custom_call" | custom-call | bytes 1024 | tf_op jit(solution)/shard_map/pallas_call | solution.py:349
  (27 shorter events, 0.1 us)
Async XLA Ops:
  0.6 15.3 %collective-permute-start = (bf16[49,64,256]{2,1,0:T(8,128)(2,1)}, bf16[49,64,256]{2,1,0:T(8,128)(2,1)S(1)}, u32[]{:S(2)}, u32[]{:S(2)}) collective-permute-start(bf16[49,64,256]{2,1,0:T(8,128)(2,1)} %bitcast.14), channel_id=1, source_target_pairs={{0,1},{1,0},{2,3},{3,2},{4,5},{5,4},{6,7},{7,6},{8,9},{9,8},{10,11... | collective-permute-start | bytes 4816904 | tf_op jit(solution)/shard_map/ppermute | solution.py:383
  3.6 27.4 %collective-permute-start.1 = (bf16[18,64,128]{2,1,0:T(8,128)(2,1)}, bf16[18,64,128]{2,1,0:T(8,128)(2,1)S(1)}, u32[]{:S(2)}, u32[]{:S(2)}) collective-permute-start(bf16[18,64,128]{2,1,0:T(8,128)(2,1)} %get-tuple-element.48), channel_id=1, source_target_pairs={{0,2},{2,4},{4,6},{6,8},{8,10},{10,12},{12,14},{14,16},{16,18},{18... | collective-permute-start | bytes 884744 | tf_op jit(solution)/shard_map/ppermute | solution.py:383
  6.2 24.8 %collective-permute-start.2 = (bf16[18,64,128]{2,1,0:T(8,128)(2,1)S(1)}, bf16[18,64,128]{2,1,0:T(8,128)(2,1)S(1)}, u32[]{:S(2)}, u32[]{:S(2)}) collective-permute-start(bf16[18,64,128]{2,1,0:T(8,128)(2,1)S(1)} %get-tuple-element.49), channel_id=1, source_target_pairs={{0,30},{2,0},{4,2},{6,4},{8,6},{10,8},{12,10},{14,12},{16,14},{18,... | collective-permute-start | bytes 884744 | tf_op jit(solution)/shard_map/ppermute | solution.py:383
  10.2 48.9 %collective-permute-start.5 = (bf16[31,64,128]{2,1,0:T(8,128)(2,1)}, bf16[31,64,128]{2,1,0:T(8,128)(2,1)S(1)}, u32[]{:S(2)}, u32[]{:S(2)}) collective-permute-start(bf16[31,64,128]{2,1,0:T(8,128)(2,1)} %get-tuple-element.53), channel_id=1, source_target_pairs={{0,2},{2,4},{4,6},{6,8},{8,10},{10,12},{12,14},{14,16},{16,18},{18... | collective-permute-start | bytes 1523720 | tf_op jit(solution)/shard_map/ppermute | solution.py:383
  10.2 48.9 %collective-permute-start.6 = (bf16[31,64,128]{2,1,0:T(8,128)(2,1)}, bf16[31,64,128]{2,1,0:T(8,128)(2,1)S(1)}, u32[]{:S(2)}, u32[]{:S(2)}) collective-permute-start(bf16[31,64,128]{2,1,0:T(8,128)(2,1)} %get-tuple-element.54), channel_id=1, source_target_pairs={{0,30},{2,0},{4,2},{6,4},{8,6},{10,8},{12,10},{14,12},{16,14},{18,... | collective-permute-start | bytes 1523720 | tf_op jit(solution)/shard_map/ppermute | solution.py:383
  15.9 1.4 %copy-start = (bf16[64,49,256]{2,0,1:T(8,128)(2,1)S(1)}, bf16[64,49,256]{2,0,1:T(8,128)(2,1)}, u32[]{:S(2)}) copy-start(bf16[64,49,256]{2,0,1:T(8,128)(2,1)} %param.8) | copy-start | bytes 4816900
  17.3 1.4 %copy-start.1 = (bf16[64,49,256]{2,0,1:T(8,128)(2,1)S(1)}, bf16[64,49,256]{2,0,1:T(8,128)(2,1)}, u32[]{:S(2)}) copy-start(bf16[64,49,256]{2,0,1:T(8,128)(2,1)} %param.6) | copy-start | bytes 4816900
  18.8 1.0 copy-start.4
  19.7 0.7 copy-start.5
  31.0 1.6 %collective-permute-start.3 = (bf16[18,64,128]{2,1,0:T(8,128)(2,1)S(1)}, bf16[18,64,128]{2,1,0:T(8,128)(2,1)S(1)}, u32[]{:S(2)}, u32[]{:S(2)}) collective-permute-start(bf16[18,64,128]{2,1,0:T(8,128)(2,1)S(1)} %get-tuple-element.51.refs_0_.refs_3_), channel_id=1, source_target_pairs={{0,1},{1,0},{2,3},{3,2},{4,5},{5,4},{6,7},{7,6},{8,9},{9,8},{10,11... | collective-permute-start | bytes 884744 | tf_op jit(solution)/shard_map/ppermute | solution.py:383
  31.0 2.0 %collective-permute-start.4 = (bf16[18,64,128]{2,1,0:T(8,128)(2,1)S(1)}, bf16[18,64,128]{2,1,0:T(8,128)(2,1)S(1)}, u32[]{:S(2)}, u32[]{:S(2)}) collective-permute-start(bf16[18,64,128]{2,1,0:T(8,128)(2,1)S(1)} %get-tuple-element.52.refs_2_.refs_5_), channel_id=1, source_target_pairs={{0,1},{1,0},{2,3},{3,2},{4,5},{5,4},{6,7},{7,6},{8,9},{9,8},{10,11... | collective-permute-start | bytes 884744 | tf_op jit(solution)/shard_map/ppermute | solution.py:383
  34.2 27.5 %copy-start.2 = (f32[4,16,256]{2,1,0:T(8,128)S(1)}, f32[4,16,256]{2,1,0:T(8,128)}, u32[]{:S(2)}) copy-start(f32[4,16,256]{2,1,0:T(8,128)} %refs_9_.1) | copy-start | bytes 196612
  34.2 27.5 %copy-start.3 = (s32[16,256]{1,0:T(8,128)S(1)}, s32[16,256]{1,0:T(8,128)}, u32[]{:S(2)}) copy-start(s32[16,256]{1,0:T(8,128)} %refs_10_.1) | copy-start | bytes 49156
  34.2 59.7 %collective-permute-start.9 = (bf16[49,64,128]{2,1,0:T(8,128)(2,1)S(1)}, bf16[49,64,128]{2,1,0:T(8,128)(2,1)S(1)}, u32[]{:S(2)}, u32[]{:S(2)}) collective-permute-start(bf16[49,64,128]{2,1,0:T(8,128)(2,1)S(1)} %get-tuple-element.74), channel_id=1, source_target_pairs={{0,2},{2,4},{4,6},{6,8},{8,10},{10,12},{12,14},{14,16},{16,18},{18... | collective-permute-start | bytes 2408456 | tf_op jit(solution)/shard_map/ppermute | solution.py:383
  36.6 57.3 %collective-permute-start.10 = (bf16[49,64,128]{2,1,0:T(8,128)(2,1)S(1)}, bf16[49,64,128]{2,1,0:T(8,128)(2,1)S(1)}, u32[]{:S(2)}, u32[]{:S(2)}) collective-permute-start(bf16[49,64,128]{2,1,0:T(8,128)(2,1)S(1)} %get-tuple-element.75), channel_id=1, source_target_pairs={{0,30},{2,0},{4,2},{6,4},{8,6},{10,8},{12,10},{14,12},{16,14},{18,... | collective-permute-start | bytes 2408456 | tf_op jit(solution)/shard_map/ppermute | solution.py:383
  59.1 1.9 %collective-permute-start.7 = (bf16[31,64,128]{2,1,0:T(8,128)(2,1)S(1)}, bf16[31,64,128]{2,1,0:T(8,128)(2,1)S(1)}, u32[]{:S(2)}, u32[]{:S(2)}) collective-permute-start(bf16[31,64,128]{2,1,0:T(8,128)(2,1)S(1)} %get-tuple-element.58.refs_0_.refs_7_), channel_id=1, source_target_pairs={{0,1},{1,0},{2,3},{3,2},{4,5},{5,4},{6,7},{7,6},{8,9},{9,8},{10,11... | collective-permute-start | bytes 1523720 | tf_op jit(solution)/shard_map/ppermute | solution.py:383
  59.1 2.6 %collective-permute-start.8 = (bf16[31,64,128]{2,1,0:T(8,128)(2,1)S(1)}, bf16[31,64,128]{2,1,0:T(8,128)(2,1)S(1)}, u32[]{:S(2)}, u32[]{:S(2)}) collective-permute-start(bf16[31,64,128]{2,1,0:T(8,128)(2,1)S(1)} %get-tuple-element.59.refs_2_.refs_9_), channel_id=1, source_target_pairs={{0,1},{1,0},{2,3},{3,2},{4,5},{5,4},{6,7},{7,6},{8,9},{9,8},{10,11... | collective-permute-start | bytes 1523720 | tf_op jit(solution)/shard_map/ppermute | solution.py:383
  72.4 6.6 %collective-permute-start.13 = (bf16[21,16,128]{2,1,0:T(8,128)(2,1)S(1)}, bf16[21,16,128]{2,1,0:T(8,128)(2,1)S(1)}, u32[]{:S(2)}, u32[]{:S(2)}) collective-permute-start(bf16[21,16,128]{2,1,0:T(8,128)(2,1)S(1)} %get-tuple-element.78), channel_id=1, source_target_pairs={{0,4},{2,6},{4,0},{6,2},{8,12},{10,14},{12,8},{14,10},{16,20},{18,... | collective-permute-start | bytes 258056 | tf_op jit(solution)/shard_map/ppermute | solution.py:388
  76.2 5.2 %collective-permute-start.14 = (bf16[21,16,128]{2,1,0:T(8,128)(2,1)S(1)}, bf16[21,16,128]{2,1,0:T(8,128)(2,1)S(1)}, u32[]{:S(2)}, u32[]{:S(2)}) collective-permute-start(bf16[21,16,128]{2,1,0:T(8,128)(2,1)S(1)} %get-tuple-element.79), channel_id=1, source_target_pairs={{0,8},{2,10},{4,12},{6,14},{8,0},{10,2},{12,4},{14,6},{16,24},{18,... | collective-permute-start | bytes 258056 | tf_op jit(solution)/shard_map/ppermute | solution.py:388
  77.0 5.4 %collective-permute-start.15 = (bf16[21,16,128]{2,1,0:T(8,128)(2,1)S(1)}, bf16[21,16,128]{2,1,0:T(8,128)(2,1)S(1)}, u32[]{:S(2)}, u32[]{:S(2)}) collective-permute-start(bf16[21,16,128]{2,1,0:T(8,128)(2,1)S(1)} %get-tuple-element.80), channel_id=1, source_target_pairs={{0,12},{2,14},{4,8},{6,10},{8,4},{10,6},{12,0},{14,2},{16,28},{18,... | collective-permute-start | bytes 258056 | tf_op jit(solution)/shard_map/ppermute | solution.py:388
  82.4 7.2 %collective-permute-start.16 = (bf16[21,16,128]{2,1,0:T(8,128)(2,1)S(1)}, bf16[21,16,128]{2,1,0:T(8,128)(2,1)S(1)}, u32[]{:S(2)}, u32[]{:S(2)}) collective-permute-start(bf16[21,16,128]{2,1,0:T(8,128)(2,1)S(1)} %get-tuple-element.82), channel_id=1, source_target_pairs={{0,16},{2,18},{4,20},{6,22},{8,24},{10,26},{12,28},{14,30},{16,0},... | collective-permute-start | bytes 258056 | tf_op jit(solution)/shard_map/ppermute | solution.py:388
  85.1 5.5 %collective-permute-start.12 = (f32[176,128]{1,0:T(8,128)S(1)}, f32[176,128]{1,0:T(8,128)S(1)}, u32[]{:S(2)}, u32[]{:S(2)}) collective-permute-start(f32[176,128]{1,0:T(8,128)S(1)} %get-tuple-element.67.refs_16_), channel_id=1, source_target_pairs={{0,30},{2,0},{4,2},{6,4},{8,6},{10,8},{12,10},{14,12},{16,14},{18,... | collective-permute-start | bytes 270344 | tf_op jit(solution)/shard_map/ppermute | solution.py:383
  85.8 8.2 %collective-permute-start.11 = (f32[176,128]{1,0:T(8,128)S(1)}, f32[176,128]{1,0:T(8,128)S(1)}, u32[]{:S(2)}, u32[]{:S(2)}) collective-permute-start(f32[176,128]{1,0:T(8,128)S(1)} %get-tuple-element.68.refs_17_), channel_id=1, source_target_pairs={{0,2},{2,4},{4,6},{6,8},{8,10},{10,12},{12,14},{14,16},{16,18},{18... | collective-permute-start | bytes 270344 | tf_op jit(solution)/shard_map/ppermute | solution.py:383
  89.7 6.7 %collective-permute-start.18 = (bf16[21,16,128]{2,1,0:T(8,128)(2,1)S(1)}, bf16[21,16,128]{2,1,0:T(8,128)(2,1)S(1)}, u32[]{:S(2)}, u32[]{:S(2)}) collective-permute-start(bf16[21,16,128]{2,1,0:T(8,128)(2,1)S(1)} %get-tuple-element.83.refs_9_), channel_id=1, source_target_pairs={{0,2},{2,0},{4,6},{6,4},{8,10},{10,8},{12,14},{14,12},{16,18},{18,... | collective-permute-start | bytes 258056 | tf_op jit(solution)/shard_map/ppermute | solution.py:388
  99.2 10.0 %collective-permute-start.19 = (bf16[31,64,256]{2,1,0:T(8,128)(2,1)S(1)}, bf16[31,64,256]{2,1,0:T(8,128)(2,1)S(1)}, u32[]{:S(2)}, u32[]{:S(2)}) collective-permute-start(bf16[31,64,256]{2,1,0:T(8,128)(2,1)S(1)} %get-tuple-element.88), channel_id=1, source_target_pairs={{0,1},{1,0},{2,3},{3,2},{4,5},{5,4},{6,7},{7,6},{8,9},{9,8},{10,11... | collective-permute-start | bytes 3047432 | tf_op jit(solution)/shard_map/ppermute | solution.py:383
  99.3 9.9 %collective-permute-start.17 = (bf16[18,64,256]{2,1,0:T(8,128)(2,1)S(1)}, bf16[18,64,256]{2,1,0:T(8,128)(2,1)S(1)}, u32[]{:S(2)}, u32[]{:S(2)}) collective-permute-start(bf16[18,64,256]{2,1,0:T(8,128)(2,1)S(1)} %get-tuple-element.85), channel_id=1, source_target_pairs={{0,1},{1,0},{2,3},{3,2},{4,5},{5,4},{6,7},{7,6},{8,9},{9,8},{10,11... | collective-permute-start | bytes 1769480 | tf_op jit(solution)/shard_map/ppermute | solution.py:383
  100.5 6.3 %collective-permute-start.22 = (bf16[21,16,128]{2,1,0:T(8,128)(2,1)S(1)}, bf16[21,16,128]{2,1,0:T(8,128)(2,1)S(1)}, u32[]{:S(2)}, u32[]{:S(2)}) collective-permute-start(bf16[21,16,128]{2,1,0:T(8,128)(2,1)S(1)} %get-tuple-element.91.refs_1_), channel_id=1, source_target_pairs={{0,12},{2,14},{4,8},{6,10},{8,4},{10,6},{12,0},{14,2},{16,28},{18,... | collective-permute-start | bytes 258056 | tf_op jit(solution)/shard_map/ppermute | solution.py:388
  100.5 6.3 %collective-permute-start.21 = (bf16[21,16,128]{2,1,0:T(8,128)(2,1)S(1)}, bf16[21,16,128]{2,1,0:T(8,128)(2,1)S(1)}, u32[]{:S(2)}, u32[]{:S(2)}) collective-permute-start(bf16[21,16,128]{2,1,0:T(8,128)(2,1)S(1)} %get-tuple-element.91.refs_1_), channel_id=1, source_target_pairs={{0,8},{2,10},{4,12},{6,14},{8,0},{10,2},{12,4},{14,6},{16,24},{18,... | collective-permute-start | bytes 258056 | tf_op jit(solution)/shard_map/ppermute | solution.py:388
  101.9 5.9 %collective-permute-start.20 = (bf16[21,16,128]{2,1,0:T(8,128)(2,1)S(1)}, bf16[21,16,128]{2,1,0:T(8,128)(2,1)S(1)}, u32[]{:S(2)}, u32[]{:S(2)}) collective-permute-start(bf16[21,16,128]{2,1,0:T(8,128)(2,1)S(1)} %get-tuple-element.91.refs_1_), channel_id=1, source_target_pairs={{0,4},{2,6},{4,0},{6,2},{8,12},{10,14},{12,8},{14,10},{16,20},{18,... | collective-permute-start | bytes 258056 | tf_op jit(solution)/shard_map/ppermute | solution.py:388

commit v9 on v8

--- a/solution.py
+++ b/solution.py
@@ -58,17 +58,21 @@
     return jnp.concatenate([rows] * (HALO // rows.shape[0]), axis=0).T
 
 
-def split_kernel(cuts, fm, *refs):
-    *parts, sems = refs
+def split_kernel(start, parts, fm, *refs):
+    *rims, sems = refs
+    size = rims[0].shape[0]
+    cuts = [size * at // parts for at in range(parts + 1)]
     copies = []
-    for at, part in enumerate(parts):
-        start, stop = cuts[at // 2]
-        atom = HALO if at % 2 == 0 else 0
-        copies.append(
-            pltpu.make_async_copy(
-                fm.at[pl.ds(start, stop - start), :, pl.ds(atom, HALO)], part, sems.at[at]
+    for side, rim in enumerate(rims):
+        atoms = pl.ds(HALO if side == 0 else 0, HALO)
+        for at, (low, high) in enumerate(zip(cuts, cuts[1:])):
+            copies.append(
+                pltpu.make_async_copy(
+                    fm.at[pl.ds(start + low, high - low), :, atoms],
+                    rim.at[pl.ds(low, high - low)],
+                    sems.at[side, at],
+                )
             )
-        )
     for copy in copies:
         copy.start()
     for copy in copies:
@@ -151,7 +155,8 @@
 def edge_kernel(heads, score_scale, start, late, *refs):
     chunks = [refs[at : at + 4] for at in range(0, 4 * late, 4)]
     (wp, qkv, cot, scores, partial, bias, valid, index_rows, index_wide,
-     halo_qkv, grad_bias, message_a, message_b) = refs[4 * late :]
+     halo_qkv, grad_bias, message_a, message_b, token) = refs[4 * late :]
+    token[...] = jnp.zeros_like(token)
     slots = valid.shape[0]
     project_halo(start, chunks, wp, halo_qkv)
     lane = lax.broadcasted_iota(jnp.int32, (HALO, 2 * heads * slots), 1)
@@ -193,9 +198,8 @@
             merged = merged + jnp.where(same, both[:, slot : slot + 1, :], 0.0)
         atom = lax.broadcasted_iota(jnp.int32, (slots, HALO), 1)
         edge_rows = 2 * heads * slots
-        message[:edge_rows, :] = merged.reshape(edge_rows, HALO)
-        message[edge_rows : edge_rows + slots, :] = (index - HALO - atom).astype(F32)
-        message[edge_rows + slots :, :] = jnp.zeros_like(message[edge_rows + slots :, :])
+        message[:edge_rows, :] = merged.reshape(edge_rows, HALO).astype(BF16)
+        message[edge_rows:, :] = (index - HALO - atom).astype(F32).astype(BF16)
 
 
 def joined_rows(early, late, first_row, rows):
@@ -214,7 +218,7 @@
     atoms = 2 * HALO
     core = place[0]
     empty = jnp.zeros((HALO, HALO), BF16)
-    coefs = [message[: 2 * heads * slots, :].T for message in (message_a, message_b)]
+    coefs = [message[: 2 * heads * slots, :].astype(F32).T for message in (message_a, message_b)]
     for head in range(heads):
         tables = []
         for quantity in (head, heads + head):
@@ -267,8 +271,8 @@
 def halo_slots(message_left, message_right, quantities, slots):
     coefs, tables = [], []
     for message, tile in ((message_left, 2), (message_right, 0)):
-        coefs.append(message[: quantities * slots, :].T)
-        offset = message[quantities * slots : (quantities + 1) * slots, :].astype(jnp.int32)
+        coefs.append(message[: quantities * slots, :].astype(F32).T)
+        offset = message[quantities * slots :, :].astype(F32).astype(jnp.int32)
         atom = lax.broadcasted_iota(jnp.int32, offset.shape, 1)
         tables.append(slot_tile(wide_transpose(offset + HALO + atom)[:, :slots], tile))
     return coefs, tables
@@ -325,15 +329,6 @@
         out[:, pl.ds(first, piece), :] = part[...].astype(F32)
 
 
-def add_kernel(*refs):
-    *parts, total, rounded = refs
-    value = parts[0][...]
-    for part in parts[1:]:
-        value = value + part[...].astype(F32)
-    total[...] = value
-    rounded[...] = value.astype(BF16)
-
-
 def call(kernel, args, outs, scratch=(), scalars=0, limit=24, stay=(), tokens=(), flops=0):
     whole = pl.BlockSpec(memory_space=pltpu.VMEM)
     small = pl.BlockSpec(memory_space=pltpu.SMEM)
@@ -402,7 +397,7 @@
     spot = (atom_place >> cut_bits[0]) & 3
     place = jnp.stack([lax.axis_index("chan"), atom_place * atoms_dev, spot])
     place = place.astype(jnp.int32)
-    feature_cut = comps // 2 - 6
+    feature_cut = comps // 2
     feature_cuts = ((0, feature_cut), (feature_cut, comps))
 
     def held(*dims, dtype=F32):
@@ -415,19 +410,18 @@
     cot = jnp.transpose(cotangent, (1, 0, 2))
     mix = jnp.transpose(weights, (0, 1, 3, 2))
     anywhere = pl.BlockSpec(memory_space=pl.ANY)
-    rim_count = 2 * len(feature_cuts)
-    feature_rims = pl.pallas_call(
-        functools.partial(split_kernel, feature_cuts),
-        out_shape=tuple(
-            held(stop - start, chan_local, HALO, dtype=BF16)
-            for start, stop in feature_cuts
-            for _ in range(2)
-        ),
-        in_specs=[anywhere],
-        out_specs=(pl.BlockSpec(memory_space=pltpu.VMEM),) * rim_count,
-        scratch_shapes=[pltpu.SemaphoreType.DMA((rim_count,))],
-        compiler_params=pltpu.CompilerParams(vmem_limit_bytes=4 * 1024 * 1024),
-    )(pltpu.with_memory_space_constraint(fm, pltpu.HBM))
+    pieces = 6
+    feature_rims = []
+    for start, stop in feature_cuts:
+        feature_rims += pl.pallas_call(
+            functools.partial(split_kernel, start, pieces),
+            out_shape=(held(stop - start, chan_local, HALO, dtype=BF16),) * 2,
+            in_specs=[anywhere],
+            out_specs=(pl.BlockSpec(memory_space=pltpu.VMEM),) * 2,
+            scratch_shapes=[pltpu.SemaphoreType.DMA((2, pieces))],
+            compiler_params=pltpu.CompilerParams(vmem_limit_bytes=4 * 1024 * 1024),
+            cost_estimate=pl.CostEstimate(flops=0, bytes_accessed=1024, transcendentals=0),
+        )(pltpu.with_memory_space_constraint(fm, pltpu.HBM))
     from_sides = [
         shifted(rim, "atom", 1 if at % 2 == 0 else -1) for at, rim in enumerate(feature_rims)
     ]
@@ -465,23 +459,26 @@
         ),
         stay=tuple(range(7)),
     )
-    rims = after(rims, (token,))
+    (rims[0],) = after(rims[:1], (token,))
+    from_left = shifted(rims[0], "atom", 1)
     late_sides = after(from_sides[2:], (token,))
     late_chunks = []
     for flm, frm in zip(late_sides[::2], late_sides[1::2]):
         late_chunks += [flm, shifted(flm, "chan", 1), frm, shifted(frm, "chan", 1)]
-    from_left, from_right = shifted(rims[0], "atom", 1), shifted(rims[1], "atom", -1)
-    halo_b, grad_bias, message_a, message_b = call(
+    halo_b, grad_bias, message_a, message_b, token = call(
         functools.partial(edge_kernel, heads, score_scale, feature_cut, len(late_chunks) // 4),
         (*late_chunks, wp, qkv, cot, scores, partial, edge_bias, valid_mask, index_rows, index_wide),
         (
             held(comps - feature_cut, 3 * chan_local, atoms_dev, dtype=BF16),
             plain(heads, slots, atoms_dev),
-            held((2 * heads + 3) * slots, HALO),
-            held((2 * heads + 3) * slots, HALO),
+            held((2 * heads + 1) * slots, HALO, dtype=BF16),
+            held((2 * heads + 1) * slots, HALO, dtype=BF16),
+            plain(8, HALO),
         ),
         stay=(*range(len(late_chunks) + 5), len(late_chunks) + 7, len(late_chunks) + 8),
     )
+    (rims[1],) = after(rims[1:], (token,))
+    from_right = shifted(rims[1], "atom", -1)
     message_left = shifted(message_b, "atom", 1)
     message_right = shifted(message_a, "atom", -1)
     piece = (3 * (LMAX + 1), chan_local // 4, channels)
@@ -505,17 +502,12 @@
         scalars=1,
         stay=tuple(range(1, 10 + 4 * len(feature_cuts))),
     )
-    def summed(kept, parts):
-        return call(
-            add_kernel, (kept, *parts), (held(*piece), plain(*piece, dtype=BF16)), limit=8, stay=(0,)
-        )
-
-    kept, rounded = summed(
-        kept, [exchanged(part, "atom", delta << cut_bits[0]) for delta, part in enumerate(sent, 1)]
-    )
+    for delta, part in enumerate(sent, 1):
+        kept = kept + exchanged(part, "atom", delta << cut_bits[0]).astype(F32)
     rest = [bit for bit in reversed(range(count.bit_length() - 1)) if bit not in cut_bits]
     for bit in rest[:-1]:
-        kept, rounded = summed(kept, [exchanged(rounded, "atom", 1 << bit)])
+        kept = kept + exchanged(kept.astype(BF16), "atom", 1 << bit).astype(F32)
+    rounded = kept.astype(BF16)
     last = exchanged(rounded, "atom", 1 << rest[-1])
     parts, tokens = [], (rounded,)
     for (start, stop), halo_qkv in zip(feature_cuts, (halo_a, halo_b)):
@@ -536,7 +528,8 @@
         )
         parts += [mine, shifted(theirs, "chan", 1)]
         tokens = (token, last)
-    kept, rounded = summed(kept, after((last,), (token,)))
+    (last,) = after((last,), (token,))
+    rounded = (kept + last.astype(F32)).astype(BF16)
     pieces = [rounded] + [exchanged(rounded, "atom", d << cut_bits[0]) for d in range(1, 4)]
     (grad_weights,) = call(
         gather_kernel,

time: 111 us -> 117 us (1.054)
  Pallas kernels: 27.1 us -> 32.7 us
  starting transfers between devices: 34.2 us -> 38.9 us
  local copies, waits for them, and re-layouts: 4.55 us -> 1 us
    ppermute x15, waiting for transfers between devices: 33.1 us -> 24.8 us  [shifted(): return lax.ppermute(value, axis, pairs)]
    ppermute x8, waiting for transfers between devices: 10.9 us -> 18.5 us  [exchanged(): lax.ppermute(value, axis, [(source, source ^ offset) for source in range(...]
    ppermute x8, starting transfers between devices: 12.2 us -> 16.3 us  [exchanged(): lax.ppermute(value, axis, [(source, source ^ offset) for source in range(...]
    unnamed x12, local copies, waits for them, and re-layouts: 4.55 us -> 1 us
    pallas_call x11 -> x8, Pallas kernels: 24.6 us -> 28.1 us  [call(): pl.pallas_call(body, out_shape=tuple(outs), in_specs=[small] * scalars +...]
    pallas_call x1 -> x2, Pallas kernels: 2.45 us -> 4.61 us  [on_device(): pl.pallas_call(functools.partial(split_kernel, start, pieces), out_shape=...]
  transfers between devices with their start and end apart: 23 -> 23, of which waited for: 14 -> 14; matrix products, arithmetic and copies ran while one was open for 0% -> 0% of each run, Pallas kernels for 21% -> 25%
where the time goes in v9:
time: 117 us
  waiting for transfers between devices  43.3 us (37%)
  starting transfers between devices  38.9 us (33%)
  Pallas kernels  32.7 us (28%)
    pallas_call x8, Pallas kernels, call(): pl.pallas_call(body, out_shape=tuple(outs), in_specs=[small] * scalars +...  28.1 us
    ppermute x15, waiting for transfers between devices, shifted(): return lax.ppermute(value, axis, pairs)  24.8 us
    ppermute x15, starting transfers between devices, shifted(): return lax.ppermute(value, axis, pairs)  22.6 us
    ppermute x8, waiting for transfers between devices, exchanged(): lax.ppermute(value, axis, [(source, source ^ offset) for source in range(...  18.5 us
    ppermute x8, starting transfers between devices, exchanged(): lax.ppermute(value, axis, [(source, source ^ offset) for source in range(...  16.3 us
    pallas_call x2, Pallas kernels, on_device(): pl.pallas_call(functools.partial(split_kernel, start, pieces), out_shape=...  4.61 us
  transfers between devices with their start and end apart: 23, of which 14 were waited for; matrix products, arithmetic and copies ran while one was open for 0% of the time, Pallas kernels for 25%

profile of v9, /device:TPU:0, one launch (start us, length us, event | category | flops | bytes accessed | tf_op | source)
XLA Modules:
  0.0 116.9 jit_solution(10294809542016956460)
XLA Ops:
  0.6 0.0 copy-start
  0.7 0.5 collective-permute-start
  1.2 2.4 %shard_map.85 = (bf16[24,64,128]{2,1,0:T(8,128)(2,1)}, bf16[24,64,128]{2,1,0:T(8,128)(2,1)}) custom-call(bf16[49,64,256]{2,1,0:T(8,128)(2,1)} %bitcast.11), custom_call_target="tpu_custom_call" | custom-call | bytes 1024 | tf_op jit(solution)/shard_map/pallas_call | solution.py:416
  3.6 2.4 %collective-permute-start.1 = (bf16[24,64,128]{2,1,0:T(8,128)(2,1)}, bf16[24,64,128]{2,1,0:T(8,128)(2,1)}, u32[]{:S(2)}, u32[]{:S(2)}) collective-permute-start(bf16[24,64,128]{2,1,0:T(8,128)(2,1)} %get-tuple-element.42), channel_id=1, source_target_pairs={{0,2},{2,4},{4,6},{6,8},{8,10},{10,12},{12,14},{14,16},{16,18},{18... | collective-permute-start | bytes 1179656 | tf_op jit(solution)/shard_map/ppermute | solution.py:378
  6.0 4.1 %collective-permute-start.2 = (bf16[24,64,128]{2,1,0:T(8,128)(2,1)}, bf16[24,64,128]{2,1,0:T(8,128)(2,1)}, u32[]{:S(2)}, u32[]{:S(2)}) collective-permute-start(bf16[24,64,128]{2,1,0:T(8,128)(2,1)} %get-tuple-element.43), channel_id=1, source_target_pairs={{0,30},{2,0},{4,2},{6,4},{8,6},{10,8},{12,10},{14,12},{16,14},{18,... | collective-permute-start | bytes 1179656 | tf_op jit(solution)/shard_map/ppermute | solution.py:378
  10.1 2.2 %shard_map.88 = (bf16[25,64,128]{2,1,0:T(8,128)(2,1)}, bf16[25,64,128]{2,1,0:T(8,128)(2,1)}) custom-call(bf16[49,64,256]{2,1,0:T(8,128)(2,1)} %bitcast.12), custom_call_target="tpu_custom_call" | custom-call | bytes 1024 | tf_op jit(solution)/shard_map/pallas_call | solution.py:416
  12.3 0.1 collective-permute-start.5
  12.4 5.6 %collective-permute-start.6 = (bf16[25,64,128]{2,1,0:T(8,128)(2,1)}, bf16[25,64,128]{2,1,0:T(8,128)(2,1)}, u32[]{:S(2)}, u32[]{:S(2)}) collective-permute-start(bf16[25,64,128]{2,1,0:T(8,128)(2,1)} %get-tuple-element.48), channel_id=1, source_target_pairs={{0,30},{2,0},{4,2},{6,4},{8,6},{10,8},{12,10},{14,12},{16,14},{18,... | collective-permute-start | bytes 1228808 | tf_op jit(solution)/shard_map/ppermute | solution.py:378
  18.0 0.1 pad_add_fusion.refs_0_
  18.1 1.0 copy-done.4
  19.0 4.7 %shard_map.86 = (bf16[49,192,256]{2,1,0:T(8,128)(2,1)S(1)}, f32[8,256,256]{2,1,0:T(8,128)S(1)}, s32[2,3,128,128]{3,2,1,0:T(8,128)S(1)}, s32[16,256]{1,0:T(8,128)...) custom-call(s32[3]{0:T(128)S(1)} %pad_add_fusion.refs_0_, ...), custom_call_target="tpu_custom_call" | custom-call | flops 12000000000 | bytes 1024 | tf_op jit(solution)/shard_map/pallas_call | solution.py:344
  23.7 9.3 %collective-permute-done.1.refs_0_ = bf16[24,64,128]{2,1,0:T(8,128)(2,1)} collective-permute-done((bf16[24,64,128]{2,1,0:T(8,128)(2,1)}, bf16[24,64,128]{2,1,0:T(8,128)(2,1)}, u32[]{:S(2)}, u32[]{:S(2)}) %collective-permute-start.1) | collective-permute-done | bytes 393248 | tf_op jit(solution)/shard_map/ppermute | solution.py:378
  33.0 0.5 collective-permute-start.4
  33.5 1.4 %collective-permute-done.3.refs_1_.refs_4_ = bf16[24,64,128]{2,1,0:T(8,128)(2,1)S(1)} collective-permute-done((bf16[24,64,128]{2,1,0:T(8,128)(2,1)}, bf16[24,64,128]{2,1,0:T(8,128)(2,1)S(1)}, u32[]{:S(2)}, u32[]{:S(2)}) %collective-permute-start.3) | collective-permute-done | bytes 393248 | tf_op jit(solution)/shard_map/ppermute | solution.py:378
  34.9 0.6 collective-permute-done.4.refs_3_.refs_6_
  35.5 2.4 %shard_map.89 = (bf16[24,192,256]{2,1,0:T(8,128)(2,1)S(1)}, f32[8,2,128,128]{3,2,1,0:T(8,128)S(1)}, f32[8,128]{1,0:T(8,128)S(1)}) custom-call(bf16[24,64,128]{2,1,0:T(8,128)(2,1)} %get-tuple-element.45.refs_0_.refs_3_, bf16[24,64,128]{2,1,0:T(8,128)(2,1)S(1)} %collective-permute-done.3.refs_1_.refs_4_, ...), custom_call_target="tpu_custom_call" | custom-call | bytes 1024 | tf_op jit(solution)/shard_map/pallas_call | solution.py:344
  37.9 3.5 %collective-permute-done.5.refs_0_ = bf16[25,64,128]{2,1,0:T(8,128)(2,1)} collective-permute-done((bf16[25,64,128]{2,1,0:T(8,128)(2,1)}, bf16[25,64,128]{2,1,0:T(8,128)(2,1)}, u32[]{:S(2)}, u32[]{:S(2)}) %collective-permute-start.5) | collective-permute-done | bytes 409632 | tf_op jit(solution)/shard_map/ppermute | solution.py:378
  41.4 1.9 %collective-permute-done.6.refs_1_ = bf16[25,64,128]{2,1,0:T(8,128)(2,1)} collective-permute-done((bf16[25,64,128]{2,1,0:T(8,128)(2,1)}, bf16[25,64,128]{2,1,0:T(8,128)(2,1)}, u32[]{:S(2)}, u32[]{:S(2)}) %collective-permute-start.6) | collective-permute-done | bytes 409632 | tf_op jit(solution)/shard_map/ppermute | solution.py:378
  43.4 0.5 collective-permute-start.8
  43.9 1.5 %collective-permute-start.9 = (bf16[49,64,128]{2,1,0:T(8,128)(2,1)S(1)}, bf16[49,64,128]{2,1,0:T(8,128)(2,1)S(1)}, u32[]{:S(2)}, u32[]{:S(2)}) collective-permute-start(bf16[49,64,128]{2,1,0:T(8,128)(2,1)S(1)} %shard_map.93), channel_id=1, source_target_pairs={{0,2},{2,4},{4,6},{6,8},{8,10},{10,12},{12,14},{14,16},{16,18},{18... | collective-permute-start | bytes 2408456 | tf_op jit(solution)/shard_map/ppermute | solution.py:378
  45.4 0.5 collective-permute-done.8.refs_3_.refs_10_
  45.9 4.9 %shard_map.91 = (bf16[25,192,256]{2,1,0:T(8,128)(2,1)S(1)}, f32[4,16,256]{2,1,0:T(8,128)}, bf16[144,128]{1,0:T(8,128)(2,1)S(1)}, bf16[144,128]{1,0:T(8,128)(2,1)S(1)}, f32[8,128]{1,0:T(8,128)S(1)}) custom-call(bf16[25,64,128]{2,1,0:T(8,128)(2,1)} %get-tuple-element.52.refs_0_.refs_7_, bf16[25,64,128]{2,1,0:T(8,128)(2,1)S(1)} %collective-permute-done.7.refs_1_.refs_8_, ...), custom_call_target="tpu_custom_call" | custom-call | bytes 1024 | tf_op jit(solution)/shard_map/pallas_call | solution.py:344
  50.8 3.6 %collective-permute-start.10 = (bf16[49,64,128]{2,1,0:T(8,128)(2,1)S(1)}, bf16[49,64,128]{2,1,0:T(8,128)(2,1)S(1)}, u32[]{:S(2)}, u32[]{:S(2)}) collective-permute-start(bf16[49,64,128]{2,1,0:T(8,128)(2,1)S(1)} %shard_map.94), channel_id=1, source_target_pairs={{0,30},{2,0},{4,2},{6,4},{8,6},{10,8},{12,10},{14,12},{16,14},{18,... | collective-permute-start | bytes 2408456 | tf_op jit(solution)/shard_map/ppermute | solution.py:378
  54.5 8.1 %shard_map.92 = (bf16[49,64,256]{2,1,0:T(8,128)(2,1)S(1)}, f32[49,64,256]{2,1,0:T(8,128)S(1)}, f32[49,64,256]{2,1,0:T(8,128)S(1)}, f32[21,16,128]{2,1,0:T(8,128)...) custom-call(s32[3]{0:T(128)S(1)} %pad_add_fusion.refs_0_, ...), custom_call_target="tpu_custom_call" | custom-call | bytes 1024 | tf_op jit(solution)/shard_map/pallas_call | solution.py:344
  62.6 0.1 collective-permute-start.13
  62.6 0.9 collective-permute-start.14
  63.5 2.6 %collective-permute-start.15 = (bf16[21,16,128]{2,1,0:T(8,128)(2,1)S(1)}, bf16[21,16,128]{2,1,0:T(8,128)(2,1)S(1)}, u32[]{:S(2)}, u32[]{:S(2)}) collective-permute-start(bf16[21,16,128]{2,1,0:T(8,128)(2,1)S(1)} %get-tuple-element.73), channel_id=1, source_target_pairs={{0,12},{2,14},{4,8},{6,10},{8,4},{10,6},{12,0},{14,2},{16,28},{18,... | collective-permute-start | bytes 258056 | tf_op jit(solution)/shard_map/ppermute | solution.py:383
  66.1 5.0 %collective-permute-done.13 = bf16[21,16,128]{2,1,0:T(8,128)(2,1)S(1)} collective-permute-done((bf16[21,16,128]{2,1,0:T(8,128)(2,1)S(1)}, bf16[21,16,128]{2,1,0:T(8,128)(2,1)S(1)}, u32[]{:S(2)}, u32[]{:S(2)}) %collective-permute-start.13) | collective-permute-done | bytes 86048 | tf_op jit(solution)/shard_map/ppermute | solution.py:383
  71.1 5.3 %collective-permute-done.14 = bf16[21,16,128]{2,1,0:T(8,128)(2,1)S(1)} collective-permute-done((bf16[21,16,128]{2,1,0:T(8,128)(2,1)S(1)}, bf16[21,16,128]{2,1,0:T(8,128)(2,1)S(1)}, u32[]{:S(2)}, u32[]{:S(2)}) %collective-permute-start.14) | collective-permute-done | bytes 86048 | tf_op jit(solution)/shard_map/ppermute | solution.py:383
  76.4 0.8 collective-permute-done.15
  77.2 0.1 fusion.1
  77.3 1.9 %collective-permute-start.16 = (bf16[21,16,128]{2,1,0:T(8,128)(2,1)S(1)}, bf16[21,16,128]{2,1,0:T(8,128)(2,1)S(1)}, u32[]{:S(2)}, u32[]{:S(2)}) collective-permute-start(bf16[21,16,128]{2,1,0:T(8,128)(2,1)S(1)} %get-tuple-element.81), channel_id=1, source_target_pairs={{0,16},{2,18},{4,20},{6,22},{8,24},{10,26},{12,28},{14,30},{16,0},... | collective-permute-start | bytes 258056 | tf_op jit(solution)/shard_map/ppermute | solution.py:383
  79.1 3.6 %collective-permute-done.16 = bf16[21,16,128]{2,1,0:T(8,128)(2,1)S(1)} collective-permute-done((bf16[21,16,128]{2,1,0:T(8,128)(2,1)S(1)}, bf16[21,16,128]{2,1,0:T(8,128)(2,1)S(1)}, u32[]{:S(2)}, u32[]{:S(2)}) %collective-permute-start.16) | collective-permute-done | bytes 86048 | tf_op jit(solution)/shard_map/ppermute | solution.py:383
  82.8 7.4 %collective-permute-start.18 = (bf16[21,16,128]{2,1,0:T(8,128)(2,1)S(1)}, bf16[21,16,128]{2,1,0:T(8,128)(2,1)S(1)}, u32[]{:S(2)}, u32[]{:S(2)}) collective-permute-start(bf16[21,16,128]{2,1,0:T(8,128)(2,1)S(1)} %fusion.refs_9_), channel_id=1, source_target_pairs={{0,2},{2,0},{4,6},{6,4},{8,10},{10,8},{12,14},{14,12},{16,18},{18,... | collective-permute-start | bytes 258056 | tf_op jit(solution)/shard_map/ppermute | solution.py:383
  90.1 3.2 %collective-permute-start.12 = (bf16[144,128]{1,0:T(8,128)(2,1)S(1)}, bf16[144,128]{1,0:T(8,128)(2,1)S(1)}, u32[]{:S(2)}, u32[]{:S(2)}) collective-permute-start(bf16[144,128]{1,0:T(8,128)(2,1)S(1)} %get-tuple-element.61.refs_16_), channel_id=1, source_target_pairs={{0,30},{2,0},{4,2},{6,4},{8,6},{10,8},{12,10},{14,12},{16,14},{18,... | collective-permute-start | bytes 110600 | tf_op jit(solution)/shard_map/ppermute | solution.py:378
  93.3 1.6 %collective-permute-done.12.refs_7_ = bf16[144,128]{1,0:T(8,128)(2,1)S(1)} collective-permute-done((bf16[144,128]{1,0:T(8,128)(2,1)S(1)}, bf16[144,128]{1,0:T(8,128)(2,1)S(1)}, u32[]{:S(2)}, u32[]{:S(2)}) %collective-permute-start.12) | collective-permute-done | bytes 36896 | tf_op jit(solution)/shard_map/ppermute | solution.py:378
  95.0 5.9 %collective-permute-done.11.refs_6_ = bf16[144,128]{1,0:T(8,128)(2,1)S(1)} collective-permute-done((bf16[144,128]{1,0:T(8,128)(2,1)S(1)}, bf16[144,128]{1,0:T(8,128)(2,1)S(1)}, u32[]{:S(2)}, u32[]{:S(2)}) %collective-permute-start.11) | collective-permute-done | bytes 36896 | tf_op jit(solution)/shard_map/ppermute | solution.py:378
  100.9 2.6 %shard_map.95 = (f32[24,64,256]{2,1,0:T(8,128)S(1)}, bf16[24,64,256]{2,1,0:T(8,128)(2,1)S(1)}, f32[8,128]{1,0:T(8,128)S(1)}) custom-call(bf16[49,64,256]{2,1,0:T(8,128)(2,1)S(1)} %get-tuple-element.63.refs_0_, f32[49,64,256]{2,1,0:T(8,128)S(1)} %get-tuple-element.64.refs_1_, f32[49,64,256]{2,1,0:T(8,128)S(1)} %get-tuple-element.65.refs_2_, ...), custom_call_target="tpu_custom_call" | custom-call | bytes 1024 | tf_op jit(solution)/shard_map/pallas_call | solution.py:344
  103.5 2.6 %shard_map.96 = (f32[25,64,256]{2,1,0:T(8,128)S(1)}, bf16[25,64,256]{2,1,0:T(8,128)(2,1)S(1)}, f32[8,128]{1,0:T(8,128)S(1)}) custom-call(bf16[49,64,256]{2,1,0:T(8,128)(2,1)S(1)} %get-tuple-element.63.refs_0_, f32[49,64,256]{2,1,0:T(8,128)S(1)} %get-tuple-element.64.refs_1_, f32[49,64,256]{2,1,0:T(8,128)S(1)} %get-tuple-element.65.refs_2_, ...), custom_call_target="tpu_custom_call" | custom-call | bytes 1024 | tf_op jit(solution)/shard_map/pallas_call | solution.py:344
  106.0 0.1 collective-permute-start.19
  106.1 0.5 collective-permute-start.17
  106.7 0.1 collective-permute-start.22
  106.7 0.1 collective-permute-start.21
  106.8 3.4 %collective-permute-start.20 = (bf16[21,16,128]{2,1,0:T(8,128)(2,1)S(1)}, bf16[21,16,128]{2,1,0:T(8,128)(2,1)S(1)}, u32[]{:S(2)}, u32[]{:S(2)}) collective-permute-start(bf16[21,16,128]{2,1,0:T(8,128)(2,1)S(1)} %add_convert_fusion.refs_1_), channel_id=1, source_target_pairs={{0,4},{2,6},{4,0},{6,2},{8,12},{10,14},{12,8},{14,10},{16,20},{18,... | collective-permute-start | bytes 258056 | tf_op jit(solution)/shard_map/ppermute | solution.py:383
  110.2 2.8 %collective-permute-done.22.refs_4_ = bf16[21,16,128]{2,1,0:T(8,128)(2,1)S(1)} collective-permute-done((bf16[21,16,128]{2,1,0:T(8,128)(2,1)S(1)}, bf16[21,16,128]{2,1,0:T(8,128)(2,1)S(1)}, u32[]{:S(2)}, u32[]{:S(2)}) %collective-permute-start.22) | collective-permute-done | bytes 86048 | tf_op jit(solution)/shard_map/ppermute | solution.py:383
  113.0 1.0 collective-permute-done.20.refs_2_
  114.0 1.4 %shard_map.99 = f32[21,64,128]{2,1,0:T(8,128)} custom-call(s32[3]{0:T(128)S(1)} %pad_add_fusion.refs_0_, bf16[21,16,128]{2,1,0:T(8,128)(2,1)S(1)} %add_convert_fusion.refs_1_, bf16[21,16,128]{2,1,0:T(8,128)(2,1)S(1)} %collective-permute-done.20.refs_2_, bf16[21,16,128]{2,1,0:T(8,128)(2,1)S(1)} %collective-permute-done.21.refs_3_, ...), custom_call_target="tpu_custom_call" | custom-call | bytes 1024 | tf_op jit(solution)/shard_map/pallas_call | solution.py:344
  115.4 1.4 %shard_map.97 = bf16[49,64,256]{2,1,0:T(8,128)(2,1)} custom-call(f32[24,64,256]{2,1,0:T(8,128)S(1)} %get-tuple-element.74.refs_0_, bf16[24,64,256]{2,1,0:T(8,128)(2,1)S(1)} %collective-permute-done.17.refs_1_, f32[25,64,256]{2,1,0:T(8,128)S(1)} %get-tuple-element.77.refs_2_, bf16[25,64,256]{2,1,0:T(8,128)(2,1)S(1)} %collective-permute-done.19.refs_3_), custom_call_target="tpu_custom_call" | custom-call | bytes 1024 | tf_op jit(solution)/shard_map/pallas_call | solution.py:344
  (29 shorter events, 0.1 us)
Async XLA Ops:
  0.6 17.4 %copy-start = (bf16[64,49,256]{2,0,1:T(8,128)(2,1)S(1)}, bf16[64,49,256]{2,0,1:T(8,128)(2,1)}, u32[]{:S(2)}) copy-start(bf16[64,49,256]{2,0,1:T(8,128)(2,1)} %param.6) | copy-start | bytes 4816900
  0.6 17.4 %copy-start.5 = (s32[16,256]{1,0:T(8,128)S(1)}, s32[16,256]{1,0:T(8,128)}, u32[]{:S(2)}) copy-start(s32[16,256]{1,0:T(8,128)} %refs_5_.1) | copy-start | bytes 49156
  0.7 17.4 %copy-start.1 = (bf16[64,49,256]{2,0,1:T(8,128)(2,1)S(1)}, bf16[64,49,256]{2,0,1:T(8,128)(2,1)}, u32[]{:S(2)}) copy-start(bf16[64,49,256]{2,0,1:T(8,128)(2,1)} %param.8) | copy-start | bytes 4816900
  0.7 17.4 %collective-permute-start = (bf16[49,64,256]{2,1,0:T(8,128)(2,1)}, bf16[49,64,256]{2,1,0:T(8,128)(2,1)}, u32[]{:S(2)}, u32[]{:S(2)}) collective-permute-start(bf16[49,64,256]{2,1,0:T(8,128)(2,1)} %bitcast.10), channel_id=1, source_target_pairs={{0,1},{1,0},{2,3},{3,2},{4,5},{5,4},{6,7},{7,6},{8,9},{9,8},{10,11... | collective-permute-start | bytes 4816904 | tf_op jit(solution)/shard_map/ppermute | solution.py:378
  3.6 29.4 %collective-permute-start.1 = (bf16[24,64,128]{2,1,0:T(8,128)(2,1)}, bf16[24,64,128]{2,1,0:T(8,128)(2,1)}, u32[]{:S(2)}, u32[]{:S(2)}) collective-permute-start(bf16[24,64,128]{2,1,0:T(8,128)(2,1)} %get-tuple-element.42), channel_id=1, source_target_pairs={{0,2},{2,4},{4,6},{6,8},{8,10},{10,12},{12,14},{14,16},{16,18},{18... | collective-permute-start | bytes 1179656 | tf_op jit(solution)/shard_map/ppermute | solution.py:378
  6.0 26.9 %collective-permute-start.2 = (bf16[24,64,128]{2,1,0:T(8,128)(2,1)}, bf16[24,64,128]{2,1,0:T(8,128)(2,1)}, u32[]{:S(2)}, u32[]{:S(2)}) collective-permute-start(bf16[24,64,128]{2,1,0:T(8,128)(2,1)} %get-tuple-element.43), channel_id=1, source_target_pairs={{0,30},{2,0},{4,2},{6,4},{8,6},{10,8},{12,10},{14,12},{16,14},{18,... | collective-permute-start | bytes 1179656 | tf_op jit(solution)/shard_map/ppermute | solution.py:378
  12.3 29.1 %collective-permute-start.5 = (bf16[25,64,128]{2,1,0:T(8,128)(2,1)}, bf16[25,64,128]{2,1,0:T(8,128)(2,1)}, u32[]{:S(2)}, u32[]{:S(2)}) collective-permute-start(bf16[25,64,128]{2,1,0:T(8,128)(2,1)} %get-tuple-element.47), channel_id=1, source_target_pairs={{0,2},{2,4},{4,6},{6,8},{8,10},{10,12},{12,14},{14,16},{16,18},{18... | collective-permute-start | bytes 1228808 | tf_op jit(solution)/shard_map/ppermute | solution.py:378
  12.4 31.0 %collective-permute-start.6 = (bf16[25,64,128]{2,1,0:T(8,128)(2,1)}, bf16[25,64,128]{2,1,0:T(8,128)(2,1)}, u32[]{:S(2)}, u32[]{:S(2)}) collective-permute-start(bf16[25,64,128]{2,1,0:T(8,128)(2,1)} %get-tuple-element.48), channel_id=1, source_target_pairs={{0,30},{2,0},{4,2},{6,4},{8,6},{10,8},{12,10},{14,12},{16,14},{18,... | collective-permute-start | bytes 1228808 | tf_op jit(solution)/shard_map/ppermute | solution.py:378
  18.1 1.0 copy-start.4
  33.0 1.9 %collective-permute-start.3 = (bf16[24,64,128]{2,1,0:T(8,128)(2,1)}, bf16[24,64,128]{2,1,0:T(8,128)(2,1)S(1)}, u32[]{:S(2)}, u32[]{:S(2)}) collective-permute-start(bf16[24,64,128]{2,1,0:T(8,128)(2,1)} %get-tuple-element.45.refs_0_.refs_3_), channel_id=1, source_target_pairs={{0,1},{1,0},{2,3},{3,2},{4,5},{5,4},{6,7},{7,6},{8,9},{9,8},{10,11... | collective-permute-start | bytes 1179656 | tf_op jit(solution)/shard_map/ppermute | solution.py:378
  33.0 2.5 %collective-permute-start.4 = (bf16[24,64,128]{2,1,0:T(8,128)(2,1)}, bf16[24,64,128]{2,1,0:T(8,128)(2,1)S(1)}, u32[]{:S(2)}, u32[]{:S(2)}) collective-permute-start(bf16[24,64,128]{2,1,0:T(8,128)(2,1)} %get-tuple-element.46.refs_2_.refs_5_), channel_id=1, source_target_pairs={{0,1},{1,0},{2,3},{3,2},{4,5},{5,4},{6,7},{7,6},{8,9},{9,8},{10,11... | collective-permute-start | bytes 1179656 | tf_op jit(solution)/shard_map/ppermute | solution.py:378
  37.9 8.0 %copy-start.2 = (f32[4,16,256]{2,1,0:T(8,128)S(1)}, f32[4,16,256]{2,1,0:T(8,128)}, u32[]{:S(2)}) copy-start(f32[4,16,256]{2,1,0:T(8,128)} %refs_9_.1) | copy-start | bytes 196612
  37.9 8.0 %copy-start.3 = (s32[16,256]{1,0:T(8,128)S(1)}, s32[16,256]{1,0:T(8,128)}, u32[]{:S(2)}) copy-start(s32[16,256]{1,0:T(8,128)} %refs_10_.1) | copy-start | bytes 49156
  43.4 2.0 %collective-permute-start.7 = (bf16[25,64,128]{2,1,0:T(8,128)(2,1)}, bf16[25,64,128]{2,1,0:T(8,128)(2,1)S(1)}, u32[]{:S(2)}, u32[]{:S(2)}) collective-permute-start(bf16[25,64,128]{2,1,0:T(8,128)(2,1)} %get-tuple-element.52.refs_0_.refs_7_), channel_id=1, source_target_pairs={{0,1},{1,0},{2,3},{3,2},{4,5},{5,4},{6,7},{7,6},{8,9},{9,8},{10,11... | collective-permute-start | bytes 1228808 | tf_op jit(solution)/shard_map/ppermute | solution.py:378
  43.4 2.5 %collective-permute-start.8 = (bf16[25,64,128]{2,1,0:T(8,128)(2,1)}, bf16[25,64,128]{2,1,0:T(8,128)(2,1)S(1)}, u32[]{:S(2)}, u32[]{:S(2)}) collective-permute-start(bf16[25,64,128]{2,1,0:T(8,128)(2,1)} %get-tuple-element.53.refs_2_.refs_9_), channel_id=1, source_target_pairs={{0,1},{1,0},{2,3},{3,2},{4,5},{5,4},{6,7},{7,6},{8,9},{9,8},{10,11... | collective-permute-start | bytes 1228808 | tf_op jit(solution)/shard_map/ppermute | solution.py:378
  43.9 57.0 %collective-permute-start.9 = (bf16[49,64,128]{2,1,0:T(8,128)(2,1)S(1)}, bf16[49,64,128]{2,1,0:T(8,128)(2,1)S(1)}, u32[]{:S(2)}, u32[]{:S(2)}) collective-permute-start(bf16[49,64,128]{2,1,0:T(8,128)(2,1)S(1)} %shard_map.93), channel_id=1, source_target_pairs={{0,2},{2,4},{4,6},{6,8},{8,10},{10,12},{12,14},{14,16},{16,18},{18... | collective-permute-start | bytes 2408456 | tf_op jit(solution)/shard_map/ppermute | solution.py:378
  50.8 50.0 %collective-permute-start.10 = (bf16[49,64,128]{2,1,0:T(8,128)(2,1)S(1)}, bf16[49,64,128]{2,1,0:T(8,128)(2,1)S(1)}, u32[]{:S(2)}, u32[]{:S(2)}) collective-permute-start(bf16[49,64,128]{2,1,0:T(8,128)(2,1)S(1)} %shard_map.94), channel_id=1, source_target_pairs={{0,30},{2,0},{4,2},{6,4},{8,6},{10,8},{12,10},{14,12},{16,14},{18,... | collective-permute-start | bytes 2408456 | tf_op jit(solution)/shard_map/ppermute | solution.py:378
  62.6 8.6 %collective-permute-start.13 = (bf16[21,16,128]{2,1,0:T(8,128)(2,1)S(1)}, bf16[21,16,128]{2,1,0:T(8,128)(2,1)S(1)}, u32[]{:S(2)}, u32[]{:S(2)}) collective-permute-start(bf16[21,16,128]{2,1,0:T(8,128)(2,1)S(1)} %get-tuple-element.71), channel_id=1, source_target_pairs={{0,4},{2,6},{4,0},{6,2},{8,12},{10,14},{12,8},{14,10},{16,20},{18,... | collective-permute-start | bytes 258056 | tf_op jit(solution)/shard_map/ppermute | solution.py:383
  62.6 13.8 %collective-permute-start.14 = (bf16[21,16,128]{2,1,0:T(8,128)(2,1)S(1)}, bf16[21,16,128]{2,1,0:T(8,128)(2,1)S(1)}, u32[]{:S(2)}, u32[]{:S(2)}) collective-permute-start(bf16[21,16,128]{2,1,0:T(8,128)(2,1)S(1)} %get-tuple-element.72), channel_id=1, source_target_pairs={{0,8},{2,10},{4,12},{6,14},{8,0},{10,2},{12,4},{14,6},{16,24},{18,... | collective-permute-start | bytes 258056 | tf_op jit(solution)/shard_map/ppermute | solution.py:383
  63.5 13.7 %collective-permute-start.15 = (bf16[21,16,128]{2,1,0:T(8,128)(2,1)S(1)}, bf16[21,16,128]{2,1,0:T(8,128)(2,1)S(1)}, u32[]{:S(2)}, u32[]{:S(2)}) collective-permute-start(bf16[21,16,128]{2,1,0:T(8,128)(2,1)S(1)} %get-tuple-element.73), channel_id=1, source_target_pairs={{0,12},{2,14},{4,8},{6,10},{8,4},{10,6},{12,0},{14,2},{16,28},{18,... | collective-permute-start | bytes 258056 | tf_op jit(solution)/shard_map/ppermute | solution.py:383
  77.3 5.4 %collective-permute-start.16 = (bf16[21,16,128]{2,1,0:T(8,128)(2,1)S(1)}, bf16[21,16,128]{2,1,0:T(8,128)(2,1)S(1)}, u32[]{:S(2)}, u32[]{:S(2)}) collective-permute-start(bf16[21,16,128]{2,1,0:T(8,128)(2,1)S(1)} %get-tuple-element.81), channel_id=1, source_target_pairs={{0,16},{2,18},{4,20},{6,22},{8,24},{10,26},{12,28},{14,30},{16,0},... | collective-permute-start | bytes 258056 | tf_op jit(solution)/shard_map/ppermute | solution.py:383
  82.8 20.7 %collective-permute-start.18 = (bf16[21,16,128]{2,1,0:T(8,128)(2,1)S(1)}, bf16[21,16,128]{2,1,0:T(8,128)(2,1)S(1)}, u32[]{:S(2)}, u32[]{:S(2)}) collective-permute-start(bf16[21,16,128]{2,1,0:T(8,128)(2,1)S(1)} %fusion.refs_9_), channel_id=1, source_target_pairs={{0,2},{2,0},{4,6},{6,4},{8,10},{10,8},{12,14},{14,12},{16,18},{18,... | collective-permute-start | bytes 258056 | tf_op jit(solution)/shard_map/ppermute | solution.py:383
  90.1 4.8 %collective-permute-start.12 = (bf16[144,128]{1,0:T(8,128)(2,1)S(1)}, bf16[144,128]{1,0:T(8,128)(2,1)S(1)}, u32[]{:S(2)}, u32[]{:S(2)}) collective-permute-start(bf16[144,128]{1,0:T(8,128)(2,1)S(1)} %get-tuple-element.61.refs_16_), channel_id=1, source_target_pairs={{0,30},{2,0},{4,2},{6,4},{8,6},{10,8},{12,10},{14,12},{16,14},{18,... | collective-permute-start | bytes 110600 | tf_op jit(solution)/shard_map/ppermute | solution.py:378
  93.3 7.6 %collective-permute-start.11 = (bf16[144,128]{1,0:T(8,128)(2,1)S(1)}, bf16[144,128]{1,0:T(8,128)(2,1)S(1)}, u32[]{:S(2)}, u32[]{:S(2)}) collective-permute-start(bf16[144,128]{1,0:T(8,128)(2,1)S(1)} %get-tuple-element.62.refs_17_), channel_id=1, source_target_pairs={{0,2},{2,4},{4,6},{6,8},{8,10},{10,12},{12,14},{14,16},{16,18},{18... | collective-permute-start | bytes 110600 | tf_op jit(solution)/shard_map/ppermute | solution.py:378
  106.0 9.4 %collective-permute-start.19 = (bf16[25,64,256]{2,1,0:T(8,128)(2,1)S(1)}, bf16[25,64,256]{2,1,0:T(8,128)(2,1)S(1)}, u32[]{:S(2)}, u32[]{:S(2)}) collective-permute-start(bf16[25,64,256]{2,1,0:T(8,128)(2,1)S(1)} %get-tuple-element.78), channel_id=1, source_target_pairs={{0,1},{1,0},{2,3},{3,2},{4,5},{5,4},{6,7},{7,6},{8,9},{9,8},{10,11... | collective-permute-start | bytes 2457608 | tf_op jit(solution)/shard_map/ppermute | solution.py:378
  106.1 9.3 %collective-permute-start.17 = (bf16[24,64,256]{2,1,0:T(8,128)(2,1)S(1)}, bf16[24,64,256]{2,1,0:T(8,128)(2,1)S(1)}, u32[]{:S(2)}, u32[]{:S(2)}) collective-permute-start(bf16[24,64,256]{2,1,0:T(8,128)(2,1)S(1)} %get-tuple-element.75), channel_id=1, source_target_pairs={{0,1},{1,0},{2,3},{3,2},{4,5},{5,4},{6,7},{7,6},{8,9},{9,8},{10,11... | collective-permute-start | bytes 2359304 | tf_op jit(solution)/shard_map/ppermute | solution.py:378
  106.7 6.4 %collective-permute-start.22 = (bf16[21,16,128]{2,1,0:T(8,128)(2,1)S(1)}, bf16[21,16,128]{2,1,0:T(8,128)(2,1)S(1)}, u32[]{:S(2)}, u32[]{:S(2)}) collective-permute-start(bf16[21,16,128]{2,1,0:T(8,128)(2,1)S(1)} %add_convert_fusion.refs_1_), channel_id=1, source_target_pairs={{0,12},{2,14},{4,8},{6,10},{8,4},{10,6},{12,0},{14,2},{16,28},{18,... | collective-permute-start | bytes 258056 | tf_op jit(solution)/shard_map/ppermute | solution.py:383
  106.7 6.3 %collective-permute-start.21 = (bf16[21,16,128]{2,1,0:T(8,128)(2,1)S(1)}, bf16[21,16,128]{2,1,0:T(8,128)(2,1)S(1)}, u32[]{:S(2)}, u32[]{:S(2)}) collective-permute-start(bf16[21,16,128]{2,1,0:T(8,128)(2,1)S(1)} %add_convert_fusion.refs_1_), channel_id=1, source_target_pairs={{0,8},{2,10},{4,12},{6,14},{8,0},{10,2},{12,4},{14,6},{16,24},{18,... | collective-permute-start | bytes 258056 | tf_op jit(solution)/shard_map/ppermute | solution.py:383
  106.8 7.2 %collective-permute-start.20 = (bf16[21,16,128]{2,1,0:T(8,128)(2,1)S(1)}, bf16[21,16,128]{2,1,0:T(8,128)(2,1)S(1)}, u32[]{:S(2)}, u32[]{:S(2)}) collective-permute-start(bf16[21,16,128]{2,1,0:T(8,128)(2,1)S(1)} %add_convert_fusion.refs_1_), channel_id=1, source_target_pairs={{0,4},{2,6},{4,0},{6,2},{8,12},{10,14},{12,8},{14,10},{16,20},{18,... | collective-permute-start | bytes 258056 | tf_op jit(solution)/shard_map/ppermute | solution.py:383

commit v10 on v6

--- a/solution.py
+++ b/solution.py
@@ -1,6 +1,5 @@
 import functools
 import math
-import operator
 
 import jax
 import jax.numpy as jnp
@@ -193,8 +192,9 @@
             same = (index == index[slot : slot + 1, :])[None]
             merged = merged + jnp.where(same, both[:, slot : slot + 1, :], 0.0)
         atom = lax.broadcasted_iota(jnp.int32, (slots, HALO), 1)
-        message[: 2 * heads * slots, :] = merged.reshape(2 * heads * slots, HALO).astype(BF16)
-        message[2 * heads * slots :, :] = (index - HALO - atom).astype(F32).astype(BF16)
+        edge_rows = 2 * heads * slots
+        message[:edge_rows, :] = merged.reshape(edge_rows, HALO).astype(BF16)
+        message[edge_rows:, :] = (index - HALO - atom).astype(F32).astype(BF16)
 
 
 def joined_rows(early, late, first_row, rows):
@@ -297,9 +297,7 @@
 
 
 def value_kernel(heads, slots, start, stop, own_value, cl, cr, message_left, message_right, wc, terms,
-                 mine, token, *theirs):
-    *theirs, grad = theirs
-    token[...] = jnp.zeros_like(token)
+                 mine, theirs, grad):
     comps, chan_local = stop - start, cl.shape[1]
     rows = chan_local // heads
     coefs, tables = halo_slots(message_left, message_right, 2 * heads, slots)
@@ -320,26 +318,18 @@
         mix = wc[degree_of(start + comp)][:, 2 * chan_local :]
         total = terms[start + comp] + nn(mix, grad[comp])
         mine[comp] = total[:chan_local]
-        part = theirs[0].shape[0]
-        theirs[comp // part][comp % part] = total[chan_local:].astype(BF16)
-
-
-def finish_kernel(parts, *refs):
-    *refs, out = refs
-    start = 0
-    for count in parts:
-        mine, theirs, refs = refs[0], refs[1 : count + 1], refs[count + 1 :]
-        at = 0
-        for part in theirs:
-            size = part.shape[0]
-            total = mine[at : at + size] + part[...].astype(F32)
-            out[start + at : start + at + size] = total.astype(BF16)
-            at += size
-        start += at
-
-
-def gather_kernel(place, part_0, part_1, part_2, part_3, out, token):
-    token[...] = jnp.zeros_like(token)
+        theirs[comp] = total[chan_local:].astype(BF16)
+
+
+def finish_kernel(*refs):
+    out, start = refs[-1], 0
+    for mine, theirs in zip(refs[:-1:2], refs[1:-1:2]):
+        stop = start + mine.shape[0]
+        out[start:stop] = (mine[...] + theirs[...].astype(F32)).astype(BF16)
+        start = stop
+
+
+def gather_kernel(place, part_0, part_1, part_2, part_3, out):
     piece = part_0.shape[1]
     spot = place[2]
     for delta, part in enumerate((part_0, part_1, part_2, part_3)):
@@ -399,12 +389,6 @@
 def exchanged(value, axis, offset):
     count = lax.axis_size(axis)
     return lax.ppermute(value, axis, [(source, source ^ offset) for source in range(count)])
-
-
-def crossed(value, target):
-    count = lax.axis_size("atom")
-    pairs = [(2 * at + core, 2 * target(at) + 1 - core) for at in range(count) for core in range(2)]
-    return shifted(lax.ppermute(value, ("atom", "chan"), pairs), "chan", 1)
 
 
 def on_device(features, weights, cotangent, edge_bias, neighbours, valid_mask):
@@ -422,9 +406,7 @@
     place = jnp.stack([lax.axis_index("chan"), atom_place * atoms_dev, spot])
     place = place.astype(jnp.int32)
     feature_cut = comps // 2
-    value_cut = comps // 2
     feature_cuts = ((0, feature_cut), (feature_cut, comps))
-    cuts = ((0, value_cut), (value_cut, comps))
 
     def held(*dims, dtype=F32):
         return pltpu.VMEM(dims, dtype)
@@ -503,8 +485,8 @@
         ),
         stay=(*range(len(late_chunks) + 5), len(late_chunks) + 7, len(late_chunks) + 8),
     )
-    message_left = crossed(message_b, lambda at: (at + 1) % count)
-    message_right = crossed(message_a, lambda at: (at - 1) % count)
+    message_left = shifted(message_b, "atom", 1)
+    message_right = shifted(message_a, "atom", -1)
     piece = (3 * (LMAX + 1), chan_local // 4, channels)
     grad_query, own_key, own_value, kept, *sent = call(
         functools.partial(grads_kernel, heads, slots, len(feature_cuts)),
@@ -526,21 +508,7 @@
         scalars=1,
         stay=tuple(range(1, 10 + 4 * len(feature_cuts))),
     )
-    for delta, part in enumerate(sent, 1):
-        kept = kept + exchanged(part, "atom", delta << cut_bits[0]).astype(F32)
-    rest = [bit for bit in range(count.bit_length() - 1) if bit not in cut_bits]
-    while rest:
-        offsets = [1 << bit for bit in rest[:2]]
-        rest = rest[2:]
-        rounded = kept.astype(BF16)
-        offsets += [sum(offsets)] * (len(offsets) - 1)
-        arrived = [
-            crossed(rounded, functools.partial(operator.xor, offset))
-            if offset == 1
-            else exchanged(rounded, "atom", offset)
-            for offset in offsets
-        ]
-        kept = functools.reduce(lambda total, part: total + part.astype(F32), arrived, kept)
+    message_left, message_right, *sent = after((message_left, message_right, *sent), ())
     terms, token = call(
         functools.partial(key_kernel, heads, slots),
         (grad_query, own_key, halo_a, halo_b, message_left, message_right, wc),
@@ -549,44 +517,44 @@
         limit=16,
         stay=(0, 1, 2, 3, 6),
     )
-    from_left, from_right, rounded = after((from_left, from_right, kept.astype(BF16)), (token,))
-    pieces = [rounded] + [exchanged(rounded, "atom", d << cut_bits[0]) for d in range(1, 4)]
-    grad_weights, gathered = call(
-        gather_kernel,
-        (place, *pieces),
-        (plain(3 * (LMAX + 1), chan_local, channels), plain(8, HALO)),
-        scalars=1,
-        limit=8,
-        flops=20 * 10**9,
-    )
-    parts, counts = [], []
-    tokens = ()
-    for start, stop in cuts:
+    for delta, part in enumerate(sent, 1):
+        kept = kept + exchanged(part, "atom", delta << cut_bits[0]).astype(F32)
+    rest = [bit for bit in reversed(range(count.bit_length() - 1)) if bit not in cut_bits]
+    for bit in rest[:-1]:
+        kept = kept + exchanged(kept.astype(BF16), "atom", 1 << bit).astype(F32)
+    (rounded,) = after((kept.astype(BF16),), (token,))
+    last = exchanged(rounded, "atom", 1 << rest[-1])
+    parts = []
+    for start, stop in feature_cuts:
         size = stop - start
-        sizes = [size]
-        mine, token, *theirs = call(
+        mine, theirs = call(
             functools.partial(value_kernel, heads, slots, start, stop),
             (own_value, from_left, from_right, message_left, message_right, wc, terms),
             (
                 held(size, chan_local, atoms_dev),
-                plain(8, HALO),
-                *(held(some, chan_local, atoms_dev, dtype=BF16) for some in sizes),
+                held(size, chan_local, atoms_dev, dtype=BF16),
             ),
             scratch=[pltpu.VMEM((size, chan_local, atoms_dev), BF16)],
             limit=16,
             stay=(0, 1, 2, 5, 6),
-            tokens=tokens,
+            tokens=(last,) if parts else (rounded,),
         )
-        tokens = (token, pieces[2])
-        counts.append(len(sizes))
-        parts += [mine, *(shifted(some, "chan", 1) for some in theirs)]
+        parts += [mine, shifted(theirs, "chan", 1)]
+    rounded = (kept + last.astype(F32)).astype(BF16)
+    pieces = [rounded] + [exchanged(rounded, "atom", d << cut_bits[0]) for d in range(1, 4)]
+    (grad_weights,) = call(
+        gather_kernel,
+        (place, *pieces),
+        (plain(3 * (LMAX + 1), chan_local, channels),),
+        scalars=1,
+        limit=8,
+    )
     (out,) = call(
-        functools.partial(finish_kernel, counts),
+        finish_kernel,
         parts,
         (plain(comps, chan_local, atoms_dev, dtype=BF16),),
         limit=8,
         stay=tuple(range(len(parts))),
-        tokens=(gathered,),
     )
     grad_features = jnp.transpose(out, (1, 0, 2))
     grad_weights = grad_weights.reshape(3, LMAX + 1, chan_local, channels)

time: 111 us -> 118 us (1.063)
  waiting for transfers between devices: 38.7 us -> 52.4 us
  starting transfers between devices: 38 us -> 31.8 us
    ppermute x16 -> x15, waiting for transfers between devices: 18.6 us -> 38.3 us  [shifted(): return lax.ppermute(value, axis, pairs)]
    ppermute x3 -> x0, waiting for transfers between devices: 7.02 us -> none  [crossed(): return shifted(lax.ppermute(value, ('atom', 'chan'), pairs), 'chan', 1)]
    ppermute x3 -> x0, starting transfers between devices: 5.34 us -> none  [crossed(): return shifted(lax.ppermute(value, ('atom', 'chan'), pairs), 'chan', 1)]
    ppermute x8, starting transfers between devices: 11.5 us -> 9.75 us  [exchanged(): lax.ppermute(value, axis, [(source, source ^ offset) for source in range(...]
    ppermute x16 -> x15, starting transfers between devices: 21.2 us -> 22.1 us  [shifted(): return lax.ppermute(value, axis, pairs)]
  transfers between devices with their start and end apart: 27 -> 23, of which waited for: 12 -> 13; matrix products, arithmetic and copies ran while one was open for 0% -> 0% of each run, Pallas kernels for 24% -> 21%
where the time goes in v10:
time: 118 us
  waiting for transfers between devices  52.4 us (44%)
  starting transfers between devices  31.8 us (27%)
  Pallas kernels  28.2 us (24%)
  local copies, waits for them, and re-layouts  4.55 us (4%)
    ppermute x15, waiting for transfers between devices, shifted(): return lax.ppermute(value, axis, pairs)  38.3 us
    pallas_call x9, Pallas kernels, call(): pl.pallas_call(body, out_shape=tuple(outs), in_specs=[small] * scalars +...  25.6 us
    ppermute x15, starting transfers between devices, shifted(): return lax.ppermute(value, axis, pairs)  22.1 us
    ppermute x8, waiting for transfers between devices, exchanged(): lax.ppermute(value, axis, [(source, source ^ offset) for source in range(...  14 us
    ppermute x8, starting transfers between devices, exchanged(): lax.ppermute(value, axis, [(source, source ^ offset) for source in range(...  9.75 us
    unnamed x12, local copies, waits for them, and re-layouts  4.55 us
    pallas_call x1, Pallas kernels, on_device(): pl.pallas_call(functools.partial(split_kernel, feature_cuts), out_shape=t...  2.54 us
  transfers between devices with their start and end apart: 23, of which 13 were waited for; matrix products, arithmetic and copies ran while one was open for 0% of the time, Pallas kernels for 21%

profile of v10, /device:TPU:0, one launch (start us, length us, event | category | flops | bytes accessed | tf_op | source)
XLA Modules:
  0.0 117.8 jit_solution(3698734430076981328)
XLA Ops:
  0.6 0.5 collective-permute-start
  1.1 2.5 %shard_map.85 = (bf16[24,64,128]{2,1,0:T(8,128)(2,1)}, bf16[24,64,128]{2,1,0:T(8,128)(2,1)}, bf16[25,64,128]{2,1,0:T(8,128)(2,1)}, bf16[25,64,128]{2,1,0:T(8,128)(2,1)}) custom-call(bf16[49,64,256]{2,1,0:T(8,128)(2,1)} %bitcast.15), custom_call_target="tpu_custom_call" | custom-call | tf_op jit(solution)/shard_map/pallas_call | solution.py:422
  3.7 2.6 %collective-permute-start.1 = (bf16[24,64,128]{2,1,0:T(8,128)(2,1)}, bf16[24,64,128]{2,1,0:T(8,128)(2,1)S(1)}, u32[]{:S(2)}, u32[]{:S(2)}) collective-permute-start(bf16[24,64,128]{2,1,0:T(8,128)(2,1)} %get-tuple-element.48), channel_id=1, source_target_pairs={{0,2},{2,4},{4,6},{6,8},{8,10},{10,12},{12,14},{14,16},{16,18},{18... | collective-permute-start | bytes 1179656 | tf_op jit(solution)/shard_map/ppermute | solution.py:386
  6.3 4.1 %collective-permute-start.2 = (bf16[24,64,128]{2,1,0:T(8,128)(2,1)}, bf16[24,64,128]{2,1,0:T(8,128)(2,1)S(1)}, u32[]{:S(2)}, u32[]{:S(2)}) collective-permute-start(bf16[24,64,128]{2,1,0:T(8,128)(2,1)} %get-tuple-element.49), channel_id=1, source_target_pairs={{0,30},{2,0},{4,2},{6,4},{8,6},{10,8},{12,10},{14,12},{16,14},{18,... | collective-permute-start | bytes 1179656 | tf_op jit(solution)/shard_map/ppermute | solution.py:386
  10.3 5.6 %collective-permute-start.6 = (bf16[25,64,128]{2,1,0:T(8,128)(2,1)}, bf16[25,64,128]{2,1,0:T(8,128)(2,1)S(1)}, u32[]{:S(2)}, u32[]{:S(2)}) collective-permute-start(bf16[25,64,128]{2,1,0:T(8,128)(2,1)} %get-tuple-element.54), channel_id=1, source_target_pairs={{0,30},{2,0},{4,2},{6,4},{8,6},{10,8},{12,10},{14,12},{16,14},{18,... | collective-permute-start | bytes 1228808 | tf_op jit(solution)/shard_map/ppermute | solution.py:386
  15.9 0.1 pad_add_fusion.refs_0_
  16.0 1.4 %copy-done = bf16[64,49,256]{2,0,1:T(8,128)(2,1)S(1)} copy-done((bf16[64,49,256]{2,0,1:T(8,128)(2,1)S(1)}, bf16[64,49,256]{2,0,1:T(8,128)(2,1)}, u32[]{:S(2)}) %copy-start) | copy-done | bytes 1605656
  17.4 1.4 %copy-done.1 = bf16[64,49,256]{2,0,1:T(8,128)(2,1)S(1)} copy-done((bf16[64,49,256]{2,0,1:T(8,128)(2,1)S(1)}, bf16[64,49,256]{2,0,1:T(8,128)(2,1)}, u32[]{:S(2)}) %copy-start.1) | copy-done | bytes 1605656
  18.9 1.0 copy-done.4
  19.8 0.7 copy-done.5
  20.6 3.8 %shard_map.86 = (bf16[49,192,256]{2,1,0:T(8,128)(2,1)S(1)}, f32[8,256,256]{2,1,0:T(8,128)S(1)}, s32[2,3,128,128]{3,2,1,0:T(8,128)S(1)}, s32[16,256]{1,0:T(8,128)...) custom-call(s32[3]{0:T(128)S(1)} %pad_add_fusion.refs_0_, ...), custom_call_target="tpu_custom_call" | custom-call | flops 12000000000 | bytes 1024 | tf_op jit(solution)/shard_map/pallas_call | solution.py:352
  24.4 8.9 %collective-permute-done.1.refs_0_ = bf16[24,64,128]{2,1,0:T(8,128)(2,1)S(1)} collective-permute-done((bf16[24,64,128]{2,1,0:T(8,128)(2,1)}, bf16[24,64,128]{2,1,0:T(8,128)(2,1)S(1)}, u32[]{:S(2)}, u32[]{:S(2)}) %collective-permute-start.1) | collective-permute-done | bytes 393248 | tf_op jit(solution)/shard_map/ppermute | solution.py:386
  33.2 0.5 collective-permute-start.4
  33.7 1.2 %collective-permute-done.3.refs_1_.refs_4_ = bf16[24,64,128]{2,1,0:T(8,128)(2,1)S(1)} collective-permute-done((bf16[24,64,128]{2,1,0:T(8,128)(2,1)S(1)}, bf16[24,64,128]{2,1,0:T(8,128)(2,1)S(1)}, u32[]{:S(2)}, u32[]{:S(2)}) %collective-permute-start.3) | collective-permute-done | bytes 393248 | tf_op jit(solution)/shard_map/ppermute | solution.py:386
  34.9 0.6 collective-permute-done.4.refs_3_.refs_6_
  35.5 1.3 %shard_map.88 = (bf16[24,192,256]{2,1,0:T(8,128)(2,1)S(1)}, f32[8,2,128,128]{3,2,1,0:T(8,128)S(1)}, f32[8,128]{1,0:T(8,128)S(1)}) custom-call(bf16[24,64,128]{2,1,0:T(8,128)(2,1)S(1)} %get-tuple-element.51.refs_0_.refs_3_, bf16[24,64,128]{2,1,0:T(8,128)(2,1)S(1)} %collective-permute-done.3.refs_1_.refs_4_, ...), custom_call_target="tpu_custom_call" | custom-call | bytes 1024 | tf_op jit(solution)/shard_map/pallas_call | solution.py:352
  36.8 4.8 %collective-permute-done.5.refs_0_ = bf16[25,64,128]{2,1,0:T(8,128)(2,1)S(1)} collective-permute-done((bf16[25,64,128]{2,1,0:T(8,128)(2,1)}, bf16[25,64,128]{2,1,0:T(8,128)(2,1)S(1)}, u32[]{:S(2)}, u32[]{:S(2)}) %collective-permute-start.5) | collective-permute-done | bytes 409632 | tf_op jit(solution)/shard_map/ppermute | solution.py:386
  41.6 1.8 %collective-permute-done.6.refs_1_ = bf16[25,64,128]{2,1,0:T(8,128)(2,1)S(1)} collective-permute-done((bf16[25,64,128]{2,1,0:T(8,128)(2,1)}, bf16[25,64,128]{2,1,0:T(8,128)(2,1)S(1)}, u32[]{:S(2)}, u32[]{:S(2)}) %collective-permute-start.6) | collective-permute-done | bytes 409632 | tf_op jit(solution)/shard_map/ppermute | solution.py:386
  43.4 0.5 collective-permute-start.8
  43.9 1.5 %collective-permute-start.9 = (bf16[49,64,128]{2,1,0:T(8,128)(2,1)S(1)}, bf16[49,64,128]{2,1,0:T(8,128)(2,1)S(1)}, u32[]{:S(2)}, u32[]{:S(2)}) collective-permute-start(bf16[49,64,128]{2,1,0:T(8,128)(2,1)S(1)} %get-tuple-element.72), channel_id=1, source_target_pairs={{0,2},{2,4},{4,6},{6,8},{8,10},{10,12},{12,14},{14,16},{16,18},{18... | collective-permute-start | bytes 2408456 | tf_op jit(solution)/shard_map/ppermute | solution.py:386
  45.4 4.1 %collective-permute-start.10 = (bf16[49,64,128]{2,1,0:T(8,128)(2,1)S(1)}, bf16[49,64,128]{2,1,0:T(8,128)(2,1)S(1)}, u32[]{:S(2)}, u32[]{:S(2)}) collective-permute-start(bf16[49,64,128]{2,1,0:T(8,128)(2,1)S(1)} %get-tuple-element.73), channel_id=1, source_target_pairs={{0,30},{2,0},{4,2},{6,4},{8,6},{10,8},{12,10},{14,12},{16,14},{18,... | collective-permute-start | bytes 2408456 | tf_op jit(solution)/shard_map/ppermute | solution.py:386
  49.6 3.8 %shard_map.90 = (bf16[25,192,256]{2,1,0:T(8,128)(2,1)S(1)}, f32[4,16,256]{2,1,0:T(8,128)}, bf16[144,128]{1,0:T(8,128)(2,1)S(1)}, bf16[144,128]{1,0:T(8,128)(2,1)S(1)}) custom-call(bf16[25,64,128]{2,1,0:T(8,128)(2,1)S(1)} %get-tuple-element.58.refs_0_.refs_7_, bf16[25,64,128]{2,1,0:T(8,128)(2,1)S(1)} %collective-permute-done.7.refs_1_.refs_8_, ...), custom_call_target="tpu_custom_call" | custom-call | bytes 1024 | tf_op jit(solution)/shard_map/pallas_call | solution.py:352
  53.4 0.3 collective-permute-start.12
  53.7 1.7 %collective-permute-start.11 = (bf16[144,128]{1,0:T(8,128)(2,1)S(1)}, bf16[144,128]{1,0:T(8,128)(2,1)S(1)}, u32[]{:S(2)}, u32[]{:S(2)}) collective-permute-start(bf16[144,128]{1,0:T(8,128)(2,1)S(1)} %get-tuple-element.68.refs_17_), channel_id=1, source_target_pairs={{0,2},{2,4},{4,6},{6,8},{8,10},{10,12},{12,14},{14,16},{16,18},{18... | collective-permute-start | bytes 110600 | tf_op jit(solution)/shard_map/ppermute | solution.py:386
  55.4 6.8 %shard_map.91 = (bf16[49,64,256]{2,1,0:T(8,128)(2,1)S(1)}, f32[49,64,256]{2,1,0:T(8,128)S(1)}, f32[49,64,256]{2,1,0:T(8,128)S(1)}, f32[21,16,128]{2,1,0:T(8,128)...) custom-call(s32[3]{0:T(128)S(1)} %pad_add_fusion.refs_0_, ...), custom_call_target="tpu_custom_call" | custom-call | bytes 1024 | tf_op jit(solution)/shard_map/pallas_call | solution.py:352
  62.2 21.1 %collective-permute-done.12.refs_1_ = bf16[144,128]{1,0:T(8,128)(2,1)S(1)} collective-permute-done((bf16[144,128]{1,0:T(8,128)(2,1)S(1)}, bf16[144,128]{1,0:T(8,128)(2,1)S(1)}, u32[]{:S(2)}, u32[]{:S(2)}) %collective-permute-start.12) | collective-permute-done | bytes 36896 | tf_op jit(solution)/shard_map/ppermute | solution.py:386
  83.3 1.9 %collective-permute-start.13 = (bf16[21,16,128]{2,1,0:T(8,128)(2,1)S(1)}, bf16[21,16,128]{2,1,0:T(8,128)(2,1)S(1)}, u32[]{:S(2)}, u32[]{:S(2)}) collective-permute-start(bf16[21,16,128]{2,1,0:T(8,128)(2,1)S(1)} %get-tuple-element.84), channel_id=1, source_target_pairs={{0,4},{2,6},{4,0},{6,2},{8,12},{10,14},{12,8},{14,10},{16,20},{18,... | collective-permute-start | bytes 258056 | tf_op jit(solution)/shard_map/ppermute | solution.py:391
  85.2 1.3 %collective-permute-start.14 = (bf16[21,16,128]{2,1,0:T(8,128)(2,1)S(1)}, bf16[21,16,128]{2,1,0:T(8,128)(2,1)S(1)}, u32[]{:S(2)}, u32[]{:S(2)}) collective-permute-start(bf16[21,16,128]{2,1,0:T(8,128)(2,1)S(1)} %get-tuple-element.85), channel_id=1, source_target_pairs={{0,8},{2,10},{4,12},{6,14},{8,0},{10,2},{12,4},{14,6},{16,24},{18,... | collective-permute-start | bytes 258056 | tf_op jit(solution)/shard_map/ppermute | solution.py:391
  86.5 0.4 collective-permute-start.15
  86.8 1.0 collective-permute-done.13
  87.8 2.3 %collective-permute-done.14 = bf16[21,16,128]{2,1,0:T(8,128)(2,1)S(1)} collective-permute-done((bf16[21,16,128]{2,1,0:T(8,128)(2,1)S(1)}, bf16[21,16,128]{2,1,0:T(8,128)(2,1)S(1)}, u32[]{:S(2)}, u32[]{:S(2)}) %collective-permute-start.14) | collective-permute-done | bytes 86048 | tf_op jit(solution)/shard_map/ppermute | solution.py:391
  90.1 1.7 %collective-permute-done.15 = bf16[21,16,128]{2,1,0:T(8,128)(2,1)S(1)} collective-permute-done((bf16[21,16,128]{2,1,0:T(8,128)(2,1)S(1)}, bf16[21,16,128]{2,1,0:T(8,128)(2,1)S(1)}, u32[]{:S(2)}, u32[]{:S(2)}) %collective-permute-start.15) | collective-permute-done | bytes 86048 | tf_op jit(solution)/shard_map/ppermute | solution.py:391
  91.9 2.6 %collective-permute-start.16 = (bf16[21,16,128]{2,1,0:T(8,128)(2,1)S(1)}, bf16[21,16,128]{2,1,0:T(8,128)(2,1)S(1)}, u32[]{:S(2)}, u32[]{:S(2)}) collective-permute-start(bf16[21,16,128]{2,1,0:T(8,128)(2,1)S(1)} %get-tuple-element.93), channel_id=1, source_target_pairs={{0,16},{2,18},{4,20},{6,22},{8,24},{10,26},{12,28},{14,30},{16,0},... | collective-permute-start | bytes 258056 | tf_op jit(solution)/shard_map/ppermute | solution.py:391
  94.5 2.9 %shard_map.94 = (f32[49,128,256]{2,1,0:T(8,128)S(1)}, f32[8,128]{1,0:T(8,128)S(1)}) custom-call(bf16[49,64,256]{2,1,0:T(8,128)(2,1)S(1)} %get-tuple-element.80.refs_0_, f32[49,64,256]{2,1,0:T(8,128)S(1)} %get-tuple-element.81.refs_1_, bf16[24,192,256]{2,1,0:T(8,128)(2,1)S(1)} %get-tuple-element.60.refs_12_.refs_2_, ...), custom_call_target="tpu_custom_call" | custom-call | bytes 1024 | tf_op jit(solution)/shard_map/pallas_call | solution.py:352
  97.5 0.8 collective-permute-done.16
  98.3 0.1 collective-permute-start.18
  98.4 4.5 %collective-permute-done.18.refs_7_ = bf16[21,16,128]{2,1,0:T(8,128)(2,1)S(1)} collective-permute-done((bf16[21,16,128]{2,1,0:T(8,128)(2,1)S(1)}, bf16[21,16,128]{2,1,0:T(8,128)(2,1)S(1)}, u32[]{:S(2)}, u32[]{:S(2)}) %collective-permute-start.18) | collective-permute-done | bytes 86048 | tf_op jit(solution)/shard_map/ppermute | solution.py:391
  102.9 2.1 %shard_map.97 = (f32[25,64,256]{2,1,0:T(8,128)S(1)}, bf16[25,64,256]{2,1,0:T(8,128)(2,1)S(1)}) custom-call(f32[49,64,256]{2,1,0:T(8,128)S(1)} %get-tuple-element.69.refs_0_, bf16[49,64,128]{2,1,0:T(8,128)(2,1)S(1)} %collective-permute-done.9.refs_1_, bf16[49,64,128]{2,1,0:T(8,128)(2,1)S(1)} %collective-permute-done.10.refs_2_, ...), custom_call_target="tpu_custom_call" | custom-call | bytes 1024 | tf_op jit(solution)/shard_map/pallas_call | solution.py:352
  105.0 0.1 collective-permute-start.19
  105.1 2.0 %shard_map.96 = (f32[24,64,256]{2,1,0:T(8,128)S(1)}, bf16[24,64,256]{2,1,0:T(8,128)(2,1)S(1)}) custom-call(f32[49,64,256]{2,1,0:T(8,128)S(1)} %get-tuple-element.69.refs_0_, bf16[49,64,128]{2,1,0:T(8,128)(2,1)S(1)} %collective-permute-done.9.refs_1_, bf16[49,64,128]{2,1,0:T(8,128)(2,1)S(1)} %collective-permute-done.10.refs_2_, ...), custom_call_target="tpu_custom_call" | custom-call | bytes 1024 | tf_op jit(solution)/shard_map/pallas_call | solution.py:352
  107.1 0.6 collective-permute-start.17
  107.7 0.7 collective-permute-start.22
  108.4 0.6 collective-permute-start.21
  109.0 2.3 %collective-permute-start.20 = (bf16[21,16,128]{2,1,0:T(8,128)(2,1)S(1)}, bf16[21,16,128]{2,1,0:T(8,128)(2,1)S(1)}, u32[]{:S(2)}, u32[]{:S(2)}) collective-permute-start(bf16[21,16,128]{2,1,0:T(8,128)(2,1)S(1)} %add_convert_fusion.refs_1_), channel_id=1, source_target_pairs={{0,4},{2,6},{4,0},{6,2},{8,12},{10,14},{12,8},{14,10},{16,20},{18,... | collective-permute-start | bytes 258056 | tf_op jit(solution)/shard_map/ppermute | solution.py:391
  111.3 2.8 %collective-permute-done.22.refs_4_ = bf16[21,16,128]{2,1,0:T(8,128)(2,1)S(1)} collective-permute-done((bf16[21,16,128]{2,1,0:T(8,128)(2,1)S(1)}, bf16[21,16,128]{2,1,0:T(8,128)(2,1)S(1)}, u32[]{:S(2)}, u32[]{:S(2)}) %collective-permute-start.22) | collective-permute-done | bytes 86048 | tf_op jit(solution)/shard_map/ppermute | solution.py:391
  114.0 0.9 collective-permute-done.20.refs_2_
  115.0 1.4 %shard_map.99 = f32[21,64,128]{2,1,0:T(8,128)} custom-call(s32[3]{0:T(128)S(1)} %pad_add_fusion.refs_0_, bf16[21,16,128]{2,1,0:T(8,128)(2,1)S(1)} %add_convert_fusion.refs_1_, bf16[21,16,128]{2,1,0:T(8,128)(2,1)S(1)} %collective-permute-done.20.refs_2_, bf16[21,16,128]{2,1,0:T(8,128)(2,1)S(1)} %collective-permute-done.21.refs_3_, ...), custom_call_target="tpu_custom_call" | custom-call | bytes 1024 | tf_op jit(solution)/shard_map/pallas_call | solution.py:352
  116.4 1.4 %shard_map.98 = bf16[49,64,256]{2,1,0:T(8,128)(2,1)} custom-call(f32[24,64,256]{2,1,0:T(8,128)S(1)} %get-tuple-element.88.refs_0_, bf16[24,64,256]{2,1,0:T(8,128)(2,1)S(1)} %collective-permute-done.17.refs_1_, f32[25,64,256]{2,1,0:T(8,128)S(1)} %get-tuple-element.90.refs_2_, bf16[25,64,256]{2,1,0:T(8,128)(2,1)S(1)} %collective-permute-done.19.refs_3_), custom_call_target="tpu_custom_call" | custom-call | bytes 1024 | tf_op jit(solution)/shard_map/pallas_call | solution.py:352
  (29 shorter events, 0.2 us)
Async XLA Ops:
  0.6 15.4 %collective-permute-start = (bf16[49,64,256]{2,1,0:T(8,128)(2,1)}, bf16[49,64,256]{2,1,0:T(8,128)(2,1)S(1)}, u32[]{:S(2)}, u32[]{:S(2)}) collective-permute-start(bf16[49,64,256]{2,1,0:T(8,128)(2,1)} %bitcast.14), channel_id=1, source_target_pairs={{0,1},{1,0},{2,3},{3,2},{4,5},{5,4},{6,7},{7,6},{8,9},{9,8},{10,11... | collective-permute-start | bytes 4816904 | tf_op jit(solution)/shard_map/ppermute | solution.py:386
  3.7 29.5 %collective-permute-start.1 = (bf16[24,64,128]{2,1,0:T(8,128)(2,1)}, bf16[24,64,128]{2,1,0:T(8,128)(2,1)S(1)}, u32[]{:S(2)}, u32[]{:S(2)}) collective-permute-start(bf16[24,64,128]{2,1,0:T(8,128)(2,1)} %get-tuple-element.48), channel_id=1, source_target_pairs={{0,2},{2,4},{4,6},{6,8},{8,10},{10,12},{12,14},{14,16},{16,18},{18... | collective-permute-start | bytes 1179656 | tf_op jit(solution)/shard_map/ppermute | solution.py:386
  6.3 27.0 %collective-permute-start.2 = (bf16[24,64,128]{2,1,0:T(8,128)(2,1)}, bf16[24,64,128]{2,1,0:T(8,128)(2,1)S(1)}, u32[]{:S(2)}, u32[]{:S(2)}) collective-permute-start(bf16[24,64,128]{2,1,0:T(8,128)(2,1)} %get-tuple-element.49), channel_id=1, source_target_pairs={{0,30},{2,0},{4,2},{6,4},{8,6},{10,8},{12,10},{14,12},{16,14},{18,... | collective-permute-start | bytes 1179656 | tf_op jit(solution)/shard_map/ppermute | solution.py:386
  10.3 31.3 %collective-permute-start.5 = (bf16[25,64,128]{2,1,0:T(8,128)(2,1)}, bf16[25,64,128]{2,1,0:T(8,128)(2,1)S(1)}, u32[]{:S(2)}, u32[]{:S(2)}) collective-permute-start(bf16[25,64,128]{2,1,0:T(8,128)(2,1)} %get-tuple-element.53), channel_id=1, source_target_pairs={{0,2},{2,4},{4,6},{6,8},{8,10},{10,12},{12,14},{14,16},{16,18},{18... | collective-permute-start | bytes 1228808 | tf_op jit(solution)/shard_map/ppermute | solution.py:386
  10.3 33.1 %collective-permute-start.6 = (bf16[25,64,128]{2,1,0:T(8,128)(2,1)}, bf16[25,64,128]{2,1,0:T(8,128)(2,1)S(1)}, u32[]{:S(2)}, u32[]{:S(2)}) collective-permute-start(bf16[25,64,128]{2,1,0:T(8,128)(2,1)} %get-tuple-element.54), channel_id=1, source_target_pairs={{0,30},{2,0},{4,2},{6,4},{8,6},{10,8},{12,10},{14,12},{16,14},{18,... | collective-permute-start | bytes 1228808 | tf_op jit(solution)/shard_map/ppermute | solution.py:386
  16.0 1.4 %copy-start = (bf16[64,49,256]{2,0,1:T(8,128)(2,1)S(1)}, bf16[64,49,256]{2,0,1:T(8,128)(2,1)}, u32[]{:S(2)}) copy-start(bf16[64,49,256]{2,0,1:T(8,128)(2,1)} %param.8) | copy-start | bytes 4816900
  17.4 1.4 %copy-start.1 = (bf16[64,49,256]{2,0,1:T(8,128)(2,1)S(1)}, bf16[64,49,256]{2,0,1:T(8,128)(2,1)}, u32[]{:S(2)}) copy-start(bf16[64,49,256]{2,0,1:T(8,128)(2,1)} %param.6) | copy-start | bytes 4816900
  18.9 1.0 copy-start.4
  19.8 0.7 copy-start.5
  33.2 1.7 %collective-permute-start.3 = (bf16[24,64,128]{2,1,0:T(8,128)(2,1)S(1)}, bf16[24,64,128]{2,1,0:T(8,128)(2,1)S(1)}, u32[]{:S(2)}, u32[]{:S(2)}) collective-permute-start(bf16[24,64,128]{2,1,0:T(8,128)(2,1)S(1)} %get-tuple-element.51.refs_0_.refs_3_), channel_id=1, source_target_pairs={{0,1},{1,0},{2,3},{3,2},{4,5},{5,4},{6,7},{7,6},{8,9},{9,8},{10,11... | collective-permute-start | bytes 1179656 | tf_op jit(solution)/shard_map/ppermute | solution.py:386
  33.2 2.3 %collective-permute-start.4 = (bf16[24,64,128]{2,1,0:T(8,128)(2,1)S(1)}, bf16[24,64,128]{2,1,0:T(8,128)(2,1)S(1)}, u32[]{:S(2)}, u32[]{:S(2)}) collective-permute-start(bf16[24,64,128]{2,1,0:T(8,128)(2,1)S(1)} %get-tuple-element.52.refs_2_.refs_5_), channel_id=1, source_target_pairs={{0,1},{1,0},{2,3},{3,2},{4,5},{5,4},{6,7},{7,6},{8,9},{9,8},{10,11... | collective-permute-start | bytes 1179656 | tf_op jit(solution)/shard_map/ppermute | solution.py:386
  36.8 12.8 %copy-start.2 = (f32[4,16,256]{2,1,0:T(8,128)S(1)}, f32[4,16,256]{2,1,0:T(8,128)}, u32[]{:S(2)}) copy-start(f32[4,16,256]{2,1,0:T(8,128)} %refs_9_.1) | copy-start | bytes 196612
  36.8 12.8 %copy-start.3 = (s32[16,256]{1,0:T(8,128)S(1)}, s32[16,256]{1,0:T(8,128)}, u32[]{:S(2)}) copy-start(s32[16,256]{1,0:T(8,128)} %refs_10_.1) | copy-start | bytes 49156
  43.4 6.1 %collective-permute-start.7 = (bf16[25,64,128]{2,1,0:T(8,128)(2,1)S(1)}, bf16[25,64,128]{2,1,0:T(8,128)(2,1)S(1)}, u32[]{:S(2)}, u32[]{:S(2)}) collective-permute-start(bf16[25,64,128]{2,1,0:T(8,128)(2,1)S(1)} %get-tuple-element.58.refs_0_.refs_7_), channel_id=1, source_target_pairs={{0,1},{1,0},{2,3},{3,2},{4,5},{5,4},{6,7},{7,6},{8,9},{9,8},{10,11... | collective-permute-start | bytes 1228808 | tf_op jit(solution)/shard_map/ppermute | solution.py:386
  43.4 6.1 %collective-permute-start.8 = (bf16[25,64,128]{2,1,0:T(8,128)(2,1)S(1)}, bf16[25,64,128]{2,1,0:T(8,128)(2,1)S(1)}, u32[]{:S(2)}, u32[]{:S(2)}) collective-permute-start(bf16[25,64,128]{2,1,0:T(8,128)(2,1)S(1)} %get-tuple-element.59.refs_2_.refs_9_), channel_id=1, source_target_pairs={{0,1},{1,0},{2,3},{3,2},{4,5},{5,4},{6,7},{7,6},{8,9},{9,8},{10,11... | collective-permute-start | bytes 1228808 | tf_op jit(solution)/shard_map/ppermute | solution.py:386
  43.9 58.9 %collective-permute-start.9 = (bf16[49,64,128]{2,1,0:T(8,128)(2,1)S(1)}, bf16[49,64,128]{2,1,0:T(8,128)(2,1)S(1)}, u32[]{:S(2)}, u32[]{:S(2)}) collective-permute-start(bf16[49,64,128]{2,1,0:T(8,128)(2,1)S(1)} %get-tuple-element.72), channel_id=1, source_target_pairs={{0,2},{2,4},{4,6},{6,8},{8,10},{10,12},{12,14},{14,16},{16,18},{18... | collective-permute-start | bytes 2408456 | tf_op jit(solution)/shard_map/ppermute | solution.py:386
  45.4 57.4 %collective-permute-start.10 = (bf16[49,64,128]{2,1,0:T(8,128)(2,1)S(1)}, bf16[49,64,128]{2,1,0:T(8,128)(2,1)S(1)}, u32[]{:S(2)}, u32[]{:S(2)}) collective-permute-start(bf16[49,64,128]{2,1,0:T(8,128)(2,1)S(1)} %get-tuple-element.73), channel_id=1, source_target_pairs={{0,30},{2,0},{4,2},{6,4},{8,6},{10,8},{12,10},{14,12},{16,14},{18,... | collective-permute-start | bytes 2408456 | tf_op jit(solution)/shard_map/ppermute | solution.py:386
  53.4 29.9 %collective-permute-start.12 = (bf16[144,128]{1,0:T(8,128)(2,1)S(1)}, bf16[144,128]{1,0:T(8,128)(2,1)S(1)}, u32[]{:S(2)}, u32[]{:S(2)}) collective-permute-start(bf16[144,128]{1,0:T(8,128)(2,1)S(1)} %get-tuple-element.67.refs_16_), channel_id=1, source_target_pairs={{0,30},{2,0},{4,2},{6,4},{8,6},{10,8},{12,10},{14,12},{16,14},{18,... | collective-permute-start | bytes 110600 | tf_op jit(solution)/shard_map/ppermute | solution.py:386
  53.7 29.7 %collective-permute-start.11 = (bf16[144,128]{1,0:T(8,128)(2,1)S(1)}, bf16[144,128]{1,0:T(8,128)(2,1)S(1)}, u32[]{:S(2)}, u32[]{:S(2)}) collective-permute-start(bf16[144,128]{1,0:T(8,128)(2,1)S(1)} %get-tuple-element.68.refs_17_), channel_id=1, source_target_pairs={{0,2},{2,4},{4,6},{6,8},{8,10},{10,12},{12,14},{14,16},{16,18},{18... | collective-permute-start | bytes 110600 | tf_op jit(solution)/shard_map/ppermute | solution.py:386
  83.3 4.5 %collective-permute-start.13 = (bf16[21,16,128]{2,1,0:T(8,128)(2,1)S(1)}, bf16[21,16,128]{2,1,0:T(8,128)(2,1)S(1)}, u32[]{:S(2)}, u32[]{:S(2)}) collective-permute-start(bf16[21,16,128]{2,1,0:T(8,128)(2,1)S(1)} %get-tuple-element.84), channel_id=1, source_target_pairs={{0,4},{2,6},{4,0},{6,2},{8,12},{10,14},{12,8},{14,10},{16,20},{18,... | collective-permute-start | bytes 258056 | tf_op jit(solution)/shard_map/ppermute | solution.py:391
  85.2 4.9 %collective-permute-start.14 = (bf16[21,16,128]{2,1,0:T(8,128)(2,1)S(1)}, bf16[21,16,128]{2,1,0:T(8,128)(2,1)S(1)}, u32[]{:S(2)}, u32[]{:S(2)}) collective-permute-start(bf16[21,16,128]{2,1,0:T(8,128)(2,1)S(1)} %get-tuple-element.85), channel_id=1, source_target_pairs={{0,8},{2,10},{4,12},{6,14},{8,0},{10,2},{12,4},{14,6},{16,24},{18,... | collective-permute-start | bytes 258056 | tf_op jit(solution)/shard_map/ppermute | solution.py:391
  86.5 5.4 %collective-permute-start.15 = (bf16[21,16,128]{2,1,0:T(8,128)(2,1)S(1)}, bf16[21,16,128]{2,1,0:T(8,128)(2,1)S(1)}, u32[]{:S(2)}, u32[]{:S(2)}) collective-permute-start(bf16[21,16,128]{2,1,0:T(8,128)(2,1)S(1)} %get-tuple-element.86), channel_id=1, source_target_pairs={{0,12},{2,14},{4,8},{6,10},{8,4},{10,6},{12,0},{14,2},{16,28},{18,... | collective-permute-start | bytes 258056 | tf_op jit(solution)/shard_map/ppermute | solution.py:391
  91.9 6.4 %collective-permute-start.16 = (bf16[21,16,128]{2,1,0:T(8,128)(2,1)S(1)}, bf16[21,16,128]{2,1,0:T(8,128)(2,1)S(1)}, u32[]{:S(2)}, u32[]{:S(2)}) collective-permute-start(bf16[21,16,128]{2,1,0:T(8,128)(2,1)S(1)} %get-tuple-element.93), channel_id=1, source_target_pairs={{0,16},{2,18},{4,20},{6,22},{8,24},{10,26},{12,28},{14,30},{16,0},... | collective-permute-start | bytes 258056 | tf_op jit(solution)/shard_map/ppermute | solution.py:391
  98.3 4.6 %collective-permute-start.18 = (bf16[21,16,128]{2,1,0:T(8,128)(2,1)S(1)}, bf16[21,16,128]{2,1,0:T(8,128)(2,1)S(1)}, u32[]{:S(2)}, u32[]{:S(2)}) collective-permute-start(bf16[21,16,128]{2,1,0:T(8,128)(2,1)S(1)} %shard_map.95.refs_7_), channel_id=1, source_target_pairs={{0,2},{2,0},{4,6},{6,4},{8,10},{10,8},{12,14},{14,12},{16,18},{18,... | collective-permute-start | bytes 258056 | tf_op jit(solution)/shard_map/ppermute | solution.py:391
  105.0 11.4 %collective-permute-start.19 = (bf16[25,64,256]{2,1,0:T(8,128)(2,1)S(1)}, bf16[25,64,256]{2,1,0:T(8,128)(2,1)S(1)}, u32[]{:S(2)}, u32[]{:S(2)}) collective-permute-start(bf16[25,64,256]{2,1,0:T(8,128)(2,1)S(1)} %get-tuple-element.91), channel_id=1, source_target_pairs={{0,1},{1,0},{2,3},{3,2},{4,5},{5,4},{6,7},{7,6},{8,9},{9,8},{10,11... | collective-permute-start | bytes 2457608 | tf_op jit(solution)/shard_map/ppermute | solution.py:386
  107.1 9.3 %collective-permute-start.17 = (bf16[24,64,256]{2,1,0:T(8,128)(2,1)S(1)}, bf16[24,64,256]{2,1,0:T(8,128)(2,1)S(1)}, u32[]{:S(2)}, u32[]{:S(2)}) collective-permute-start(bf16[24,64,256]{2,1,0:T(8,128)(2,1)S(1)} %get-tuple-element.89), channel_id=1, source_target_pairs={{0,1},{1,0},{2,3},{3,2},{4,5},{5,4},{6,7},{7,6},{8,9},{9,8},{10,11... | collective-permute-start | bytes 2359304 | tf_op jit(solution)/shard_map/ppermute | solution.py:386
  107.7 6.3 %collective-permute-start.22 = (bf16[21,16,128]{2,1,0:T(8,128)(2,1)S(1)}, bf16[21,16,128]{2,1,0:T(8,128)(2,1)S(1)}, u32[]{:S(2)}, u32[]{:S(2)}) collective-permute-start(bf16[21,16,128]{2,1,0:T(8,128)(2,1)S(1)} %add_convert_fusion.refs_1_), channel_id=1, source_target_pairs={{0,12},{2,14},{4,8},{6,10},{8,4},{10,6},{12,0},{14,2},{16,28},{18,... | collective-permute-start | bytes 258056 | tf_op jit(solution)/shard_map/ppermute | solution.py:391
  108.4 5.6 %collective-permute-start.21 = (bf16[21,16,128]{2,1,0:T(8,128)(2,1)S(1)}, bf16[21,16,128]{2,1,0:T(8,128)(2,1)S(1)}, u32[]{:S(2)}, u32[]{:S(2)}) collective-permute-start(bf16[21,16,128]{2,1,0:T(8,128)(2,1)S(1)} %add_convert_fusion.refs_1_), channel_id=1, source_target_pairs={{0,8},{2,10},{4,12},{6,14},{8,0},{10,2},{12,4},{14,6},{16,24},{18,... | collective-permute-start | bytes 258056 | tf_op jit(solution)/shard_map/ppermute | solution.py:391
  109.0 6.0 %collective-permute-start.20 = (bf16[21,16,128]{2,1,0:T(8,128)(2,1)S(1)}, bf16[21,16,128]{2,1,0:T(8,128)(2,1)S(1)}, u32[]{:S(2)}, u32[]{:S(2)}) collective-permute-start(bf16[21,16,128]{2,1,0:T(8,128)(2,1)S(1)} %add_convert_fusion.refs_1_), channel_id=1, source_target_pairs={{0,4},{2,6},{4,0},{6,2},{8,12},{10,14},{12,8},{14,10},{16,20},{18,... | collective-permute-start | bytes 258056 | tf_op jit(solution)/shard_map/ppermute | solution.py:391

commit v11 on v7

--- a/solution.py
+++ b/solution.py
@@ -193,9 +193,8 @@
             merged = merged + jnp.where(same, both[:, slot : slot + 1, :], 0.0)
         atom = lax.broadcasted_iota(jnp.int32, (slots, HALO), 1)
         edge_rows = 2 * heads * slots
-        message[:edge_rows, :] = merged.reshape(edge_rows, HALO)
-        message[edge_rows : edge_rows + slots, :] = (index - HALO - atom).astype(F32)
-        message[edge_rows + slots :, :] = jnp.zeros_like(message[edge_rows + slots :, :])
+        message[:edge_rows, :] = merged.reshape(edge_rows, HALO).astype(BF16)
+        message[edge_rows:, :] = (index - HALO - atom).astype(F32).astype(BF16)
 
 
 def joined_rows(early, late, first_row, rows):
@@ -214,7 +213,7 @@
     atoms = 2 * HALO
     core = place[0]
     empty = jnp.zeros((HALO, HALO), BF16)
-    coefs = [message[: 2 * heads * slots, :].T for message in (message_a, message_b)]
+    coefs = [message[: 2 * heads * slots, :].astype(F32).T for message in (message_a, message_b)]
     for head in range(heads):
         tables = []
         for quantity in (head, heads + head):
@@ -267,8 +266,8 @@
 def halo_slots(message_left, message_right, quantities, slots):
     coefs, tables = [], []
     for message, tile in ((message_left, 2), (message_right, 0)):
-        coefs.append(message[: quantities * slots, :].T)
-        offset = message[quantities * slots : (quantities + 1) * slots, :].astype(jnp.int32)
+        coefs.append(message[: quantities * slots, :].astype(F32).T)
+        offset = message[quantities * slots :, :].astype(F32).astype(jnp.int32)
         atom = lax.broadcasted_iota(jnp.int32, offset.shape, 1)
         tables.append(slot_tile(wide_transpose(offset + HALO + atom)[:, :slots], tile))
     return coefs, tables
@@ -468,8 +467,8 @@
         (
             held(comps - feature_cut, 3 * chan_local, atoms_dev, dtype=BF16),
             plain(heads, slots, atoms_dev),
-            held((2 * heads + 3) * slots, HALO),
-            held((2 * heads + 3) * slots, HALO),
+            held((2 * heads + 1) * slots, HALO, dtype=BF16),
+            held((2 * heads + 1) * slots, HALO, dtype=BF16),
         ),
         stay=(*range(len(late_chunks) + 5), len(late_chunks) + 7, len(late_chunks) + 8),
     )
@@ -499,8 +498,9 @@
     for delta, part in enumerate(sent, 1):
         kept = kept + exchanged(part, "atom", delta << cut_bits[0]).astype(F32)
     rest = [bit for bit in reversed(range(count.bit_length() - 1)) if bit not in cut_bits]
-    for bit in rest:
-        arrived = exchanged(kept.astype(BF16), "atom", 1 << bit)
+    for at, bit in enumerate(rest):
+        also = 1 << rest[at - 1] if 0 < at == len(rest) - 1 else 0
+        arrived = exchanged(kept.astype(BF16), "atom", 1 << bit | also)
         if bit == rest[-1]:
             from_left, from_right, message_left, message_right, arrived = after(
                 (from_left, from_right, message_left, message_right, arrived), ()

time: 101 us -> 104 us (1.030)
  waiting for transfers between devices: 34.4 us -> 37.4 us
    ppermute x15, waiting for transfers between devices: 24 us -> 26.4 us  [shifted(): return lax.ppermute(value, axis, pairs)]
    ppermute x15, starting transfers between devices: 23.6 us -> 24.7 us  [shifted(): return lax.ppermute(value, axis, pairs)]
where the time goes in v11:
time: 104 us
  waiting for transfers between devices  37.4 us (36%)
  starting transfers between devices  34.9 us (34%)
  Pallas kernels  28.1 us (27%)
  local copies, waits for them, and re-layouts  2.41 us (2%)
    ppermute x15, waiting for transfers between devices, shifted(): return lax.ppermute(value, axis, pairs)  26.4 us
    pallas_call x8, Pallas kernels, call(): pl.pallas_call(body, out_shape=tuple(outs), in_specs=[small] * scalars +...  25.5 us
    ppermute x15, starting transfers between devices, shifted(): return lax.ppermute(value, axis, pairs)  24.7 us
    ppermute x8, waiting for transfers between devices, exchanged(): lax.ppermute(value, axis, [(source, source ^ offset) for source in range(...  11 us
    ppermute x8, starting transfers between devices, exchanged(): lax.ppermute(value, axis, [(source, source ^ offset) for source in range(...  10.2 us
    pallas_call x1, Pallas kernels, on_device(): pl.pallas_call(functools.partial(split_kernel, feature_cuts), out_shape=t...  2.54 us
    unnamed x12, local copies, waits for them, and re-layouts  2.41 us
  transfers between devices with their start and end apart: 23, of which 10 were waited for; matrix products, arithmetic and copies ran while one was open for 0% of the time, Pallas kernels for 26%

profile of v11, /device:TPU:0, one launch (start us, length us, event | category | flops | bytes accessed | tf_op | source)
XLA Modules:
  0.0 103.8 jit_solution(2541691487343334266)
XLA Ops:
  0.7 0.5 collective-permute-start
  1.2 2.5 %shard_map.85 = (bf16[24,64,128]{2,1,0:T(8,128)(2,1)}, bf16[24,64,128]{2,1,0:T(8,128)(2,1)}, bf16[25,64,128]{2,1,0:T(8,128)(2,1)}, bf16[25,64,128]{2,1,0:T(8,128)(2,1)}) custom-call(bf16[49,64,256]{2,1,0:T(8,128)(2,1)} %bitcast.15), custom_call_target="tpu_custom_call" | custom-call | tf_op jit(solution)/shard_map/pallas_call | solution.py:409
  3.7 2.7 %collective-permute-start.1 = (bf16[24,64,128]{2,1,0:T(8,128)(2,1)}, bf16[24,64,128]{2,1,0:T(8,128)(2,1)S(1)}, u32[]{:S(2)}, u32[]{:S(2)}) collective-permute-start(bf16[24,64,128]{2,1,0:T(8,128)(2,1)} %get-tuple-element.47), channel_id=1, source_target_pairs={{0,2},{2,4},{4,6},{6,8},{8,10},{10,12},{12,14},{14,16},{16,18},{18... | collective-permute-start | bytes 1179656 | tf_op jit(solution)/shard_map/ppermute | solution.py:373
  6.4 4.1 %collective-permute-start.2 = (bf16[24,64,128]{2,1,0:T(8,128)(2,1)}, bf16[24,64,128]{2,1,0:T(8,128)(2,1)S(1)}, u32[]{:S(2)}, u32[]{:S(2)}) collective-permute-start(bf16[24,64,128]{2,1,0:T(8,128)(2,1)} %get-tuple-element.48), channel_id=1, source_target_pairs={{0,30},{2,0},{4,2},{6,4},{8,6},{10,8},{12,10},{14,12},{16,14},{18,... | collective-permute-start | bytes 1179656 | tf_op jit(solution)/shard_map/ppermute | solution.py:373
  10.5 5.6 %collective-permute-start.6 = (bf16[25,64,128]{2,1,0:T(8,128)(2,1)}, bf16[25,64,128]{2,1,0:T(8,128)(2,1)S(1)}, u32[]{:S(2)}, u32[]{:S(2)}) collective-permute-start(bf16[25,64,128]{2,1,0:T(8,128)(2,1)} %get-tuple-element.53), channel_id=1, source_target_pairs={{0,30},{2,0},{4,2},{6,4},{8,6},{10,8},{12,10},{14,12},{16,14},{18,... | collective-permute-start | bytes 1228808 | tf_op jit(solution)/shard_map/ppermute | solution.py:373
  16.1 0.1 pad_add_fusion.refs_0_
  16.2 0.0 copy-start.1
  16.2 1.4 %copy-done.1 = bf16[64,49,256]{2,0,1:T(8,128)(2,1)S(1)} copy-done((bf16[64,49,256]{2,0,1:T(8,128)(2,1)S(1)}, bf16[64,49,256]{2,0,1:T(8,128)(2,1)}, u32[]{:S(2)}) %copy-start.1) | copy-done | bytes 1605656
  17.6 1.0 copy-done.4
  18.6 4.7 %shard_map.86 = (bf16[49,192,256]{2,1,0:T(8,128)(2,1)S(1)}, f32[8,256,256]{2,1,0:T(8,128)S(1)}, s32[2,3,128,128]{3,2,1,0:T(8,128)S(1)}, s32[16,256]{1,0:T(8,128)...) custom-call(s32[3]{0:T(128)S(1)} %pad_add_fusion.refs_0_, ...), custom_call_target="tpu_custom_call" | custom-call | flops 12000000000 | bytes 1024 | tf_op jit(solution)/shard_map/pallas_call | solution.py:339
  23.2 10.1 %collective-permute-done.1.refs_0_ = bf16[24,64,128]{2,1,0:T(8,128)(2,1)S(1)} collective-permute-done((bf16[24,64,128]{2,1,0:T(8,128)(2,1)}, bf16[24,64,128]{2,1,0:T(8,128)(2,1)S(1)}, u32[]{:S(2)}, u32[]{:S(2)}) %collective-permute-start.1) | collective-permute-done | bytes 393248 | tf_op jit(solution)/shard_map/ppermute | solution.py:373
  33.4 0.0 collective-permute-start.3
  33.4 0.5 collective-permute-start.4
  33.9 1.2 %collective-permute-done.3.refs_1_.refs_4_ = bf16[24,64,128]{2,1,0:T(8,128)(2,1)S(1)} collective-permute-done((bf16[24,64,128]{2,1,0:T(8,128)(2,1)S(1)}, bf16[24,64,128]{2,1,0:T(8,128)(2,1)S(1)}, u32[]{:S(2)}, u32[]{:S(2)}) %collective-permute-start.3) | collective-permute-done | bytes 393248 | tf_op jit(solution)/shard_map/ppermute | solution.py:373
  35.1 0.6 collective-permute-done.4.refs_3_.refs_6_
  35.7 1.3 %shard_map.88 = (bf16[24,192,256]{2,1,0:T(8,128)(2,1)S(1)}, f32[8,2,128,128]{3,2,1,0:T(8,128)S(1)}, f32[8,128]{1,0:T(8,128)S(1)}) custom-call(bf16[24,64,128]{2,1,0:T(8,128)(2,1)S(1)} %get-tuple-element.50.refs_0_.refs_3_, bf16[24,64,128]{2,1,0:T(8,128)(2,1)S(1)} %collective-permute-done.3.refs_1_.refs_4_, ...), custom_call_target="tpu_custom_call" | custom-call | bytes 1024 | tf_op jit(solution)/shard_map/pallas_call | solution.py:339
  37.0 0.0 copy-start.2
  37.0 0.0 copy-start.3
  37.0 4.6 %collective-permute-done.5.refs_0_ = bf16[25,64,128]{2,1,0:T(8,128)(2,1)S(1)} collective-permute-done((bf16[25,64,128]{2,1,0:T(8,128)(2,1)}, bf16[25,64,128]{2,1,0:T(8,128)(2,1)S(1)}, u32[]{:S(2)}, u32[]{:S(2)}) %collective-permute-start.5) | collective-permute-done | bytes 409632 | tf_op jit(solution)/shard_map/ppermute | solution.py:373
  41.6 1.8 %collective-permute-done.6.refs_1_ = bf16[25,64,128]{2,1,0:T(8,128)(2,1)S(1)} collective-permute-done((bf16[25,64,128]{2,1,0:T(8,128)(2,1)}, bf16[25,64,128]{2,1,0:T(8,128)(2,1)S(1)}, u32[]{:S(2)}, u32[]{:S(2)}) %collective-permute-start.6) | collective-permute-done | bytes 409632 | tf_op jit(solution)/shard_map/ppermute | solution.py:373
  43.4 0.0 collective-permute-start.7
  43.4 0.5 collective-permute-start.8
  44.0 1.5 %collective-permute-start.9 = (bf16[49,64,128]{2,1,0:T(8,128)(2,1)S(1)}, bf16[49,64,128]{2,1,0:T(8,128)(2,1)S(1)}, u32[]{:S(2)}, u32[]{:S(2)}) collective-permute-start(bf16[49,64,128]{2,1,0:T(8,128)(2,1)S(1)} %get-tuple-element.73), channel_id=1, source_target_pairs={{0,2},{2,4},{4,6},{6,8},{8,10},{10,12},{12,14},{14,16},{16,18},{18... | collective-permute-start | bytes 2408456 | tf_op jit(solution)/shard_map/ppermute | solution.py:373
  45.4 4.1 %collective-permute-start.10 = (bf16[49,64,128]{2,1,0:T(8,128)(2,1)S(1)}, bf16[49,64,128]{2,1,0:T(8,128)(2,1)S(1)}, u32[]{:S(2)}, u32[]{:S(2)}) collective-permute-start(bf16[49,64,128]{2,1,0:T(8,128)(2,1)S(1)} %get-tuple-element.74), channel_id=1, source_target_pairs={{0,30},{2,0},{4,2},{6,4},{8,6},{10,8},{12,10},{14,12},{16,14},{18,... | collective-permute-start | bytes 2408456 | tf_op jit(solution)/shard_map/ppermute | solution.py:373
  49.6 3.8 %shard_map.90 = (bf16[25,192,256]{2,1,0:T(8,128)(2,1)S(1)}, f32[4,16,256]{2,1,0:T(8,128)}, bf16[144,128]{1,0:T(8,128)(2,1)S(1)}, bf16[144,128]{1,0:T(8,128)(2,1)S(1)}) custom-call(bf16[25,64,128]{2,1,0:T(8,128)(2,1)S(1)} %get-tuple-element.57.refs_0_.refs_7_, bf16[25,64,128]{2,1,0:T(8,128)(2,1)S(1)} %collective-permute-done.7.refs_1_.refs_8_, ...), custom_call_target="tpu_custom_call" | custom-call | bytes 1024 | tf_op jit(solution)/shard_map/pallas_call | solution.py:339
  53.4 7.7 %shard_map.91 = (bf16[49,64,256]{2,1,0:T(8,128)(2,1)S(1)}, f32[49,64,256]{2,1,0:T(8,128)S(1)}, f32[49,64,256]{2,1,0:T(8,128)S(1)}, f32[21,16,128]{2,1,0:T(8,128)...) custom-call(s32[3]{0:T(128)S(1)} %pad_add_fusion.refs_0_, ...), custom_call_target="tpu_custom_call" | custom-call | bytes 1024 | tf_op jit(solution)/shard_map/pallas_call | solution.py:339
  61.1 0.1 collective-permute-start.13
  61.2 0.3 collective-permute-start.14
  61.5 3.2 %collective-permute-start.15 = (bf16[21,16,128]{2,1,0:T(8,128)(2,1)S(1)}, bf16[21,16,128]{2,1,0:T(8,128)(2,1)S(1)}, u32[]{:S(2)}, u32[]{:S(2)}) collective-permute-start(bf16[21,16,128]{2,1,0:T(8,128)(2,1)S(1)} %get-tuple-element.78), channel_id=1, source_target_pairs={{0,12},{2,14},{4,8},{6,10},{8,4},{10,6},{12,0},{14,2},{16,28},{18,... | collective-permute-start | bytes 258056 | tf_op jit(solution)/shard_map/ppermute | solution.py:378
  64.7 6.6 %collective-permute-done.13 = bf16[21,16,128]{2,1,0:T(8,128)(2,1)S(1)} collective-permute-done((bf16[21,16,128]{2,1,0:T(8,128)(2,1)S(1)}, bf16[21,16,128]{2,1,0:T(8,128)(2,1)S(1)}, u32[]{:S(2)}, u32[]{:S(2)}) %collective-permute-start.13) | collective-permute-done | bytes 86048 | tf_op jit(solution)/shard_map/ppermute | solution.py:378
  71.2 0.1 fusion.1
  71.3 2.0 %collective-permute-start.16 = (bf16[21,16,128]{2,1,0:T(8,128)(2,1)S(1)}, bf16[21,16,128]{2,1,0:T(8,128)(2,1)S(1)}, u32[]{:S(2)}, u32[]{:S(2)}) collective-permute-start(bf16[21,16,128]{2,1,0:T(8,128)(2,1)S(1)} %get-tuple-element.91), channel_id=1, source_target_pairs={{0,16},{2,18},{4,20},{6,22},{8,24},{10,26},{12,28},{14,30},{16,0},... | collective-permute-start | bytes 258056 | tf_op jit(solution)/shard_map/ppermute | solution.py:378
  73.3 4.4 %collective-permute-done.16 = bf16[21,16,128]{2,1,0:T(8,128)(2,1)S(1)} collective-permute-done((bf16[21,16,128]{2,1,0:T(8,128)(2,1)S(1)}, bf16[21,16,128]{2,1,0:T(8,128)(2,1)S(1)}, u32[]{:S(2)}, u32[]{:S(2)}) %collective-permute-start.16) | collective-permute-done | bytes 86048 | tf_op jit(solution)/shard_map/ppermute | solution.py:378
  77.7 1.2 %collective-permute-start.17 = (bf16[21,16,128]{2,1,0:T(8,128)(2,1)S(1)}, bf16[21,16,128]{2,1,0:T(8,128)(2,1)S(1)}, u32[]{:S(2)}, u32[]{:S(2)}) collective-permute-start(bf16[21,16,128]{2,1,0:T(8,128)(2,1)S(1)} %fusion), channel_id=1, source_target_pairs={{0,18},{2,16},{4,22},{6,20},{8,26},{10,24},{12,30},{14,28},{16,2},... | collective-permute-start | bytes 258056 | tf_op jit(solution)/shard_map/ppermute | solution.py:378
  78.9 4.5 %collective-permute-start.12 = (bf16[144,128]{1,0:T(8,128)(2,1)S(1)}, bf16[144,128]{1,0:T(8,128)(2,1)S(1)}, u32[]{:S(2)}, u32[]{:S(2)}) collective-permute-start(bf16[144,128]{1,0:T(8,128)(2,1)S(1)} %get-tuple-element.66.refs_16_), channel_id=1, source_target_pairs={{0,30},{2,0},{4,2},{6,4},{8,6},{10,8},{12,10},{14,12},{16,14},{18,... | collective-permute-start | bytes 110600 | tf_op jit(solution)/shard_map/ppermute | solution.py:373
  83.4 0.0 collective-permute-start.11
  83.4 1.8 %collective-permute-done.12.refs_3_ = bf16[144,128]{1,0:T(8,128)(2,1)S(1)} collective-permute-done((bf16[144,128]{1,0:T(8,128)(2,1)S(1)}, bf16[144,128]{1,0:T(8,128)(2,1)S(1)}, u32[]{:S(2)}, u32[]{:S(2)}) %collective-permute-start.12) | collective-permute-done | bytes 36896 | tf_op jit(solution)/shard_map/ppermute | solution.py:373
  85.2 5.7 %collective-permute-done.11.refs_2_ = bf16[144,128]{1,0:T(8,128)(2,1)S(1)} collective-permute-done((bf16[144,128]{1,0:T(8,128)(2,1)S(1)}, bf16[144,128]{1,0:T(8,128)(2,1)S(1)}, u32[]{:S(2)}, u32[]{:S(2)}) %collective-permute-start.11) | collective-permute-done | bytes 36896 | tf_op jit(solution)/shard_map/ppermute | solution.py:373
  91.0 0.1 collective-permute-start.19
  91.1 0.1 collective-permute-start.22
  91.2 3.4 %collective-permute-start.21 = (bf16[21,16,128]{2,1,0:T(8,128)(2,1)S(1)}, bf16[21,16,128]{2,1,0:T(8,128)(2,1)S(1)}, u32[]{:S(2)}, u32[]{:S(2)}) collective-permute-start(bf16[21,16,128]{2,1,0:T(8,128)(2,1)S(1)} %add_convert_fusion.refs_1_), channel_id=1, source_target_pairs={{0,4},{2,6},{4,0},{6,2},{8,12},{10,14},{12,8},{14,10},{16,20},{18,... | collective-permute-start | bytes 258056 | tf_op jit(solution)/shard_map/ppermute | solution.py:378
  94.6 2.6 %shard_map.94 = (f32[24,64,256]{2,1,0:T(8,128)S(1)}, bf16[24,64,256]{2,1,0:T(8,128)(2,1)S(1)}, f32[8,128]{1,0:T(8,128)S(1)}) custom-call(bf16[49,64,256]{2,1,0:T(8,128)(2,1)S(1)} %get-tuple-element.68.refs_0_, f32[49,64,256]{2,1,0:T(8,128)S(1)} %get-tuple-element.69.refs_1_, f32[49,64,256]{2,1,0:T(8,128)S(1)} %get-tuple-element.70.refs_2_, ...), custom_call_target="tpu_custom_call" | custom-call | bytes 1024 | tf_op jit(solution)/shard_map/pallas_call | solution.py:339
  97.2 0.1 collective-permute-start.18
  97.3 2.6 %shard_map.95 = (f32[25,64,256]{2,1,0:T(8,128)S(1)}, bf16[25,64,256]{2,1,0:T(8,128)(2,1)S(1)}, f32[8,128]{1,0:T(8,128)}) custom-call(bf16[49,64,256]{2,1,0:T(8,128)(2,1)S(1)} %get-tuple-element.68.refs_0_, f32[49,64,256]{2,1,0:T(8,128)S(1)} %get-tuple-element.69.refs_1_, f32[49,64,256]{2,1,0:T(8,128)S(1)} %get-tuple-element.70.refs_2_, ...), custom_call_target="tpu_custom_call" | custom-call | bytes 1024 | tf_op jit(solution)/shard_map/pallas_call | solution.py:339
  99.8 0.6 collective-permute-start.20
  100.4 1.4 %shard_map.97 = f32[21,64,128]{2,1,0:T(8,128)} custom-call(s32[3]{0:T(128)S(1)} %pad_add_fusion.refs_0_, bf16[21,16,128]{2,1,0:T(8,128)(2,1)S(1)} %add_convert_fusion.refs_1_, bf16[21,16,128]{2,1,0:T(8,128)(2,1)S(1)} %collective-permute-done.21.refs_2_, bf16[21,16,128]{2,1,0:T(8,128)(2,1)S(1)} %collective-permute-done.19.refs_10_.refs_3_, ...), custom_call_target="tpu_custom_call" | custom-call | flops 20000000000 | bytes 1024 | tf_op jit(solution)/shard_map/pallas_call | solution.py:339
  101.8 0.5 collective-permute-done.20.refs_3_
  102.3 1.5 %shard_map.96 = bf16[49,64,256]{2,1,0:T(8,128)(2,1)} custom-call(f32[24,64,256]{2,1,0:T(8,128)S(1)} %get-tuple-element.84.refs_0_, bf16[24,64,256]{2,1,0:T(8,128)(2,1)S(1)} %collective-permute-done.18.refs_1_, f32[25,64,256]{2,1,0:T(8,128)S(1)} %get-tuple-element.88.refs_2_, bf16[25,64,256]{2,1,0:T(8,128)(2,1)S(1)} %collective-permute-done.20.refs_3_), custom_call_target="tpu_custom_call" | custom-call | bytes 1024 | tf_op jit(solution)/shard_map/pallas_call | solution.py:339
  (27 shorter events, 0.1 us)
Async XLA Ops:
  0.6 15.5 %copy-start.5 = (s32[16,256]{1,0:T(8,128)S(1)}, s32[16,256]{1,0:T(8,128)}, u32[]{:S(2)}) copy-start(s32[16,256]{1,0:T(8,128)} %refs_5_.1) | copy-start | bytes 49156
  0.6 15.5 %copy-start = (bf16[64,49,256]{2,0,1:T(8,128)(2,1)S(1)}, bf16[64,49,256]{2,0,1:T(8,128)(2,1)}, u32[]{:S(2)}) copy-start(bf16[64,49,256]{2,0,1:T(8,128)(2,1)} %param.8) | copy-start | bytes 4816900
  0.7 15.5 %collective-permute-start = (bf16[49,64,256]{2,1,0:T(8,128)(2,1)}, bf16[49,64,256]{2,1,0:T(8,128)(2,1)}, u32[]{:S(2)}, u32[]{:S(2)}) collective-permute-start(bf16[49,64,256]{2,1,0:T(8,128)(2,1)} %bitcast.14), channel_id=1, source_target_pairs={{0,1},{1,0},{2,3},{3,2},{4,5},{5,4},{6,7},{7,6},{8,9},{9,8},{10,11... | collective-permute-start | bytes 4816904 | tf_op jit(solution)/shard_map/ppermute | solution.py:373
  3.7 29.7 %collective-permute-start.1 = (bf16[24,64,128]{2,1,0:T(8,128)(2,1)}, bf16[24,64,128]{2,1,0:T(8,128)(2,1)S(1)}, u32[]{:S(2)}, u32[]{:S(2)}) collective-permute-start(bf16[24,64,128]{2,1,0:T(8,128)(2,1)} %get-tuple-element.47), channel_id=1, source_target_pairs={{0,2},{2,4},{4,6},{6,8},{8,10},{10,12},{12,14},{14,16},{16,18},{18... | collective-permute-start | bytes 1179656 | tf_op jit(solution)/shard_map/ppermute | solution.py:373
  6.4 27.0 %collective-permute-start.2 = (bf16[24,64,128]{2,1,0:T(8,128)(2,1)}, bf16[24,64,128]{2,1,0:T(8,128)(2,1)S(1)}, u32[]{:S(2)}, u32[]{:S(2)}) collective-permute-start(bf16[24,64,128]{2,1,0:T(8,128)(2,1)} %get-tuple-element.48), channel_id=1, source_target_pairs={{0,30},{2,0},{4,2},{6,4},{8,6},{10,8},{12,10},{14,12},{16,14},{18,... | collective-permute-start | bytes 1179656 | tf_op jit(solution)/shard_map/ppermute | solution.py:373
  10.5 31.1 %collective-permute-start.5 = (bf16[25,64,128]{2,1,0:T(8,128)(2,1)}, bf16[25,64,128]{2,1,0:T(8,128)(2,1)S(1)}, u32[]{:S(2)}, u32[]{:S(2)}) collective-permute-start(bf16[25,64,128]{2,1,0:T(8,128)(2,1)} %get-tuple-element.52), channel_id=1, source_target_pairs={{0,2},{2,4},{4,6},{6,8},{8,10},{10,12},{12,14},{14,16},{16,18},{18... | collective-permute-start | bytes 1228808 | tf_op jit(solution)/shard_map/ppermute | solution.py:373
  10.5 33.0 %collective-permute-start.6 = (bf16[25,64,128]{2,1,0:T(8,128)(2,1)}, bf16[25,64,128]{2,1,0:T(8,128)(2,1)S(1)}, u32[]{:S(2)}, u32[]{:S(2)}) collective-permute-start(bf16[25,64,128]{2,1,0:T(8,128)(2,1)} %get-tuple-element.53), channel_id=1, source_target_pairs={{0,30},{2,0},{4,2},{6,4},{8,6},{10,8},{12,10},{14,12},{16,14},{18,... | collective-permute-start | bytes 1228808 | tf_op jit(solution)/shard_map/ppermute | solution.py:373
  16.2 1.4 %copy-start.1 = (bf16[64,49,256]{2,0,1:T(8,128)(2,1)S(1)}, bf16[64,49,256]{2,0,1:T(8,128)(2,1)}, u32[]{:S(2)}) copy-start(bf16[64,49,256]{2,0,1:T(8,128)(2,1)} %param.6) | copy-start | bytes 4816900
  17.6 1.0 copy-start.4
  33.4 1.7 %collective-permute-start.3 = (bf16[24,64,128]{2,1,0:T(8,128)(2,1)S(1)}, bf16[24,64,128]{2,1,0:T(8,128)(2,1)S(1)}, u32[]{:S(2)}, u32[]{:S(2)}) collective-permute-start(bf16[24,64,128]{2,1,0:T(8,128)(2,1)S(1)} %get-tuple-element.50.refs_0_.refs_3_), channel_id=1, source_target_pairs={{0,1},{1,0},{2,3},{3,2},{4,5},{5,4},{6,7},{7,6},{8,9},{9,8},{10,11... | collective-permute-start | bytes 1179656 | tf_op jit(solution)/shard_map/ppermute | solution.py:373
  33.4 2.3 %collective-permute-start.4 = (bf16[24,64,128]{2,1,0:T(8,128)(2,1)S(1)}, bf16[24,64,128]{2,1,0:T(8,128)(2,1)S(1)}, u32[]{:S(2)}, u32[]{:S(2)}) collective-permute-start(bf16[24,64,128]{2,1,0:T(8,128)(2,1)S(1)} %get-tuple-element.51.refs_2_.refs_5_), channel_id=1, source_target_pairs={{0,1},{1,0},{2,3},{3,2},{4,5},{5,4},{6,7},{7,6},{8,9},{9,8},{10,11... | collective-permute-start | bytes 1179656 | tf_op jit(solution)/shard_map/ppermute | solution.py:373
  37.0 12.6 %copy-start.2 = (f32[4,16,256]{2,1,0:T(8,128)S(1)}, f32[4,16,256]{2,1,0:T(8,128)}, u32[]{:S(2)}) copy-start(f32[4,16,256]{2,1,0:T(8,128)} %refs_9_.1) | copy-start | bytes 196612
  37.0 12.6 %copy-start.3 = (s32[16,256]{1,0:T(8,128)S(1)}, s32[16,256]{1,0:T(8,128)}, u32[]{:S(2)}) copy-start(s32[16,256]{1,0:T(8,128)} %refs_10_.1) | copy-start | bytes 49156
  43.4 6.1 %collective-permute-start.7 = (bf16[25,64,128]{2,1,0:T(8,128)(2,1)S(1)}, bf16[25,64,128]{2,1,0:T(8,128)(2,1)S(1)}, u32[]{:S(2)}, u32[]{:S(2)}) collective-permute-start(bf16[25,64,128]{2,1,0:T(8,128)(2,1)S(1)} %get-tuple-element.57.refs_0_.refs_7_), channel_id=1, source_target_pairs={{0,1},{1,0},{2,3},{3,2},{4,5},{5,4},{6,7},{7,6},{8,9},{9,8},{10,11... | collective-permute-start | bytes 1228808 | tf_op jit(solution)/shard_map/ppermute | solution.py:373
  43.4 6.1 %collective-permute-start.8 = (bf16[25,64,128]{2,1,0:T(8,128)(2,1)S(1)}, bf16[25,64,128]{2,1,0:T(8,128)(2,1)S(1)}, u32[]{:S(2)}, u32[]{:S(2)}) collective-permute-start(bf16[25,64,128]{2,1,0:T(8,128)(2,1)S(1)} %get-tuple-element.58.refs_2_.refs_9_), channel_id=1, source_target_pairs={{0,1},{1,0},{2,3},{3,2},{4,5},{5,4},{6,7},{7,6},{8,9},{9,8},{10,11... | collective-permute-start | bytes 1228808 | tf_op jit(solution)/shard_map/ppermute | solution.py:373
  44.0 47.0 %collective-permute-start.9 = (bf16[49,64,128]{2,1,0:T(8,128)(2,1)S(1)}, bf16[49,64,128]{2,1,0:T(8,128)(2,1)S(1)}, u32[]{:S(2)}, u32[]{:S(2)}) collective-permute-start(bf16[49,64,128]{2,1,0:T(8,128)(2,1)S(1)} %get-tuple-element.73), channel_id=1, source_target_pairs={{0,2},{2,4},{4,6},{6,8},{8,10},{10,12},{12,14},{14,16},{16,18},{18... | collective-permute-start | bytes 2408456 | tf_op jit(solution)/shard_map/ppermute | solution.py:373
  45.4 45.5 %collective-permute-start.10 = (bf16[49,64,128]{2,1,0:T(8,128)(2,1)S(1)}, bf16[49,64,128]{2,1,0:T(8,128)(2,1)S(1)}, u32[]{:S(2)}, u32[]{:S(2)}) collective-permute-start(bf16[49,64,128]{2,1,0:T(8,128)(2,1)S(1)} %get-tuple-element.74), channel_id=1, source_target_pairs={{0,30},{2,0},{4,2},{6,4},{8,6},{10,8},{12,10},{14,12},{16,14},{18,... | collective-permute-start | bytes 2408456 | tf_op jit(solution)/shard_map/ppermute | solution.py:373
  61.1 10.1 %collective-permute-start.13 = (bf16[21,16,128]{2,1,0:T(8,128)(2,1)S(1)}, bf16[21,16,128]{2,1,0:T(8,128)(2,1)S(1)}, u32[]{:S(2)}, u32[]{:S(2)}) collective-permute-start(bf16[21,16,128]{2,1,0:T(8,128)(2,1)S(1)} %get-tuple-element.76), channel_id=1, source_target_pairs={{0,4},{2,6},{4,0},{6,2},{8,12},{10,14},{12,8},{14,10},{16,20},{18,... | collective-permute-start | bytes 258056 | tf_op jit(solution)/shard_map/ppermute | solution.py:378
  61.2 10.0 %collective-permute-start.14 = (bf16[21,16,128]{2,1,0:T(8,128)(2,1)S(1)}, bf16[21,16,128]{2,1,0:T(8,128)(2,1)S(1)}, u32[]{:S(2)}, u32[]{:S(2)}) collective-permute-start(bf16[21,16,128]{2,1,0:T(8,128)(2,1)S(1)} %get-tuple-element.77), channel_id=1, source_target_pairs={{0,8},{2,10},{4,12},{6,14},{8,0},{10,2},{12,4},{14,6},{16,24},{18,... | collective-permute-start | bytes 258056 | tf_op jit(solution)/shard_map/ppermute | solution.py:378
  61.5 9.8 %collective-permute-start.15 = (bf16[21,16,128]{2,1,0:T(8,128)(2,1)S(1)}, bf16[21,16,128]{2,1,0:T(8,128)(2,1)S(1)}, u32[]{:S(2)}, u32[]{:S(2)}) collective-permute-start(bf16[21,16,128]{2,1,0:T(8,128)(2,1)S(1)} %get-tuple-element.78), channel_id=1, source_target_pairs={{0,12},{2,14},{4,8},{6,10},{8,4},{10,6},{12,0},{14,2},{16,28},{18,... | collective-permute-start | bytes 258056 | tf_op jit(solution)/shard_map/ppermute | solution.py:378
  71.3 6.4 %collective-permute-start.16 = (bf16[21,16,128]{2,1,0:T(8,128)(2,1)S(1)}, bf16[21,16,128]{2,1,0:T(8,128)(2,1)S(1)}, u32[]{:S(2)}, u32[]{:S(2)}) collective-permute-start(bf16[21,16,128]{2,1,0:T(8,128)(2,1)S(1)} %get-tuple-element.91), channel_id=1, source_target_pairs={{0,16},{2,18},{4,20},{6,22},{8,24},{10,26},{12,28},{14,30},{16,0},... | collective-permute-start | bytes 258056 | tf_op jit(solution)/shard_map/ppermute | solution.py:378
  77.7 13.3 %collective-permute-start.17 = (bf16[21,16,128]{2,1,0:T(8,128)(2,1)S(1)}, bf16[21,16,128]{2,1,0:T(8,128)(2,1)S(1)}, u32[]{:S(2)}, u32[]{:S(2)}) collective-permute-start(bf16[21,16,128]{2,1,0:T(8,128)(2,1)S(1)} %fusion), channel_id=1, source_target_pairs={{0,18},{2,16},{4,22},{6,20},{8,26},{10,24},{12,30},{14,28},{16,2},... | collective-permute-start | bytes 258056 | tf_op jit(solution)/shard_map/ppermute | solution.py:378
  78.9 6.3 %collective-permute-start.12 = (bf16[144,128]{1,0:T(8,128)(2,1)S(1)}, bf16[144,128]{1,0:T(8,128)(2,1)S(1)}, u32[]{:S(2)}, u32[]{:S(2)}) collective-permute-start(bf16[144,128]{1,0:T(8,128)(2,1)S(1)} %get-tuple-element.66.refs_16_), channel_id=1, source_target_pairs={{0,30},{2,0},{4,2},{6,4},{8,6},{10,8},{12,10},{14,12},{16,14},{18,... | collective-permute-start | bytes 110600 | tf_op jit(solution)/shard_map/ppermute | solution.py:373
  83.4 7.6 %collective-permute-start.11 = (bf16[144,128]{1,0:T(8,128)(2,1)S(1)}, bf16[144,128]{1,0:T(8,128)(2,1)S(1)}, u32[]{:S(2)}, u32[]{:S(2)}) collective-permute-start(bf16[144,128]{1,0:T(8,128)(2,1)S(1)} %get-tuple-element.67.refs_17_), channel_id=1, source_target_pairs={{0,2},{2,4},{4,6},{6,8},{8,10},{10,12},{12,14},{14,16},{16,18},{18... | collective-permute-start | bytes 110600 | tf_op jit(solution)/shard_map/ppermute | solution.py:373
  91.0 6.2 %collective-permute-start.19 = (bf16[21,16,128]{2,1,0:T(8,128)(2,1)S(1)}, bf16[21,16,128]{2,1,0:T(8,128)(2,1)S(1)}, u32[]{:S(2)}, u32[]{:S(2)}) collective-permute-start(bf16[21,16,128]{2,1,0:T(8,128)(2,1)S(1)} %add_convert_fusion.refs_1_), channel_id=1, source_target_pairs={{0,8},{2,10},{4,12},{6,14},{8,0},{10,2},{12,4},{14,6},{16,24},{18,... | collective-permute-start | bytes 258056 | tf_op jit(solution)/shard_map/ppermute | solution.py:378
  91.1 9.3 %collective-permute-start.22 = (bf16[21,16,128]{2,1,0:T(8,128)(2,1)S(1)}, bf16[21,16,128]{2,1,0:T(8,128)(2,1)S(1)}, u32[]{:S(2)}, u32[]{:S(2)}) collective-permute-start(bf16[21,16,128]{2,1,0:T(8,128)(2,1)S(1)} %add_convert_fusion.refs_1_), channel_id=1, source_target_pairs={{0,12},{2,14},{4,8},{6,10},{8,4},{10,6},{12,0},{14,2},{16,28},{18,... | collective-permute-start | bytes 258056 | tf_op jit(solution)/shard_map/ppermute | solution.py:378
  91.2 9.2 %collective-permute-start.21 = (bf16[21,16,128]{2,1,0:T(8,128)(2,1)S(1)}, bf16[21,16,128]{2,1,0:T(8,128)(2,1)S(1)}, u32[]{:S(2)}, u32[]{:S(2)}) collective-permute-start(bf16[21,16,128]{2,1,0:T(8,128)(2,1)S(1)} %add_convert_fusion.refs_1_), channel_id=1, source_target_pairs={{0,4},{2,6},{4,0},{6,2},{8,12},{10,14},{12,8},{14,10},{16,20},{18,... | collective-permute-start | bytes 258056 | tf_op jit(solution)/shard_map/ppermute | solution.py:378
  97.2 4.7 %collective-permute-start.18 = (bf16[24,64,256]{2,1,0:T(8,128)(2,1)S(1)}, bf16[24,64,256]{2,1,0:T(8,128)(2,1)S(1)}, u32[]{:S(2)}, u32[]{:S(2)}) collective-permute-start(bf16[24,64,256]{2,1,0:T(8,128)(2,1)S(1)} %get-tuple-element.85), channel_id=1, source_target_pairs={{0,1},{1,0},{2,3},{3,2},{4,5},{5,4},{6,7},{7,6},{8,9},{9,8},{10,11... | collective-permute-start | bytes 2359304 | tf_op jit(solution)/shard_map/ppermute | solution.py:373
  99.8 2.5 %collective-permute-start.20 = (bf16[25,64,256]{2,1,0:T(8,128)(2,1)S(1)}, bf16[25,64,256]{2,1,0:T(8,128)(2,1)S(1)}, u32[]{:S(2)}, u32[]{:S(2)}) collective-permute-start(bf16[25,64,256]{2,1,0:T(8,128)(2,1)S(1)} %get-tuple-element.89), channel_id=1, source_target_pairs={{0,1},{1,0},{2,3},{3,2},{4,5},{5,4},{6,7},{7,6},{8,9},{9,8},{10,11... | collective-permute-start | bytes 2457608 | tf_op jit(solution)/shard_map/ppermute | solution.py:373

commit v12 on v7

--- a/solution.py
+++ b/solution.py
@@ -499,8 +499,9 @@
     for delta, part in enumerate(sent, 1):
         kept = kept + exchanged(part, "atom", delta << cut_bits[0]).astype(F32)
     rest = [bit for bit in reversed(range(count.bit_length() - 1)) if bit not in cut_bits]
-    for bit in rest:
-        arrived = exchanged(kept.astype(BF16), "atom", 1 << bit)
+    for at, bit in enumerate(rest):
+        also = 1 << rest[at - 1] if 0 < at == len(rest) - 1 else 0
+        arrived = exchanged(kept.astype(BF16), "atom", 1 << bit | also)
         if bit == rest[-1]:
             from_left, from_right, message_left, message_right, arrived = after(
                 (from_left, from_right, message_left, message_right, arrived), ()

time: 101 us -> 100 us (0.990)
    ppermute x8, waiting for transfers between devices: 10.4 us -> 7.55 us  [exchanged(): lax.ppermute(value, axis, [(source, source ^ offset) for source in range(...]
    ppermute x15, waiting for transfers between devices: 24 us -> 26.8 us  [shifted(): return lax.ppermute(value, axis, pairs)]
  transfers between devices with their start and end apart: 23 -> 23, of which waited for: 10 -> 9; matrix products, arithmetic and copies ran while one was open for 0% -> 0% of each run, Pallas kernels for 26% -> 27%
where the time goes in v12:
time: 100 us
  starting transfers between devices  34.3 us (34%)
  waiting for transfers between devices  34.3 us (34%)
  Pallas kernels  28.1 us (28%)
  local copies, waits for them, and re-layouts  2.41 us (2%)
    ppermute x15, waiting for transfers between devices, shifted(): return lax.ppermute(value, axis, pairs)  26.8 us
    pallas_call x8, Pallas kernels, call(): pl.pallas_call(body, out_shape=tuple(outs), in_specs=[small] * scalars +...  25.6 us
    ppermute x15, starting transfers between devices, shifted(): return lax.ppermute(value, axis, pairs)  23.6 us
    ppermute x8, starting transfers between devices, exchanged(): lax.ppermute(value, axis, [(source, source ^ offset) for source in range(...  10.7 us
    ppermute x8, waiting for transfers between devices, exchanged(): lax.ppermute(value, axis, [(source, source ^ offset) for source in range(...  7.55 us
    pallas_call x1, Pallas kernels, on_device(): pl.pallas_call(functools.partial(split_kernel, feature_cuts), out_shape=t...  2.54 us
    unnamed x12, local copies, waits for them, and re-layouts  2.41 us
  transfers between devices with their start and end apart: 23, of which 9 were waited for; matrix products, arithmetic and copies ran while one was open for 0% of the time, Pallas kernels for 27%

profile of v12, /device:TPU:0, one launch (start us, length us, event | category | flops | bytes accessed | tf_op | source)
XLA Modules:
  0.0 100.2 jit_solution(17866765148209028950)
XLA Ops:
  0.7 0.5 collective-permute-start
  1.2 2.5 %shard_map.85 = (bf16[24,64,128]{2,1,0:T(8,128)(2,1)}, bf16[24,64,128]{2,1,0:T(8,128)(2,1)}, bf16[25,64,128]{2,1,0:T(8,128)(2,1)}, bf16[25,64,128]{2,1,0:T(8,128)(2,1)}) custom-call(bf16[49,64,256]{2,1,0:T(8,128)(2,1)} %bitcast.15), custom_call_target="tpu_custom_call" | custom-call | tf_op jit(solution)/shard_map/pallas_call | solution.py:410
  3.7 2.7 %collective-permute-start.1 = (bf16[24,64,128]{2,1,0:T(8,128)(2,1)}, bf16[24,64,128]{2,1,0:T(8,128)(2,1)S(1)}, u32[]{:S(2)}, u32[]{:S(2)}) collective-permute-start(bf16[24,64,128]{2,1,0:T(8,128)(2,1)} %get-tuple-element.47), channel_id=1, source_target_pairs={{0,2},{2,4},{4,6},{6,8},{8,10},{10,12},{12,14},{14,16},{16,18},{18... | collective-permute-start | bytes 1179656 | tf_op jit(solution)/shard_map/ppermute | solution.py:374
  6.4 4.1 %collective-permute-start.2 = (bf16[24,64,128]{2,1,0:T(8,128)(2,1)}, bf16[24,64,128]{2,1,0:T(8,128)(2,1)S(1)}, u32[]{:S(2)}, u32[]{:S(2)}) collective-permute-start(bf16[24,64,128]{2,1,0:T(8,128)(2,1)} %get-tuple-element.48), channel_id=1, source_target_pairs={{0,30},{2,0},{4,2},{6,4},{8,6},{10,8},{12,10},{14,12},{16,14},{18,... | collective-permute-start | bytes 1179656 | tf_op jit(solution)/shard_map/ppermute | solution.py:374
  10.5 5.6 %collective-permute-start.6 = (bf16[25,64,128]{2,1,0:T(8,128)(2,1)}, bf16[25,64,128]{2,1,0:T(8,128)(2,1)S(1)}, u32[]{:S(2)}, u32[]{:S(2)}) collective-permute-start(bf16[25,64,128]{2,1,0:T(8,128)(2,1)} %get-tuple-element.53), channel_id=1, source_target_pairs={{0,30},{2,0},{4,2},{6,4},{8,6},{10,8},{12,10},{14,12},{16,14},{18,... | collective-permute-start | bytes 1228808 | tf_op jit(solution)/shard_map/ppermute | solution.py:374
  16.1 0.1 pad_add_fusion.refs_0_
  16.2 0.0 copy-start.1
  16.2 1.4 %copy-done.1 = bf16[64,49,256]{2,0,1:T(8,128)(2,1)S(1)} copy-done((bf16[64,49,256]{2,0,1:T(8,128)(2,1)S(1)}, bf16[64,49,256]{2,0,1:T(8,128)(2,1)}, u32[]{:S(2)}) %copy-start.1) | copy-done | bytes 1605656
  17.6 1.0 copy-done.4
  18.6 4.7 %shard_map.86 = (bf16[49,192,256]{2,1,0:T(8,128)(2,1)S(1)}, f32[8,256,256]{2,1,0:T(8,128)S(1)}, s32[2,3,128,128]{3,2,1,0:T(8,128)S(1)}, s32[16,256]{1,0:T(8,128)...) custom-call(s32[3]{0:T(128)S(1)} %pad_add_fusion.refs_0_, ...), custom_call_target="tpu_custom_call" | custom-call | flops 12000000000 | bytes 1024 | tf_op jit(solution)/shard_map/pallas_call | solution.py:340
  23.3 10.1 %collective-permute-done.1.refs_0_ = bf16[24,64,128]{2,1,0:T(8,128)(2,1)S(1)} collective-permute-done((bf16[24,64,128]{2,1,0:T(8,128)(2,1)}, bf16[24,64,128]{2,1,0:T(8,128)(2,1)S(1)}, u32[]{:S(2)}, u32[]{:S(2)}) %collective-permute-start.1) | collective-permute-done | bytes 393248 | tf_op jit(solution)/shard_map/ppermute | solution.py:374
  33.4 0.0 collective-permute-start.3
  33.4 0.5 collective-permute-start.4
  33.9 1.2 %collective-permute-done.3.refs_1_.refs_4_ = bf16[24,64,128]{2,1,0:T(8,128)(2,1)S(1)} collective-permute-done((bf16[24,64,128]{2,1,0:T(8,128)(2,1)S(1)}, bf16[24,64,128]{2,1,0:T(8,128)(2,1)S(1)}, u32[]{:S(2)}, u32[]{:S(2)}) %collective-permute-start.3) | collective-permute-done | bytes 393248 | tf_op jit(solution)/shard_map/ppermute | solution.py:374
  35.1 0.6 collective-permute-done.4.refs_3_.refs_6_
  35.7 1.3 %shard_map.88 = (bf16[24,192,256]{2,1,0:T(8,128)(2,1)S(1)}, f32[8,2,128,128]{3,2,1,0:T(8,128)S(1)}, f32[8,128]{1,0:T(8,128)S(1)}) custom-call(bf16[24,64,128]{2,1,0:T(8,128)(2,1)S(1)} %get-tuple-element.50.refs_0_.refs_3_, bf16[24,64,128]{2,1,0:T(8,128)(2,1)S(1)} %collective-permute-done.3.refs_1_.refs_4_, ...), custom_call_target="tpu_custom_call" | custom-call | bytes 1024 | tf_op jit(solution)/shard_map/pallas_call | solution.py:340
  37.0 0.0 copy-start.2
  37.0 0.0 copy-start.3
  37.0 4.6 %collective-permute-done.5.refs_0_ = bf16[25,64,128]{2,1,0:T(8,128)(2,1)S(1)} collective-permute-done((bf16[25,64,128]{2,1,0:T(8,128)(2,1)}, bf16[25,64,128]{2,1,0:T(8,128)(2,1)S(1)}, u32[]{:S(2)}, u32[]{:S(2)}) %collective-permute-start.5) | collective-permute-done | bytes 409632 | tf_op jit(solution)/shard_map/ppermute | solution.py:374
  41.6 1.8 %collective-permute-done.6.refs_1_ = bf16[25,64,128]{2,1,0:T(8,128)(2,1)S(1)} collective-permute-done((bf16[25,64,128]{2,1,0:T(8,128)(2,1)}, bf16[25,64,128]{2,1,0:T(8,128)(2,1)S(1)}, u32[]{:S(2)}, u32[]{:S(2)}) %collective-permute-start.6) | collective-permute-done | bytes 409632 | tf_op jit(solution)/shard_map/ppermute | solution.py:374
  43.4 0.0 collective-permute-start.7
  43.4 0.5 collective-permute-start.8
  44.0 1.5 %collective-permute-start.9 = (bf16[49,64,128]{2,1,0:T(8,128)(2,1)S(1)}, bf16[49,64,128]{2,1,0:T(8,128)(2,1)S(1)}, u32[]{:S(2)}, u32[]{:S(2)}) collective-permute-start(bf16[49,64,128]{2,1,0:T(8,128)(2,1)S(1)} %get-tuple-element.73), channel_id=1, source_target_pairs={{0,2},{2,4},{4,6},{6,8},{8,10},{10,12},{12,14},{14,16},{16,18},{18... | collective-permute-start | bytes 2408456 | tf_op jit(solution)/shard_map/ppermute | solution.py:374
  45.4 4.1 %collective-permute-start.10 = (bf16[49,64,128]{2,1,0:T(8,128)(2,1)S(1)}, bf16[49,64,128]{2,1,0:T(8,128)(2,1)S(1)}, u32[]{:S(2)}, u32[]{:S(2)}) collective-permute-start(bf16[49,64,128]{2,1,0:T(8,128)(2,1)S(1)} %get-tuple-element.74), channel_id=1, source_target_pairs={{0,30},{2,0},{4,2},{6,4},{8,6},{10,8},{12,10},{14,12},{16,14},{18,... | collective-permute-start | bytes 2408456 | tf_op jit(solution)/shard_map/ppermute | solution.py:374
  49.6 0.0 collective-permute-done.7.refs_1_.refs_8_
  49.6 0.0 collective-permute-done.8.refs_3_.refs_10_
  49.6 3.8 %shard_map.90 = (bf16[25,192,256]{2,1,0:T(8,128)(2,1)S(1)}, f32[4,16,256]{2,1,0:T(8,128)}, f32[176,128]{1,0:T(8,128)S(1)}, f32[176,128]{1,0:T(8,128)S(1)}) custom-call(bf16[25,64,128]{2,1,0:T(8,128)(2,1)S(1)} %get-tuple-element.57.refs_0_.refs_7_, bf16[25,64,128]{2,1,0:T(8,128)(2,1)S(1)} %collective-permute-done.7.refs_1_.refs_8_, ...), custom_call_target="tpu_custom_call" | custom-call | bytes 1024 | tf_op jit(solution)/shard_map/pallas_call | solution.py:340
  53.4 7.7 %shard_map.91 = (bf16[49,64,256]{2,1,0:T(8,128)(2,1)S(1)}, f32[49,64,256]{2,1,0:T(8,128)S(1)}, f32[49,64,256]{2,1,0:T(8,128)S(1)}, f32[21,16,128]{2,1,0:T(8,128)...) custom-call(s32[3]{0:T(128)S(1)} %pad_add_fusion.refs_0_, ...), custom_call_target="tpu_custom_call" | custom-call | bytes 1024 | tf_op jit(solution)/shard_map/pallas_call | solution.py:340
  61.2 0.1 collective-permute-start.13
  61.2 0.3 collective-permute-start.14
  61.5 3.2 %collective-permute-start.15 = (bf16[21,16,128]{2,1,0:T(8,128)(2,1)S(1)}, bf16[21,16,128]{2,1,0:T(8,128)(2,1)S(1)}, u32[]{:S(2)}, u32[]{:S(2)}) collective-permute-start(bf16[21,16,128]{2,1,0:T(8,128)(2,1)S(1)} %get-tuple-element.78), channel_id=1, source_target_pairs={{0,12},{2,14},{4,8},{6,10},{8,4},{10,6},{12,0},{14,2},{16,28},{18,... | collective-permute-start | bytes 258056 | tf_op jit(solution)/shard_map/ppermute | solution.py:379
  64.7 6.5 %collective-permute-done.13 = bf16[21,16,128]{2,1,0:T(8,128)(2,1)S(1)} collective-permute-done((bf16[21,16,128]{2,1,0:T(8,128)(2,1)S(1)}, bf16[21,16,128]{2,1,0:T(8,128)(2,1)S(1)}, u32[]{:S(2)}, u32[]{:S(2)}) %collective-permute-start.13) | collective-permute-done | bytes 86048 | tf_op jit(solution)/shard_map/ppermute | solution.py:379
  71.2 0.1 fusion.1
  71.3 1.9 %collective-permute-start.16 = (bf16[21,16,128]{2,1,0:T(8,128)(2,1)S(1)}, bf16[21,16,128]{2,1,0:T(8,128)(2,1)S(1)}, u32[]{:S(2)}, u32[]{:S(2)}) collective-permute-start(bf16[21,16,128]{2,1,0:T(8,128)(2,1)S(1)} %get-tuple-element.91), channel_id=1, source_target_pairs={{0,16},{2,18},{4,20},{6,22},{8,24},{10,26},{12,28},{14,30},{16,0},... | collective-permute-start | bytes 258056 | tf_op jit(solution)/shard_map/ppermute | solution.py:379
  73.2 3.5 %collective-permute-start.12 = (f32[176,128]{1,0:T(8,128)S(1)}, f32[176,128]{1,0:T(8,128)S(1)}, u32[]{:S(2)}, u32[]{:S(2)}) collective-permute-start(f32[176,128]{1,0:T(8,128)S(1)} %get-tuple-element.66.refs_16_), channel_id=1, source_target_pairs={{0,30},{2,0},{4,2},{6,4},{8,6},{10,8},{12,10},{14,12},{16,14},{18,... | collective-permute-start | bytes 270344 | tf_op jit(solution)/shard_map/ppermute | solution.py:374
  76.7 0.0 collective-permute-start.11
  76.7 1.0 %collective-permute-done.16 = bf16[21,16,128]{2,1,0:T(8,128)(2,1)S(1)} collective-permute-done((bf16[21,16,128]{2,1,0:T(8,128)(2,1)S(1)}, bf16[21,16,128]{2,1,0:T(8,128)(2,1)S(1)}, u32[]{:S(2)}, u32[]{:S(2)}) %collective-permute-start.16) | collective-permute-done | bytes 86048 | tf_op jit(solution)/shard_map/ppermute | solution.py:379
  77.7 1.3 %collective-permute-start.17 = (bf16[21,16,128]{2,1,0:T(8,128)(2,1)S(1)}, bf16[21,16,128]{2,1,0:T(8,128)(2,1)S(1)}, u32[]{:S(2)}, u32[]{:S(2)}) collective-permute-start(bf16[21,16,128]{2,1,0:T(8,128)(2,1)S(1)} %fusion), channel_id=1, source_target_pairs={{0,18},{2,16},{4,22},{6,20},{8,26},{10,24},{12,30},{14,28},{16,2},... | collective-permute-start | bytes 258056 | tf_op jit(solution)/shard_map/ppermute | solution.py:379
  79.0 8.0 %collective-permute-done.12.refs_3_ = f32[176,128]{1,0:T(8,128)S(1)} collective-permute-done((f32[176,128]{1,0:T(8,128)S(1)}, f32[176,128]{1,0:T(8,128)S(1)}, u32[]{:S(2)}, u32[]{:S(2)}) %collective-permute-start.12) | collective-permute-done | bytes 90144 | tf_op jit(solution)/shard_map/ppermute | solution.py:374
  87.0 1.3 %collective-permute-start.19 = (bf16[21,16,128]{2,1,0:T(8,128)(2,1)S(1)}, bf16[21,16,128]{2,1,0:T(8,128)(2,1)S(1)}, u32[]{:S(2)}, u32[]{:S(2)}) collective-permute-start(bf16[21,16,128]{2,1,0:T(8,128)(2,1)S(1)} %add_convert_fusion.refs_1_), channel_id=1, source_target_pairs={{0,8},{2,10},{4,12},{6,14},{8,0},{10,2},{12,4},{14,6},{16,24},{18,... | collective-permute-start | bytes 258056 | tf_op jit(solution)/shard_map/ppermute | solution.py:379
  88.3 2.7 %collective-permute-start.22 = (bf16[21,16,128]{2,1,0:T(8,128)(2,1)S(1)}, bf16[21,16,128]{2,1,0:T(8,128)(2,1)S(1)}, u32[]{:S(2)}, u32[]{:S(2)}) collective-permute-start(bf16[21,16,128]{2,1,0:T(8,128)(2,1)S(1)} %add_convert_fusion.refs_1_), channel_id=1, source_target_pairs={{0,12},{2,14},{4,8},{6,10},{8,4},{10,6},{12,0},{14,2},{16,28},{18,... | collective-permute-start | bytes 258056 | tf_op jit(solution)/shard_map/ppermute | solution.py:379
  91.0 2.5 %shard_map.94 = (f32[24,64,256]{2,1,0:T(8,128)S(1)}, bf16[24,64,256]{2,1,0:T(8,128)(2,1)S(1)}, f32[8,128]{1,0:T(8,128)S(1)}) custom-call(bf16[49,64,256]{2,1,0:T(8,128)(2,1)S(1)} %get-tuple-element.68.refs_0_, f32[49,64,256]{2,1,0:T(8,128)S(1)} %get-tuple-element.69.refs_1_, f32[49,64,256]{2,1,0:T(8,128)S(1)} %get-tuple-element.70.refs_2_, ...), custom_call_target="tpu_custom_call" | custom-call | bytes 1024 | tf_op jit(solution)/shard_map/pallas_call | solution.py:340
  93.5 0.1 collective-permute-start.18
  93.6 2.6 %shard_map.95 = (f32[25,64,256]{2,1,0:T(8,128)S(1)}, bf16[25,64,256]{2,1,0:T(8,128)(2,1)S(1)}, f32[8,128]{1,0:T(8,128)}) custom-call(bf16[49,64,256]{2,1,0:T(8,128)(2,1)S(1)} %get-tuple-element.68.refs_0_, f32[49,64,256]{2,1,0:T(8,128)S(1)} %get-tuple-element.69.refs_1_, f32[49,64,256]{2,1,0:T(8,128)S(1)} %get-tuple-element.70.refs_2_, ...), custom_call_target="tpu_custom_call" | custom-call | bytes 1024 | tf_op jit(solution)/shard_map/pallas_call | solution.py:340
  96.2 0.6 collective-permute-start.20
  96.7 1.4 %shard_map.97 = f32[21,64,128]{2,1,0:T(8,128)} custom-call(s32[3]{0:T(128)S(1)} %pad_add_fusion.refs_0_, bf16[21,16,128]{2,1,0:T(8,128)(2,1)S(1)} %add_convert_fusion.refs_1_, bf16[21,16,128]{2,1,0:T(8,128)(2,1)S(1)} %collective-permute-done.21.refs_2_, bf16[21,16,128]{2,1,0:T(8,128)(2,1)S(1)} %collective-permute-done.19.refs_10_.refs_3_, ...), custom_call_target="tpu_custom_call" | custom-call | flops 20000000000 | bytes 1024 | tf_op jit(solution)/shard_map/pallas_call | solution.py:340
  98.2 0.5 collective-permute-done.20.refs_3_
  98.7 1.5 %shard_map.96 = bf16[49,64,256]{2,1,0:T(8,128)(2,1)} custom-call(f32[24,64,256]{2,1,0:T(8,128)S(1)} %get-tuple-element.84.refs_0_, bf16[24,64,256]{2,1,0:T(8,128)(2,1)S(1)} %collective-permute-done.18.refs_1_, f32[25,64,256]{2,1,0:T(8,128)S(1)} %get-tuple-element.88.refs_2_, bf16[25,64,256]{2,1,0:T(8,128)(2,1)S(1)} %collective-permute-done.20.refs_3_), custom_call_target="tpu_custom_call" | custom-call | bytes 1024 | tf_op jit(solution)/shard_map/pallas_call | solution.py:340
  (27 shorter events, 0.1 us)
Async XLA Ops:
  0.6 15.5 %copy-start.5 = (s32[16,256]{1,0:T(8,128)S(1)}, s32[16,256]{1,0:T(8,128)}, u32[]{:S(2)}) copy-start(s32[16,256]{1,0:T(8,128)} %refs_5_.1) | copy-start | bytes 49156
  0.6 15.5 %copy-start = (bf16[64,49,256]{2,0,1:T(8,128)(2,1)S(1)}, bf16[64,49,256]{2,0,1:T(8,128)(2,1)}, u32[]{:S(2)}) copy-start(bf16[64,49,256]{2,0,1:T(8,128)(2,1)} %param.8) | copy-start | bytes 4816900
  0.7 15.5 %collective-permute-start = (bf16[49,64,256]{2,1,0:T(8,128)(2,1)}, bf16[49,64,256]{2,1,0:T(8,128)(2,1)}, u32[]{:S(2)}, u32[]{:S(2)}) collective-permute-start(bf16[49,64,256]{2,1,0:T(8,128)(2,1)} %bitcast.14), channel_id=1, source_target_pairs={{0,1},{1,0},{2,3},{3,2},{4,5},{5,4},{6,7},{7,6},{8,9},{9,8},{10,11... | collective-permute-start | bytes 4816904 | tf_op jit(solution)/shard_map/ppermute | solution.py:374
  3.7 29.7 %collective-permute-start.1 = (bf16[24,64,128]{2,1,0:T(8,128)(2,1)}, bf16[24,64,128]{2,1,0:T(8,128)(2,1)S(1)}, u32[]{:S(2)}, u32[]{:S(2)}) collective-permute-start(bf16[24,64,128]{2,1,0:T(8,128)(2,1)} %get-tuple-element.47), channel_id=1, source_target_pairs={{0,2},{2,4},{4,6},{6,8},{8,10},{10,12},{12,14},{14,16},{16,18},{18... | collective-permute-start | bytes 1179656 | tf_op jit(solution)/shard_map/ppermute | solution.py:374
  6.4 27.0 %collective-permute-start.2 = (bf16[24,64,128]{2,1,0:T(8,128)(2,1)}, bf16[24,64,128]{2,1,0:T(8,128)(2,1)S(1)}, u32[]{:S(2)}, u32[]{:S(2)}) collective-permute-start(bf16[24,64,128]{2,1,0:T(8,128)(2,1)} %get-tuple-element.48), channel_id=1, source_target_pairs={{0,30},{2,0},{4,2},{6,4},{8,6},{10,8},{12,10},{14,12},{16,14},{18,... | collective-permute-start | bytes 1179656 | tf_op jit(solution)/shard_map/ppermute | solution.py:374
  10.5 31.1 %collective-permute-start.5 = (bf16[25,64,128]{2,1,0:T(8,128)(2,1)}, bf16[25,64,128]{2,1,0:T(8,128)(2,1)S(1)}, u32[]{:S(2)}, u32[]{:S(2)}) collective-permute-start(bf16[25,64,128]{2,1,0:T(8,128)(2,1)} %get-tuple-element.52), channel_id=1, source_target_pairs={{0,2},{2,4},{4,6},{6,8},{8,10},{10,12},{12,14},{14,16},{16,18},{18... | collective-permute-start | bytes 1228808 | tf_op jit(solution)/shard_map/ppermute | solution.py:374
  10.5 33.0 %collective-permute-start.6 = (bf16[25,64,128]{2,1,0:T(8,128)(2,1)}, bf16[25,64,128]{2,1,0:T(8,128)(2,1)S(1)}, u32[]{:S(2)}, u32[]{:S(2)}) collective-permute-start(bf16[25,64,128]{2,1,0:T(8,128)(2,1)} %get-tuple-element.53), channel_id=1, source_target_pairs={{0,30},{2,0},{4,2},{6,4},{8,6},{10,8},{12,10},{14,12},{16,14},{18,... | collective-permute-start | bytes 1228808 | tf_op jit(solution)/shard_map/ppermute | solution.py:374
  16.2 1.4 %copy-start.1 = (bf16[64,49,256]{2,0,1:T(8,128)(2,1)S(1)}, bf16[64,49,256]{2,0,1:T(8,128)(2,1)}, u32[]{:S(2)}) copy-start(bf16[64,49,256]{2,0,1:T(8,128)(2,1)} %param.6) | copy-start | bytes 4816900
  17.6 1.0 copy-start.4
  33.4 1.7 %collective-permute-start.3 = (bf16[24,64,128]{2,1,0:T(8,128)(2,1)S(1)}, bf16[24,64,128]{2,1,0:T(8,128)(2,1)S(1)}, u32[]{:S(2)}, u32[]{:S(2)}) collective-permute-start(bf16[24,64,128]{2,1,0:T(8,128)(2,1)S(1)} %get-tuple-element.50.refs_0_.refs_3_), channel_id=1, source_target_pairs={{0,1},{1,0},{2,3},{3,2},{4,5},{5,4},{6,7},{7,6},{8,9},{9,8},{10,11... | collective-permute-start | bytes 1179656 | tf_op jit(solution)/shard_map/ppermute | solution.py:374
  33.4 2.3 %collective-permute-start.4 = (bf16[24,64,128]{2,1,0:T(8,128)(2,1)S(1)}, bf16[24,64,128]{2,1,0:T(8,128)(2,1)S(1)}, u32[]{:S(2)}, u32[]{:S(2)}) collective-permute-start(bf16[24,64,128]{2,1,0:T(8,128)(2,1)S(1)} %get-tuple-element.51.refs_2_.refs_5_), channel_id=1, source_target_pairs={{0,1},{1,0},{2,3},{3,2},{4,5},{5,4},{6,7},{7,6},{8,9},{9,8},{10,11... | collective-permute-start | bytes 1179656 | tf_op jit(solution)/shard_map/ppermute | solution.py:374
  37.0 12.6 %copy-start.2 = (f32[4,16,256]{2,1,0:T(8,128)S(1)}, f32[4,16,256]{2,1,0:T(8,128)}, u32[]{:S(2)}) copy-start(f32[4,16,256]{2,1,0:T(8,128)} %refs_9_.1) | copy-start | bytes 196612
  37.0 12.6 %copy-start.3 = (s32[16,256]{1,0:T(8,128)S(1)}, s32[16,256]{1,0:T(8,128)}, u32[]{:S(2)}) copy-start(s32[16,256]{1,0:T(8,128)} %refs_10_.1) | copy-start | bytes 49156
  43.4 6.1 %collective-permute-start.7 = (bf16[25,64,128]{2,1,0:T(8,128)(2,1)S(1)}, bf16[25,64,128]{2,1,0:T(8,128)(2,1)S(1)}, u32[]{:S(2)}, u32[]{:S(2)}) collective-permute-start(bf16[25,64,128]{2,1,0:T(8,128)(2,1)S(1)} %get-tuple-element.57.refs_0_.refs_7_), channel_id=1, source_target_pairs={{0,1},{1,0},{2,3},{3,2},{4,5},{5,4},{6,7},{7,6},{8,9},{9,8},{10,11... | collective-permute-start | bytes 1228808 | tf_op jit(solution)/shard_map/ppermute | solution.py:374
  43.4 6.1 %collective-permute-start.8 = (bf16[25,64,128]{2,1,0:T(8,128)(2,1)S(1)}, bf16[25,64,128]{2,1,0:T(8,128)(2,1)S(1)}, u32[]{:S(2)}, u32[]{:S(2)}) collective-permute-start(bf16[25,64,128]{2,1,0:T(8,128)(2,1)S(1)} %get-tuple-element.58.refs_2_.refs_9_), channel_id=1, source_target_pairs={{0,1},{1,0},{2,3},{3,2},{4,5},{5,4},{6,7},{7,6},{8,9},{9,8},{10,11... | collective-permute-start | bytes 1228808 | tf_op jit(solution)/shard_map/ppermute | solution.py:374
  44.0 43.0 %collective-permute-start.9 = (bf16[49,64,128]{2,1,0:T(8,128)(2,1)S(1)}, bf16[49,64,128]{2,1,0:T(8,128)(2,1)S(1)}, u32[]{:S(2)}, u32[]{:S(2)}) collective-permute-start(bf16[49,64,128]{2,1,0:T(8,128)(2,1)S(1)} %get-tuple-element.73), channel_id=1, source_target_pairs={{0,2},{2,4},{4,6},{6,8},{8,10},{10,12},{12,14},{14,16},{16,18},{18... | collective-permute-start | bytes 2408456 | tf_op jit(solution)/shard_map/ppermute | solution.py:374
  45.4 41.5 %collective-permute-start.10 = (bf16[49,64,128]{2,1,0:T(8,128)(2,1)S(1)}, bf16[49,64,128]{2,1,0:T(8,128)(2,1)S(1)}, u32[]{:S(2)}, u32[]{:S(2)}) collective-permute-start(bf16[49,64,128]{2,1,0:T(8,128)(2,1)S(1)} %get-tuple-element.74), channel_id=1, source_target_pairs={{0,30},{2,0},{4,2},{6,4},{8,6},{10,8},{12,10},{14,12},{16,14},{18,... | collective-permute-start | bytes 2408456 | tf_op jit(solution)/shard_map/ppermute | solution.py:374
  61.2 10.1 %collective-permute-start.13 = (bf16[21,16,128]{2,1,0:T(8,128)(2,1)S(1)}, bf16[21,16,128]{2,1,0:T(8,128)(2,1)S(1)}, u32[]{:S(2)}, u32[]{:S(2)}) collective-permute-start(bf16[21,16,128]{2,1,0:T(8,128)(2,1)S(1)} %get-tuple-element.76), channel_id=1, source_target_pairs={{0,4},{2,6},{4,0},{6,2},{8,12},{10,14},{12,8},{14,10},{16,20},{18,... | collective-permute-start | bytes 258056 | tf_op jit(solution)/shard_map/ppermute | solution.py:379
  61.2 10.0 %collective-permute-start.14 = (bf16[21,16,128]{2,1,0:T(8,128)(2,1)S(1)}, bf16[21,16,128]{2,1,0:T(8,128)(2,1)S(1)}, u32[]{:S(2)}, u32[]{:S(2)}) collective-permute-start(bf16[21,16,128]{2,1,0:T(8,128)(2,1)S(1)} %get-tuple-element.77), channel_id=1, source_target_pairs={{0,8},{2,10},{4,12},{6,14},{8,0},{10,2},{12,4},{14,6},{16,24},{18,... | collective-permute-start | bytes 258056 | tf_op jit(solution)/shard_map/ppermute | solution.py:379
  61.5 9.7 %collective-permute-start.15 = (bf16[21,16,128]{2,1,0:T(8,128)(2,1)S(1)}, bf16[21,16,128]{2,1,0:T(8,128)(2,1)S(1)}, u32[]{:S(2)}, u32[]{:S(2)}) collective-permute-start(bf16[21,16,128]{2,1,0:T(8,128)(2,1)S(1)} %get-tuple-element.78), channel_id=1, source_target_pairs={{0,12},{2,14},{4,8},{6,10},{8,4},{10,6},{12,0},{14,2},{16,28},{18,... | collective-permute-start | bytes 258056 | tf_op jit(solution)/shard_map/ppermute | solution.py:379
  71.3 6.4 %collective-permute-start.16 = (bf16[21,16,128]{2,1,0:T(8,128)(2,1)S(1)}, bf16[21,16,128]{2,1,0:T(8,128)(2,1)S(1)}, u32[]{:S(2)}, u32[]{:S(2)}) collective-permute-start(bf16[21,16,128]{2,1,0:T(8,128)(2,1)S(1)} %get-tuple-element.91), channel_id=1, source_target_pairs={{0,16},{2,18},{4,20},{6,22},{8,24},{10,26},{12,28},{14,30},{16,0},... | collective-permute-start | bytes 258056 | tf_op jit(solution)/shard_map/ppermute | solution.py:379
  73.2 13.7 %collective-permute-start.12 = (f32[176,128]{1,0:T(8,128)S(1)}, f32[176,128]{1,0:T(8,128)S(1)}, u32[]{:S(2)}, u32[]{:S(2)}) collective-permute-start(f32[176,128]{1,0:T(8,128)S(1)} %get-tuple-element.66.refs_16_), channel_id=1, source_target_pairs={{0,30},{2,0},{4,2},{6,4},{8,6},{10,8},{12,10},{14,12},{16,14},{18,... | collective-permute-start | bytes 270344 | tf_op jit(solution)/shard_map/ppermute | solution.py:374
  76.7 10.3 %collective-permute-start.11 = (f32[176,128]{1,0:T(8,128)S(1)}, f32[176,128]{1,0:T(8,128)S(1)}, u32[]{:S(2)}, u32[]{:S(2)}) collective-permute-start(f32[176,128]{1,0:T(8,128)S(1)} %get-tuple-element.67.refs_17_), channel_id=1, source_target_pairs={{0,2},{2,4},{4,6},{6,8},{8,10},{10,12},{12,14},{14,16},{16,18},{18... | collective-permute-start | bytes 270344 | tf_op jit(solution)/shard_map/ppermute | solution.py:374
  77.7 9.2 %collective-permute-start.17 = (bf16[21,16,128]{2,1,0:T(8,128)(2,1)S(1)}, bf16[21,16,128]{2,1,0:T(8,128)(2,1)S(1)}, u32[]{:S(2)}, u32[]{:S(2)}) collective-permute-start(bf16[21,16,128]{2,1,0:T(8,128)(2,1)S(1)} %fusion), channel_id=1, source_target_pairs={{0,18},{2,16},{4,22},{6,20},{8,26},{10,24},{12,30},{14,28},{16,2},... | collective-permute-start | bytes 258056 | tf_op jit(solution)/shard_map/ppermute | solution.py:379
  87.0 6.6 %collective-permute-start.19 = (bf16[21,16,128]{2,1,0:T(8,128)(2,1)S(1)}, bf16[21,16,128]{2,1,0:T(8,128)(2,1)S(1)}, u32[]{:S(2)}, u32[]{:S(2)}) collective-permute-start(bf16[21,16,128]{2,1,0:T(8,128)(2,1)S(1)} %add_convert_fusion.refs_1_), channel_id=1, source_target_pairs={{0,8},{2,10},{4,12},{6,14},{8,0},{10,2},{12,4},{14,6},{16,24},{18,... | collective-permute-start | bytes 258056 | tf_op jit(solution)/shard_map/ppermute | solution.py:379
  88.3 8.5 %collective-permute-start.22 = (bf16[21,16,128]{2,1,0:T(8,128)(2,1)S(1)}, bf16[21,16,128]{2,1,0:T(8,128)(2,1)S(1)}, u32[]{:S(2)}, u32[]{:S(2)}) collective-permute-start(bf16[21,16,128]{2,1,0:T(8,128)(2,1)S(1)} %add_convert_fusion.refs_1_), channel_id=1, source_target_pairs={{0,12},{2,14},{4,8},{6,10},{8,4},{10,6},{12,0},{14,2},{16,28},{18,... | collective-permute-start | bytes 258056 | tf_op jit(solution)/shard_map/ppermute | solution.py:379
  91.0 5.8 %collective-permute-start.21 = (bf16[21,16,128]{2,1,0:T(8,128)(2,1)S(1)}, bf16[21,16,128]{2,1,0:T(8,128)(2,1)S(1)}, u32[]{:S(2)}, u32[]{:S(2)}) collective-permute-start(bf16[21,16,128]{2,1,0:T(8,128)(2,1)S(1)} %add_convert_fusion.refs_1_), channel_id=1, source_target_pairs={{0,4},{2,6},{4,0},{6,2},{8,12},{10,14},{12,8},{14,10},{16,20},{18,... | collective-permute-start | bytes 258056 | tf_op jit(solution)/shard_map/ppermute | solution.py:379
  93.5 4.7 %collective-permute-start.18 = (bf16[24,64,256]{2,1,0:T(8,128)(2,1)S(1)}, bf16[24,64,256]{2,1,0:T(8,128)(2,1)S(1)}, u32[]{:S(2)}, u32[]{:S(2)}) collective-permute-start(bf16[24,64,256]{2,1,0:T(8,128)(2,1)S(1)} %get-tuple-element.85), channel_id=1, source_target_pairs={{0,1},{1,0},{2,3},{3,2},{4,5},{5,4},{6,7},{7,6},{8,9},{9,8},{10,11... | collective-permute-start | bytes 2359304 | tf_op jit(solution)/shard_map/ppermute | solution.py:374
  96.2 2.5 %collective-permute-start.20 = (bf16[25,64,256]{2,1,0:T(8,128)(2,1)S(1)}, bf16[25,64,256]{2,1,0:T(8,128)(2,1)S(1)}, u32[]{:S(2)}, u32[]{:S(2)}) collective-permute-start(bf16[25,64,256]{2,1,0:T(8,128)(2,1)S(1)} %get-tuple-element.89), channel_id=1, source_target_pairs={{0,1},{1,0},{2,3},{3,2},{4,5},{5,4},{6,7},{7,6},{8,9},{9,8},{10,11... | collective-permute-start | bytes 2457608 | tf_op jit(solution)/shard_map/ppermute | solution.py:374

commit v13 on v12

--- a/solution.py
+++ b/solution.py
@@ -325,6 +325,15 @@
         out[:, pl.ds(first, piece), :] = part[...].astype(F32)
 
 
+def add_kernel(*refs):
+    *parts, total, rounded = refs
+    value = parts[0][...]
+    for part in parts[1:]:
+        value = value + part[...].astype(F32)
+    total[...] = value
+    rounded[...] = value.astype(BF16)
+
+
 def call(kernel, args, outs, scratch=(), scalars=0, limit=24, stay=(), tokens=(), flops=0):
     whole = pl.BlockSpec(memory_space=pltpu.VMEM)
     small = pl.BlockSpec(memory_space=pltpu.SMEM)
@@ -496,18 +505,23 @@
         scalars=1,
         stay=tuple(range(1, 10 + 4 * len(feature_cuts))),
     )
-    for delta, part in enumerate(sent, 1):
-        kept = kept + exchanged(part, "atom", delta << cut_bits[0]).astype(F32)
+    def summed(kept, parts):
+        return call(
+            add_kernel, (kept, *parts), (held(*piece), plain(*piece, dtype=BF16)), limit=8, stay=(0,)
+        )
+
+    def plainly(kept, parts):
+        kept = functools.reduce(lambda total, part: total + part.astype(F32), parts, kept)
+        return kept, kept.astype(BF16)
+
+    arrived = [exchanged(part, "atom", delta << cut_bits[0]) for delta, part in enumerate(sent, 1)]
+    kept, rounded = summed(kept, arrived)
     rest = [bit for bit in reversed(range(count.bit_length() - 1)) if bit not in cut_bits]
     for at, bit in enumerate(rest):
-        also = 1 << rest[at - 1] if 0 < at == len(rest) - 1 else 0
-        arrived = exchanged(kept.astype(BF16), "atom", 1 << bit | also)
-        if bit == rest[-1]:
-            from_left, from_right, message_left, message_right, arrived = after(
-                (from_left, from_right, message_left, message_right, arrived), ()
-            )
-        kept = kept + arrived.astype(F32)
-    rounded = kept.astype(BF16)
+        final = 0 < at == len(rest) - 1
+        also = 1 << rest[at - 1] if final else 0
+        arrived = [exchanged(rounded, "atom", 1 << bit | also)]
+        kept, rounded = (summed if final else plainly)(kept, arrived)
     pieces = [rounded] + [exchanged(rounded, "atom", d << cut_bits[0]) for d in range(1, 4)]
     (grad_weights,) = call(
         gather_kernel,
@@ -517,7 +531,7 @@
         limit=8,
         flops=20 * 10**9,
     )
-    parts, tokens = [], ()
+    parts, tokens = [], (rounded,)
     for (start, stop), halo_qkv in zip(feature_cuts, (halo_a, halo_b)):
         size = stop - start
         mine, theirs, token = call(

time: 100 us -> 99.9 us (level)
    ppermute x15, waiting for transfers between devices: 26.8 us -> 20 us  [shifted(): return lax.ppermute(value, axis, pairs)]
    ppermute x8, waiting for transfers between devices: 7.55 us -> 13.6 us  [exchanged(): lax.ppermute(value, axis, [(source, source ^ offset) for source in range(...]
    pallas_call x8 -> x10, Pallas kernels: 25.6 us -> 26.3 us  [call(): pl.pallas_call(body, out_shape=tuple(outs), in_specs=[small] * scalars +...]
  transfers between devices with their start and end apart: 23 -> 23, of which waited for: 9 -> 10; matrix products, arithmetic and copies ran while one was open for 0% -> 0% of each run, Pallas kernels for 27% -> 28%
where the time goes in v13:
time: 99.9 us; the launch traced here: 99.6 us
  starting transfers between devices  33.8 us (34%)
  waiting for transfers between devices  33.6 us (34%)
  Pallas kernels  28.9 us (29%)
  local copies, waits for them, and re-layouts  2.41 us (2%)
    pallas_call x10, Pallas kernels, call(): pl.pallas_call(body, out_shape=tuple(outs), in_specs=[small] * scalars +...  26.3 us
    ppermute x15, starting transfers between devices, shifted(): return lax.ppermute(value, axis, pairs)  23.6 us
    ppermute x15, waiting for transfers between devices, shifted(): return lax.ppermute(value, axis, pairs)  20 us
    ppermute x8, waiting for transfers between devices, exchanged(): lax.ppermute(value, axis, [(source, source ^ offset) for source in range(...  13.6 us
    ppermute x8, starting transfers between devices, exchanged(): lax.ppermute(value, axis, [(source, source ^ offset) for source in range(...  10.2 us
    pallas_call x1, Pallas kernels, on_device(): pl.pallas_call(functools.partial(split_kernel, feature_cuts), out_shape=t...  2.54 us
    unnamed x12, local copies, waits for them, and re-layouts  2.41 us
  transfers between devices with their start and end apart: 23, of which 10 were waited for; matrix products, arithmetic and copies ran while one was open for 0% of the time, Pallas kernels for 28%

profile of v13, /device:TPU:0, one launch (start us, length us, event | category | flops | bytes accessed | tf_op | source)
XLA Modules:
  0.0 99.6 jit_solution(9651349006034184839)
XLA Ops:
  0.7 0.5 collective-permute-start
  1.2 2.5 %shard_map.85 = (bf16[24,64,128]{2,1,0:T(8,128)(2,1)}, bf16[24,64,128]{2,1,0:T(8,128)(2,1)}, bf16[25,64,128]{2,1,0:T(8,128)(2,1)}, bf16[25,64,128]{2,1,0:T(8,128)(2,1)}) custom-call(bf16[49,64,256]{2,1,0:T(8,128)(2,1)} %bitcast.15), custom_call_target="tpu_custom_call" | custom-call | tf_op jit(solution)/shard_map/pallas_call | solution.py:419
  3.7 2.7 %collective-permute-start.1 = (bf16[24,64,128]{2,1,0:T(8,128)(2,1)}, bf16[24,64,128]{2,1,0:T(8,128)(2,1)S(1)}, u32[]{:S(2)}, u32[]{:S(2)}) collective-permute-start(bf16[24,64,128]{2,1,0:T(8,128)(2,1)} %get-tuple-element.45), channel_id=1, source_target_pairs={{0,2},{2,4},{4,6},{6,8},{8,10},{10,12},{12,14},{14,16},{16,18},{18... | collective-permute-start | bytes 1179656 | tf_op jit(solution)/shard_map/ppermute | solution.py:383
  6.4 4.1 %collective-permute-start.2 = (bf16[24,64,128]{2,1,0:T(8,128)(2,1)}, bf16[24,64,128]{2,1,0:T(8,128)(2,1)S(1)}, u32[]{:S(2)}, u32[]{:S(2)}) collective-permute-start(bf16[24,64,128]{2,1,0:T(8,128)(2,1)} %get-tuple-element.46), channel_id=1, source_target_pairs={{0,30},{2,0},{4,2},{6,4},{8,6},{10,8},{12,10},{14,12},{16,14},{18,... | collective-permute-start | bytes 1179656 | tf_op jit(solution)/shard_map/ppermute | solution.py:383
  10.5 0.0 collective-permute-start.5
  10.5 5.6 %collective-permute-start.6 = (bf16[25,64,128]{2,1,0:T(8,128)(2,1)}, bf16[25,64,128]{2,1,0:T(8,128)(2,1)S(1)}, u32[]{:S(2)}, u32[]{:S(2)}) collective-permute-start(bf16[25,64,128]{2,1,0:T(8,128)(2,1)} %get-tuple-element.51), channel_id=1, source_target_pairs={{0,30},{2,0},{4,2},{6,4},{8,6},{10,8},{12,10},{14,12},{16,14},{18,... | collective-permute-start | bytes 1228808 | tf_op jit(solution)/shard_map/ppermute | solution.py:383
  16.1 0.1 pad_add_fusion.refs_0_
  16.2 0.0 collective-permute-done.refs_2_
  16.2 0.0 copy-start.1
  16.2 1.4 %copy-done.1 = bf16[64,49,256]{2,0,1:T(8,128)(2,1)S(1)} copy-done((bf16[64,49,256]{2,0,1:T(8,128)(2,1)S(1)}, bf16[64,49,256]{2,0,1:T(8,128)(2,1)}, u32[]{:S(2)}) %copy-start.1) | copy-done | bytes 1605656
  17.6 1.0 copy-done.4
  18.6 4.7 %shard_map.86 = (bf16[49,192,256]{2,1,0:T(8,128)(2,1)S(1)}, f32[8,256,256]{2,1,0:T(8,128)S(1)}, s32[2,3,128,128]{3,2,1,0:T(8,128)S(1)}, s32[16,256]{1,0:T(8,128)...) custom-call(s32[3]{0:T(128)S(1)} %pad_add_fusion.refs_0_, ...), custom_call_target="tpu_custom_call" | custom-call | flops 12000000000 | bytes 1024 | tf_op jit(solution)/shard_map/pallas_call | solution.py:349
  23.3 10.1 %collective-permute-done.1.refs_0_ = bf16[24,64,128]{2,1,0:T(8,128)(2,1)S(1)} collective-permute-done((bf16[24,64,128]{2,1,0:T(8,128)(2,1)}, bf16[24,64,128]{2,1,0:T(8,128)(2,1)S(1)}, u32[]{:S(2)}, u32[]{:S(2)}) %collective-permute-start.1) | collective-permute-done | bytes 393248 | tf_op jit(solution)/shard_map/ppermute | solution.py:383
  33.4 0.0 collective-permute-done.2.refs_1_
  33.4 0.0 collective-permute-start.3
  33.4 0.5 collective-permute-start.4
  33.9 1.2 %collective-permute-done.3.refs_1_.refs_4_ = bf16[24,64,128]{2,1,0:T(8,128)(2,1)S(1)} collective-permute-done((bf16[24,64,128]{2,1,0:T(8,128)(2,1)S(1)}, bf16[24,64,128]{2,1,0:T(8,128)(2,1)S(1)}, u32[]{:S(2)}, u32[]{:S(2)}) %collective-permute-start.3) | collective-permute-done | bytes 393248 | tf_op jit(solution)/shard_map/ppermute | solution.py:383
  35.1 0.6 collective-permute-done.4.refs_3_.refs_6_
  35.7 1.3 %shard_map.88 = (bf16[24,192,256]{2,1,0:T(8,128)(2,1)S(1)}, f32[8,2,128,128]{3,2,1,0:T(8,128)S(1)}, f32[8,128]{1,0:T(8,128)S(1)}) custom-call(bf16[24,64,128]{2,1,0:T(8,128)(2,1)S(1)} %get-tuple-element.48.refs_0_.refs_3_, bf16[24,64,128]{2,1,0:T(8,128)(2,1)S(1)} %collective-permute-done.3.refs_1_.refs_4_, ...), custom_call_target="tpu_custom_call" | custom-call | bytes 1024 | tf_op jit(solution)/shard_map/pallas_call | solution.py:349
  37.0 0.0 copy-start.2
  37.0 0.0 copy-start.3
  37.0 4.6 %collective-permute-done.5.refs_0_ = bf16[25,64,128]{2,1,0:T(8,128)(2,1)S(1)} collective-permute-done((bf16[25,64,128]{2,1,0:T(8,128)(2,1)}, bf16[25,64,128]{2,1,0:T(8,128)(2,1)S(1)}, u32[]{:S(2)}, u32[]{:S(2)}) %collective-permute-start.5) | collective-permute-done | bytes 409632 | tf_op jit(solution)/shard_map/ppermute | solution.py:383
  41.6 1.8 %collective-permute-done.6.refs_1_ = bf16[25,64,128]{2,1,0:T(8,128)(2,1)S(1)} collective-permute-done((bf16[25,64,128]{2,1,0:T(8,128)(2,1)}, bf16[25,64,128]{2,1,0:T(8,128)(2,1)S(1)}, u32[]{:S(2)}, u32[]{:S(2)}) %collective-permute-start.6) | collective-permute-done | bytes 409632 | tf_op jit(solution)/shard_map/ppermute | solution.py:383
  43.4 0.5 collective-permute-start.8
  44.0 1.5 %collective-permute-start.9 = (bf16[49,64,128]{2,1,0:T(8,128)(2,1)S(1)}, bf16[49,64,128]{2,1,0:T(8,128)(2,1)S(1)}, u32[]{:S(2)}, u32[]{:S(2)}) collective-permute-start(bf16[49,64,128]{2,1,0:T(8,128)(2,1)S(1)} %get-tuple-element.71), channel_id=1, source_target_pairs={{0,2},{2,4},{4,6},{6,8},{8,10},{10,12},{12,14},{14,16},{16,18},{18... | collective-permute-start | bytes 2408456 | tf_op jit(solution)/shard_map/ppermute | solution.py:383
  45.4 4.1 %collective-permute-start.10 = (bf16[49,64,128]{2,1,0:T(8,128)(2,1)S(1)}, bf16[49,64,128]{2,1,0:T(8,128)(2,1)S(1)}, u32[]{:S(2)}, u32[]{:S(2)}) collective-permute-start(bf16[49,64,128]{2,1,0:T(8,128)(2,1)S(1)} %get-tuple-element.72), channel_id=1, source_target_pairs={{0,30},{2,0},{4,2},{6,4},{8,6},{10,8},{12,10},{14,12},{16,14},{18,... | collective-permute-start | bytes 2408456 | tf_op jit(solution)/shard_map/ppermute | solution.py:383
  49.6 3.8 %shard_map.90 = (bf16[25,192,256]{2,1,0:T(8,128)(2,1)S(1)}, f32[4,16,256]{2,1,0:T(8,128)}, f32[176,128]{1,0:T(8,128)S(1)}, f32[176,128]{1,0:T(8,128)S(1)}) custom-call(bf16[25,64,128]{2,1,0:T(8,128)(2,1)S(1)} %get-tuple-element.55.refs_0_.refs_7_, bf16[25,64,128]{2,1,0:T(8,128)(2,1)S(1)} %collective-permute-done.7.refs_1_.refs_8_, ...), custom_call_target="tpu_custom_call" | custom-call | bytes 1024 | tf_op jit(solution)/shard_map/pallas_call | solution.py:349
  53.4 7.7 %shard_map.91 = (bf16[49,64,256]{2,1,0:T(8,128)(2,1)S(1)}, f32[49,64,256]{2,1,0:T(8,128)S(1)}, f32[49,64,256]{2,1,0:T(8,128)S(1)}, f32[21,16,128]{2,1,0:T(8,128)...) custom-call(s32[3]{0:T(128)S(1)} %pad_add_fusion.refs_0_, ...), custom_call_target="tpu_custom_call" | custom-call | bytes 1024 | tf_op jit(solution)/shard_map/pallas_call | solution.py:349
  61.2 0.1 collective-permute-start.13
  61.2 0.3 collective-permute-start.14
  61.5 3.2 %collective-permute-start.15 = (bf16[21,16,128]{2,1,0:T(8,128)(2,1)S(1)}, bf16[21,16,128]{2,1,0:T(8,128)(2,1)S(1)}, u32[]{:S(2)}, u32[]{:S(2)}) collective-permute-start(bf16[21,16,128]{2,1,0:T(8,128)(2,1)S(1)} %get-tuple-element.77), channel_id=1, source_target_pairs={{0,12},{2,14},{4,8},{6,10},{8,4},{10,6},{12,0},{14,2},{16,28},{18,... | collective-permute-start | bytes 258056 | tf_op jit(solution)/shard_map/ppermute | solution.py:388
  64.7 6.5 %collective-permute-done.13.refs_1_ = bf16[21,16,128]{2,1,0:T(8,128)(2,1)S(1)} collective-permute-done((bf16[21,16,128]{2,1,0:T(8,128)(2,1)S(1)}, bf16[21,16,128]{2,1,0:T(8,128)(2,1)S(1)}, u32[]{:S(2)}, u32[]{:S(2)}) %collective-permute-start.13) | collective-permute-done | bytes 86048 | tf_op jit(solution)/shard_map/ppermute | solution.py:388
  71.3 1.9 %collective-permute-start.16 = (bf16[21,16,128]{2,1,0:T(8,128)(2,1)S(1)}, bf16[21,16,128]{2,1,0:T(8,128)(2,1)S(1)}, u32[]{:S(2)}, u32[]{:S(2)}) collective-permute-start(bf16[21,16,128]{2,1,0:T(8,128)(2,1)S(1)} %get-tuple-element.79), channel_id=1, source_target_pairs={{0,16},{2,18},{4,20},{6,22},{8,24},{10,26},{12,28},{14,30},{16,0},... | collective-permute-start | bytes 258056 | tf_op jit(solution)/shard_map/ppermute | solution.py:388
  73.2 3.5 %collective-permute-start.12 = (f32[176,128]{1,0:T(8,128)S(1)}, f32[176,128]{1,0:T(8,128)S(1)}, u32[]{:S(2)}, u32[]{:S(2)}) collective-permute-start(f32[176,128]{1,0:T(8,128)S(1)} %get-tuple-element.64.refs_16_), channel_id=1, source_target_pairs={{0,30},{2,0},{4,2},{6,4},{8,6},{10,8},{12,10},{14,12},{16,14},{18,... | collective-permute-start | bytes 270344 | tf_op jit(solution)/shard_map/ppermute | solution.py:383
  76.7 0.0 collective-permute-start.11
  76.7 1.0 %collective-permute-done.16 = bf16[21,16,128]{2,1,0:T(8,128)(2,1)S(1)} collective-permute-done((bf16[21,16,128]{2,1,0:T(8,128)(2,1)S(1)}, bf16[21,16,128]{2,1,0:T(8,128)(2,1)S(1)}, u32[]{:S(2)}, u32[]{:S(2)}) %collective-permute-start.16) | collective-permute-done | bytes 86048 | tf_op jit(solution)/shard_map/ppermute | solution.py:388
  77.7 1.3 %collective-permute-start.17 = (bf16[21,16,128]{2,1,0:T(8,128)(2,1)S(1)}, bf16[21,16,128]{2,1,0:T(8,128)(2,1)S(1)}, u32[]{:S(2)}, u32[]{:S(2)}) collective-permute-start(bf16[21,16,128]{2,1,0:T(8,128)(2,1)S(1)} %get-tuple-element.87), channel_id=1, source_target_pairs={{0,18},{2,16},{4,22},{6,20},{8,26},{10,24},{12,30},{14,28},{16,2},... | collective-permute-start | bytes 258056 | tf_op jit(solution)/shard_map/ppermute | solution.py:388
  79.0 6.1 %collective-permute-done.17.refs_1_ = bf16[21,16,128]{2,1,0:T(8,128)(2,1)S(1)} collective-permute-done((bf16[21,16,128]{2,1,0:T(8,128)(2,1)S(1)}, bf16[21,16,128]{2,1,0:T(8,128)(2,1)S(1)}, u32[]{:S(2)}, u32[]{:S(2)}) %collective-permute-start.17) | collective-permute-done | bytes 86048 | tf_op jit(solution)/shard_map/ppermute | solution.py:388
  85.1 0.7 shard_map.94
  85.8 1.2 %collective-permute-done.12.refs_7_ = f32[176,128]{1,0:T(8,128)S(1)} collective-permute-done((f32[176,128]{1,0:T(8,128)S(1)}, f32[176,128]{1,0:T(8,128)S(1)}, u32[]{:S(2)}, u32[]{:S(2)}) %collective-permute-start.12) | collective-permute-done | bytes 90144 | tf_op jit(solution)/shard_map/ppermute | solution.py:383
  87.0 3.4 %collective-permute-start.22 = (bf16[21,16,128]{2,1,0:T(8,128)(2,1)S(1)}, bf16[21,16,128]{2,1,0:T(8,128)(2,1)S(1)}, u32[]{:S(2)}, u32[]{:S(2)}) collective-permute-start(bf16[21,16,128]{2,1,0:T(8,128)(2,1)S(1)} %get-tuple-element.80.refs_9_.refs_1_), channel_id=1, source_target_pairs={{0,12},{2,14},{4,8},{6,10},{8,4},{10,6},{12,0},{14,2},{16,28},{18,... | collective-permute-start | bytes 258056 | tf_op jit(solution)/shard_map/ppermute | solution.py:388
  90.4 2.6 %shard_map.95 = (f32[24,64,256]{2,1,0:T(8,128)S(1)}, bf16[24,64,256]{2,1,0:T(8,128)(2,1)S(1)}, f32[8,128]{1,0:T(8,128)S(1)}) custom-call(bf16[49,64,256]{2,1,0:T(8,128)(2,1)S(1)} %get-tuple-element.66.refs_0_, f32[49,64,256]{2,1,0:T(8,128)S(1)} %get-tuple-element.67.refs_1_, f32[49,64,256]{2,1,0:T(8,128)S(1)} %get-tuple-element.68.refs_2_, ...), custom_call_target="tpu_custom_call" | custom-call | bytes 1024 | tf_op jit(solution)/shard_map/pallas_call | solution.py:349
  93.0 0.1 collective-permute-start.18
  93.1 2.6 %shard_map.96 = (f32[25,64,256]{2,1,0:T(8,128)S(1)}, bf16[25,64,256]{2,1,0:T(8,128)(2,1)S(1)}, f32[8,128]{1,0:T(8,128)}) custom-call(bf16[49,64,256]{2,1,0:T(8,128)(2,1)S(1)} %get-tuple-element.66.refs_0_, f32[49,64,256]{2,1,0:T(8,128)S(1)} %get-tuple-element.67.refs_1_, f32[49,64,256]{2,1,0:T(8,128)S(1)} %get-tuple-element.68.refs_2_, ...), custom_call_target="tpu_custom_call" | custom-call | bytes 1024 | tf_op jit(solution)/shard_map/pallas_call | solution.py:349
  95.6 0.6 collective-permute-start.20
  96.2 1.4 %shard_map.98 = f32[21,64,128]{2,1,0:T(8,128)} custom-call(s32[3]{0:T(128)S(1)} %pad_add_fusion.refs_0_, bf16[21,16,128]{2,1,0:T(8,128)(2,1)S(1)} %get-tuple-element.80.refs_9_.refs_1_, bf16[21,16,128]{2,1,0:T(8,128)(2,1)S(1)} %collective-permute-done.21.refs_2_, bf16[21,16,128]{2,1,0:T(8,128)(2,1)S(1)} %collective-permute-done.19.refs_10_.refs_3_, ...), custom_call_target="tpu_custom_call" | custom-call | flops 20000000000 | bytes 1024 | tf_op jit(solution)/shard_map/pallas_call | solution.py:349
  97.6 0.5 collective-permute-done.20.refs_3_
  98.1 1.5 %shard_map.97 = bf16[49,64,256]{2,1,0:T(8,128)(2,1)} custom-call(f32[24,64,256]{2,1,0:T(8,128)S(1)} %get-tuple-element.81.refs_0_, bf16[24,64,256]{2,1,0:T(8,128)(2,1)S(1)} %collective-permute-done.18.refs_1_, f32[25,64,256]{2,1,0:T(8,128)S(1)} %get-tuple-element.84.refs_2_, bf16[25,64,256]{2,1,0:T(8,128)(2,1)S(1)} %collective-permute-done.20.refs_3_), custom_call_target="tpu_custom_call" | custom-call | bytes 1024 | tf_op jit(solution)/shard_map/pallas_call | solution.py:349
  (26 shorter events, 0.1 us)
Async XLA Ops:
  0.6 15.5 %copy-start.5 = (s32[16,256]{1,0:T(8,128)S(1)}, s32[16,256]{1,0:T(8,128)}, u32[]{:S(2)}) copy-start(s32[16,256]{1,0:T(8,128)} %refs_5_.1) | copy-start | bytes 49156
  0.6 15.5 %copy-start = (bf16[64,49,256]{2,0,1:T(8,128)(2,1)S(1)}, bf16[64,49,256]{2,0,1:T(8,128)(2,1)}, u32[]{:S(2)}) copy-start(bf16[64,49,256]{2,0,1:T(8,128)(2,1)} %param.8) | copy-start | bytes 4816900
  0.7 15.5 %collective-permute-start = (bf16[49,64,256]{2,1,0:T(8,128)(2,1)}, bf16[49,64,256]{2,1,0:T(8,128)(2,1)}, u32[]{:S(2)}, u32[]{:S(2)}) collective-permute-start(bf16[49,64,256]{2,1,0:T(8,128)(2,1)} %bitcast.14), channel_id=1, source_target_pairs={{0,1},{1,0},{2,3},{3,2},{4,5},{5,4},{6,7},{7,6},{8,9},{9,8},{10,11... | collective-permute-start | bytes 4816904 | tf_op jit(solution)/shard_map/ppermute | solution.py:383
  3.7 29.7 %collective-permute-start.1 = (bf16[24,64,128]{2,1,0:T(8,128)(2,1)}, bf16[24,64,128]{2,1,0:T(8,128)(2,1)S(1)}, u32[]{:S(2)}, u32[]{:S(2)}) collective-permute-start(bf16[24,64,128]{2,1,0:T(8,128)(2,1)} %get-tuple-element.45), channel_id=1, source_target_pairs={{0,2},{2,4},{4,6},{6,8},{8,10},{10,12},{12,14},{14,16},{16,18},{18... | collective-permute-start | bytes 1179656 | tf_op jit(solution)/shard_map/ppermute | solution.py:383
  6.4 27.0 %collective-permute-start.2 = (bf16[24,64,128]{2,1,0:T(8,128)(2,1)}, bf16[24,64,128]{2,1,0:T(8,128)(2,1)S(1)}, u32[]{:S(2)}, u32[]{:S(2)}) collective-permute-start(bf16[24,64,128]{2,1,0:T(8,128)(2,1)} %get-tuple-element.46), channel_id=1, source_target_pairs={{0,30},{2,0},{4,2},{6,4},{8,6},{10,8},{12,10},{14,12},{16,14},{18,... | collective-permute-start | bytes 1179656 | tf_op jit(solution)/shard_map/ppermute | solution.py:383
  10.5 31.1 %collective-permute-start.5 = (bf16[25,64,128]{2,1,0:T(8,128)(2,1)}, bf16[25,64,128]{2,1,0:T(8,128)(2,1)S(1)}, u32[]{:S(2)}, u32[]{:S(2)}) collective-permute-start(bf16[25,64,128]{2,1,0:T(8,128)(2,1)} %get-tuple-element.50), channel_id=1, source_target_pairs={{0,2},{2,4},{4,6},{6,8},{8,10},{10,12},{12,14},{14,16},{16,18},{18... | collective-permute-start | bytes 1228808 | tf_op jit(solution)/shard_map/ppermute | solution.py:383
  10.5 33.0 %collective-permute-start.6 = (bf16[25,64,128]{2,1,0:T(8,128)(2,1)}, bf16[25,64,128]{2,1,0:T(8,128)(2,1)S(1)}, u32[]{:S(2)}, u32[]{:S(2)}) collective-permute-start(bf16[25,64,128]{2,1,0:T(8,128)(2,1)} %get-tuple-element.51), channel_id=1, source_target_pairs={{0,30},{2,0},{4,2},{6,4},{8,6},{10,8},{12,10},{14,12},{16,14},{18,... | collective-permute-start | bytes 1228808 | tf_op jit(solution)/shard_map/ppermute | solution.py:383
  16.2 1.4 %copy-start.1 = (bf16[64,49,256]{2,0,1:T(8,128)(2,1)S(1)}, bf16[64,49,256]{2,0,1:T(8,128)(2,1)}, u32[]{:S(2)}) copy-start(bf16[64,49,256]{2,0,1:T(8,128)(2,1)} %param.6) | copy-start | bytes 4816900
  17.6 1.0 copy-start.4
  33.4 1.7 %collective-permute-start.3 = (bf16[24,64,128]{2,1,0:T(8,128)(2,1)S(1)}, bf16[24,64,128]{2,1,0:T(8,128)(2,1)S(1)}, u32[]{:S(2)}, u32[]{:S(2)}) collective-permute-start(bf16[24,64,128]{2,1,0:T(8,128)(2,1)S(1)} %get-tuple-element.48.refs_0_.refs_3_), channel_id=1, source_target_pairs={{0,1},{1,0},{2,3},{3,2},{4,5},{5,4},{6,7},{7,6},{8,9},{9,8},{10,11... | collective-permute-start | bytes 1179656 | tf_op jit(solution)/shard_map/ppermute | solution.py:383
  33.4 2.3 %collective-permute-start.4 = (bf16[24,64,128]{2,1,0:T(8,128)(2,1)S(1)}, bf16[24,64,128]{2,1,0:T(8,128)(2,1)S(1)}, u32[]{:S(2)}, u32[]{:S(2)}) collective-permute-start(bf16[24,64,128]{2,1,0:T(8,128)(2,1)S(1)} %get-tuple-element.49.refs_2_.refs_5_), channel_id=1, source_target_pairs={{0,1},{1,0},{2,3},{3,2},{4,5},{5,4},{6,7},{7,6},{8,9},{9,8},{10,11... | collective-permute-start | bytes 1179656 | tf_op jit(solution)/shard_map/ppermute | solution.py:383
  37.0 12.6 %copy-start.2 = (f32[4,16,256]{2,1,0:T(8,128)S(1)}, f32[4,16,256]{2,1,0:T(8,128)}, u32[]{:S(2)}) copy-start(f32[4,16,256]{2,1,0:T(8,128)} %refs_9_.1) | copy-start | bytes 196612
  37.0 12.6 %copy-start.3 = (s32[16,256]{1,0:T(8,128)S(1)}, s32[16,256]{1,0:T(8,128)}, u32[]{:S(2)}) copy-start(s32[16,256]{1,0:T(8,128)} %refs_10_.1) | copy-start | bytes 49156
  43.4 6.1 %collective-permute-start.7 = (bf16[25,64,128]{2,1,0:T(8,128)(2,1)S(1)}, bf16[25,64,128]{2,1,0:T(8,128)(2,1)S(1)}, u32[]{:S(2)}, u32[]{:S(2)}) collective-permute-start(bf16[25,64,128]{2,1,0:T(8,128)(2,1)S(1)} %get-tuple-element.55.refs_0_.refs_7_), channel_id=1, source_target_pairs={{0,1},{1,0},{2,3},{3,2},{4,5},{5,4},{6,7},{7,6},{8,9},{9,8},{10,11... | collective-permute-start | bytes 1228808 | tf_op jit(solution)/shard_map/ppermute | solution.py:383
  43.4 6.1 %collective-permute-start.8 = (bf16[25,64,128]{2,1,0:T(8,128)(2,1)S(1)}, bf16[25,64,128]{2,1,0:T(8,128)(2,1)S(1)}, u32[]{:S(2)}, u32[]{:S(2)}) collective-permute-start(bf16[25,64,128]{2,1,0:T(8,128)(2,1)S(1)} %get-tuple-element.56.refs_2_.refs_9_), channel_id=1, source_target_pairs={{0,1},{1,0},{2,3},{3,2},{4,5},{5,4},{6,7},{7,6},{8,9},{9,8},{10,11... | collective-permute-start | bytes 1228808 | tf_op jit(solution)/shard_map/ppermute | solution.py:383
  44.0 46.4 %collective-permute-start.9 = (bf16[49,64,128]{2,1,0:T(8,128)(2,1)S(1)}, bf16[49,64,128]{2,1,0:T(8,128)(2,1)S(1)}, u32[]{:S(2)}, u32[]{:S(2)}) collective-permute-start(bf16[49,64,128]{2,1,0:T(8,128)(2,1)S(1)} %get-tuple-element.71), channel_id=1, source_target_pairs={{0,2},{2,4},{4,6},{6,8},{8,10},{10,12},{12,14},{14,16},{16,18},{18... | collective-permute-start | bytes 2408456 | tf_op jit(solution)/shard_map/ppermute | solution.py:383
  45.4 45.0 %collective-permute-start.10 = (bf16[49,64,128]{2,1,0:T(8,128)(2,1)S(1)}, bf16[49,64,128]{2,1,0:T(8,128)(2,1)S(1)}, u32[]{:S(2)}, u32[]{:S(2)}) collective-permute-start(bf16[49,64,128]{2,1,0:T(8,128)(2,1)S(1)} %get-tuple-element.72), channel_id=1, source_target_pairs={{0,30},{2,0},{4,2},{6,4},{8,6},{10,8},{12,10},{14,12},{16,14},{18,... | collective-permute-start | bytes 2408456 | tf_op jit(solution)/shard_map/ppermute | solution.py:383
  61.2 10.1 %collective-permute-start.13 = (bf16[21,16,128]{2,1,0:T(8,128)(2,1)S(1)}, bf16[21,16,128]{2,1,0:T(8,128)(2,1)S(1)}, u32[]{:S(2)}, u32[]{:S(2)}) collective-permute-start(bf16[21,16,128]{2,1,0:T(8,128)(2,1)S(1)} %get-tuple-element.75), channel_id=1, source_target_pairs={{0,4},{2,6},{4,0},{6,2},{8,12},{10,14},{12,8},{14,10},{16,20},{18,... | collective-permute-start | bytes 258056 | tf_op jit(solution)/shard_map/ppermute | solution.py:388
  61.2 10.0 %collective-permute-start.14 = (bf16[21,16,128]{2,1,0:T(8,128)(2,1)S(1)}, bf16[21,16,128]{2,1,0:T(8,128)(2,1)S(1)}, u32[]{:S(2)}, u32[]{:S(2)}) collective-permute-start(bf16[21,16,128]{2,1,0:T(8,128)(2,1)S(1)} %get-tuple-element.76), channel_id=1, source_target_pairs={{0,8},{2,10},{4,12},{6,14},{8,0},{10,2},{12,4},{14,6},{16,24},{18,... | collective-permute-start | bytes 258056 | tf_op jit(solution)/shard_map/ppermute | solution.py:388
  61.5 9.7 %collective-permute-start.15 = (bf16[21,16,128]{2,1,0:T(8,128)(2,1)S(1)}, bf16[21,16,128]{2,1,0:T(8,128)(2,1)S(1)}, u32[]{:S(2)}, u32[]{:S(2)}) collective-permute-start(bf16[21,16,128]{2,1,0:T(8,128)(2,1)S(1)} %get-tuple-element.77), channel_id=1, source_target_pairs={{0,12},{2,14},{4,8},{6,10},{8,4},{10,6},{12,0},{14,2},{16,28},{18,... | collective-permute-start | bytes 258056 | tf_op jit(solution)/shard_map/ppermute | solution.py:388
  71.3 6.4 %collective-permute-start.16 = (bf16[21,16,128]{2,1,0:T(8,128)(2,1)S(1)}, bf16[21,16,128]{2,1,0:T(8,128)(2,1)S(1)}, u32[]{:S(2)}, u32[]{:S(2)}) collective-permute-start(bf16[21,16,128]{2,1,0:T(8,128)(2,1)S(1)} %get-tuple-element.79), channel_id=1, source_target_pairs={{0,16},{2,18},{4,20},{6,22},{8,24},{10,26},{12,28},{14,30},{16,0},... | collective-permute-start | bytes 258056 | tf_op jit(solution)/shard_map/ppermute | solution.py:388
  73.2 13.7 %collective-permute-start.12 = (f32[176,128]{1,0:T(8,128)S(1)}, f32[176,128]{1,0:T(8,128)S(1)}, u32[]{:S(2)}, u32[]{:S(2)}) collective-permute-start(f32[176,128]{1,0:T(8,128)S(1)} %get-tuple-element.64.refs_16_), channel_id=1, source_target_pairs={{0,30},{2,0},{4,2},{6,4},{8,6},{10,8},{12,10},{14,12},{16,14},{18,... | collective-permute-start | bytes 270344 | tf_op jit(solution)/shard_map/ppermute | solution.py:383
  76.7 13.7 %collective-permute-start.11 = (f32[176,128]{1,0:T(8,128)S(1)}, f32[176,128]{1,0:T(8,128)S(1)}, u32[]{:S(2)}, u32[]{:S(2)}) collective-permute-start(f32[176,128]{1,0:T(8,128)S(1)} %get-tuple-element.65.refs_17_), channel_id=1, source_target_pairs={{0,2},{2,4},{4,6},{6,8},{8,10},{10,12},{12,14},{14,16},{16,18},{18... | collective-permute-start | bytes 270344 | tf_op jit(solution)/shard_map/ppermute | solution.py:383
  77.7 7.3 %collective-permute-start.17 = (bf16[21,16,128]{2,1,0:T(8,128)(2,1)S(1)}, bf16[21,16,128]{2,1,0:T(8,128)(2,1)S(1)}, u32[]{:S(2)}, u32[]{:S(2)}) collective-permute-start(bf16[21,16,128]{2,1,0:T(8,128)(2,1)S(1)} %get-tuple-element.87), channel_id=1, source_target_pairs={{0,18},{2,16},{4,22},{6,20},{8,26},{10,24},{12,30},{14,28},{16,2},... | collective-permute-start | bytes 258056 | tf_op jit(solution)/shard_map/ppermute | solution.py:388
  85.8 7.3 %collective-permute-start.19 = (bf16[21,16,128]{2,1,0:T(8,128)(2,1)S(1)}, bf16[21,16,128]{2,1,0:T(8,128)(2,1)S(1)}, u32[]{:S(2)}, u32[]{:S(2)}) collective-permute-start(bf16[21,16,128]{2,1,0:T(8,128)(2,1)S(1)} %get-tuple-element.80.refs_9_.refs_1_), channel_id=1, source_target_pairs={{0,8},{2,10},{4,12},{6,14},{8,0},{10,2},{12,4},{14,6},{16,24},{18,... | collective-permute-start | bytes 258056 | tf_op jit(solution)/shard_map/ppermute | solution.py:388
  87.0 9.2 %collective-permute-start.22 = (bf16[21,16,128]{2,1,0:T(8,128)(2,1)S(1)}, bf16[21,16,128]{2,1,0:T(8,128)(2,1)S(1)}, u32[]{:S(2)}, u32[]{:S(2)}) collective-permute-start(bf16[21,16,128]{2,1,0:T(8,128)(2,1)S(1)} %get-tuple-element.80.refs_9_.refs_1_), channel_id=1, source_target_pairs={{0,12},{2,14},{4,8},{6,10},{8,4},{10,6},{12,0},{14,2},{16,28},{18,... | collective-permute-start | bytes 258056 | tf_op jit(solution)/shard_map/ppermute | solution.py:388
  90.4 5.8 %collective-permute-start.21 = (bf16[21,16,128]{2,1,0:T(8,128)(2,1)S(1)}, bf16[21,16,128]{2,1,0:T(8,128)(2,1)S(1)}, u32[]{:S(2)}, u32[]{:S(2)}) collective-permute-start(bf16[21,16,128]{2,1,0:T(8,128)(2,1)S(1)} %get-tuple-element.80.refs_9_.refs_1_), channel_id=1, source_target_pairs={{0,4},{2,6},{4,0},{6,2},{8,12},{10,14},{12,8},{14,10},{16,20},{18,... | collective-permute-start | bytes 258056 | tf_op jit(solution)/shard_map/ppermute | solution.py:388
  93.0 4.7 %collective-permute-start.18 = (bf16[24,64,256]{2,1,0:T(8,128)(2,1)S(1)}, bf16[24,64,256]{2,1,0:T(8,128)(2,1)S(1)}, u32[]{:S(2)}, u32[]{:S(2)}) collective-permute-start(bf16[24,64,256]{2,1,0:T(8,128)(2,1)S(1)} %get-tuple-element.82), channel_id=1, source_target_pairs={{0,1},{1,0},{2,3},{3,2},{4,5},{5,4},{6,7},{7,6},{8,9},{9,8},{10,11... | collective-permute-start | bytes 2359304 | tf_op jit(solution)/shard_map/ppermute | solution.py:383
  95.6 2.5 %collective-permute-start.20 = (bf16[25,64,256]{2,1,0:T(8,128)(2,1)S(1)}, bf16[25,64,256]{2,1,0:T(8,128)(2,1)S(1)}, u32[]{:S(2)}, u32[]{:S(2)}) collective-permute-start(bf16[25,64,256]{2,1,0:T(8,128)(2,1)S(1)} %get-tuple-element.85), channel_id=1, source_target_pairs={{0,1},{1,0},{2,3},{3,2},{4,5},{5,4},{6,7},{7,6},{8,9},{9,8},{10,11... | collective-permute-start | bytes 2457608 | tf_op jit(solution)/shard_map/ppermute | solution.py:383

commit v14 on v13

--- a/solution.py
+++ b/solution.py
@@ -309,20 +309,17 @@
         theirs[comp] = total[chan_local:].astype(BF16)
 
 
-def finish_kernel(*refs):
-    out, start = refs[-1], 0
-    for mine, theirs in zip(refs[:-1:2], refs[1:-1:2]):
+def finish_kernel(place, part_0, part_1, part_2, part_3, *refs):
+    *sides, out, weight_out = refs
+    piece = part_0.shape[1]
+    for delta, part in enumerate((part_0, part_1, part_2, part_3)):
+        first = pl.multiple_of((place[2] ^ delta) * piece, piece)
+        weight_out[:, pl.ds(first, piece), :] = part[...].astype(F32)
+    start = 0
+    for mine, theirs in zip(sides[::2], sides[1::2]):
         stop = start + mine.shape[0]
         out[start:stop] = (mine[...] + theirs[...].astype(F32)).astype(BF16)
         start = stop
-
-
-def gather_kernel(place, part_0, part_1, part_2, part_3, out):
-    piece = part_0.shape[1]
-    spot = place[2]
-    for delta, part in enumerate((part_0, part_1, part_2, part_3)):
-        first = pl.multiple_of((spot ^ delta) * piece, piece)
-        out[:, pl.ds(first, piece), :] = part[...].astype(F32)
 
 
 def add_kernel(*refs):
@@ -523,14 +520,6 @@
         arrived = [exchanged(rounded, "atom", 1 << bit | also)]
         kept, rounded = (summed if final else plainly)(kept, arrived)
     pieces = [rounded] + [exchanged(rounded, "atom", d << cut_bits[0]) for d in range(1, 4)]
-    (grad_weights,) = call(
-        gather_kernel,
-        (place, *pieces),
-        (plain(3 * (LMAX + 1), chan_local, channels),),
-        scalars=1,
-        limit=8,
-        flops=20 * 10**9,
-    )
     parts, tokens = [], (rounded,)
     for (start, stop), halo_qkv in zip(feature_cuts, (halo_a, halo_b)):
         size = stop - start
@@ -549,13 +538,18 @@
             tokens=tokens,
         )
         parts += [mine, shifted(theirs, "chan", 1)]
-        tokens = (token, pieces[2])
-    (out,) = call(
+        tokens = (token, *pieces[1:])
+    out, grad_weights = call(
         finish_kernel,
-        parts,
-        (plain(comps, chan_local, atoms_dev, dtype=BF16),),
+        (place, *pieces, *parts),
+        (
+            plain(comps, chan_local, atoms_dev, dtype=BF16),
+            plain(3 * (LMAX + 1), chan_local, channels),
+        ),
+        scalars=1,
         limit=8,
-        stay=tuple(range(len(parts))),
+        stay=tuple(range(5, 5 + len(parts))),
+        flops=0,
     )
     grad_features = jnp.transpose(out, (1, 0, 2))
     grad_weights = grad_weights.reshape(3, LMAX + 1, chan_local, channels)

time: 99.9 us -> 103 us (1.031)
  waiting for transfers between devices: 33.6 us -> 36.6 us
  starting transfers between devices: 33.8 us -> 35.1 us
    ppermute x8, waiting for transfers between devices: 13.6 us -> 15.3 us  [exchanged(): lax.ppermute(value, axis, [(source, source ^ offset) for source in range(...]
    ppermute x8, starting transfers between devices: 10.2 us -> 11.6 us  [exchanged(): lax.ppermute(value, axis, [(source, source ^ offset) for source in range(...]
    ppermute x15, waiting for transfers between devices: 20 us -> 21.3 us  [shifted(): return lax.ppermute(value, axis, pairs)]
    pallas_call x10 -> x9, Pallas kernels: 26.3 us -> 25.6 us  [call(): pl.pallas_call(body, out_shape=tuple(outs), in_specs=[small] * scalars +...]
  transfers between devices with their start and end apart: 23 -> 23, of which waited for: 10 -> 11; matrix products, arithmetic and copies ran while one was open for 0% -> 0% of each run, Pallas kernels for 28% -> 23%
where the time goes in v14:
time: 103 us
  waiting for transfers between devices  36.6 us (36%)
  starting transfers between devices  35.1 us (34%)
  Pallas kernels  28.2 us (27%)
  local copies, waits for them, and re-layouts  2.41 us (2%)
    pallas_call x9, Pallas kernels, call(): pl.pallas_call(body, out_shape=tuple(outs), in_specs=[small] * scalars +...  25.6 us
    ppermute x15, starting transfers between devices, shifted(): return lax.ppermute(value, axis, pairs)  23.5 us
    ppermute x15, waiting for transfers between devices, shifted(): return lax.ppermute(value, axis, pairs)  21.3 us
    ppermute x8, waiting for transfers between devices, exchanged(): lax.ppermute(value, axis, [(source, source ^ offset) for source in range(...  15.3 us
    ppermute x8, starting transfers between devices, exchanged(): lax.ppermute(value, axis, [(source, source ^ offset) for source in range(...  11.6 us
    pallas_call x1, Pallas kernels, on_device(): pl.pallas_call(functools.partial(split_kernel, feature_cuts), out_shape=t...  2.54 us
    unnamed x12, local copies, waits for them, and re-layouts  2.41 us
  transfers between devices with their start and end apart: 23, of which 11 were waited for; matrix products, arithmetic and copies ran while one was open for 0% of the time, Pallas kernels for 23%

profile of v14, /device:TPU:0, one launch (start us, length us, event | category | flops | bytes accessed | tf_op | source)
XLA Modules:
  0.0 103.2 jit_solution(10927505816624085561)
XLA Ops:
  0.7 0.5 collective-permute-start
  1.2 2.5 %shard_map.85 = (bf16[24,64,128]{2,1,0:T(8,128)(2,1)}, bf16[24,64,128]{2,1,0:T(8,128)(2,1)}, bf16[25,64,128]{2,1,0:T(8,128)(2,1)}, bf16[25,64,128]{2,1,0:T(8,128)(2,1)}) custom-call(bf16[49,64,256]{2,1,0:T(8,128)(2,1)} %bitcast.15), custom_call_target="tpu_custom_call" | custom-call | tf_op jit(solution)/shard_map/pallas_call | solution.py:416
  3.7 2.7 %collective-permute-start.1 = (bf16[24,64,128]{2,1,0:T(8,128)(2,1)}, bf16[24,64,128]{2,1,0:T(8,128)(2,1)S(1)}, u32[]{:S(2)}, u32[]{:S(2)}) collective-permute-start(bf16[24,64,128]{2,1,0:T(8,128)(2,1)} %get-tuple-element.47), channel_id=1, source_target_pairs={{0,2},{2,4},{4,6},{6,8},{8,10},{10,12},{12,14},{14,16},{16,18},{18... | collective-permute-start | bytes 1179656 | tf_op jit(solution)/shard_map/ppermute | solution.py:380
  6.4 4.1 %collective-permute-start.2 = (bf16[24,64,128]{2,1,0:T(8,128)(2,1)}, bf16[24,64,128]{2,1,0:T(8,128)(2,1)S(1)}, u32[]{:S(2)}, u32[]{:S(2)}) collective-permute-start(bf16[24,64,128]{2,1,0:T(8,128)(2,1)} %get-tuple-element.48), channel_id=1, source_target_pairs={{0,30},{2,0},{4,2},{6,4},{8,6},{10,8},{12,10},{14,12},{16,14},{18,... | collective-permute-start | bytes 1179656 | tf_op jit(solution)/shard_map/ppermute | solution.py:380
  10.5 0.0 collective-permute-start.5
  10.5 5.6 %collective-permute-start.6 = (bf16[25,64,128]{2,1,0:T(8,128)(2,1)}, bf16[25,64,128]{2,1,0:T(8,128)(2,1)S(1)}, u32[]{:S(2)}, u32[]{:S(2)}) collective-permute-start(bf16[25,64,128]{2,1,0:T(8,128)(2,1)} %get-tuple-element.53), channel_id=1, source_target_pairs={{0,30},{2,0},{4,2},{6,4},{8,6},{10,8},{12,10},{14,12},{16,14},{18,... | collective-permute-start | bytes 1228808 | tf_op jit(solution)/shard_map/ppermute | solution.py:380
  16.1 0.1 pad_add_fusion.refs_0_
  16.2 0.0 collective-permute-done.refs_2_
  16.2 0.0 copy-start.1
  16.2 1.4 %copy-done.1 = bf16[64,49,256]{2,0,1:T(8,128)(2,1)S(1)} copy-done((bf16[64,49,256]{2,0,1:T(8,128)(2,1)S(1)}, bf16[64,49,256]{2,0,1:T(8,128)(2,1)}, u32[]{:S(2)}) %copy-start.1) | copy-done | bytes 1605656
  17.6 1.0 copy-done.4
  18.6 4.7 %shard_map.86 = (bf16[49,192,256]{2,1,0:T(8,128)(2,1)S(1)}, f32[8,256,256]{2,1,0:T(8,128)S(1)}, s32[2,3,128,128]{3,2,1,0:T(8,128)S(1)}, s32[16,256]{1,0:T(8,128)...) custom-call(s32[3]{0:T(128)S(1)} %pad_add_fusion.refs_0_, ...), custom_call_target="tpu_custom_call" | custom-call | flops 12000000000 | bytes 1024 | tf_op jit(solution)/shard_map/pallas_call | solution.py:346
  23.3 10.1 %collective-permute-done.1.refs_0_ = bf16[24,64,128]{2,1,0:T(8,128)(2,1)S(1)} collective-permute-done((bf16[24,64,128]{2,1,0:T(8,128)(2,1)}, bf16[24,64,128]{2,1,0:T(8,128)(2,1)S(1)}, u32[]{:S(2)}, u32[]{:S(2)}) %collective-permute-start.1) | collective-permute-done | bytes 393248 | tf_op jit(solution)/shard_map/ppermute | solution.py:380
  33.4 0.5 collective-permute-start.4
  33.9 1.2 %collective-permute-done.3.refs_1_.refs_4_ = bf16[24,64,128]{2,1,0:T(8,128)(2,1)S(1)} collective-permute-done((bf16[24,64,128]{2,1,0:T(8,128)(2,1)S(1)}, bf16[24,64,128]{2,1,0:T(8,128)(2,1)S(1)}, u32[]{:S(2)}, u32[]{:S(2)}) %collective-permute-start.3) | collective-permute-done | bytes 393248 | tf_op jit(solution)/shard_map/ppermute | solution.py:380
  35.1 0.6 collective-permute-done.4.refs_3_.refs_6_
  35.7 1.3 %shard_map.88 = (bf16[24,192,256]{2,1,0:T(8,128)(2,1)S(1)}, f32[8,2,128,128]{3,2,1,0:T(8,128)S(1)}, f32[8,128]{1,0:T(8,128)S(1)}) custom-call(bf16[24,64,128]{2,1,0:T(8,128)(2,1)S(1)} %get-tuple-element.50.refs_0_.refs_3_, bf16[24,64,128]{2,1,0:T(8,128)(2,1)S(1)} %collective-permute-done.3.refs_1_.refs_4_, ...), custom_call_target="tpu_custom_call" | custom-call | bytes 1024 | tf_op jit(solution)/shard_map/pallas_call | solution.py:346
  37.0 0.0 copy-start.2
  37.0 0.0 copy-start.3
  37.0 4.6 %collective-permute-done.5.refs_0_ = bf16[25,64,128]{2,1,0:T(8,128)(2,1)S(1)} collective-permute-done((bf16[25,64,128]{2,1,0:T(8,128)(2,1)}, bf16[25,64,128]{2,1,0:T(8,128)(2,1)S(1)}, u32[]{:S(2)}, u32[]{:S(2)}) %collective-permute-start.5) | collective-permute-done | bytes 409632 | tf_op jit(solution)/shard_map/ppermute | solution.py:380
  41.6 1.8 %collective-permute-done.6.refs_1_ = bf16[25,64,128]{2,1,0:T(8,128)(2,1)S(1)} collective-permute-done((bf16[25,64,128]{2,1,0:T(8,128)(2,1)}, bf16[25,64,128]{2,1,0:T(8,128)(2,1)S(1)}, u32[]{:S(2)}, u32[]{:S(2)}) %collective-permute-start.6) | collective-permute-done | bytes 409632 | tf_op jit(solution)/shard_map/ppermute | solution.py:380
  43.4 0.5 collective-permute-start.8
  44.0 1.5 %collective-permute-start.17 = (bf16[49,64,128]{2,1,0:T(8,128)(2,1)S(1)}, bf16[49,64,128]{2,1,0:T(8,128)(2,1)S(1)}, u32[]{:S(2)}, u32[]{:S(2)}) collective-permute-start(bf16[49,64,128]{2,1,0:T(8,128)(2,1)S(1)} %get-tuple-element.80), channel_id=1, source_target_pairs={{0,2},{2,4},{4,6},{6,8},{8,10},{10,12},{12,14},{14,16},{16,18},{18... | collective-permute-start | bytes 2408456 | tf_op jit(solution)/shard_map/ppermute | solution.py:380
  45.4 4.1 %collective-permute-start.18 = (bf16[49,64,128]{2,1,0:T(8,128)(2,1)S(1)}, bf16[49,64,128]{2,1,0:T(8,128)(2,1)S(1)}, u32[]{:S(2)}, u32[]{:S(2)}) collective-permute-start(bf16[49,64,128]{2,1,0:T(8,128)(2,1)S(1)} %get-tuple-element.81), channel_id=1, source_target_pairs={{0,30},{2,0},{4,2},{6,4},{8,6},{10,8},{12,10},{14,12},{16,14},{18,... | collective-permute-start | bytes 2408456 | tf_op jit(solution)/shard_map/ppermute | solution.py:380
  49.6 3.8 %shard_map.90 = (bf16[25,192,256]{2,1,0:T(8,128)(2,1)S(1)}, f32[4,16,256]{2,1,0:T(8,128)}, f32[176,128]{1,0:T(8,128)S(1)}, f32[176,128]{1,0:T(8,128)S(1)}) custom-call(bf16[25,64,128]{2,1,0:T(8,128)(2,1)S(1)} %get-tuple-element.57.refs_0_.refs_7_, bf16[25,64,128]{2,1,0:T(8,128)(2,1)S(1)} %collective-permute-done.7.refs_1_.refs_8_, ...), custom_call_target="tpu_custom_call" | custom-call | bytes 1024 | tf_op jit(solution)/shard_map/pallas_call | solution.py:346
  53.4 7.7 %shard_map.91 = (bf16[49,64,256]{2,1,0:T(8,128)(2,1)S(1)}, f32[49,64,256]{2,1,0:T(8,128)S(1)}, f32[49,64,256]{2,1,0:T(8,128)S(1)}, f32[21,16,128]{2,1,0:T(8,128)...) custom-call(s32[3]{0:T(128)S(1)} %pad_add_fusion.refs_0_, ...), custom_call_target="tpu_custom_call" | custom-call | bytes 1024 | tf_op jit(solution)/shard_map/pallas_call | solution.py:346
  61.1 0.1 collective-permute-start.9
  61.2 0.3 collective-permute-start.10
  61.5 3.2 %collective-permute-start.11 = (bf16[21,16,128]{2,1,0:T(8,128)(2,1)S(1)}, bf16[21,16,128]{2,1,0:T(8,128)(2,1)S(1)}, u32[]{:S(2)}, u32[]{:S(2)}) collective-permute-start(bf16[21,16,128]{2,1,0:T(8,128)(2,1)S(1)} %get-tuple-element.71), channel_id=1, source_target_pairs={{0,12},{2,14},{4,8},{6,10},{8,4},{10,6},{12,0},{14,2},{16,28},{18,... | collective-permute-start | bytes 258056 | tf_op jit(solution)/shard_map/ppermute | solution.py:385
  64.7 6.5 %collective-permute-done.9.refs_1_ = bf16[21,16,128]{2,1,0:T(8,128)(2,1)S(1)} collective-permute-done((bf16[21,16,128]{2,1,0:T(8,128)(2,1)S(1)}, bf16[21,16,128]{2,1,0:T(8,128)(2,1)S(1)}, u32[]{:S(2)}, u32[]{:S(2)}) %collective-permute-start.9) | collective-permute-done | bytes 86048 | tf_op jit(solution)/shard_map/ppermute | solution.py:385
  71.3 1.9 %collective-permute-start.12 = (bf16[21,16,128]{2,1,0:T(8,128)(2,1)S(1)}, bf16[21,16,128]{2,1,0:T(8,128)(2,1)S(1)}, u32[]{:S(2)}, u32[]{:S(2)}) collective-permute-start(bf16[21,16,128]{2,1,0:T(8,128)(2,1)S(1)} %get-tuple-element.73), channel_id=1, source_target_pairs={{0,16},{2,18},{4,20},{6,22},{8,24},{10,26},{12,28},{14,30},{16,0},... | collective-permute-start | bytes 258056 | tf_op jit(solution)/shard_map/ppermute | solution.py:385
  73.2 3.4 %collective-permute-start.20 = (f32[176,128]{1,0:T(8,128)S(1)}, f32[176,128]{1,0:T(8,128)S(1)}, u32[]{:S(2)}, u32[]{:S(2)}) collective-permute-start(f32[176,128]{1,0:T(8,128)S(1)} %get-tuple-element.66.refs_16_), channel_id=1, source_target_pairs={{0,30},{2,0},{4,2},{6,4},{8,6},{10,8},{12,10},{14,12},{16,14},{18,... | collective-permute-start | bytes 270344 | tf_op jit(solution)/shard_map/ppermute | solution.py:380
  76.7 0.0 collective-permute-start.19
  76.7 1.0 collective-permute-done.12
  77.7 1.3 %collective-permute-start.13 = (bf16[21,16,128]{2,1,0:T(8,128)(2,1)S(1)}, bf16[21,16,128]{2,1,0:T(8,128)(2,1)S(1)}, u32[]{:S(2)}, u32[]{:S(2)}) collective-permute-start(bf16[21,16,128]{2,1,0:T(8,128)(2,1)S(1)} %get-tuple-element.91), channel_id=1, source_target_pairs={{0,18},{2,16},{4,22},{6,20},{8,26},{10,24},{12,30},{14,28},{16,2},... | collective-permute-start | bytes 258056 | tf_op jit(solution)/shard_map/ppermute | solution.py:385
  79.0 6.1 %collective-permute-done.13.refs_1_ = bf16[21,16,128]{2,1,0:T(8,128)(2,1)S(1)} collective-permute-done((bf16[21,16,128]{2,1,0:T(8,128)(2,1)S(1)}, bf16[21,16,128]{2,1,0:T(8,128)(2,1)S(1)}, u32[]{:S(2)}, u32[]{:S(2)}) %collective-permute-start.13) | collective-permute-done | bytes 86048 | tf_op jit(solution)/shard_map/ppermute | solution.py:385
  85.1 0.7 shard_map.93
  85.8 2.3 %collective-permute-start.16 = (bf16[21,16,128]{2,1,0:T(8,128)(2,1)S(1)}, bf16[21,16,128]{2,1,0:T(8,128)(2,1)S(1)}, u32[]{:S(2)}, u32[]{:S(2)}) collective-permute-start(bf16[21,16,128]{2,1,0:T(8,128)(2,1)S(1)} %get-tuple-element.74.refs_9_.refs_1_), channel_id=1, source_target_pairs={{0,12},{2,14},{4,8},{6,10},{8,4},{10,6},{12,0},{14,2},{16,28},{18,... | collective-permute-start | bytes 258056 | tf_op jit(solution)/shard_map/ppermute | solution.py:385
  88.1 2.3 %collective-permute-start.15 = (bf16[21,16,128]{2,1,0:T(8,128)(2,1)S(1)}, bf16[21,16,128]{2,1,0:T(8,128)(2,1)S(1)}, u32[]{:S(2)}, u32[]{:S(2)}) collective-permute-start(bf16[21,16,128]{2,1,0:T(8,128)(2,1)S(1)} %get-tuple-element.74.refs_9_.refs_1_), channel_id=1, source_target_pairs={{0,8},{2,10},{4,12},{6,14},{8,0},{10,2},{12,4},{14,6},{16,24},{18,... | collective-permute-start | bytes 258056 | tf_op jit(solution)/shard_map/ppermute | solution.py:385
  90.4 0.2 collective-permute-start.14
  90.6 2.6 %shard_map.95 = (f32[24,64,256]{2,1,0:T(8,128)S(1)}, bf16[24,64,256]{2,1,0:T(8,128)(2,1)S(1)}, f32[8,128]{1,0:T(8,128)S(1)}) custom-call(bf16[49,64,256]{2,1,0:T(8,128)(2,1)S(1)} %get-tuple-element.75.refs_0_, f32[49,64,256]{2,1,0:T(8,128)S(1)} %get-tuple-element.76.refs_1_, f32[49,64,256]{2,1,0:T(8,128)S(1)} %get-tuple-element.77.refs_2_, ...), custom_call_target="tpu_custom_call" | custom-call | bytes 1024 | tf_op jit(solution)/shard_map/pallas_call | solution.py:346
  93.2 0.6 collective-permute-done.15.refs_11_.refs_3_
  93.8 1.1 %collective-permute-done.14.refs_10_.refs_2_ = bf16[21,16,128]{2,1,0:T(8,128)(2,1)S(1)} collective-permute-done((bf16[21,16,128]{2,1,0:T(8,128)(2,1)S(1)}, bf16[21,16,128]{2,1,0:T(8,128)(2,1)S(1)}, u32[]{:S(2)}, u32[]{:S(2)}) %collective-permute-start.14) | collective-permute-done | bytes 86048 | tf_op jit(solution)/shard_map/ppermute | solution.py:385
  94.9 2.6 %shard_map.96 = (f32[25,64,256]{2,1,0:T(8,128)S(1)}, bf16[25,64,256]{2,1,0:T(8,128)(2,1)S(1)}, f32[8,128]{1,0:T(8,128)}) custom-call(bf16[49,64,256]{2,1,0:T(8,128)(2,1)S(1)} %get-tuple-element.75.refs_0_, f32[49,64,256]{2,1,0:T(8,128)S(1)} %get-tuple-element.76.refs_1_, f32[49,64,256]{2,1,0:T(8,128)S(1)} %get-tuple-element.77.refs_2_, ...), custom_call_target="tpu_custom_call" | custom-call | bytes 1024 | tf_op jit(solution)/shard_map/pallas_call | solution.py:346
  97.5 0.1 collective-permute-start.22
  97.5 0.5 collective-permute-start.21
  98.0 2.9 %collective-permute-done.21.refs_6_ = bf16[24,64,256]{2,1,0:T(8,128)(2,1)S(1)} collective-permute-done((bf16[24,64,256]{2,1,0:T(8,128)(2,1)S(1)}, bf16[24,64,256]{2,1,0:T(8,128)(2,1)S(1)}, u32[]{:S(2)}, u32[]{:S(2)}) %collective-permute-start.21) | collective-permute-done | bytes 786464 | tf_op jit(solution)/shard_map/ppermute | solution.py:380
  101.0 2.2 %shard_map.97 = (bf16[49,64,256]{2,1,0:T(8,128)(2,1)}, f32[21,64,128]{2,1,0:T(8,128)}) custom-call(s32[3]{0:T(128)S(1)} %pad_add_fusion.refs_0_, bf16[21,16,128]{2,1,0:T(8,128)(2,1)S(1)} %get-tuple-element.74.refs_9_.refs_1_, bf16[21,16,128]{2,1,0:T(8,128)(2,1)S(1)} %collective-permute-done.14.refs_10_.refs_2_, ...), custom_call_target="tpu_custom_call" | custom-call | bytes 1024 | tf_op jit(solution)/shard_map/pallas_call | solution.py:346
  (25 shorter events, 0.1 us)
Async XLA Ops:
  0.6 15.5 %copy-start.5 = (s32[16,256]{1,0:T(8,128)S(1)}, s32[16,256]{1,0:T(8,128)}, u32[]{:S(2)}) copy-start(s32[16,256]{1,0:T(8,128)} %refs_5_.1) | copy-start | bytes 49156
  0.6 15.5 %copy-start = (bf16[64,49,256]{2,0,1:T(8,128)(2,1)S(1)}, bf16[64,49,256]{2,0,1:T(8,128)(2,1)}, u32[]{:S(2)}) copy-start(bf16[64,49,256]{2,0,1:T(8,128)(2,1)} %param.8) | copy-start | bytes 4816900
  0.7 15.5 %collective-permute-start = (bf16[49,64,256]{2,1,0:T(8,128)(2,1)}, bf16[49,64,256]{2,1,0:T(8,128)(2,1)}, u32[]{:S(2)}, u32[]{:S(2)}) collective-permute-start(bf16[49,64,256]{2,1,0:T(8,128)(2,1)} %bitcast.14), channel_id=1, source_target_pairs={{0,1},{1,0},{2,3},{3,2},{4,5},{5,4},{6,7},{7,6},{8,9},{9,8},{10,11... | collective-permute-start | bytes 4816904 | tf_op jit(solution)/shard_map/ppermute | solution.py:380
  3.7 29.7 %collective-permute-start.1 = (bf16[24,64,128]{2,1,0:T(8,128)(2,1)}, bf16[24,64,128]{2,1,0:T(8,128)(2,1)S(1)}, u32[]{:S(2)}, u32[]{:S(2)}) collective-permute-start(bf16[24,64,128]{2,1,0:T(8,128)(2,1)} %get-tuple-element.47), channel_id=1, source_target_pairs={{0,2},{2,4},{4,6},{6,8},{8,10},{10,12},{12,14},{14,16},{16,18},{18... | collective-permute-start | bytes 1179656 | tf_op jit(solution)/shard_map/ppermute | solution.py:380
  6.4 27.0 %collective-permute-start.2 = (bf16[24,64,128]{2,1,0:T(8,128)(2,1)}, bf16[24,64,128]{2,1,0:T(8,128)(2,1)S(1)}, u32[]{:S(2)}, u32[]{:S(2)}) collective-permute-start(bf16[24,64,128]{2,1,0:T(8,128)(2,1)} %get-tuple-element.48), channel_id=1, source_target_pairs={{0,30},{2,0},{4,2},{6,4},{8,6},{10,8},{12,10},{14,12},{16,14},{18,... | collective-permute-start | bytes 1179656 | tf_op jit(solution)/shard_map/ppermute | solution.py:380
  10.5 31.1 %collective-permute-start.5 = (bf16[25,64,128]{2,1,0:T(8,128)(2,1)}, bf16[25,64,128]{2,1,0:T(8,128)(2,1)S(1)}, u32[]{:S(2)}, u32[]{:S(2)}) collective-permute-start(bf16[25,64,128]{2,1,0:T(8,128)(2,1)} %get-tuple-element.52), channel_id=1, source_target_pairs={{0,2},{2,4},{4,6},{6,8},{8,10},{10,12},{12,14},{14,16},{16,18},{18... | collective-permute-start | bytes 1228808 | tf_op jit(solution)/shard_map/ppermute | solution.py:380
  10.5 33.0 %collective-permute-start.6 = (bf16[25,64,128]{2,1,0:T(8,128)(2,1)}, bf16[25,64,128]{2,1,0:T(8,128)(2,1)S(1)}, u32[]{:S(2)}, u32[]{:S(2)}) collective-permute-start(bf16[25,64,128]{2,1,0:T(8,128)(2,1)} %get-tuple-element.53), channel_id=1, source_target_pairs={{0,30},{2,0},{4,2},{6,4},{8,6},{10,8},{12,10},{14,12},{16,14},{18,... | collective-permute-start | bytes 1228808 | tf_op jit(solution)/shard_map/ppermute | solution.py:380
  16.2 1.4 %copy-start.1 = (bf16[64,49,256]{2,0,1:T(8,128)(2,1)S(1)}, bf16[64,49,256]{2,0,1:T(8,128)(2,1)}, u32[]{:S(2)}) copy-start(bf16[64,49,256]{2,0,1:T(8,128)(2,1)} %param.6) | copy-start | bytes 4816900
  17.6 1.0 copy-start.4
  33.4 1.7 %collective-permute-start.3 = (bf16[24,64,128]{2,1,0:T(8,128)(2,1)S(1)}, bf16[24,64,128]{2,1,0:T(8,128)(2,1)S(1)}, u32[]{:S(2)}, u32[]{:S(2)}) collective-permute-start(bf16[24,64,128]{2,1,0:T(8,128)(2,1)S(1)} %get-tuple-element.50.refs_0_.refs_3_), channel_id=1, source_target_pairs={{0,1},{1,0},{2,3},{3,2},{4,5},{5,4},{6,7},{7,6},{8,9},{9,8},{10,11... | collective-permute-start | bytes 1179656 | tf_op jit(solution)/shard_map/ppermute | solution.py:380
  33.4 2.3 %collective-permute-start.4 = (bf16[24,64,128]{2,1,0:T(8,128)(2,1)S(1)}, bf16[24,64,128]{2,1,0:T(8,128)(2,1)S(1)}, u32[]{:S(2)}, u32[]{:S(2)}) collective-permute-start(bf16[24,64,128]{2,1,0:T(8,128)(2,1)S(1)} %get-tuple-element.51.refs_2_.refs_5_), channel_id=1, source_target_pairs={{0,1},{1,0},{2,3},{3,2},{4,5},{5,4},{6,7},{7,6},{8,9},{9,8},{10,11... | collective-permute-start | bytes 1179656 | tf_op jit(solution)/shard_map/ppermute | solution.py:380
  37.0 12.6 %copy-start.2 = (f32[4,16,256]{2,1,0:T(8,128)S(1)}, f32[4,16,256]{2,1,0:T(8,128)}, u32[]{:S(2)}) copy-start(f32[4,16,256]{2,1,0:T(8,128)} %refs_9_.1) | copy-start | bytes 196612
  37.0 12.6 %copy-start.3 = (s32[16,256]{1,0:T(8,128)S(1)}, s32[16,256]{1,0:T(8,128)}, u32[]{:S(2)}) copy-start(s32[16,256]{1,0:T(8,128)} %refs_10_.1) | copy-start | bytes 49156
  43.4 6.1 %collective-permute-start.7 = (bf16[25,64,128]{2,1,0:T(8,128)(2,1)S(1)}, bf16[25,64,128]{2,1,0:T(8,128)(2,1)S(1)}, u32[]{:S(2)}, u32[]{:S(2)}) collective-permute-start(bf16[25,64,128]{2,1,0:T(8,128)(2,1)S(1)} %get-tuple-element.57.refs_0_.refs_7_), channel_id=1, source_target_pairs={{0,1},{1,0},{2,3},{3,2},{4,5},{5,4},{6,7},{7,6},{8,9},{9,8},{10,11... | collective-permute-start | bytes 1228808 | tf_op jit(solution)/shard_map/ppermute | solution.py:380
  43.4 6.1 %collective-permute-start.8 = (bf16[25,64,128]{2,1,0:T(8,128)(2,1)S(1)}, bf16[25,64,128]{2,1,0:T(8,128)(2,1)S(1)}, u32[]{:S(2)}, u32[]{:S(2)}) collective-permute-start(bf16[25,64,128]{2,1,0:T(8,128)(2,1)S(1)} %get-tuple-element.58.refs_2_.refs_9_), channel_id=1, source_target_pairs={{0,1},{1,0},{2,3},{3,2},{4,5},{5,4},{6,7},{7,6},{8,9},{9,8},{10,11... | collective-permute-start | bytes 1228808 | tf_op jit(solution)/shard_map/ppermute | solution.py:380
  44.0 46.7 %collective-permute-start.17 = (bf16[49,64,128]{2,1,0:T(8,128)(2,1)S(1)}, bf16[49,64,128]{2,1,0:T(8,128)(2,1)S(1)}, u32[]{:S(2)}, u32[]{:S(2)}) collective-permute-start(bf16[49,64,128]{2,1,0:T(8,128)(2,1)S(1)} %get-tuple-element.80), channel_id=1, source_target_pairs={{0,2},{2,4},{4,6},{6,8},{8,10},{10,12},{12,14},{14,16},{16,18},{18... | collective-permute-start | bytes 2408456 | tf_op jit(solution)/shard_map/ppermute | solution.py:380
  45.4 45.2 %collective-permute-start.18 = (bf16[49,64,128]{2,1,0:T(8,128)(2,1)S(1)}, bf16[49,64,128]{2,1,0:T(8,128)(2,1)S(1)}, u32[]{:S(2)}, u32[]{:S(2)}) collective-permute-start(bf16[49,64,128]{2,1,0:T(8,128)(2,1)S(1)} %get-tuple-element.81), channel_id=1, source_target_pairs={{0,30},{2,0},{4,2},{6,4},{8,6},{10,8},{12,10},{14,12},{16,14},{18,... | collective-permute-start | bytes 2408456 | tf_op jit(solution)/shard_map/ppermute | solution.py:380
  61.1 10.1 %collective-permute-start.9 = (bf16[21,16,128]{2,1,0:T(8,128)(2,1)S(1)}, bf16[21,16,128]{2,1,0:T(8,128)(2,1)S(1)}, u32[]{:S(2)}, u32[]{:S(2)}) collective-permute-start(bf16[21,16,128]{2,1,0:T(8,128)(2,1)S(1)} %get-tuple-element.69), channel_id=1, source_target_pairs={{0,4},{2,6},{4,0},{6,2},{8,12},{10,14},{12,8},{14,10},{16,20},{18,... | collective-permute-start | bytes 258056 | tf_op jit(solution)/shard_map/ppermute | solution.py:385
  61.2 10.0 %collective-permute-start.10 = (bf16[21,16,128]{2,1,0:T(8,128)(2,1)S(1)}, bf16[21,16,128]{2,1,0:T(8,128)(2,1)S(1)}, u32[]{:S(2)}, u32[]{:S(2)}) collective-permute-start(bf16[21,16,128]{2,1,0:T(8,128)(2,1)S(1)} %get-tuple-element.70), channel_id=1, source_target_pairs={{0,8},{2,10},{4,12},{6,14},{8,0},{10,2},{12,4},{14,6},{16,24},{18,... | collective-permute-start | bytes 258056 | tf_op jit(solution)/shard_map/ppermute | solution.py:385
  61.5 9.7 %collective-permute-start.11 = (bf16[21,16,128]{2,1,0:T(8,128)(2,1)S(1)}, bf16[21,16,128]{2,1,0:T(8,128)(2,1)S(1)}, u32[]{:S(2)}, u32[]{:S(2)}) collective-permute-start(bf16[21,16,128]{2,1,0:T(8,128)(2,1)S(1)} %get-tuple-element.71), channel_id=1, source_target_pairs={{0,12},{2,14},{4,8},{6,10},{8,4},{10,6},{12,0},{14,2},{16,28},{18,... | collective-permute-start | bytes 258056 | tf_op jit(solution)/shard_map/ppermute | solution.py:385
  71.3 6.4 %collective-permute-start.12 = (bf16[21,16,128]{2,1,0:T(8,128)(2,1)S(1)}, bf16[21,16,128]{2,1,0:T(8,128)(2,1)S(1)}, u32[]{:S(2)}, u32[]{:S(2)}) collective-permute-start(bf16[21,16,128]{2,1,0:T(8,128)(2,1)S(1)} %get-tuple-element.73), channel_id=1, source_target_pairs={{0,16},{2,18},{4,20},{6,22},{8,24},{10,26},{12,28},{14,30},{16,0},... | collective-permute-start | bytes 258056 | tf_op jit(solution)/shard_map/ppermute | solution.py:385
  73.2 14.8 %collective-permute-start.20 = (f32[176,128]{1,0:T(8,128)S(1)}, f32[176,128]{1,0:T(8,128)S(1)}, u32[]{:S(2)}, u32[]{:S(2)}) collective-permute-start(f32[176,128]{1,0:T(8,128)S(1)} %get-tuple-element.66.refs_16_), channel_id=1, source_target_pairs={{0,30},{2,0},{4,2},{6,4},{8,6},{10,8},{12,10},{14,12},{16,14},{18,... | collective-permute-start | bytes 270344 | tf_op jit(solution)/shard_map/ppermute | solution.py:380
  76.7 13.7 %collective-permute-start.19 = (f32[176,128]{1,0:T(8,128)S(1)}, f32[176,128]{1,0:T(8,128)S(1)}, u32[]{:S(2)}, u32[]{:S(2)}) collective-permute-start(f32[176,128]{1,0:T(8,128)S(1)} %get-tuple-element.67.refs_17_), channel_id=1, source_target_pairs={{0,2},{2,4},{4,6},{6,8},{8,10},{10,12},{12,14},{14,16},{16,18},{18... | collective-permute-start | bytes 270344 | tf_op jit(solution)/shard_map/ppermute | solution.py:380
  77.7 7.3 %collective-permute-start.13 = (bf16[21,16,128]{2,1,0:T(8,128)(2,1)S(1)}, bf16[21,16,128]{2,1,0:T(8,128)(2,1)S(1)}, u32[]{:S(2)}, u32[]{:S(2)}) collective-permute-start(bf16[21,16,128]{2,1,0:T(8,128)(2,1)S(1)} %get-tuple-element.91), channel_id=1, source_target_pairs={{0,18},{2,16},{4,22},{6,20},{8,26},{10,24},{12,30},{14,28},{16,2},... | collective-permute-start | bytes 258056 | tf_op jit(solution)/shard_map/ppermute | solution.py:385
  85.8 7.4 %collective-permute-start.16 = (bf16[21,16,128]{2,1,0:T(8,128)(2,1)S(1)}, bf16[21,16,128]{2,1,0:T(8,128)(2,1)S(1)}, u32[]{:S(2)}, u32[]{:S(2)}) collective-permute-start(bf16[21,16,128]{2,1,0:T(8,128)(2,1)S(1)} %get-tuple-element.74.refs_9_.refs_1_), channel_id=1, source_target_pairs={{0,12},{2,14},{4,8},{6,10},{8,4},{10,6},{12,0},{14,2},{16,28},{18,... | collective-permute-start | bytes 258056 | tf_op jit(solution)/shard_map/ppermute | solution.py:385
  88.1 5.7 %collective-permute-start.15 = (bf16[21,16,128]{2,1,0:T(8,128)(2,1)S(1)}, bf16[21,16,128]{2,1,0:T(8,128)(2,1)S(1)}, u32[]{:S(2)}, u32[]{:S(2)}) collective-permute-start(bf16[21,16,128]{2,1,0:T(8,128)(2,1)S(1)} %get-tuple-element.74.refs_9_.refs_1_), channel_id=1, source_target_pairs={{0,8},{2,10},{4,12},{6,14},{8,0},{10,2},{12,4},{14,6},{16,24},{18,... | collective-permute-start | bytes 258056 | tf_op jit(solution)/shard_map/ppermute | solution.py:385
  90.4 4.5 %collective-permute-start.14 = (bf16[21,16,128]{2,1,0:T(8,128)(2,1)S(1)}, bf16[21,16,128]{2,1,0:T(8,128)(2,1)S(1)}, u32[]{:S(2)}, u32[]{:S(2)}) collective-permute-start(bf16[21,16,128]{2,1,0:T(8,128)(2,1)S(1)} %get-tuple-element.74.refs_9_.refs_1_), channel_id=1, source_target_pairs={{0,4},{2,6},{4,0},{6,2},{8,12},{10,14},{12,8},{14,10},{16,20},{18,... | collective-permute-start | bytes 258056 | tf_op jit(solution)/shard_map/ppermute | solution.py:385
  97.5 3.5 %collective-permute-start.22 = (bf16[25,64,256]{2,1,0:T(8,128)(2,1)S(1)}, bf16[25,64,256]{2,1,0:T(8,128)(2,1)S(1)}, u32[]{:S(2)}, u32[]{:S(2)}) collective-permute-start(bf16[25,64,256]{2,1,0:T(8,128)(2,1)S(1)} %get-tuple-element.87), channel_id=1, source_target_pairs={{0,1},{1,0},{2,3},{3,2},{4,5},{5,4},{6,7},{7,6},{8,9},{9,8},{10,11... | collective-permute-start | bytes 2457608 | tf_op jit(solution)/shard_map/ppermute | solution.py:380
  97.5 3.4 %collective-permute-start.21 = (bf16[24,64,256]{2,1,0:T(8,128)(2,1)S(1)}, bf16[24,64,256]{2,1,0:T(8,128)(2,1)S(1)}, u32[]{:S(2)}, u32[]{:S(2)}) collective-permute-start(bf16[24,64,256]{2,1,0:T(8,128)(2,1)S(1)} %get-tuple-element.84), channel_id=1, source_target_pairs={{0,1},{1,0},{2,3},{3,2},{4,5},{5,4},{6,7},{7,6},{8,9},{9,8},{10,11... | collective-permute-start | bytes 2359304 | tf_op jit(solution)/shard_map/ppermute | solution.py:380
